TPU v7x, 512 devices: a whole 4x8x8 slice. The times are simulated.
512 devices in a mesh: lat: 16 (over y_hi, z), lon: 32 (over y_lo, x, core).
Axes of the slice: x: 4, y: 8 (y_hi: 2, y_lo: 4; y = y_hi * 4 + y_lo), z: 8, core: 2. Of those that a mesh axis runs over, the one named last changes fastest.
Arguments:
- tokens: bfloat16 [128, 512, 1152], P('lat', 'lon'), may hold values from -8 to 8
- gain: float32 [1152], replicated, may hold values from 0.25 to 1.75
- w_query: bfloat16 [1152, 576], P('lat'), may hold values from -1 to 1
- w_key: bfloat16 [1152, 576], P('lat'), may hold values from -1 to 1
- w_value: bfloat16 [1152, 576], P('lat'), may hold values from -0.1875 to 0.1875
- w_out: bfloat16 [576, 1152], P('lat'), may hold values from -0.25 to 0.25
- w_pixel: bfloat16 [1152, 192], replicated, may hold values from -0.1875 to 0.1875
- measured: float32 [128, 512, 64], P('lat', 'lon'), may hold values from -6 to 6
- filter_color: int32 [128, 512, 64], P('lat', 'lon'), may hold values from 0 to 2
- block_mask: int32 [16, 64, 3, 5], P('lat', 'lon'), may hold values from 0 to 1, as said below
Outputs:
- denoised: bfloat16 [128, 512, 1152], P('lat', 'lon')
- guidance: float32 [128, 512, 1152], P('lat', 'lon')
Inputs may be any that keep to these rules, and one draw needn't show every extreme that they name: For each query block and row offset r the ones form one run of offsets centred on o = 2, of half-length 0 to 2; entries whose key block row a + r - 1 lies outside 0..15 are 0; block_mask[a, c, 1, 2] is 1.
All inputs are finite; a program needn't handle non-finite values.
Results may differ from a plain program's by a relative error of at most 0.028.
Values may be sent and summed in bfloat16 or wider, within the bound.
No kernel may reach another device: no remote copies, remote signals or barrier semaphores. Data moves between devices by JAX's collectives and lax.ppermute only.
A program may use at most 64 MiB of HBM per device.

v0:
```python
import jax
import jax.numpy as jnp
from jax import lax
from jax.sharding import PartitionSpec as P

H = 8


def extended(x, sides, width, wrap):
    for axis, dim in sides:
        peers, length = (lax.axis_size(axis), x.shape[dim])
        up = [(i, (i + 1) % peers) for i in range(peers if wrap else peers - 1)]
        down = [(j, i) for i, j in up]
        last = lax.slice_in_dim(x, length - width, length, axis=dim)
        initial = lax.slice_in_dim(x, 0, width, axis=dim)
        before = lax.ppermute(last, axis, up)
        after = lax.ppermute(initial, axis, down)
        x = jnp.concatenate([before, x, after], axis=dim)
    return x


def layer_norm(values, gain):
    center = values - jnp.mean(values, axis=-1, keepdims=True)
    spread = jnp.mean(center * center, axis=-1, keepdims=True)
    return center * lax.rsqrt(spread + 1e-06) * gain


def token_mask(blocks, row_count, col_count):
    groups = col_count // 8
    spanned = 2 * groups + 1
    placed = jnp.zeros((groups, 3, 3 * groups), jnp.int32)
    for column in range(groups):
        placed = placed.at[column, :, column : column + spanned].set(blocks[column])
    placed = jnp.repeat(jnp.repeat(jnp.repeat(placed, 8, axis=0), 8, axis=1), 8, axis=2)
    placed = jnp.broadcast_to(placed[None], (row_count, col_count, 3 * row_count, 3 * col_count))
    return placed.reshape(row_count * col_count, 9 * row_count * col_count) > 0


def contract_last(left, right):
    return lax.dot_general(
        left, right, (((1,), (1,)), ((), ())), preferred_element_type=jnp.float32
    )


def contract_first(left, right):
    return lax.dot_general(
        left, right, (((0,), (0,)), ((), ())), preferred_element_type=jnp.float32
    )


def on_device(
    tokens, gain, w_query, w_key, w_value, w_out, w_pixel, measured, filter_color, block_mask
):
    row_count, col_count, model_width = tokens.shape
    token_count = row_count * col_count
    full_query, full_key, full_value, full_out = (
        lax.all_gather(w_query, "lat", axis=0, tiled=True),
        lax.all_gather(w_key, "lat", axis=0, tiled=True),
        lax.all_gather(w_value, "lat", axis=0, tiled=True),
        lax.all_gather(w_out, "lat", axis=0, tiled=True),
    )
    inner_width = full_query.shape[1]
    head_dim = inner_width // H
    factor = head_dim ** (-0.5)
    flat_tokens = tokens.astype(jnp.float32).reshape(token_count, model_width)
    normed, norm_back = jax.vjp(lambda entries: layer_norm(entries, gain), flat_tokens)
    hidden = normed.astype(jnp.bfloat16)
    queries = jnp.dot(hidden, full_query, preferred_element_type=jnp.float32).astype(jnp.bfloat16)
    keys = jnp.dot(hidden, full_key, preferred_element_type=jnp.float32).astype(jnp.bfloat16)
    values = jnp.dot(hidden, full_value, preferred_element_type=jnp.float32).astype(jnp.bfloat16)
    paired = jnp.concatenate([keys, values], axis=1).reshape(row_count, col_count, 2 * inner_width)
    banded = extended(paired, (("lat", 0),), row_count, False)
    window = extended(banded, (("lon", 1),), col_count, True)
    window = window.reshape(9 * token_count, 2 * inner_width)
    key_win = window[:, :inner_width]
    value_win = window[:, inner_width:]
    allowed = token_mask(block_mask[0], row_count, col_count)

    def head_scores(head_index):
        offset = head_index * head_dim
        query_h = lax.dynamic_slice_in_dim(queries, offset, head_dim, 1)
        key_h = lax.dynamic_slice_in_dim(key_win, offset, head_dim, 1)
        value_h = lax.dynamic_slice_in_dim(value_win, offset, head_dim, 1)
        scores = contract_last(query_h, key_h) * factor
        scores = jnp.where(allowed, scores, -1e30)
        row_peak = jnp.max(scores, axis=1, keepdims=True)
        row_total = jnp.sum(
            jnp.where(allowed, jnp.exp(scores - row_peak), 0.0), axis=1, keepdims=True
        )
        logsum = row_peak + jnp.log(row_total)
        probability = jnp.where(allowed, jnp.exp(scores - logsum), 0.0)
        return (query_h, key_h, value_h, probability)

    def forward(head_index, attended):
        query_h, key_h, value_h, probability = head_scores(head_index)
        piece_o = jnp.dot(
            probability.astype(jnp.bfloat16), value_h, preferred_element_type=jnp.float32
        ).astype(jnp.bfloat16)
        return lax.dynamic_update_slice_in_dim(attended, piece_o, head_index * head_dim, 1)

    attended = lax.fori_loop(0, H, forward, jnp.zeros((token_count, inner_width), jnp.bfloat16))
    denoised = (
        flat_tokens + jnp.dot(attended, full_out, preferred_element_type=jnp.float32)
    ).astype(jnp.bfloat16)
    colors = jnp.dot(denoised, w_pixel, preferred_element_type=jnp.float32).reshape(
        token_count, 3, -1
    )
    flat_filter = filter_color.reshape(token_count, -1)
    picked = flat_filter[:, None, :] == jnp.arange(3, dtype=jnp.int32)[None, :, None]
    predicted = jnp.sum(jnp.where(picked, colors, 0.0), axis=1)
    misfit = predicted - measured.reshape(token_count, -1)
    spread_back = (
        jnp.where(picked, misfit[:, None, :], 0.0).astype(jnp.bfloat16).reshape(token_count, -1)
    )
    outer_grad = contract_last(spread_back, w_pixel)
    upstream = contract_last(outer_grad.astype(jnp.bfloat16), full_out).astype(jnp.bfloat16)

    def backward(head_index, carry):
        grad_query, grad_key, grad_value = carry
        query_h, key_h, value_h, probability = head_scores(head_index)
        offset = head_index * head_dim
        up_h = lax.dynamic_slice_in_dim(upstream, offset, head_dim, 1)
        att_h = lax.dynamic_slice_in_dim(attended, offset, head_dim, 1)
        inner_sum = jnp.sum(up_h.astype(jnp.float32) * att_h.astype(jnp.float32), axis=1)
        dprob = contract_last(up_h, value_h)
        dscore = (probability * (dprob - inner_sum[:, None]) * factor).astype(jnp.bfloat16)
        piece_q = jnp.dot(dscore, key_h, preferred_element_type=jnp.float32).astype(jnp.bfloat16)
        piece_k = contract_first(dscore, query_h).astype(jnp.bfloat16)
        piece_v = contract_first(probability.astype(jnp.bfloat16), up_h).astype(jnp.bfloat16)
        grad_query = lax.dynamic_update_slice_in_dim(grad_query, piece_q, offset, 1)
        grad_key = lax.dynamic_update_slice_in_dim(grad_key, piece_k, offset, 1)
        grad_value = lax.dynamic_update_slice_in_dim(grad_value, piece_v, offset, 1)
        return (grad_query, grad_key, grad_value)

    window_zeros = jnp.zeros((9 * token_count, inner_width), jnp.bfloat16)
    grad_query, grad_key, grad_value = lax.fori_loop(
        0,
        H,
        backward,
        (jnp.zeros((token_count, inner_width), jnp.bfloat16), window_zeros, window_zeros),
    )
    returned = jnp.concatenate([grad_key, grad_value], axis=1).reshape(
        3 * row_count, 3 * col_count, 2 * inner_width
    )
    margins = jnp.concatenate([returned[:, :col_count], returned[:, 2 * col_count :]], axis=1)
    arrived = extended(margins, (("lon", 1),), col_count, True)
    middle = returned[:, col_count : 2 * col_count].astype(jnp.float32)
    middle = (
        middle
        + arrived[:, :col_count].astype(jnp.float32)
        + arrived[:, 3 * col_count :].astype(jnp.float32)
    )
    row_edges = jnp.concatenate([middle[:row_count], middle[2 * row_count :]], axis=0)
    landed = extended(row_edges.astype(jnp.bfloat16), (("lat", 0),), row_count, False).astype(
        row_edges.dtype
    )
    owned = middle[row_count : 2 * row_count] + landed[:row_count] + landed[3 * row_count :]
    owned = owned.reshape(token_count, 2 * inner_width)
    key_own = owned[:, :inner_width].astype(jnp.bfloat16)
    value_own = owned[:, inner_width:].astype(jnp.bfloat16)
    grad_hidden = (
        contract_last(grad_query, full_query)
        + contract_last(key_own, full_key)
        + contract_last(value_own, full_value)
    )
    guidance = norm_back(grad_hidden)[0] + outer_grad
    return (
        denoised.reshape(row_count, col_count, model_width),
        guidance.reshape(row_count, col_count, model_width),
    )


def solution(mesh):
    return jax.shard_map(
        on_device,
        mesh=mesh,
        in_specs=(
            P("lat", "lon", None),
            P(),
            P("lat", None),
            P("lat", None),
            P("lat", None),
            P("lat", None),
            P(),
            P("lat", "lon", None),
            P("lat", "lon", None),
            P("lat", "lon", None, None),
        ),
        out_specs=(P("lat", "lon", None), P("lat", "lon", None)),
        check_vma=False,
    )
```

profile of v0, /device:TPU:47, one launch (start us, length us, event | category | flops | bytes accessed | tf_op | source)
XLA Modules:
  0.0 549.4 jit_solution(2838408682413345109)
XLA Ops:
  13.6 92.4 %all-gather.10.cloned.1.call-done = bf16[1152,576]{1,0:T(8,128)(2,1)} async-done(((bf16[72,576]{1,0:T(8,128)(2,1)}), bf16[1152,576]{1,0:T(8,128)(2,1)}) %all-gather.10.cloned.1.call-update) | async-done | bytes 1327120 | tf_op jit(solution)/shard_map/all_gather | solution.py:59
  106.0 2.0 convolution_convert_fusion.5
  108.1 92.7 %all-gather.8.cloned.1.call-done = bf16[1152,576]{1,0:T(8,128)(2,1)} async-done(((bf16[72,576]{1,0:T(8,128)(2,1)}), bf16[1152,576]{1,0:T(8,128)(2,1)}) %all-gather.8.cloned.1.call-update) | async-done | bytes 1327120 | tf_op jit(solution)/shard_map/all_gather | solution.py:58
  200.8 2.0 convolution_convert_fusion.6
  203.1 7.4 %collective-permute-start.1 = (bf16[8,16,1152]{2,1,0:T(8,128)(2,1)S(1)}, bf16[8,16,1152]{2,1,0:T(8,128)(2,1)S(1)}, u32[]{:S(2)}, u32[]{:S(2)}) collective-permute-start(bf16[8,16,1152]{2,1,0:T(8,128)(2,1)S(1)} %bitcast.72), channel_id=1, source_target_pairs={{32,0},{64,32},{96,64},{128,96},{160,128},{192,160},{224,192},{256... | collective-permute-start | bytes 884744 | tf_op jit(solution)/shard_map/ppermute | solution.py:17
  210.5 1.9 collective-permute-start
  213.1 7.2 %collective-permute-done.1 = bf16[8,16,1152]{2,1,0:T(8,128)(2,1)S(1)} collective-permute-done((bf16[8,16,1152]{2,1,0:T(8,128)(2,1)S(1)}, bf16[8,16,1152]{2,1,0:T(8,128)(2,1)S(1)}, u32[]{:S(2)}, u32[]{:S(2)}) %collective-permute-start.1) | collective-permute-done | bytes 294944 | tf_op jit(solution)/shard_map/ppermute | solution.py:17
  220.3 11.8 %collective-permute-done = bf16[8,16,1152]{2,1,0:T(8,128)(2,1)S(1)} collective-permute-done((bf16[8,16,1152]{2,1,0:T(8,128)(2,1)S(1)}, bf16[8,16,1152]{2,1,0:T(8,128)(2,1)S(1)}, u32[]{:S(2)}, u32[]{:S(2)}) %collective-permute-start) | collective-permute-done | bytes 294944 | tf_op jit(solution)/shard_map/ppermute | solution.py:16
  232.3 4.2 collective-permute-start.3
  236.5 3.9 collective-permute-start.2
  241.2 61.4 %all-gather.6.cloned.1.call-done = bf16[1152,576]{1,0:T(8,128)(2,1)} async-done(((bf16[72,576]{1,0:T(8,128)(2,1)}), bf16[1152,576]{1,0:T(8,128)(2,1)}) %all-gather.6.cloned.1.call-update) | async-done | bytes 1327120 | tf_op jit(solution)/shard_map/all_gather | solution.py:57
  302.5 2.0 convolution_convert_fusion.7
  304.7 92.4 %all-gather.12.cloned.1.call-done = bf16[16,36,1152]{2,1,0:T(8,128)(2,1)} async-done(((bf16[1,36,1152]{2,1,0:T(8,128)(2,1)}), bf16[16,36,1152]{2,1,0:T(8,128)(2,1)}) %all-gather.12.cloned.1.call-update) | async-done | bytes 1327120 | tf_op jit(solution)/shard_map/all_gather | solution.py:60
  397.1 3.2 reshape.217
  400.4 2.7 pad_maximum_fusion
  403.1 1.9 fusion.48
  405.0 24.7 %while.34 = (s32[]{:T(128)}, bf16[128,576]{0,1:T(8,128)(2,1)S(1)}, bf16[128,576]{1,0:T(8,128)(2,1)S(1)}, bf16[1152,576]{1,0:T(8,128)(2,1)S(1)}, bf16[1152,576]{1...) while((s32[]{:T(128)}, bf16[128,576]{0,1:T(8,128)(2,1)S(1)}, ...), condition=%wide.region_5.0_spmd.clone, body=%wide.region_2.5_spmd.clone.sunk | while | flops 43803524 | bytes 3319443 | solution.py:101
  406.6 1.5 fusion.88
  409.7 1.5 fusion.88
  412.8 1.5 fusion.88
  415.9 1.5 fusion.88
  419.0 1.5 fusion.88
  422.0 1.5 fusion.88
  425.1 1.5 fusion.88
  428.2 1.5 fusion.88
  429.8 1.8 fusion.36
  434.5 1.3 broadcast_in_dim.97.clone
  436.9 51.7 %while.35 = (s32[]{:T(128)}, bf16[128,576]{0,1:T(8,128)(2,1)}, bf16[1152,576]{0,1:T(8,128)(2,1)}, bf16[1152,576]{0,1:T(8,128)(2,1)}, bf16[128,576]{1,0:T(8,128)(...) while((s32[]{:T(128)}, bf16[128,576]{0,1:T(8,128)(2,1)}, ...), condition=%wide.region_11.12_spmd.clone, body=%wide.region_7.11_spmd.clone.sunk | while | flops 108591872 | bytes 5826743 | solution.py:136
  438.8 1.5 fusion.96
  445.3 1.5 fusion.96
  451.7 1.5 fusion.96
  458.2 1.5 fusion.96
  464.6 1.5 fusion.96
  471.1 1.5 fusion.96
  477.6 1.5 fusion.96
  484.0 1.5 fusion.96
  488.6 2.2 copy.83
  490.8 1.7 copy.82
  492.5 2.2 pad_maximum_fusion.1
  494.9 7.5 %collective-permute-start.4 = (bf16[24,16,1152]{2,1,0:T(8,128)(2,1)S(1)}, bf16[24,16,1152]{2,1,0:T(8,128)(2,1)S(1)}, u32[]{:S(2)}, u32[]{:S(2)}) collective-permute-start(bf16[24,16,1152]{2,1,0:T(8,128)(2,1)S(1)} %get-tuple-element.484), channel_id=1, source_target_pairs={{0,1},{1,2},{2,3},{3,4},{4,5},{5,6},{6,7},{7,8},{8,9},{9,10},{10,1... | collective-permute-start | bytes 2654216 | tf_op jit(solution)/shard_map/ppermute | solution.py:16
  502.4 1.9 collective-permute-start.5
  504.3 8.0 %collective-permute-done.4 = bf16[24,16,1152]{2,1,0:T(8,128)(2,1)S(1)} collective-permute-done((bf16[24,16,1152]{2,1,0:T(8,128)(2,1)S(1)}, bf16[24,16,1152]{2,1,0:T(8,128)(2,1)S(1)}, u32[]{:S(2)}, u32[]{:S(2)}) %collective-permute-start.4) | collective-permute-done | bytes 884768 | tf_op jit(solution)/shard_map/ppermute | solution.py:16
  512.3 6.5 %collective-permute-done.5 = bf16[24,16,1152]{2,1,0:T(8,128)(2,1)S(1)} collective-permute-done((bf16[24,16,1152]{2,1,0:T(8,128)(2,1)S(1)}, bf16[24,16,1152]{2,1,0:T(8,128)(2,1)S(1)}, u32[]{:S(2)}, u32[]{:S(2)}) %collective-permute-start.5) | collective-permute-done | bytes 884768 | tf_op jit(solution)/shard_map/ppermute | solution.py:17
  519.3 2.3 collective-permute-start.6
  521.5 9.2 %collective-permute-start.7 = (bf16[8,16,1152]{2,1,0:T(8,128)(2,1)S(1)}, bf16[8,16,1152]{2,1,0:T(8,128)(2,1)S(1)}, u32[]{:S(2)}, u32[]{:S(2)}) collective-permute-start(bf16[8,16,1152]{2,1,0:T(8,128)(2,1)S(1)} %get-tuple-element.489), channel_id=1, source_target_pairs={{32,0},{64,32},{96,64},{128,96},{160,128},{192,160},{224,192},{256... | collective-permute-start | bytes 884744 | tf_op jit(solution)/shard_map/ppermute | solution.py:17
  530.7 1.5 fusion.52
  532.2 5.2 collective-permute-done.6
  537.4 1.8 collective-permute-done.7
  (219 shorter events, 67.9 us)
Async XLA Ops:
  7.2 424.4 %copy-start = (bf16[1152,192]{0,1:T(8,128)(2,1)S(1)}, bf16[1152,192]{0,1:T(8,128)(2,1)}, u32[]{:S(2)}) copy-start(bf16[1152,192]{0,1:T(8,128)(2,1)} %param.24) | copy-start | bytes 1327108
  7.2 98.8 %all-gather.10.cloned.1.call-start = ((), (), s32[]{:S(2)}) async-start(), calls=%async_computation.2 | async-start | bytes 1566720 | tf_op jit(solution)/shard_map/all_gather | solution.py:59
  7.9 192.9 %all-gather.8.cloned.1.call-start = ((), (), s32[]{:S(2)}) async-start(), calls=%async_computation.1 | async-start | bytes 1566720 | tf_op jit(solution)/shard_map/all_gather | solution.py:58
  8.7 293.9 %all-gather.6.cloned.1.call-start = ((), (), s32[]{:S(2)}) async-start(), calls=%async_computation | async-start | bytes 1566720 | tf_op jit(solution)/shard_map/all_gather | solution.py:57
  9.4 387.7 %all-gather.12.cloned.1.call-start = ((), (), s32[]{:S(2)}) async-start(), calls=%async_computation.3 | async-start | bytes 1566720 | tf_op jit(solution)/shard_map/all_gather | solution.py:60
  108.1 104.4 %copy-start.13 = (s32[1,2,3,5]{3,1,2,0:T(2,128)S(1)}, s32[1,2,3,5]{3,1,2,0:T(2,128)}, u32[]{:S(2)}) copy-start(s32[1,2,3,5]{3,1,2,0:T(2,128)} %param.27) | copy-start | bytes 364
  202.8 37.9 %copy-start.10 = (s32[8,16,64]{2,1,0:T(8,128)S(1)}, s32[8,16,64]{2,1,0:T(8,128)}, u32[]{:S(2)}) copy-start(s32[8,16,64]{2,1,0:T(8,128)} %param.26) | copy-start | bytes 98308
  202.8 38.0 %copy-start.11 = (f32[8,16,64]{2,1,0:T(8,128)S(1)}, f32[8,16,64]{2,1,0:T(8,128)}, u32[]{:S(2)}) copy-start(f32[8,16,64]{2,1,0:T(8,128)} %param.25) | copy-start | bytes 98308
  203.1 17.3 %collective-permute-start.1 = (bf16[8,16,1152]{2,1,0:T(8,128)(2,1)S(1)}, bf16[8,16,1152]{2,1,0:T(8,128)(2,1)S(1)}, u32[]{:S(2)}, u32[]{:S(2)}) collective-permute-start(bf16[8,16,1152]{2,1,0:T(8,128)(2,1)S(1)} %bitcast.72), channel_id=1, source_target_pairs={{32,0},{64,32},{96,64},{128,96},{160,128},{192,160},{224,192},{256... | collective-permute-start | bytes 884744 | tf_op jit(solution)/shard_map/ppermute | solution.py:17
  210.5 21.7 %collective-permute-start = (bf16[8,16,1152]{2,1,0:T(8,128)(2,1)S(1)}, bf16[8,16,1152]{2,1,0:T(8,128)(2,1)S(1)}, u32[]{:S(2)}, u32[]{:S(2)}) collective-permute-start(bf16[8,16,1152]{2,1,0:T(8,128)(2,1)S(1)} %bitcast.73), channel_id=1, source_target_pairs={{0,32},{32,64},{64,96},{96,128},{128,160},{160,192},{192,224},{224... | collective-permute-start | bytes 884744 | tf_op jit(solution)/shard_map/ppermute | solution.py:16
  232.3 168.1 %collective-permute-start.3 = (bf16[24,16,1152]{2,1,0:T(8,128)(2,1)S(1)}, bf16[24,16,1152]{2,1,0:T(8,128)(2,1)}, u32[]{:S(2)}, u32[]{:S(2)}) collective-permute-start(bf16[24,16,1152]{2,1,0:T(8,128)(2,1)S(1)} %pad_maximum_fusion.2), channel_id=1, source_target_pairs={{1,0},{2,1},{3,2},{4,3},{5,4},{6,5},{7,6},{8,7},{9,8},{10,9},{11,1... | collective-permute-start | bytes 2654216 | tf_op jit(solution)/shard_map/ppermute | solution.py:17
  236.5 163.8 %collective-permute-start.2 = (bf16[24,16,1152]{2,1,0:T(8,128)(2,1)S(1)}, bf16[24,16,1152]{2,1,0:T(8,128)(2,1)}, u32[]{:S(2)}, u32[]{:S(2)}) collective-permute-start(bf16[24,16,1152]{2,1,0:T(8,128)(2,1)S(1)} %pad_maximum_fusion.2), channel_id=1, source_target_pairs={{0,1},{1,2},{2,3},{3,4},{4,5},{5,6},{6,7},{7,8},{8,9},{9,10},{10,1... | collective-permute-start | bytes 2654216 | tf_op jit(solution)/shard_map/ppermute | solution.py:16
  405.0 24.8 %copy-start.1 = (bf16[8,16,1152]{2,1,0:T(8,128)(2,1)S(1)}, bf16[8,16,1152]{2,1,0:T(8,128)(2,1)}, u32[]{:S(2)}) copy-start(bf16[8,16,1152]{2,1,0:T(8,128)(2,1)} %param.18) | copy-start | bytes 884740
  431.6 2.0 copy-start.9
  431.6 1.4 copy-start.2
  433.0 0.8 copy-start.7
  488.6 2.2 copy-start.6
  494.9 17.5 %collective-permute-start.4 = (bf16[24,16,1152]{2,1,0:T(8,128)(2,1)S(1)}, bf16[24,16,1152]{2,1,0:T(8,128)(2,1)S(1)}, u32[]{:S(2)}, u32[]{:S(2)}) collective-permute-start(bf16[24,16,1152]{2,1,0:T(8,128)(2,1)S(1)} %get-tuple-element.484), channel_id=1, source_target_pairs={{0,1},{1,2},{2,3},{3,4},{4,5},{5,6},{6,7},{7,8},{8,9},{9,10},{10,1... | collective-permute-start | bytes 2654216 | tf_op jit(solution)/shard_map/ppermute | solution.py:16
  502.4 16.5 %collective-permute-start.5 = (bf16[24,16,1152]{2,1,0:T(8,128)(2,1)S(1)}, bf16[24,16,1152]{2,1,0:T(8,128)(2,1)S(1)}, u32[]{:S(2)}, u32[]{:S(2)}) collective-permute-start(bf16[24,16,1152]{2,1,0:T(8,128)(2,1)S(1)} %get-tuple-element.485), channel_id=1, source_target_pairs={{1,0},{2,1},{3,2},{4,3},{5,4},{6,5},{7,6},{8,7},{9,8},{10,9},{11,1... | collective-permute-start | bytes 2654216 | tf_op jit(solution)/shard_map/ppermute | solution.py:17
  518.8 11.9 %copy-start.5 = (bf16[1152,576]{1,0:T(8,128)(2,1)S(1)}, bf16[1152,576]{1,0:T(8,128)(2,1)}, u32[]{:S(2)}) copy-start(bf16[1152,576]{1,0:T(8,128)(2,1)} %all-gather.6.cloned.1.call-done) | copy-start | bytes 3981316
  519.3 18.1 %collective-permute-start.6 = (bf16[8,16,1152]{2,1,0:T(8,128)(2,1)S(1)}, bf16[8,16,1152]{2,1,0:T(8,128)(2,1)S(1)}, u32[]{:S(2)}, u32[]{:S(2)}) collective-permute-start(bf16[8,16,1152]{2,1,0:T(8,128)(2,1)S(1)} %get-tuple-element.488), channel_id=1, source_target_pairs={{0,32},{32,64},{64,96},{96,128},{128,160},{160,192},{192,224},{224... | collective-permute-start | bytes 884744 | tf_op jit(solution)/shard_map/ppermute | solution.py:16
  521.5 17.6 %collective-permute-start.7 = (bf16[8,16,1152]{2,1,0:T(8,128)(2,1)S(1)}, bf16[8,16,1152]{2,1,0:T(8,128)(2,1)S(1)}, u32[]{:S(2)}, u32[]{:S(2)}) collective-permute-start(bf16[8,16,1152]{2,1,0:T(8,128)(2,1)S(1)} %get-tuple-element.489), channel_id=1, source_target_pairs={{32,0},{64,32},{96,64},{128,96},{160,128},{192,160},{224,192},{256... | collective-permute-start | bytes 884744 | tf_op jit(solution)/shard_map/ppermute | solution.py:17
  532.2 7.1 %copy-start.4 = (bf16[1152,576]{1,0:T(8,128)(2,1)S(1)}, bf16[1152,576]{1,0:T(8,128)(2,1)}, u32[]{:S(2)}) copy-start(bf16[1152,576]{1,0:T(8,128)(2,1)} %all-gather.8.cloned.1.call-done) | copy-start | bytes 3981316
  539.3 1.4 copy-start.3
  539.3 1.4 copy-start.12
  540.7 1.1 copy-start.8
Sparse Core Ops, SparseCore 0:
  11.2 94.7 all-gather.9
  109.2 91.5 all-gather.7
  204.0 98.5 all-gather.5
  305.6 91.5 all-gather.11
where the time goes:
time: 551 us; the launch traced here: 549 us
  waiting for transfers between devices  382 us (69%)
  matrix products  67.3 us (12%)
  starting transfers between devices  38.5 us (7%)
  local copies, waits for them, and re-layouts  30.3 us (5%)
  other arithmetic  16.3 us (3%)
  between operations  14.2 us (3%)
    all_gather x1, waiting for transfers between devices, on_device(): lax.all_gather(w_key, 'lat', axis=0, tiled=True)  92.7 us
    all_gather x1, waiting for transfers between devices, on_device(): lax.all_gather(w_value, 'lat', axis=0, tiled=True)  92.4 us
    all_gather x1, waiting for transfers between devices, on_device(): lax.all_gather(w_out, 'lat', axis=0, tiled=True)  92.4 us
    all_gather x1, waiting for transfers between devices, on_device(): lax.all_gather(w_query, 'lat', axis=0, tiled=True)  61.4 us
    ppermute x4, waiting for transfers between devices, extended(): before = lax.ppermute(last, axis, up)  25 us
    ppermute x4, starting transfers between devices, extended(): after = lax.ppermute(initial, axis, down)  22.7 us
    dot_general x29, matrix products, contract_last(): lax.dot_general(left, right, (((1,), (1,)), ((), ())), preferred_element_...  22.6 us
    dot_general x16, matrix products, contract_first(): lax.dot_general(left, right, (((0,), (0,)), ((), ())), preferred_element_...  15.9 us
  transfers between devices with their start and end apart: 12, of which 10 were waited for; matrix products, arithmetic and copies ran while one was open for 3% of the time, Pallas kernels for 0%

commit v1 on v0

v1 whole, which is shorter than its diff:
```python
import functools

import jax
import jax.numpy as jnp
import numpy as np
from jax import lax
from jax.experimental import pallas as pl
from jax.experimental.pallas import tpu as pltpu
from jax.sharding import Mesh, PartitionSpec as P

H = 8
HD = 72
HW = 576
D = 1152
T = 128
QKV = 3 * HW
FACTOR = HD ** (-0.5)
SCALE2 = FACTOR * 1.4426950408889634
OFF = -1e30
BF = jnp.bfloat16
F32 = jnp.float32
VMEM = pl.BlockSpec(memory_space=pltpu.VMEM)
SMEM = pl.BlockSpec(memory_space=pltpu.SMEM)
ANY = pl.BlockSpec(memory_space=pl.ANY)
K0, V0, Q0 = 0, HW, 2 * HW
VB = 512


def params(limit=40):
    return pltpu.CompilerParams(vmem_limit_bytes=limit * 1024 * 1024)


def nt(left, right):
    return lax.dot_general(left, right, (((1,), (1,)), ((), ())), preferred_element_type=F32)


def nn(left, right):
    return jnp.dot(left, right, preferred_element_type=F32)


def window(first):
    return first // 128 * 128, -(-(first + HD) // 128) * 128


def head_only(x, first, start):
    lane = lax.broadcasted_iota(jnp.int32, x.shape, 1) + start
    return jnp.where((lane >= first) & (lane < first + HD), x, jnp.zeros_like(x))


def norm_parts(x):
    center = x - jnp.mean(x, axis=-1, keepdims=True)
    rstd = lax.rsqrt(jnp.mean(center * center, axis=-1, keepdims=True) + 1e-6)
    return center, rstd


def order_kernel(target_ref, order_ref):
    rows = lax.broadcasted_iota(jnp.int32, (D, D), 0)
    order_ref[...] = jnp.where(rows == target_ref[...], 1.0, 0.0).astype(BF)


def hidden_kernel(x_ref, gain_ref, order_ref, out_ref):
    for i in range(x_ref.shape[0] // T):
        center, rstd = norm_parts(x_ref[i * T : (i + 1) * T, :].astype(F32))
        hidden = (center * rstd * gain_ref[...]).astype(BF)
        out_ref[i * T : (i + 1) * T, :] = nn(hidden, order_ref[...]).astype(BF)


def forward_kernel(
    core_ref, blocks_ref, hw_ref, hc_ref, he_ref, u0, m1, m2, m3, t1, t2, t3, mh, th, wout_ref, wpix_ref,
    x_ref, meas_ref, filt_ref,
    w_ref, win_ref, e_ref, den_ref, og_ref, pack_ref, stat_ref,
    wo_ref, bias_ref, att_ref, sems,
):
    core = core_ref[0]
    copies = [
        pltpu.make_async_copy(src, w_ref.at[pl.ds(144 * i, 144)], sems.at[i])
        for i, src in enumerate((u0, m1, m2, m3, t1, t2, t3))
    ]
    copies.append(pltpu.make_async_copy(mh, w_ref.at[pl.ds(1008, 80)], sems.at[7]))
    first = pl.multiple_of(16 * (1 - core), 16)
    copies.append(pltpu.make_async_copy(th.at[pl.ds(first, 64)], w_ref.at[pl.ds(1088, 64)], sems.at[8]))
    copies.append(pltpu.make_async_copy(wout_ref, wo_ref.at[pl.ds(64, HW)], sems.at[9]))
    for c in copies:
        c.start()
    wo_ref[0:64, :] = jnp.zeros((64, D), BF)
    att_ref[...] = jnp.zeros_like(att_ref)

    qc = (lax.broadcasted_iota(jnp.int32, (T, T), 0) & 8) > 0
    kc = (lax.broadcasted_iota(jnp.int32, (T, T), 1) & 8) > 0

    def allowed(c, r, w):
        return blocks_ref[(c * 3 + r) * 5 + w - c].astype(F32) if 0 <= w - c < 5 else jnp.float32(0.0)

    lane_c = (lax.broadcasted_iota(jnp.int32, (1, T), 1) & 8) > 0
    rows = []
    for r in range(3):
        for w in range(6):
            rows.append(jnp.where(lane_c, allowed(1, r, w), allowed(0, r, w)))
    for t in range(3):
        for r in range(3):
            seen = jnp.where(
                qc,
                jnp.where(kc, allowed(1, r, 2 * t + 1), allowed(1, r, 2 * t)),
                jnp.where(kc, allowed(0, r, 2 * t + 1), allowed(0, r, 2 * t)),
            )
            j = 3 * t + r
            bias_ref[:, j * T : (j + 1) * T] = (1.0 - seen) * OFF
    for c in copies[:9]:
        c.wait()
    for g, h_ref in enumerate((hw_ref, hc_ref, he_ref)):
        for part in range(3):
            s = slice(part * T, (part + 1) * T)
            win_ref[(g * 3 + part) * T : (g * 3 + part + 1) * T, :] = nn(h_ref[s, :], w_ref[...]).astype(BF)

    own = slice(4 * T, 5 * T)
    lanes = lax.broadcasted_iota(jnp.int32, (T, T), 1)
    stats = jnp.zeros((T, T), F32)
    for e in range(H):
        a, b = window(K0 + HD * e)
        q = head_only(win_ref[own, Q0 + a : Q0 + b], HD * e, a) if Q0 + b <= QKV else head_only(
            jnp.concatenate([win_ref[own, Q0 + a : QKV], jnp.zeros((T, Q0 + b - QKV), BF)], axis=1), HD * e, a)
        s = nt(q, win_ref[:, a:b]) * SCALE2 + bias_ref[...]
        peak = jnp.max(s, axis=1, keepdims=True)
        p = jnp.exp2(s - peak)
        total = jnp.sum(p, axis=1, keepdims=True)
        low = p.astype(BF)
        e_ref[e * T : (e + 1) * T, :] = low
        inv = 1.0 / total
        stats = jnp.where(lanes == e, peak + jnp.log2(total), stats)
        stats = jnp.where(lanes == 16 + e, inv, stats)
        a, b = window(V0 + HD * e)
        o = nn(low, win_ref[:, a:b]) * inv
        att_ref[:, a - VB : b - VB] += head_only(o, V0 + HD * e, a)
    copies[9].wait()
    att = att_ref[...].astype(BF)
    den = (x_ref[...].astype(F32) + nn(att, wo_ref[...])).astype(BF)
    den_ref[...] = den
    colors = nn(den, wpix_ref[...])
    filt = filt_ref[...]
    misfit = -meas_ref[...]
    for c in range(3):
        misfit = misfit + jnp.where(filt == c, colors[:, 64 * c : 64 * c + 64], 0.0)
    spread = jnp.concatenate([jnp.where(filt == c, misfit, 0.0) for c in range(3)], axis=1).astype(BF)
    og = nt(spread, wpix_ref[...])
    og_ref[...] = og
    up = nt(og.astype(BF), wo_ref[...]).astype(BF)
    pack_ref[0:T, :] = up
    prod = up.astype(F32) * att.astype(F32)
    for e in range(H):
        a, b = window(V0 + HD * e)
        inner = jnp.sum(head_only(prod[:, a - VB : b - VB], V0 + HD * e, a), axis=1, keepdims=True)
        stats = jnp.where(lanes == 8 + e, inner, stats)
    stat_ref[...] = stats
    turned = stats.T[0:16, :]
    high = turned.astype(BF)
    rest = turned - high.astype(F32)
    mid = rest.astype(BF)
    low = (rest - mid.astype(F32)).astype(BF)
    pack_ref[T : T + 16, :] = jnp.concatenate(
        [
            high,
            mid,
            low,
            jnp.concatenate(rows[:16], axis=0).astype(BF),
            jnp.concatenate(rows[16:] + [jnp.zeros((14, T), F32)], axis=0).astype(BF),
        ],
        axis=1,
    )


def query_kernel(win_ref, e_ref, up_ref, stat_ref, gq_ref, acc_ref):
    acc_ref[...] = jnp.zeros_like(acc_ref)
    for e in range(H):
        a, b = window(V0 + HD * e)
        up = head_only(up_ref[0:T, a - VB : b - VB], V0 + HD * e, a)
        dprob = nt(up, win_ref[:, a:b])
        p = e_ref[e * T : (e + 1) * T, :].astype(F32)
        ds = (p * (dprob - stat_ref[:, 8 + e : 9 + e])).astype(BF)
        a, b = window(K0 + HD * e)
        dq = nn(ds, win_ref[:, a:b]) * (stat_ref[:, 16 + e : 17 + e] * FACTOR)
        acc_ref[:, a:b] += head_only(dq, HD * e, a)
    gq_ref[...] = acc_ref[:, 0:HW].astype(BF)


def key_side(win_ref, groups, gk_ref, gv_ref):
    own = slice(4 * T, 5 * T)
    kc = (lax.broadcasted_iota(jnp.int32, (T, T), 0) & 8) > 0
    for t, pack_ref in groups:
        bias, stats, ups = [], [], []
        for r in range(3):
            base = r * 144
            ups.append(pack_ref[base : base + T, :])
            extra = pack_ref[base + T : base + T + 16, :].astype(F32)
            stats.append(extra[:, 0:128] + extra[:, 128:256] + extra[:, 256:384])
            seen = []
            for w in range(2):
                i = (2 - r) * 6 + (2 - t) * 2 + w
                seen.append(extra[i : i + 1, 384:512] if i < 16 else extra[i - 16 : i - 15, 512:640])
            bias.append((1.0 - jnp.where(kc, seen[1], seen[0])) * OFF)
        bias = jnp.concatenate(bias, axis=1)
        stats = jnp.concatenate(stats, axis=1)
        ups = jnp.concatenate(ups, axis=0)
        q_rows = slice(t * 3 * T, (t + 1) * 3 * T)
        for e in range(H):
            a, b = window(K0 + HD * e)
            if Q0 + b <= QKV:
                q = win_ref[q_rows, Q0 + a : Q0 + b]
            else:
                q = jnp.concatenate([win_ref[q_rows, Q0 + a : QKV], jnp.zeros((3 * T, Q0 + b - QKV), BF)], axis=1)
            k = head_only(win_ref[own, a:b], HD * e, a)
            s = nt(k, q) * SCALE2 + bias
            p = jnp.exp2(s - stats[e : e + 1, :])
            c, d = window(V0 + HD * e)
            v = head_only(win_ref[own, c:d], V0 + HD * e, c)
            up = ups[:, c - VB : d - VB]
            ds = (p * (nt(v, up) - stats[8 + e : 9 + e, :])).astype(BF)
            gk_ref[:, a:b] += head_only(nn(ds, q), HD * e, a)
            gv_ref[:, c - VB : d - VB] += head_only(nn(p.astype(BF), up), V0 + HD * e, c)


def key_centre_kernel(win_ref, pack_ref, gk_ref, gv_ref):
    gk_ref[...] = jnp.zeros_like(gk_ref)
    gv_ref[...] = jnp.zeros_like(gv_ref)
    key_side(win_ref, ((1, pack_ref),), gk_ref, gv_ref)


def finish_kernel(
    win_ref, packw_ref, packe_ref, gk0_ref, gv0_ref, gq_ref, w_ref, order_ref, x_ref, gain_ref, og_ref,
    out_ref, gk_ref, gv_ref,
):
    gk_ref[...] = gk0_ref[...]
    gv_ref[...] = gv0_ref[...]
    key_side(win_ref, ((0, packw_ref), (2, packe_ref)), gk_ref, gv_ref)
    gk = (gk_ref[:, 0:HW] * FACTOR).astype(BF)
    gv = gv_ref[:, 64:640].astype(BF)
    grads = jnp.concatenate([gk, gv, gq_ref[...]], axis=1)
    moved = nt(grads, w_ref[...])
    high = moved.astype(BF)
    rest = moved - high.astype(F32)
    mid = rest.astype(BF)
    low = (rest - mid.astype(F32)).astype(BF)
    order = order_ref[...]
    grad = (nt(high, order) + nt(mid, order) + nt(low, order)) * gain_ref[...]
    center, rstd = norm_parts(x_ref[...].astype(F32))
    xhat = center * rstd
    mean_g = jnp.mean(grad, axis=-1, keepdims=True)
    mean_gx = jnp.mean(grad * xhat, axis=-1, keepdims=True)
    out_ref[...] = rstd * (grad - mean_g - xhat * mean_gx) + og_ref[...]


def shaped(shape, dtype=BF):
    return jax.ShapeDtypeStruct(shape, dtype)


def weight_targets(z, yh, core):
    place = np.arange(D)
    block, row = place // 144, place % 144
    step = np.select([block == 7], [4], np.where(block > 3, block - 3, block))
    sign = np.where(block > 3, 1, -1)
    last0 = row
    last1 = np.where(row < 80, row + 64, row - 80)
    zs = jnp.where(core == 0, z + jnp.asarray(sign * step), z - jnp.asarray(sign * step)) & 7
    inside = jnp.where(core == 0, jnp.asarray(last0), jnp.asarray(np.where(block == 7, last1, row)))
    other = inside >= 72
    ys = jnp.where(other, 1 - yh, yh)
    return ((ys * 8 + zs) * 72 + inside - 72 * other.astype(jnp.int32)).astype(jnp.int32).reshape(1, D)


def on_device(tokens, gain, w_query, w_key, w_value, w_out, w_pixel, measured, filter_color, block_mask):
    yh, z, core = lax.axis_index("yh"), lax.axis_index("z"), lax.axis_index("core")
    x = tokens.reshape(T, D)
    gain = gain.reshape(1, D)
    ring = [(2 * i, 2 * ((i + 1) % 8)) for i in range(8)] + [(2 * i + 1, 2 * ((i + 7) % 8) + 1) for i in range(8)]
    south = [(i, i + 1) for i in range(15)]
    north = [(j, i) for i, j in south]
    east = [(i, (i + 1) % 32) for i in range(32)]
    west = [(j, i) for i, j in east]
    lat, lon = ("yh", "z"), ("yl", "x", "core")

    def swap(v):
        return lax.ppermute(v, "core", [(0, 1), (1, 0)])

    def step(v):
        return lax.ppermute(v, ("z", "core"), ring)

    def columns(own):
        before = lax.ppermute(own, lat, south)
        after = lax.ppermute(own, lat, north)
        return jnp.concatenate([before, own, after], axis=0)

    def sides(column):
        return lax.ppermute(column, lon, east), lax.ppermute(column, lon, west)

    mine = jnp.concatenate([w_key, w_value, w_query], axis=1)
    other = lax.ppermute(mine, "yh", [(0, 1), (1, 0)])
    out_other = lax.ppermute(w_out, "yh", [(0, 1), (1, 0)])
    both = jnp.concatenate([mine, other], axis=0)
    out_both = jnp.stack([jnp.where(yh == 0, w_out, out_other), jnp.where(yh == 0, out_other, w_out)])
    full_out = lax.all_gather(out_both, "z", axis=1).reshape(HW, D)
    m1 = step(both)
    t1 = swap(m1)
    m2 = step(m1)
    t2 = swap(m2)
    m3 = step(m2)
    t3 = swap(m3)
    mh = step(jnp.where(core == 0, m3[0:80], m3[64:144]))
    th = swap(mh)

    column = columns(x)
    from_west, from_east = sides(column)
    order = pl.pallas_call(
        order_kernel, out_shape=shaped((D, D)), in_specs=[VMEM], out_specs=VMEM, compiler_params=params(),
    )(weight_targets(z, yh, core))

    def hidden(v):
        return pl.pallas_call(
            hidden_kernel, out_shape=shaped((3 * T, D)), in_specs=[VMEM] * 3, out_specs=VMEM, compiler_params=params(),
        )(v, gain, order)

    hw, hc, he = hidden(from_west), hidden(column), hidden(from_east)
    w, win, e, den, og, pack, stat = pl.pallas_call(
        forward_kernel,
        out_shape=(
            shaped((D, QKV)), shaped((9 * T, QKV)), shaped((H * T, 9 * T)), shaped((T, D)), shaped((T, D), F32),
            shaped((144, 640)), shaped((T, T), F32),
        ),
        in_specs=[SMEM, SMEM] + [VMEM] * 3 + [ANY] * 10 + [VMEM] * 4,
        out_specs=(VMEM,) * 7,
        scratch_shapes=[
            pltpu.VMEM((640, D), BF), pltpu.VMEM((T, 9 * T), F32), pltpu.VMEM((T, 640), F32),
            pltpu.SemaphoreType.DMA((10,)),
        ],
        compiler_params=params(),
    )(
        core.reshape(1).astype(jnp.int32), block_mask.reshape(30), hw, hc, he, both, m1, m2, m3, t1, t2, t3, mh, th,
        full_out, w_pixel, x, measured.reshape(T, 64), filter_color.reshape(T, 64),
    )
    packs = columns(pack)
    gq = pl.pallas_call(
        query_kernel, out_shape=shaped((T, HW)), in_specs=[VMEM] * 4, out_specs=VMEM,
        scratch_shapes=[pltpu.VMEM((T, 640), F32)], compiler_params=params(),
        cost_estimate=pl.CostEstimate(flops=8_000_000_000, bytes_accessed=6_000_000, transcendentals=0),
    )(win, e, pack, stat)
    packs_west, packs_east = sides(packs)
    gk, gv = pl.pallas_call(
        key_centre_kernel, out_shape=(shaped((T, 640), F32),) * 2, in_specs=[VMEM] * 2, out_specs=(VMEM,) * 2,
        compiler_params=params(),
        cost_estimate=pl.CostEstimate(flops=8_000_000_000, bytes_accessed=6_000_000, transcendentals=0),
    )(win, packs)
    guidance = pl.pallas_call(
        finish_kernel, out_shape=shaped((T, D), F32), in_specs=[VMEM] * 11, out_specs=VMEM,
        scratch_shapes=[pltpu.VMEM((T, 640), F32)] * 2, compiler_params=params(),
    )(win, packs_west, packs_east, gk, gv, gq, w, order, x, gain, og)
    return den.reshape(tokens.shape), guidance.reshape(tokens.shape)


def solution(mesh):
    split = Mesh(mesh.devices.reshape(2, 8, 4, 4, 2), ("yh", "z", "yl", "x", "core"))
    lat, lon = ("yh", "z"), ("yl", "x", "core")
    return jax.shard_map(
        on_device,
        mesh=split,
        in_specs=(
            P(lat, lon, None), P(), P(lat, None), P(lat, None), P(lat, None), P(lat, None), P(),
            P(lat, lon, None), P(lat, lon, None), P(lat, lon, None, None),
        ),
        out_specs=(P(lat, lon, None), P(lat, lon, None)),
        check_vma=False,
    )
```

time: 551 us -> 190 us (0.34)
  the two profiles are of different devices: /device:TPU:47 before, /device:TPU:48 now
where the time goes in v1:
time: 190 us; the launch traced here: 189 us
  starting transfers between devices  60.9 us (32%)
  waiting for transfers between devices  59.6 us (31%)
  Pallas kernels  36.5 us (19%)
  local copies, waits for them, and re-layouts  15.4 us (8%)
  between operations  14.6 us (8%)
  other arithmetic  2.14 us (1%)
    ppermute x2, waiting for transfers between devices, columns(): before = lax.ppermute(own, lat, south)  22.3 us
    ppermute x4, waiting for transfers between devices, step(): return lax.ppermute(v, ('z', 'core'), ring)  19 us
    pallas_call x1, Pallas kernels, on_device(): pl.pallas_call(forward_kernel, out_shape=(shaped((D, QKV)), shaped((9 * T...  16.7 us
    ppermute x4, starting transfers between devices, step(): return lax.ppermute(v, ('z', 'core'), ring)  13.7 us
    ppermute x4, starting transfers between devices, sides(): return (lax.ppermute(column, lon, east), lax.ppermute(column, lon, west))  12.8 us
    unnamed x58, local copies, waits for them, and re-layouts  11.2 us
    ppermute x4, starting transfers between devices, swap(): return lax.ppermute(v, 'core', [(0, 1), (1, 0)])  10.9 us
    ppermute x1, waiting for transfers between devices, on_device(): other = lax.ppermute(mine, 'yh', [(0, 1), (1, 0)])  9.47 us
  transfers between devices with their start and end apart: 19, of which 8 were waited for; matrix products, arithmetic and copies ran while one was open for 3% of the time, Pallas kernels for 6%

profile of v1, /device:TPU:48, one launch (start us, length us, event | category | flops | bytes accessed | tf_op | source)
XLA Modules:
  0.0 189.2 jit_solution(16484479889200150099)
XLA Ops:
  7.2 1.1 concatenate.13
  8.4 3.8 %collective-permute-start.4 = (bf16[72,1728]{1,0:T(8,128)(2,1)S(1)}, bf16[72,1728]{1,0:T(8,128)(2,1)S(1)}, u32[]{:S(2)}, u32[]{:S(2)}) collective-permute-start(bf16[72,1728]{1,0:T(8,128)(2,1)S(1)} %concatenate.13), channel_id=1, source_target_pairs={{0,256},{256,0},{1,257},{257,1},{2,258},{258,2},{3,259},{259,3},{4... | collective-permute-start | bytes 746504 | tf_op jit(solution)/shard_map/ppermute | solution.py:295
  12.2 5.9 %collective-permute-start.13 = (bf16[36,1152]{1,0:T(8,128)(2,1)}, bf16[36,1152]{1,0:T(8,128)(2,1)S(1)}, u32[]{:S(2)}, u32[]{:S(2)}) collective-permute-start(bf16[36,1152]{1,0:T(8,128)(2,1)} %param.19), channel_id=1, source_target_pairs={{0,256},{256,0},{1,257},{257,1},{2,258},{258,2},{3,259},{259,3},{4... | collective-permute-start | bytes 248840 | tf_op jit(solution)/shard_map/ppermute | solution.py:296
  18.1 9.5 %collective-permute-done.4 = bf16[72,1728]{1,0:T(8,128)(2,1)S(1)} collective-permute-done((bf16[72,1728]{1,0:T(8,128)(2,1)S(1)}, bf16[72,1728]{1,0:T(8,128)(2,1)S(1)}, u32[]{:S(2)}, u32[]{:S(2)}) %collective-permute-start.4) | collective-permute-done | bytes 248864 | tf_op jit(solution)/shard_map/ppermute | solution.py:295
  27.7 7.1 %collective-permute-start.5 = (bf16[144,1728]{1,0:T(8,128)(2,1)S(1)}, bf16[144,1728]{1,0:T(8,128)(2,1)}, u32[]{:S(2)}, u32[]{:S(2)}) collective-permute-start(bf16[144,1728]{1,0:T(8,128)(2,1)S(1)} %pad_maximum_fusion.1.u0), channel_id=1, source_target_pairs={{0,32},{32,64},{64,96},{96,128},{128,160},{160,192},{192,224},{224... | collective-permute-start | bytes 1493000 | tf_op jit(solution)/shard_map/ppermute | solution.py:284
  34.8 0.9 select_bitcast_fusion.1
  35.9 0.8 copy.25
  36.7 12.0 %collective-permute-done.5.m1 = bf16[144,1728]{1,0:T(8,128)(2,1)} collective-permute-done((bf16[144,1728]{1,0:T(8,128)(2,1)S(1)}, bf16[144,1728]{1,0:T(8,128)(2,1)}, u32[]{:S(2)}, u32[]{:S(2)}) %collective-permute-start.5) | collective-permute-done | bytes 497696 | tf_op jit(solution)/shard_map/ppermute | solution.py:284
  48.6 1.9 %collective-permute-start.6 = (bf16[144,1728]{1,0:T(8,128)(2,1)}, bf16[144,1728]{1,0:T(8,128)(2,1)}, u32[]{:S(2)}, u32[]{:S(2)}) collective-permute-start(bf16[144,1728]{1,0:T(8,128)(2,1)} %collective-permute-done.5.m1), channel_id=1, source_target_pairs={{0,32},{32,64},{64,96},{96,128},{128,160},{160,192},{192,224},{224... | collective-permute-start | bytes 1493000 | tf_op jit(solution)/shard_map/ppermute | solution.py:284
  50.6 5.8 %collective-permute-start.1 = (bf16[128,1152]{1,0:T(8,128)(2,1)S(1)}, bf16[128,1152]{1,0:T(8,128)(2,1)S(1)}, u32[]{:S(2)}, u32[]{:S(2)}) collective-permute-start(bf16[128,1152]{1,0:T(8,128)(2,1)S(1)} %bitcast.12), channel_id=1, source_target_pairs={{32,0},{64,32},{96,64},{128,96},{160,128},{192,160},{224,192},{256... | collective-permute-start | bytes 884744 | tf_op jit(solution)/shard_map/ppermute | solution.py:288
  56.4 1.9 %collective-permute-start = (bf16[128,1152]{1,0:T(8,128)(2,1)S(1)}, bf16[128,1152]{1,0:T(8,128)(2,1)S(1)}, u32[]{:S(2)}, u32[]{:S(2)}) collective-permute-start(bf16[128,1152]{1,0:T(8,128)(2,1)S(1)} %bitcast.13), channel_id=1, source_target_pairs={{0,32},{32,64},{64,96},{96,128},{128,160},{160,192},{192,224},{224... | collective-permute-start | bytes 884744 | tf_op jit(solution)/shard_map/ppermute | solution.py:287
  58.3 7.0 %collective-permute-done.6.m2 = bf16[144,1728]{1,0:T(8,128)(2,1)} collective-permute-done((bf16[144,1728]{1,0:T(8,128)(2,1)}, bf16[144,1728]{1,0:T(8,128)(2,1)}, u32[]{:S(2)}, u32[]{:S(2)}) %collective-permute-start.6) | collective-permute-done | bytes 497696 | tf_op jit(solution)/shard_map/ppermute | solution.py:284
  65.4 2.8 %collective-permute-start.7 = (bf16[144,1728]{1,0:T(8,128)(2,1)}, bf16[144,1728]{1,0:T(8,128)(2,1)}, u32[]{:S(2)}, u32[]{:S(2)}) collective-permute-start(bf16[144,1728]{1,0:T(8,128)(2,1)} %collective-permute-done.6.m2), channel_id=1, source_target_pairs={{0,32},{32,64},{64,96},{96,128},{128,160},{160,192},{192,224},{224... | collective-permute-start | bytes 1493000 | tf_op jit(solution)/shard_map/ppermute | solution.py:284
  68.2 15.8 %collective-permute-done = bf16[128,1152]{1,0:T(8,128)(2,1)S(1)} collective-permute-done((bf16[128,1152]{1,0:T(8,128)(2,1)S(1)}, bf16[128,1152]{1,0:T(8,128)(2,1)S(1)}, u32[]{:S(2)}, u32[]{:S(2)}) %collective-permute-start) | collective-permute-done | bytes 294944 | tf_op jit(solution)/shard_map/ppermute | solution.py:287
  84.0 1.9 %collective-permute-start.3 = (bf16[384,1152]{1,0:T(8,128)(2,1)S(1)}, bf16[384,1152]{1,0:T(8,128)(2,1)S(1)}, u32[]{:S(2)}, u32[]{:S(2)}) collective-permute-start(bf16[384,1152]{1,0:T(8,128)(2,1)S(1)} %pad_maximum_fusion.x_ref), channel_id=1, source_target_pairs={{1,0},{2,1},{3,2},{4,3},{5,4},{6,5},{7,6},{8,7},{9,8},{10,9},{11,1... | collective-permute-start | bytes 2654216 | tf_op jit(solution)/shard_map/ppermute | solution.py:292
  85.9 2.4 %collective-permute-start.2 = (bf16[384,1152]{1,0:T(8,128)(2,1)S(1)}, bf16[384,1152]{1,0:T(8,128)(2,1)}, u32[]{:S(2)}, u32[]{:S(2)}) collective-permute-start(bf16[384,1152]{1,0:T(8,128)(2,1)S(1)} %pad_maximum_fusion.x_ref), channel_id=1, source_target_pairs={{0,1},{1,2},{2,3},{3,4},{4,5},{5,6},{6,7},{7,8},{8,9},{9,10},{10,1... | collective-permute-start | bytes 2654216 | tf_op jit(solution)/shard_map/ppermute | solution.py:292
  88.3 1.1 slice_select_fusion
  89.4 1.9 %collective-permute-start.11 = (bf16[80,1728]{1,0:T(8,128)(2,1)S(1)}, bf16[80,1728]{1,0:T(8,128)(2,1)}, u32[]{:S(2)}, u32[]{:S(2)}) collective-permute-start(bf16[80,1728]{1,0:T(8,128)(2,1)S(1)} %slice_select_fusion), channel_id=1, source_target_pairs={{0,32},{32,64},{64,96},{96,128},{128,160},{160,192},{192,224},{224... | collective-permute-start | bytes 829448 | tf_op jit(solution)/shard_map/ppermute | solution.py:284
  91.4 3.0 %collective-permute-start.8 = (bf16[144,1728]{1,0:T(8,128)(2,1)}, bf16[144,1728]{1,0:T(8,128)(2,1)}, u32[]{:S(2)}, u32[]{:S(2)}) collective-permute-start(bf16[144,1728]{1,0:T(8,128)(2,1)} %collective-permute-done.5.m1), channel_id=1, source_target_pairs={{0,1},{1,0},{2,3},{3,2},{4,5},{5,4},{6,7},{7,6},{8,9},{9,8},{10,11... | collective-permute-start | bytes 1493000 | tf_op jit(solution)/shard_map/ppermute | solution.py:281
  94.4 1.9 %collective-permute-start.9 = (bf16[144,1728]{1,0:T(8,128)(2,1)}, bf16[144,1728]{1,0:T(8,128)(2,1)}, u32[]{:S(2)}, u32[]{:S(2)}) collective-permute-start(bf16[144,1728]{1,0:T(8,128)(2,1)} %collective-permute-done.6.m2), channel_id=1, source_target_pairs={{0,1},{1,0},{2,3},{3,2},{4,5},{5,4},{6,7},{7,6},{8,9},{9,8},{10,11... | collective-permute-start | bytes 1493000 | tf_op jit(solution)/shard_map/ppermute | solution.py:281
  96.4 0.9 copy-done.15
  97.4 4.0 %collective-permute-start.10 = (bf16[144,1728]{1,0:T(8,128)(2,1)}, bf16[144,1728]{1,0:T(8,128)(2,1)}, u32[]{:S(2)}, u32[]{:S(2)}) collective-permute-start(bf16[144,1728]{1,0:T(8,128)(2,1)} %collective-permute-done.7.m3), channel_id=1, source_target_pairs={{0,1},{1,0},{2,3},{3,2},{4,5},{5,4},{6,7},{7,6},{8,9},{9,8},{10,11... | collective-permute-start | bytes 1493000 | tf_op jit(solution)/shard_map/ppermute | solution.py:281
  101.4 1.9 %collective-permute-start.12 = (bf16[80,1728]{1,0:T(8,128)(2,1)}, bf16[80,1728]{1,0:T(8,128)(2,1)}, u32[]{:S(2)}, u32[]{:S(2)}) collective-permute-start(bf16[80,1728]{1,0:T(8,128)(2,1)} %collective-permute-done.11.mh), channel_id=1, source_target_pairs={{0,1},{1,0},{2,3},{3,2},{4,5},{5,4},{6,7},{7,6},{8,9},{9,8},{10,11... | collective-permute-start | bytes 829448 | tf_op jit(solution)/shard_map/ppermute | solution.py:281
  103.4 0.6 reshape.35.blocks_ref
  104.1 1.1 copy.27.wpix_ref
  105.6 1.8 shard_map.151.hc_ref
  107.4 1.8 shard_map.152.he_ref
  109.3 0.9 copy-done.5
  110.2 3.0 %shard_map.150.hw_ref = bf16[384,1152]{1,0:T(8,128)(2,1)S(1)} custom-call(bf16[384,1152]{1,0:T(8,128)(2,1)} %collective-permute-done.2.x_ref, f32[1,1152]{1,0:T(1,128)S(1)} %reshape.37.gain_ref, bf16[1152,1152]{1,0:T(8,128)(2,1)S(1)} %shard_map.149.order_ref), custom_call_target="tpu_custom_call" | custom-call | tf_op jit(solution)/shard_map/pallas_call | solution.py:316
  113.2 0.9 copy-done.7
  114.1 1.6 copy.26
  116.2 1.0 copy-done.10
  117.2 1.1 copy-done.12
  118.2 1.0 copy-done.14
  119.3 0.8 copy-done.17
  120.1 0.8 copy-done.18
  120.9 16.7 %shard_map.153 = (bf16[1152,1728]{1,0:T(8,128)(2,1)}, bf16[1152,1728]{1,0:T(8,128)(2,1)}, bf16[1024,1152]{1,0:T(8,128)(2,1)S(1)}, bf16[128,1152]{1,0:T(8,128)(2,...) custom-call(s32[1]{0:T(128)} %bitcast.core_ref, s32[30]{0:T(128)S(1)} %copy-done.19, ...), custom_call_target="tpu_custom_call" | custom-call | tf_op jit(solution)/shard_map/pallas_call | solution.py:321
  137.6 1.9 %collective-permute-start.15 = (bf16[144,640]{1,0:T(8,128)(2,1)S(1)}, bf16[144,640]{1,0:T(8,128)(2,1)S(1)}, u32[]{:S(2)}, u32[]{:S(2)}) collective-permute-start(bf16[144,640]{1,0:T(8,128)(2,1)S(1)} %get-tuple-element.13.up_ref), channel_id=1, source_target_pairs={{32,0},{64,32},{96,64},{128,96},{160,128},{192,160},{224,192},{256... | collective-permute-start | bytes 552968 | tf_op jit(solution)/shard_map/ppermute | solution.py:288
  139.6 3.9 %collective-permute-start.14 = (bf16[144,640]{1,0:T(8,128)(2,1)S(1)}, bf16[144,640]{1,0:T(8,128)(2,1)S(1)}, u32[]{:S(2)}, u32[]{:S(2)}) collective-permute-start(bf16[144,640]{1,0:T(8,128)(2,1)S(1)} %get-tuple-element.13.up_ref), channel_id=1, source_target_pairs={{0,32},{32,64},{64,96},{96,128},{128,160},{160,192},{192,224},{224... | collective-permute-start | bytes 552968 | tf_op jit(solution)/shard_map/ppermute | solution.py:287
  143.5 2.2 %copy-done.1 = bf16[1152,1728]{1,0:T(8,128)(2,1)S(1)} copy-done((bf16[1152,1728]{1,0:T(8,128)(2,1)S(1)}, bf16[1152,1728]{1,0:T(8,128)(2,1)}, u32[]{:S(2)}) %copy-start.1) | copy-done | bytes 3981336
  145.7 2.3 %shard_map.155.gq_ref = bf16[128,576]{1,0:T(8,128)(2,1)S(1)} custom-call(bf16[1152,1728]{1,0:T(8,128)(2,1)S(1)} %copy-done.1, bf16[1024,1152]{1,0:T(8,128)(2,1)S(1)} %get-tuple-element.16.e_ref, bf16[144,640]{1,0:T(8,128)(2,1)S(1)} %get-tuple-element.13.up_ref, f32[128,128]{1,0:T(8,128)S(1)} %get-tuple-element.17.stat_ref), custom_call_target="tpu_custom_call" | custom-call | flops 8000000000 | bytes 6000000 | tf_op jit(solution)/shard_map/pallas_call | solution.py:339
  148.0 6.5 %collective-permute-done.14 = bf16[144,640]{1,0:T(8,128)(2,1)S(1)} collective-permute-done((bf16[144,640]{1,0:T(8,128)(2,1)S(1)}, bf16[144,640]{1,0:T(8,128)(2,1)S(1)}, u32[]{:S(2)}, u32[]{:S(2)}) %collective-permute-start.14) | collective-permute-done | bytes 184352 | tf_op jit(solution)/shard_map/ppermute | solution.py:287
  154.6 6.4 %collective-permute-start.17 = (bf16[432,640]{1,0:T(8,128)(2,1)S(1)}, bf16[432,640]{1,0:T(8,128)(2,1)S(1)}, u32[]{:S(2)}, u32[]{:S(2)}) collective-permute-start(bf16[432,640]{1,0:T(8,128)(2,1)S(1)} %constant_dynamic-update-slice_fusion.pack_ref), channel_id=1, source_target_pairs={{1,0},{2,1},{3,2},{4,3},{5,4},{6,5},{7,6},{8,7},{9,8},{10,9},{11,1... | collective-permute-start | bytes 1658888 | tf_op jit(solution)/shard_map/ppermute | solution.py:292
  161.0 2.1 %collective-permute-start.16 = (bf16[432,640]{1,0:T(8,128)(2,1)S(1)}, bf16[432,640]{1,0:T(8,128)(2,1)S(1)}, u32[]{:S(2)}, u32[]{:S(2)}) collective-permute-start(bf16[432,640]{1,0:T(8,128)(2,1)S(1)} %constant_dynamic-update-slice_fusion.pack_ref), channel_id=1, source_target_pairs={{0,1},{1,2},{2,3},{3,4},{4,5},{5,6},{6,7},{7,8},{8,9},{9,10},{10,1... | collective-permute-start | bytes 1658888 | tf_op jit(solution)/shard_map/ppermute | solution.py:292
  163.2 2.1 %shard_map.154 = (f32[128,640]{1,0:T(8,128)S(1)}, f32[128,640]{1,0:T(8,128)S(1)}) custom-call(bf16[1152,1728]{1,0:T(8,128)(2,1)S(1)} %copy-done.1, bf16[432,640]{1,0:T(8,128)(2,1)S(1)} %constant_dynamic-update-slice_fusion.pack_ref), custom_call_target="tpu_custom_call" | custom-call | flops 8000000000 | bytes 6000000 | tf_op jit(solution)/shard_map/pallas_call | solution.py:345
  165.3 2.7 %collective-permute-done.17.packe_ref = bf16[432,640]{1,0:T(8,128)(2,1)S(1)} collective-permute-done((bf16[432,640]{1,0:T(8,128)(2,1)S(1)}, bf16[432,640]{1,0:T(8,128)(2,1)S(1)}, u32[]{:S(2)}, u32[]{:S(2)}) %collective-permute-start.17) | collective-permute-done | bytes 552992 | tf_op jit(solution)/shard_map/ppermute | solution.py:292
  168.0 5.9 %collective-permute-done.16.packw_ref = bf16[432,640]{1,0:T(8,128)(2,1)S(1)} collective-permute-done((bf16[432,640]{1,0:T(8,128)(2,1)S(1)}, bf16[432,640]{1,0:T(8,128)(2,1)S(1)}, u32[]{:S(2)}, u32[]{:S(2)}) %collective-permute-start.16) | collective-permute-done | bytes 552992 | tf_op jit(solution)/shard_map/ppermute | solution.py:292
  173.9 8.4 %shard_map.156 = f32[128,1152]{1,0:T(8,128)} custom-call(bf16[1152,1728]{1,0:T(8,128)(2,1)S(1)} %copy-done.2, bf16[432,640]{1,0:T(8,128)(2,1)S(1)} %collective-permute-done.16.packw_ref, bf16[432,640]{1,0:T(8,128)(2,1)S(1)} %collective-permute-done.17.packe_ref, f32[128,640]{1,0:T(8,128)S(1)} %get-tuple-element.14.gk0_ref, ...), custom_call_target="tpu_custom_call" | custom-call | tf_op jit(solution)/shard_map/pallas_call | solution.py:350
  (70 shorter events, 1.4 us)
Async XLA Ops:
  7.2 43.4 %copy-start.9 = (bf16[8,16,1152]{2,1,0:T(8,128)(2,1)S(1)}, bf16[8,16,1152]{2,1,0:T(8,128)(2,1)}, u32[]{:S(2)}) copy-start(bf16[8,16,1152]{2,1,0:T(8,128)(2,1)} %param.14) | copy-start | bytes 884740
  7.2 106.9 %all-gather.3.cloned.1.call-start = ((), (), s32[]{:S(2)}) async-start(), calls=%async_computation | async-start | bytes 1492992 | tf_op jit(solution)/shard_map/all_gather | solution.py:299
  8.4 19.2 %collective-permute-start.4 = (bf16[72,1728]{1,0:T(8,128)(2,1)S(1)}, bf16[72,1728]{1,0:T(8,128)(2,1)S(1)}, u32[]{:S(2)}, u32[]{:S(2)}) collective-permute-start(bf16[72,1728]{1,0:T(8,128)(2,1)S(1)} %concatenate.13), channel_id=1, source_target_pairs={{0,256},{256,0},{1,257},{257,1},{2,258},{258,2},{3,259},{259,3},{4... | collective-permute-start | bytes 746504 | tf_op jit(solution)/shard_map/ppermute | solution.py:295
  12.2 22.6 %collective-permute-start.13 = (bf16[36,1152]{1,0:T(8,128)(2,1)}, bf16[36,1152]{1,0:T(8,128)(2,1)S(1)}, u32[]{:S(2)}, u32[]{:S(2)}) collective-permute-start(bf16[36,1152]{1,0:T(8,128)(2,1)} %param.19), channel_id=1, source_target_pairs={{0,256},{256,0},{1,257},{257,1},{2,258},{258,2},{3,259},{259,3},{4... | collective-permute-start | bytes 248840 | tf_op jit(solution)/shard_map/ppermute | solution.py:296
  27.7 61.8 %copy-start.13 = (bf16[144,1728]{1,0:T(8,128)(2,1)}, bf16[144,1728]{1,0:T(8,128)(2,1)S(1)}, u32[]{:S(2)}) copy-start(bf16[144,1728]{1,0:T(8,128)(2,1)S(1)} %pad_maximum_fusion.1.u0) | copy-start | bytes 1492996
  27.7 21.0 %collective-permute-start.5 = (bf16[144,1728]{1,0:T(8,128)(2,1)S(1)}, bf16[144,1728]{1,0:T(8,128)(2,1)}, u32[]{:S(2)}, u32[]{:S(2)}) collective-permute-start(bf16[144,1728]{1,0:T(8,128)(2,1)S(1)} %pad_maximum_fusion.1.u0), channel_id=1, source_target_pairs={{0,32},{32,64},{64,96},{96,128},{128,160},{160,192},{192,224},{224... | collective-permute-start | bytes 1493000 | tf_op jit(solution)/shard_map/ppermute | solution.py:284
  35.7 67.6 %copy-start.26 = (s32[1,2,3,5]{3,1,2,0:T(2,128)S(1)}, s32[1,2,3,5]{3,1,2,0:T(2,128)}, u32[]{:S(2)}) copy-start(s32[1,2,3,5]{3,1,2,0:T(2,128)} %param.23) | copy-start | bytes 364
  35.7 68.2 %copy-start.21 = (f32[1152]{0:T(1024)S(1)}, f32[1152]{0:T(1024)}, u32[]{:S(2)}) copy-start(f32[1152]{0:T(1024)} %param.15) | copy-start | bytes 13828
  35.8 68.2 %copy-start.22 = (s32[1152]{0:T(1024)S(1)}, s32[1152]{0:T(1024)}, u32[]{:S(2)}) copy-start(s32[1152]{0:T(1024)} %constant.42) | copy-start | bytes 13828
  35.8 68.2 %copy-start.23 = (s32[1152]{0:T(1024)S(1)}, s32[1152]{0:T(1024)}, u32[]{:S(2)}) copy-start(s32[1152]{0:T(1024)} %constant.33.clone) | copy-start | bytes 13828
  35.8 68.2 %copy-start.24 = (s32[1152]{0:T(1024)S(1)}, s32[1152]{0:T(1024)}, u32[]{:S(2)}) copy-start(s32[1152]{0:T(1024)} %constant.32.clone) | copy-start | bytes 13828
  35.8 68.2 %copy-start.25 = (s32[1152]{0:T(1024)S(1)}, s32[1152]{0:T(1024)}, u32[]{:S(2)}) copy-start(s32[1152]{0:T(1024)} %constant.31.clone) | copy-start | bytes 13828
  35.8 68.3 %copy-start.20 = (bf16[1152,192]{0,1:T(8,128)(2,1)S(1)}, bf16[1152,192]{0,1:T(8,128)(2,1)}, u32[]{:S(2)}) copy-start(bf16[1152,192]{0,1:T(8,128)(2,1)} %param.20) | copy-start | bytes 1327108
  48.6 16.7 %collective-permute-start.6 = (bf16[144,1728]{1,0:T(8,128)(2,1)}, bf16[144,1728]{1,0:T(8,128)(2,1)}, u32[]{:S(2)}, u32[]{:S(2)}) collective-permute-start(bf16[144,1728]{1,0:T(8,128)(2,1)} %collective-permute-done.5.m1), channel_id=1, source_target_pairs={{0,32},{32,64},{64,96},{96,128},{128,160},{160,192},{192,224},{224... | collective-permute-start | bytes 1493000 | tf_op jit(solution)/shard_map/ppermute | solution.py:284
  50.6 17.6 %collective-permute-start.1 = (bf16[128,1152]{1,0:T(8,128)(2,1)S(1)}, bf16[128,1152]{1,0:T(8,128)(2,1)S(1)}, u32[]{:S(2)}, u32[]{:S(2)}) collective-permute-start(bf16[128,1152]{1,0:T(8,128)(2,1)S(1)} %bitcast.12), channel_id=1, source_target_pairs={{32,0},{64,32},{96,64},{128,96},{160,128},{192,160},{224,192},{256... | collective-permute-start | bytes 884744 | tf_op jit(solution)/shard_map/ppermute | solution.py:288
  56.4 27.5 %collective-permute-start = (bf16[128,1152]{1,0:T(8,128)(2,1)S(1)}, bf16[128,1152]{1,0:T(8,128)(2,1)S(1)}, u32[]{:S(2)}, u32[]{:S(2)}) collective-permute-start(bf16[128,1152]{1,0:T(8,128)(2,1)S(1)} %bitcast.13), channel_id=1, source_target_pairs={{0,32},{32,64},{64,96},{96,128},{128,160},{160,192},{192,224},{224... | collective-permute-start | bytes 884744 | tf_op jit(solution)/shard_map/ppermute | solution.py:287
  65.4 23.0 %collective-permute-start.7 = (bf16[144,1728]{1,0:T(8,128)(2,1)}, bf16[144,1728]{1,0:T(8,128)(2,1)}, u32[]{:S(2)}, u32[]{:S(2)}) collective-permute-start(bf16[144,1728]{1,0:T(8,128)(2,1)} %collective-permute-done.6.m2), channel_id=1, source_target_pairs={{0,32},{32,64},{64,96},{96,128},{128,160},{160,192},{192,224},{224... | collective-permute-start | bytes 1493000 | tf_op jit(solution)/shard_map/ppermute | solution.py:284
  84.0 12.5 %collective-permute-start.3 = (bf16[384,1152]{1,0:T(8,128)(2,1)S(1)}, bf16[384,1152]{1,0:T(8,128)(2,1)S(1)}, u32[]{:S(2)}, u32[]{:S(2)}) collective-permute-start(bf16[384,1152]{1,0:T(8,128)(2,1)S(1)} %pad_maximum_fusion.x_ref), channel_id=1, source_target_pairs={{1,0},{2,1},{3,2},{4,3},{5,4},{6,5},{7,6},{8,7},{9,8},{10,9},{11,1... | collective-permute-start | bytes 2654216 | tf_op jit(solution)/shard_map/ppermute | solution.py:292
  85.9 24.3 %collective-permute-start.2 = (bf16[384,1152]{1,0:T(8,128)(2,1)S(1)}, bf16[384,1152]{1,0:T(8,128)(2,1)}, u32[]{:S(2)}, u32[]{:S(2)}) collective-permute-start(bf16[384,1152]{1,0:T(8,128)(2,1)S(1)} %pad_maximum_fusion.x_ref), channel_id=1, source_target_pairs={{0,1},{1,2},{2,3},{3,4},{4,5},{5,6},{6,7},{7,8},{8,9},{9,10},{10,1... | collective-permute-start | bytes 2654216 | tf_op jit(solution)/shard_map/ppermute | solution.py:292
  89.4 12.0 %collective-permute-start.11 = (bf16[80,1728]{1,0:T(8,128)(2,1)S(1)}, bf16[80,1728]{1,0:T(8,128)(2,1)}, u32[]{:S(2)}, u32[]{:S(2)}) collective-permute-start(bf16[80,1728]{1,0:T(8,128)(2,1)S(1)} %slice_select_fusion), channel_id=1, source_target_pairs={{0,32},{32,64},{64,96},{96,128},{128,160},{160,192},{192,224},{224... | collective-permute-start | bytes 829448 | tf_op jit(solution)/shard_map/ppermute | solution.py:284
  91.4 24.4 %collective-permute-start.8 = (bf16[144,1728]{1,0:T(8,128)(2,1)}, bf16[144,1728]{1,0:T(8,128)(2,1)}, u32[]{:S(2)}, u32[]{:S(2)}) collective-permute-start(bf16[144,1728]{1,0:T(8,128)(2,1)} %collective-permute-done.5.m1), channel_id=1, source_target_pairs={{0,1},{1,0},{2,3},{3,2},{4,5},{5,4},{6,7},{7,6},{8,9},{9,8},{10,11... | collective-permute-start | bytes 1493000 | tf_op jit(solution)/shard_map/ppermute | solution.py:281
  94.4 21.4 %collective-permute-start.9 = (bf16[144,1728]{1,0:T(8,128)(2,1)}, bf16[144,1728]{1,0:T(8,128)(2,1)}, u32[]{:S(2)}, u32[]{:S(2)}) collective-permute-start(bf16[144,1728]{1,0:T(8,128)(2,1)} %collective-permute-done.6.m2), channel_id=1, source_target_pairs={{0,1},{1,0},{2,3},{3,2},{4,5},{5,4},{6,7},{7,6},{8,9},{9,8},{10,11... | collective-permute-start | bytes 1493000 | tf_op jit(solution)/shard_map/ppermute | solution.py:281
  96.4 0.9 copy-start.15
  97.4 18.4 %collective-permute-start.10 = (bf16[144,1728]{1,0:T(8,128)(2,1)}, bf16[144,1728]{1,0:T(8,128)(2,1)}, u32[]{:S(2)}, u32[]{:S(2)}) collective-permute-start(bf16[144,1728]{1,0:T(8,128)(2,1)} %collective-permute-done.7.m3), channel_id=1, source_target_pairs={{0,1},{1,0},{2,3},{3,2},{4,5},{5,4},{6,7},{7,6},{8,9},{9,8},{10,11... | collective-permute-start | bytes 1493000 | tf_op jit(solution)/shard_map/ppermute | solution.py:281
  101.4 14.3 %collective-permute-start.12 = (bf16[80,1728]{1,0:T(8,128)(2,1)}, bf16[80,1728]{1,0:T(8,128)(2,1)}, u32[]{:S(2)}, u32[]{:S(2)}) collective-permute-start(bf16[80,1728]{1,0:T(8,128)(2,1)} %collective-permute-done.11.mh), channel_id=1, source_target_pairs={{0,1},{1,0},{2,3},{3,2},{4,5},{5,4},{6,7},{7,6},{8,9},{9,8},{10,11... | collective-permute-start | bytes 829448 | tf_op jit(solution)/shard_map/ppermute | solution.py:281
  105.6 1.8 copy-start.16
  107.4 1.8 copy-start.3
  109.3 0.9 copy-start.5
  113.2 0.9 copy-start.7
  114.1 1.7 copy-start.4
  114.1 1.7 copy-start.19
  114.1 1.8 copy-start.6
  114.1 2.1 %copy-start.8 = (bf16[384,1152]{1,0:T(8,128)(2,1)S(1)}, bf16[384,1152]{1,0:T(8,128)(2,1)}, u32[]{:S(2)}) copy-start(bf16[384,1152]{1,0:T(8,128)(2,1)} %copy-done.7) | copy-start | bytes 2654212
  116.2 1.0 copy-start.10
  117.2 1.1 copy-start.12
  118.2 1.0 copy-start.14
  119.3 0.8 copy-start.17
  120.1 0.8 copy-start.18
  137.6 16.9 %collective-permute-start.15 = (bf16[144,640]{1,0:T(8,128)(2,1)S(1)}, bf16[144,640]{1,0:T(8,128)(2,1)S(1)}, u32[]{:S(2)}, u32[]{:S(2)}) collective-permute-start(bf16[144,640]{1,0:T(8,128)(2,1)S(1)} %get-tuple-element.13.up_ref), channel_id=1, source_target_pairs={{32,0},{64,32},{96,64},{128,96},{160,128},{192,160},{224,192},{256... | collective-permute-start | bytes 552968 | tf_op jit(solution)/shard_map/ppermute | solution.py:288
  139.6 14.9 %collective-permute-start.14 = (bf16[144,640]{1,0:T(8,128)(2,1)S(1)}, bf16[144,640]{1,0:T(8,128)(2,1)S(1)}, u32[]{:S(2)}, u32[]{:S(2)}) collective-permute-start(bf16[144,640]{1,0:T(8,128)(2,1)S(1)} %get-tuple-element.13.up_ref), channel_id=1, source_target_pairs={{0,32},{32,64},{64,96},{96,128},{128,160},{160,192},{192,224},{224... | collective-permute-start | bytes 552968 | tf_op jit(solution)/shard_map/ppermute | solution.py:287
  143.5 2.2 %copy-start.1 = (bf16[1152,1728]{1,0:T(8,128)(2,1)S(1)}, bf16[1152,1728]{1,0:T(8,128)(2,1)}, u32[]{:S(2)}) copy-start(bf16[1152,1728]{1,0:T(8,128)(2,1)} %get-tuple-element.12.win_ref) | copy-start | bytes 11943940
  154.6 19.3 %copy-start.11 = (bf16[8,16,1152]{2,1,0:T(8,128)(2,1)S(1)}, bf16[8,16,1152]{2,1,0:T(8,128)(2,1)}, u32[]{:S(2)}) copy-start(bf16[8,16,1152]{2,1,0:T(8,128)(2,1)} %param.14) | copy-start | bytes 884740
  154.6 13.4 %collective-permute-start.17 = (bf16[432,640]{1,0:T(8,128)(2,1)S(1)}, bf16[432,640]{1,0:T(8,128)(2,1)S(1)}, u32[]{:S(2)}, u32[]{:S(2)}) collective-permute-start(bf16[432,640]{1,0:T(8,128)(2,1)S(1)} %constant_dynamic-update-slice_fusion.pack_ref), channel_id=1, source_target_pairs={{1,0},{2,1},{3,2},{4,3},{5,4},{6,5},{7,6},{8,7},{9,8},{10,9},{11,1... | collective-permute-start | bytes 1658888 | tf_op jit(solution)/shard_map/ppermute | solution.py:292
  161.0 12.9 %collective-permute-start.16 = (bf16[432,640]{1,0:T(8,128)(2,1)S(1)}, bf16[432,640]{1,0:T(8,128)(2,1)S(1)}, u32[]{:S(2)}, u32[]{:S(2)}) collective-permute-start(bf16[432,640]{1,0:T(8,128)(2,1)S(1)} %constant_dynamic-update-slice_fusion.pack_ref), channel_id=1, source_target_pairs={{0,1},{1,2},{2,3},{3,4},{4,5},{5,6},{6,7},{7,8},{8,9},{9,10},{10,1... | collective-permute-start | bytes 1658888 | tf_op jit(solution)/shard_map/ppermute | solution.py:292
  163.2 10.8 %copy-start = (bf16[1152,1728]{1,0:T(8,128)(2,1)S(1)}, bf16[1152,1728]{1,0:T(8,128)(2,1)}, u32[]{:S(2)}) copy-start(bf16[1152,1728]{1,0:T(8,128)(2,1)} %get-tuple-element.18.w_ref) | copy-start | bytes 11943940
  163.2 10.8 %copy-start.2 = (bf16[1152,1728]{1,0:T(8,128)(2,1)S(1)}, bf16[1152,1728]{1,0:T(8,128)(2,1)}, u32[]{:S(2)}) copy-start(bf16[1152,1728]{1,0:T(8,128)(2,1)} %get-tuple-element.12.win_ref) | copy-start | bytes 11943940
Sparse Core Ops, SparseCore 0:
  36.8 49.4 all-gather.2

commit v2 on v1

--- a/solution.py
+++ b/solution.py
@@ -65,25 +65,22 @@
         out_ref[i * T : (i + 1) * T, :] = nn(hidden, order_ref[...]).astype(BF)
 
 
-def forward_kernel(
-    core_ref, blocks_ref, hw_ref, hc_ref, he_ref, u0, m1, m2, m3, t1, t2, t3, mh, th, wout_ref, wpix_ref,
-    x_ref, meas_ref, filt_ref,
-    w_ref, win_ref, e_ref, den_ref, og_ref, pack_ref, stat_ref,
-    wo_ref, bias_ref, att_ref, sems,
-):
-    core = core_ref[0]
+def collect(blocks, w_ref, sems):
     copies = [
-        pltpu.make_async_copy(src, w_ref.at[pl.ds(144 * i, 144)], sems.at[i])
-        for i, src in enumerate((u0, m1, m2, m3, t1, t2, t3))
+        pltpu.make_async_copy(src, w_ref.at[pl.ds(144 * i, 144)], sems.at[i]) for i, src in enumerate(blocks)
     ]
-    copies.append(pltpu.make_async_copy(mh, w_ref.at[pl.ds(1008, 80)], sems.at[7]))
-    first = pl.multiple_of(16 * (1 - core), 16)
-    copies.append(pltpu.make_async_copy(th.at[pl.ds(first, 64)], w_ref.at[pl.ds(1088, 64)], sems.at[8]))
-    copies.append(pltpu.make_async_copy(wout_ref, wo_ref.at[pl.ds(64, HW)], sems.at[9]))
     for c in copies:
         c.start()
-    wo_ref[0:64, :] = jnp.zeros((64, D), BF)
-    att_ref[...] = jnp.zeros_like(att_ref)
+    return copies
+
+
+def forward_kernel(
+    blocks_ref, hw_ref, hc_ref, he_ref, b0, b1, b2, b3, b4, b5, b6, b7,
+    win_ref, e_ref, att_ref, stat_ref, rows_ref,
+    w_ref, bias_ref, acc_ref, sems,
+):
+    copies = collect((b0, b1, b2, b3, b4, b5, b6, b7), w_ref, sems)
+    acc_ref[...] = jnp.zeros_like(acc_ref)
 
     qc = (lax.broadcasted_iota(jnp.int32, (T, T), 0) & 8) > 0
     kc = (lax.broadcasted_iota(jnp.int32, (T, T), 1) & 8) > 0
@@ -96,6 +93,7 @@
     for r in range(3):
         for w in range(6):
             rows.append(jnp.where(lane_c, allowed(1, r, w), allowed(0, r, w)))
+    rows_ref[...] = jnp.concatenate(rows + [jnp.zeros((14, T), F32)], axis=0)
     for t in range(3):
         for r in range(3):
             seen = jnp.where(
@@ -105,7 +103,7 @@
             )
             j = 3 * t + r
             bias_ref[:, j * T : (j + 1) * T] = (1.0 - seen) * OFF
-    for c in copies[:9]:
+    for c in copies:
         c.wait()
     for g, h_ref in enumerate((hw_ref, hc_ref, he_ref)):
         for part in range(3):
@@ -130,22 +128,33 @@
         stats = jnp.where(lanes == 16 + e, inv, stats)
         a, b = window(V0 + HD * e)
         o = nn(low, win_ref[:, a:b]) * inv
-        att_ref[:, a - VB : b - VB] += head_only(o, V0 + HD * e, a)
-    copies[9].wait()
-    att = att_ref[...].astype(BF)
-    den = (x_ref[...].astype(F32) + nn(att, wo_ref[...])).astype(BF)
+        acc_ref[:, a - VB : b - VB] += head_only(o, V0 + HD * e, a)
+    att_ref[...] = acc_ref[...].astype(BF)
+    stat_ref[...] = stats
+
+
+def pixel_kernel(
+    att_ref, stat0_ref, rows_ref, place_ref, wout_ref, wpix_ref, x_ref, meas_ref, filt_ref,
+    den_ref, og_ref, pack_ref, stat_ref,
+):
+    lane_of = lax.broadcasted_iota(jnp.int32, (640, HW), 0)
+    order = jnp.where(lane_of == place_ref[...], 1.0, 0.0).astype(BF)
+    att = att_ref[...]
+    den = (x_ref[...].astype(F32) + nn(nn(att, order).astype(BF), wout_ref[...])).astype(BF)
     den_ref[...] = den
-    colors = nn(den, wpix_ref[...])
+    colors = nt(den, wpix_ref[...])
     filt = filt_ref[...]
     misfit = -meas_ref[...]
     for c in range(3):
         misfit = misfit + jnp.where(filt == c, colors[:, 64 * c : 64 * c + 64], 0.0)
     spread = jnp.concatenate([jnp.where(filt == c, misfit, 0.0) for c in range(3)], axis=1).astype(BF)
-    og = nt(spread, wpix_ref[...])
+    og = nn(spread, wpix_ref[...])
     og_ref[...] = og
-    up = nt(og.astype(BF), wo_ref[...]).astype(BF)
+    up = nt(nt(og.astype(BF), wout_ref[...]).astype(BF), order).astype(BF)
     pack_ref[0:T, :] = up
     prod = up.astype(F32) * att.astype(F32)
+    lanes = lax.broadcasted_iota(jnp.int32, (T, T), 1)
+    stats = stat0_ref[...]
     for e in range(H):
         a, b = window(V0 + HD * e)
         inner = jnp.sum(head_only(prod[:, a - VB : b - VB], V0 + HD * e, a), axis=1, keepdims=True)
@@ -157,14 +166,7 @@
     mid = rest.astype(BF)
     low = (rest - mid.astype(F32)).astype(BF)
     pack_ref[T : T + 16, :] = jnp.concatenate(
-        [
-            high,
-            mid,
-            low,
-            jnp.concatenate(rows[:16], axis=0).astype(BF),
-            jnp.concatenate(rows[16:] + [jnp.zeros((14, T), F32)], axis=0).astype(BF),
-        ],
-        axis=1,
+        [high, mid, low, rows_ref[0:16, :].astype(BF), rows_ref[16:32, :].astype(BF)], axis=1
     )
 
 
@@ -225,15 +227,19 @@
 
 
 def finish_kernel(
-    win_ref, packw_ref, packe_ref, gk0_ref, gv0_ref, gq_ref, w_ref, order_ref, x_ref, gain_ref, og_ref,
-    out_ref, gk_ref, gv_ref,
+    win_ref, packw_ref, packe_ref, gk0_ref, gv0_ref, gq_ref, order_ref, x_ref, gain_ref, og_ref,
+    b0, b1, b2, b3, b4, b5, b6, b7,
+    out_ref, gk_ref, gv_ref, w_ref, sems,
 ):
+    copies = collect((b0, b1, b2, b3, b4, b5, b6, b7), w_ref, sems)
     gk_ref[...] = gk0_ref[...]
     gv_ref[...] = gv0_ref[...]
     key_side(win_ref, ((0, packw_ref), (2, packe_ref)), gk_ref, gv_ref)
     gk = (gk_ref[:, 0:HW] * FACTOR).astype(BF)
     gv = gv_ref[:, 64:640].astype(BF)
     grads = jnp.concatenate([gk, gv, gq_ref[...]], axis=1)
+    for c in copies:
+        c.wait()
     moved = nt(grads, w_ref[...])
     high = moved.astype(BF)
     rest = moved - high.astype(F32)
@@ -252,36 +258,62 @@
     return jax.ShapeDtypeStruct(shape, dtype)
 
 
-def weight_targets(z, yh, core):
+def weight_targets(yh, z, x, core):
     place = np.arange(D)
     block, row = place // 144, place % 144
-    step = np.select([block == 7], [4], np.where(block > 3, block - 3, block))
-    sign = np.where(block > 3, 1, -1)
-    last0 = row
-    last1 = np.where(row < 80, row + 64, row - 80)
-    zs = jnp.where(core == 0, z + jnp.asarray(sign * step), z - jnp.asarray(sign * step)) & 7
-    inside = jnp.where(core == 0, jnp.asarray(last0), jnp.asarray(np.where(block == 7, last1, row)))
-    other = inside >= 72
-    ys = jnp.where(other, 1 - yh, yh)
-    return ((ys * 8 + zs) * 72 + inside - 72 * other.astype(jnp.int32)).astype(jnp.int32).reshape(1, D)
+    second = row >= 72
+    xs = (x + jnp.asarray(np.array([0, 3, 1, 2] * 2)[block])) & 3
+    cs = core ^ jnp.asarray((block >= 4).astype(np.int32))
+    last = xs == 3
+    hops = jnp.where(last & second, 0, xs + 1)
+    zs = (z + jnp.where(cs == 0, -hops, hops)) & 7
+    other = jnp.logical_xor(second, last & (cs == 1)).astype(jnp.int32)
+    return (((yh ^ other) * 8 + zs) * 72 + row % 72).astype(jnp.int32).reshape(1, D)
+
+
+def device(yh, z, yl, x, core):
+    return (((yh * 8 + z % 8) * 4 + yl) * 4 + x) * 2 + core
+
+
+def fetch_routes():
+    first, second, mirrored = [], [], []
+    for yh in range(2):
+        for z in range(8):
+            for yl in range(4):
+                for x in range(4):
+                    for core in range(2):
+                        me = device(yh, z, yl, x, core)
+                        far = z + (x + 1 if core else -x - 1)
+                        partner = device(1 - yh, z, 3 - yl, x, core)
+                        mirrored.append((partner, me))
+                        if x < 3:
+                            first.append((device(yh, far, yl, x, core), me))
+                            second.append((device(1 - yh, far, 3 - yl, x, core), me))
+                        elif core == 0:
+                            first.append((device(yh, far, yl, x, core), me))
+                            second.append((partner, me))
+                        else:
+                            first.append((device(1 - yh, far, 3 - yl, x, core), me))
+                            second.append((me, me))
+    return first, second, mirrored
 
 
 def on_device(tokens, gain, w_query, w_key, w_value, w_out, w_pixel, measured, filter_color, block_mask):
-    yh, z, core = lax.axis_index("yh"), lax.axis_index("z"), lax.axis_index("core")
+    yh, z, xi, core = (lax.axis_index(n) for n in ("yh", "z", "x", "core"))
     x = tokens.reshape(T, D)
     gain = gain.reshape(1, D)
-    ring = [(2 * i, 2 * ((i + 1) % 8)) for i in range(8)] + [(2 * i + 1, 2 * ((i + 7) % 8) + 1) for i in range(8)]
     south = [(i, i + 1) for i in range(15)]
     north = [(j, i) for i, j in south]
     east = [(i, (i + 1) % 32) for i in range(32)]
     west = [(j, i) for i, j in east]
     lat, lon = ("yh", "z"), ("yl", "x", "core")
+    first, second, mirrored = fetch_routes()
 
     def swap(v):
         return lax.ppermute(v, "core", [(0, 1), (1, 0)])
 
-    def step(v):
-        return lax.ppermute(v, ("z", "core"), ring)
+    def along(v, shift):
+        return lax.ppermute(v, "x", [(i, (i + shift) % 4) for i in range(4)])
 
     def columns(own):
         before = lax.ppermute(own, lat, south)
@@ -291,66 +323,72 @@
     def sides(column):
         return lax.ppermute(column, lon, east), lax.ppermute(column, lon, west)
 
+    out_other = lax.ppermute(w_out, lat + lon, mirrored)
+    out_both = jnp.concatenate([jnp.where(yh == 0, w_out, out_other), jnp.where(yh == 0, out_other, w_out)], axis=0)
+    full_out = lax.all_gather(out_both, "z", axis=0, tiled=True)
+    place = np.arange(HW)
+    place = (64 + (place // 36 % 2 * 8 + place // 72) * 36 + place % 36).astype(np.int32).reshape(1, HW)
     mine = jnp.concatenate([w_key, w_value, w_query], axis=1)
-    other = lax.ppermute(mine, "yh", [(0, 1), (1, 0)])
-    out_other = lax.ppermute(w_out, "yh", [(0, 1), (1, 0)])
-    both = jnp.concatenate([mine, other], axis=0)
-    out_both = jnp.stack([jnp.where(yh == 0, w_out, out_other), jnp.where(yh == 0, out_other, w_out)])
-    full_out = lax.all_gather(out_both, "z", axis=1).reshape(HW, D)
-    m1 = step(both)
-    t1 = swap(m1)
-    m2 = step(m1)
-    t2 = swap(m2)
-    m3 = step(m2)
-    t3 = swap(m3)
-    mh = step(jnp.where(core == 0, m3[0:80], m3[64:144]))
-    th = swap(mh)
+    fetched = jnp.concatenate(
+        [lax.ppermute(mine, lat + lon, first), lax.ppermute(mine, lat + lon, second)], axis=0
+    )
+    right, left = along(fetched, 1), along(fetched, 3)
+    across = jnp.concatenate([along(right[:72], 1), along(left[72:], 3)], axis=0)
+    held = (fetched, right, left, across)
+    blocks = held + tuple(swap(v) for v in held)
 
     column = columns(x)
     from_west, from_east = sides(column)
     order = pl.pallas_call(
-        order_kernel, out_shape=shaped((D, D)), in_specs=[VMEM], out_specs=VMEM, compiler_params=params(),
-    )(weight_targets(z, yh, core))
+        order_kernel, out_shape=shaped((D, D)), in_specs=[VMEM], out_specs=VMEM, compiler_params=params(16),
+        cost_estimate=pl.CostEstimate(flops=2_000_000_000, bytes_accessed=3_000_000, transcendentals=0),
+    )(weight_targets(yh, z, xi, core))
 
     def hidden(v):
         return pl.pallas_call(
-            hidden_kernel, out_shape=shaped((3 * T, D)), in_specs=[VMEM] * 3, out_specs=VMEM, compiler_params=params(),
+            hidden_kernel, out_shape=shaped((3 * T, D)), in_specs=[VMEM] * 3, out_specs=VMEM,
+            compiler_params=params(16),
+            cost_estimate=pl.CostEstimate(flops=3_000_000_000, bytes_accessed=5_000_000, transcendentals=0),
         )(v, gain, order)
 
     hw, hc, he = hidden(from_west), hidden(column), hidden(from_east)
-    w, win, e, den, og, pack, stat = pl.pallas_call(
+    win, e, att, stat0, rows = pl.pallas_call(
         forward_kernel,
         out_shape=(
-            shaped((D, QKV)), shaped((9 * T, QKV)), shaped((H * T, 9 * T)), shaped((T, D)), shaped((T, D), F32),
-            shaped((144, 640)), shaped((T, T), F32),
+            shaped((9 * T, QKV)), shaped((H * T, 9 * T)), shaped((T, 640)), shaped((T, T), F32), shaped((32, T), F32),
         ),
-        in_specs=[SMEM, SMEM] + [VMEM] * 3 + [ANY] * 10 + [VMEM] * 4,
-        out_specs=(VMEM,) * 7,
+        in_specs=[SMEM] + [VMEM] * 3 + [ANY] * 8,
+        out_specs=(VMEM,) * 5,
         scratch_shapes=[
-            pltpu.VMEM((640, D), BF), pltpu.VMEM((T, 9 * T), F32), pltpu.VMEM((T, 640), F32),
-            pltpu.SemaphoreType.DMA((10,)),
+            pltpu.VMEM((D, QKV), BF), pltpu.VMEM((T, 9 * T), F32), pltpu.VMEM((T, 640), F32),
+            pltpu.SemaphoreType.DMA((8,)),
         ],
-        compiler_params=params(),
-    )(
-        core.reshape(1).astype(jnp.int32), block_mask.reshape(30), hw, hc, he, both, m1, m2, m3, t1, t2, t3, mh, th,
-        full_out, w_pixel, x, measured.reshape(T, 64), filter_color.reshape(T, 64),
-    )
+        compiler_params=params(28),
+        cost_estimate=pl.CostEstimate(flops=12_000_000_000, bytes_accessed=8_000_000, transcendentals=1_000_000),
+    )(block_mask.reshape(30), hw, hc, he, *blocks)
+    den, og, pack, stat = pl.pallas_call(
+        pixel_kernel,
+        out_shape=(shaped((T, D)), shaped((T, D), F32), shaped((144, 640)), shaped((T, T), F32)),
+        in_specs=[VMEM] * 9, out_specs=(VMEM,) * 4,
+        compiler_params=params(16),
+    )(att, stat0, rows, jnp.asarray(place), full_out, w_pixel.T, x, measured.reshape(T, 64), filter_color.reshape(T, 64))
     packs = columns(pack)
     gq = pl.pallas_call(
         query_kernel, out_shape=shaped((T, HW)), in_specs=[VMEM] * 4, out_specs=VMEM,
-        scratch_shapes=[pltpu.VMEM((T, 640), F32)], compiler_params=params(),
-        cost_estimate=pl.CostEstimate(flops=8_000_000_000, bytes_accessed=6_000_000, transcendentals=0),
+        scratch_shapes=[pltpu.VMEM((T, 640), F32)], compiler_params=params(16),
+        cost_estimate=pl.CostEstimate(flops=4_000_000_000, bytes_accessed=6_000_000, transcendentals=0),
     )(win, e, pack, stat)
     packs_west, packs_east = sides(packs)
     gk, gv = pl.pallas_call(
         key_centre_kernel, out_shape=(shaped((T, 640), F32),) * 2, in_specs=[VMEM] * 2, out_specs=(VMEM,) * 2,
-        compiler_params=params(),
-        cost_estimate=pl.CostEstimate(flops=8_000_000_000, bytes_accessed=6_000_000, transcendentals=0),
+        compiler_params=params(16),
+        cost_estimate=pl.CostEstimate(flops=4_000_000_000, bytes_accessed=6_000_000, transcendentals=0),
     )(win, packs)
     guidance = pl.pallas_call(
-        finish_kernel, out_shape=shaped((T, D), F32), in_specs=[VMEM] * 11, out_specs=VMEM,
-        scratch_shapes=[pltpu.VMEM((T, 640), F32)] * 2, compiler_params=params(),
-    )(win, packs_west, packs_east, gk, gv, gq, w, order, x, gain, og)
+        finish_kernel, out_shape=shaped((T, D), F32), in_specs=[VMEM] * 10 + [ANY] * 8, out_specs=VMEM,
+        scratch_shapes=[pltpu.VMEM((T, 640), F32)] * 2 + [pltpu.VMEM((D, QKV), BF), pltpu.SemaphoreType.DMA((8,))],
+        compiler_params=params(24),
+    )(win, packs_west, packs_east, gk, gv, gq, order, x, gain, og, *blocks)
     return den.reshape(tokens.shape), guidance.reshape(tokens.shape)
 
 

time: 190 us -> 177 us (0.932)
  the two profiles are of different devices: /device:TPU:48 before, /device:TPU:39 now
where the time goes in v2:
time: 177 us; the launch traced here: 176 us
  starting transfers between devices  68.6 us (39%)
  Pallas kernels  37.9 us (21%)
  waiting for transfers between devices  29.6 us (17%)
  local copies, waits for them, and re-layouts  21.2 us (12%)
  between operations  14.6 us (8%)
  other arithmetic  4.49 us (3%)
    unnamed x61, local copies, waits for them, and re-layouts  17.6 us
    ppermute x2, starting transfers between devices, columns(): after = lax.ppermute(own, lat, north)  16.3 us
    ppermute x4, starting transfers between devices, sides(): return (lax.ppermute(column, lon, east), lax.ppermute(column, lon, west))  15.1 us
    ppermute x1, waiting for transfers between devices, on_device(): lax.ppermute(mine, lat + lon, first)  13.5 us
    pallas_call x1, Pallas kernels, on_device(): pl.pallas_call(forward_kernel, out_shape=(shaped((9 * T, QKV)), shaped((H...  12.5 us
    pallas_call x1, Pallas kernels, on_device(): pl.pallas_call(finish_kernel, out_shape=shaped((T, D), F32), in_specs=[VM...  10.8 us
    ppermute x4, starting transfers between devices, along(): return lax.ppermute(v, 'x', [(i, (i + shift) % 4) for i in range(4)])  10.7 us
    ppermute x4, starting transfers between devices, swap(): return lax.ppermute(v, 'core', [(0, 1), (1, 0)])  9.3 us
  transfers between devices with their start and end apart: 20, of which 7 were waited for; matrix products, arithmetic and copies ran while one was open for 5% of the time, Pallas kernels for 14%

profile of v2, /device:TPU:39, one launch (start us, length us, event | category | flops | bytes accessed | tf_op | source)
XLA Modules:
  0.0 176.2 jit_solution(2038012248654324481)
XLA Ops:
  7.2 4.0 %collective-permute-start = (bf16[128,1152]{1,0:T(8,128)(2,1)}, bf16[128,1152]{1,0:T(8,128)(2,1)}, u32[]{:S(2)}, u32[]{:S(2)}) collective-permute-start(bf16[128,1152]{1,0:T(8,128)(2,1)} %bitcast.6), channel_id=1, source_target_pairs={{0,32},{32,64},{64,96},{96,128},{128,160},{160,192},{192,224},{224... | collective-permute-start | bytes 884744 | tf_op jit(solution)/shard_map/ppermute | solution.py:319
  11.2 8.1 %collective-permute-start.1 = (bf16[128,1152]{1,0:T(8,128)(2,1)}, bf16[128,1152]{1,0:T(8,128)(2,1)}, u32[]{:S(2)}, u32[]{:S(2)}) collective-permute-start(bf16[128,1152]{1,0:T(8,128)(2,1)} %bitcast.7), channel_id=1, source_target_pairs={{32,0},{64,32},{96,64},{128,96},{160,128},{192,160},{224,192},{256... | collective-permute-start | bytes 884744 | tf_op jit(solution)/shard_map/ppermute | solution.py:320
  19.4 1.1 concatenate.19
  20.5 4.9 %collective-permute-start.4 = (bf16[72,1728]{1,0:T(8,128)(2,1)S(1)}, bf16[72,1728]{1,0:T(8,128)(2,1)}, u32[]{:S(2)}, u32[]{:S(2)}) collective-permute-start(bf16[72,1728]{1,0:T(8,128)(2,1)S(1)} %concatenate.19), channel_id=1, source_target_pairs={{224,0},{33,1},{194,2},{67,3},{164,4},{101,5},{134,6},{415,7},{232... | collective-permute-start | bytes 746504 | tf_op jit(solution)/shard_map/ppermute | solution.py:333
  26.0 4.4 %collective-permute-start.14 = (bf16[36,1152]{1,0:T(8,128)(2,1)}, bf16[36,1152]{1,0:T(8,128)(2,1)}, u32[]{:S(2)}, u32[]{:S(2)}) collective-permute-start(bf16[36,1152]{1,0:T(8,128)(2,1)} %param.20), channel_id=1, source_target_pairs={{280,0},{281,1},{282,2},{283,3},{284,4},{285,5},{286,6},{287,7},{2... | collective-permute-start | bytes 248840 | tf_op jit(solution)/shard_map/ppermute | solution.py:326
  32.6 13.5 %collective-permute-done.4 = bf16[72,1728]{1,0:T(8,128)(2,1)} collective-permute-done((bf16[72,1728]{1,0:T(8,128)(2,1)S(1)}, bf16[72,1728]{1,0:T(8,128)(2,1)}, u32[]{:S(2)}, u32[]{:S(2)}) %collective-permute-start.4) | collective-permute-done | bytes 248864 | tf_op jit(solution)/shard_map/ppermute | solution.py:333
  46.1 1.7 constant_dynamic-update-slice_fusion.1
  48.5 1.9 %collective-permute-start.6 = (bf16[144,1728]{1,0:T(8,128)(2,1)}, bf16[144,1728]{1,0:T(8,128)(2,1)S(1)}, u32[]{:S(2)}, u32[]{:S(2)}) collective-permute-start(bf16[144,1728]{1,0:T(8,128)(2,1)} %constant_dynamic-update-slice_fusion.b0), channel_id=1, source_target_pairs={{0,2},{2,4},{4,6},{6,0},{1,3},{3,5},{5,7},{7,1},{8,10},{10,12},{12... | collective-permute-start | bytes 1493000 | tf_op jit(solution)/shard_map/ppermute | solution.py:316
  50.4 3.4 %collective-permute-start.7 = (bf16[144,1728]{1,0:T(8,128)(2,1)}, bf16[144,1728]{1,0:T(8,128)(2,1)}, u32[]{:S(2)}, u32[]{:S(2)}) collective-permute-start(bf16[144,1728]{1,0:T(8,128)(2,1)} %constant_dynamic-update-slice_fusion.b0), channel_id=1, source_target_pairs={{0,6},{2,0},{4,2},{6,4},{1,7},{3,1},{5,3},{7,5},{8,14},{10,8},{12,... | collective-permute-start | bytes 1493000 | tf_op jit(solution)/shard_map/ppermute | solution.py:316
  53.8 1.0 broadcast_select_fusion.1
  54.8 2.1 %pad_maximum_fusion.x_ref = bf16[384,1152]{1,0:T(8,128)(2,1)} fusion(bf16[128,1152]{1,0:T(8,128)(2,1)} %collective-permute-done.1, bf16[128,1152]{1,0:T(8,128)(2,1)S(1)} %bitcast.8, bf16[128,1152]{1,0:T(8,128)(2,1)} %collective-permute-done), kind=kLoop, calls=%fused_computation | loop fusion | flops 2654208 | bytes 1769472 | tf_op jit(solution)/shard_map/concatenate | solution.py:321
  56.9 1.9 %collective-permute-start.2 = (bf16[384,1152]{1,0:T(8,128)(2,1)}, bf16[384,1152]{1,0:T(8,128)(2,1)}, u32[]{:S(2)}, u32[]{:S(2)}) collective-permute-start(bf16[384,1152]{1,0:T(8,128)(2,1)} %pad_maximum_fusion.x_ref), channel_id=1, source_target_pairs={{0,1},{1,2},{2,3},{3,4},{4,5},{5,6},{6,7},{7,8},{8,9},{9,10},{10,1... | collective-permute-start | bytes 2654216 | tf_op jit(solution)/shard_map/ppermute | solution.py:324
  59.5 2.4 %collective-permute-start.10 = (bf16[144,1728]{1,0:T(8,128)(2,1)}, bf16[144,1728]{1,0:T(8,128)(2,1)S(1)}, u32[]{:S(2)}, u32[]{:S(2)}) collective-permute-start(bf16[144,1728]{1,0:T(8,128)(2,1)} %constant_dynamic-update-slice_fusion.b0), channel_id=1, source_target_pairs={{0,1},{1,0},{2,3},{3,2},{4,5},{5,4},{6,7},{7,6},{8,9},{9,8},{10,11... | collective-permute-start | bytes 1493000 | tf_op jit(solution)/shard_map/ppermute | solution.py:313
  61.9 1.9 %collective-permute-start.3 = (bf16[384,1152]{1,0:T(8,128)(2,1)}, bf16[384,1152]{1,0:T(8,128)(2,1)S(1)}, u32[]{:S(2)}, u32[]{:S(2)}) collective-permute-start(bf16[384,1152]{1,0:T(8,128)(2,1)} %pad_maximum_fusion.x_ref), channel_id=1, source_target_pairs={{1,0},{2,1},{3,2},{4,3},{5,4},{6,5},{7,6},{8,7},{9,8},{10,9},{11,1... | collective-permute-start | bytes 2654216 | tf_op jit(solution)/shard_map/ppermute | solution.py:324
  64.2 3.5 %collective-permute-start.8 = (bf16[72,1728]{1,0:T(8,128)(2,1)S(1)}, bf16[72,1728]{1,0:T(8,128)(2,1)S(1)}, u32[]{:S(2)}, u32[]{:S(2)}) collective-permute-start(bf16[72,1728]{1,0:T(8,128)(2,1)S(1)} %slice.8), channel_id=1, source_target_pairs={{0,2},{2,4},{4,6},{6,0},{1,3},{3,5},{5,7},{7,1},{8,10},{10,12},{12... | collective-permute-start | bytes 746504 | tf_op jit(solution)/shard_map/ppermute | solution.py:316
  67.7 1.0 slice.9
  68.7 1.9 %collective-permute-start.9 = (bf16[72,1728]{1,0:T(8,128)(2,1)S(1)}, bf16[72,1728]{1,0:T(8,128)(2,1)S(1)}, u32[]{:S(2)}, u32[]{:S(2)}) collective-permute-start(bf16[72,1728]{1,0:T(8,128)(2,1)S(1)} %slice.9), channel_id=1, source_target_pairs={{0,6},{2,0},{4,2},{6,4},{1,7},{3,1},{5,3},{7,5},{8,14},{10,8},{12,... | collective-permute-start | bytes 746504 | tf_op jit(solution)/shard_map/ppermute | solution.py:316
  70.6 2.9 %shard_map.160.hc_ref = bf16[384,1152]{1,0:T(8,128)(2,1)S(1)} custom-call(bf16[384,1152]{1,0:T(8,128)(2,1)} %pad_maximum_fusion.x_ref, f32[1,1152]{1,0:T(1,128)S(1)} %reshape.30.gain_ref, bf16[1152,1152]{1,0:T(8,128)(2,1)S(1)} %shard_map.158.order_ref), custom_call_target="tpu_custom_call" | custom-call | flops 3000000000 | bytes 5000000 | tf_op jit(solution)/shard_map/pallas_call | solution.py:348
  73.5 5.8 %collective-permute-done.8 = bf16[72,1728]{1,0:T(8,128)(2,1)S(1)} collective-permute-done((bf16[72,1728]{1,0:T(8,128)(2,1)S(1)}, bf16[72,1728]{1,0:T(8,128)(2,1)S(1)}, u32[]{:S(2)}, u32[]{:S(2)}) %collective-permute-start.8) | collective-permute-done | bytes 248864 | tf_op jit(solution)/shard_map/ppermute | solution.py:316
  79.3 1.9 %collective-permute-start.11 = (bf16[144,1728]{1,0:T(8,128)(2,1)S(1)}, bf16[144,1728]{1,0:T(8,128)(2,1)S(1)}, u32[]{:S(2)}, u32[]{:S(2)}) collective-permute-start(bf16[144,1728]{1,0:T(8,128)(2,1)S(1)} %collective-permute-done.6.b1), channel_id=1, source_target_pairs={{0,1},{1,0},{2,3},{3,2},{4,5},{5,4},{6,7},{7,6},{8,9},{9,8},{10,11... | collective-permute-start | bytes 1493000 | tf_op jit(solution)/shard_map/ppermute | solution.py:313
  81.2 2.6 %collective-permute-done.9 = bf16[72,1728]{1,0:T(8,128)(2,1)S(1)} collective-permute-done((bf16[72,1728]{1,0:T(8,128)(2,1)S(1)}, bf16[72,1728]{1,0:T(8,128)(2,1)S(1)}, u32[]{:S(2)}, u32[]{:S(2)}) %collective-permute-start.9) | collective-permute-done | bytes 248864 | tf_op jit(solution)/shard_map/ppermute | solution.py:316
  83.9 3.1 %collective-permute-start.12 = (bf16[144,1728]{1,0:T(8,128)(2,1)}, bf16[144,1728]{1,0:T(8,128)(2,1)S(1)}, u32[]{:S(2)}, u32[]{:S(2)}) collective-permute-start(bf16[144,1728]{1,0:T(8,128)(2,1)} %collective-permute-done.7.b2), channel_id=1, source_target_pairs={{0,1},{1,0},{2,3},{3,2},{4,5},{5,4},{6,7},{7,6},{8,9},{9,8},{10,11... | collective-permute-start | bytes 1493000 | tf_op jit(solution)/shard_map/ppermute | solution.py:313
  87.0 1.9 %collective-permute-start.13 = (bf16[144,1728]{1,0:T(8,128)(2,1)S(1)}, bf16[144,1728]{1,0:T(8,128)(2,1)S(1)}, u32[]{:S(2)}, u32[]{:S(2)}) collective-permute-start(bf16[144,1728]{1,0:T(8,128)(2,1)S(1)} %constant_dynamic-update-slice_fusion.2.b3), channel_id=1, source_target_pairs={{0,1},{1,0},{2,3},{3,2},{4,5},{5,4},{6,7},{7,6},{8,9},{9,8},{10,11... | collective-permute-start | bytes 1493000 | tf_op jit(solution)/shard_map/ppermute | solution.py:313
  88.9 2.9 %shard_map.159.hw_ref = bf16[384,1152]{1,0:T(8,128)(2,1)S(1)} custom-call(bf16[384,1152]{1,0:T(8,128)(2,1)} %collective-permute-done.2.x_ref, f32[1,1152]{1,0:T(1,128)S(1)} %reshape.30.gain_ref, bf16[1152,1152]{1,0:T(8,128)(2,1)S(1)} %shard_map.158.order_ref), custom_call_target="tpu_custom_call" | custom-call | flops 3000000000 | bytes 5000000 | tf_op jit(solution)/shard_map/pallas_call | solution.py:348
  91.8 1.7 shard_map.161.he_ref
  93.6 12.5 %shard_map.162 = (bf16[1152,1728]{1,0:T(8,128)(2,1)S(1)}, bf16[1024,1152]{1,0:T(8,128)(2,1)S(1)}, bf16[128,640]{1,0:T(8,128)(2,1)S(1)}, f32[128,128]{1,0:T(8,128)S(1)}, f32[32,128]{1,0:T(8,128)S(1)}) custom-call(s32[30]{0:T(128)S(1)} %copy-done.23, bf16[384,1152]{1,0:T(8,128)(2,1)S(1)} %shard_map.159.hw_ref, bf16[384,1152]{1,0:T(8,128)(2,1)S(1)} %shard_map.160.hc_ref, ...), custom_call_target="tpu_custom_call" | custom-call | flops 12000000000 | bytes 8000000 | tf_op jit(solution)/shard_map/pallas_call | solution.py:355
  106.2 1.9 %copy-done = bf16[1152,1728]{1,0:T(8,128)(2,1)} copy-done((bf16[1152,1728]{1,0:T(8,128)(2,1)}, bf16[1152,1728]{1,0:T(8,128)(2,1)S(1)}, u32[]{:S(2)}) %copy-start) | copy-done | bytes 3981336
  108.1 0.8 copy-done.7
  108.9 0.8 copy-done.9
  109.7 0.8 copy-done.11
  112.6 1.4 copy-done.24
  114.1 1.3 copy-done.4
  115.4 1.0 copy-done.15
  116.4 0.9 copy-done.17
  117.3 0.8 copy-done.19
  118.2 0.8 copy-done.21
  119.7 2.2 %shard_map.163 = (bf16[128,1152]{1,0:T(8,128)(2,1)}, f32[128,1152]{1,0:T(8,128)S(1)}, bf16[144,640]{1,0:T(8,128)(2,1)S(1)}, f32[128,128]{1,0:T(8,128)S(1)}) custom-call(bf16[128,640]{1,0:T(8,128)(2,1)S(1)} %copy-done.17, f32[128,128]{1,0:T(8,128)S(1)} %copy-done.21, f32[32,128]{1,0:T(8,128)S(1)} %get-tuple-element.15.rows_ref, s32[1,576]{1,0:T(1,128)S(1)} %copy-done.22, ...), custom_call_target="tpu_custom_call" | custom-call | tf_op jit(solution)/shard_map/pallas_call | solution.py:369
  121.9 3.2 %collective-permute-start.15 = (bf16[144,640]{1,0:T(8,128)(2,1)S(1)}, bf16[144,640]{1,0:T(8,128)(2,1)S(1)}, u32[]{:S(2)}, u32[]{:S(2)}) collective-permute-start(bf16[144,640]{1,0:T(8,128)(2,1)S(1)} %get-tuple-element.18.up_ref), channel_id=1, source_target_pairs={{0,32},{32,64},{64,96},{96,128},{128,160},{160,192},{192,224},{224... | collective-permute-start | bytes 552968 | tf_op jit(solution)/shard_map/ppermute | solution.py:319
  125.1 8.1 %collective-permute-start.16 = (bf16[144,640]{1,0:T(8,128)(2,1)S(1)}, bf16[144,640]{1,0:T(8,128)(2,1)S(1)}, u32[]{:S(2)}, u32[]{:S(2)}) collective-permute-start(bf16[144,640]{1,0:T(8,128)(2,1)S(1)} %get-tuple-element.18.up_ref), channel_id=1, source_target_pairs={{32,0},{64,32},{96,64},{128,96},{160,128},{192,160},{224,192},{256... | collective-permute-start | bytes 552968 | tf_op jit(solution)/shard_map/ppermute | solution.py:320
  133.2 2.3 %collective-permute-done.15 = bf16[144,640]{1,0:T(8,128)(2,1)S(1)} collective-permute-done((bf16[144,640]{1,0:T(8,128)(2,1)S(1)}, bf16[144,640]{1,0:T(8,128)(2,1)S(1)}, u32[]{:S(2)}, u32[]{:S(2)}) %collective-permute-start.15) | collective-permute-done | bytes 184352 | tf_op jit(solution)/shard_map/ppermute | solution.py:319
  135.6 0.8 collective-permute-done.16
  136.4 9.1 %collective-permute-start.17 = (bf16[432,640]{1,0:T(8,128)(2,1)S(1)}, bf16[432,640]{1,0:T(8,128)(2,1)S(1)}, u32[]{:S(2)}, u32[]{:S(2)}) collective-permute-start(bf16[432,640]{1,0:T(8,128)(2,1)S(1)} %constant_dynamic-update-slice_fusion.4.pack_ref), channel_id=1, source_target_pairs={{0,1},{1,2},{2,3},{3,4},{4,5},{5,6},{6,7},{7,8},{8,9},{9,10},{10,1... | collective-permute-start | bytes 1658888 | tf_op jit(solution)/shard_map/ppermute | solution.py:324
  145.6 2.1 %collective-permute-start.18 = (bf16[432,640]{1,0:T(8,128)(2,1)S(1)}, bf16[432,640]{1,0:T(8,128)(2,1)S(1)}, u32[]{:S(2)}, u32[]{:S(2)}) collective-permute-start(bf16[432,640]{1,0:T(8,128)(2,1)S(1)} %constant_dynamic-update-slice_fusion.4.pack_ref), channel_id=1, source_target_pairs={{1,0},{2,1},{3,2},{4,3},{5,4},{6,5},{7,6},{8,7},{9,8},{10,9},{11,1... | collective-permute-start | bytes 1658888 | tf_op jit(solution)/shard_map/ppermute | solution.py:324
  147.7 2.2 %copy-done.1 = bf16[1152,1728]{1,0:T(8,128)(2,1)S(1)} copy-done((bf16[1152,1728]{1,0:T(8,128)(2,1)S(1)}, bf16[1152,1728]{1,0:T(8,128)(2,1)}, u32[]{:S(2)}) %copy-start.1) | copy-done | bytes 3981336
  149.9 2.3 %shard_map.165.gq_ref = bf16[128,576]{1,0:T(8,128)(2,1)S(1)} custom-call(bf16[1152,1728]{1,0:T(8,128)(2,1)S(1)} %copy-done.1, bf16[1024,1152]{1,0:T(8,128)(2,1)S(1)} %copy-done.25, bf16[144,640]{1,0:T(8,128)(2,1)S(1)} %get-tuple-element.18.up_ref, f32[128,128]{1,0:T(8,128)S(1)} %get-tuple-element.22.stat_ref), custom_call_target="tpu_custom_call" | custom-call | flops 4000000000 | bytes 6000000 | tf_op jit(solution)/shard_map/pallas_call | solution.py:376
  152.2 2.1 %shard_map.164 = (f32[128,640]{1,0:T(8,128)S(1)}, f32[128,640]{1,0:T(8,128)S(1)}) custom-call(bf16[1152,1728]{1,0:T(8,128)(2,1)S(1)} %copy-done.1, bf16[432,640]{1,0:T(8,128)(2,1)S(1)} %constant_dynamic-update-slice_fusion.4.pack_ref), custom_call_target="tpu_custom_call" | custom-call | flops 4000000000 | bytes 6000000 | tf_op jit(solution)/shard_map/pallas_call | solution.py:382
  154.3 4.1 %collective-permute-done.18.packe_ref = bf16[432,640]{1,0:T(8,128)(2,1)S(1)} collective-permute-done((bf16[432,640]{1,0:T(8,128)(2,1)S(1)}, bf16[432,640]{1,0:T(8,128)(2,1)S(1)}, u32[]{:S(2)}, u32[]{:S(2)}) %collective-permute-start.18) | collective-permute-done | bytes 552992 | tf_op jit(solution)/shard_map/ppermute | solution.py:324
  158.5 10.8 %shard_map.166 = f32[128,1152]{1,0:T(8,128)} custom-call(bf16[1152,1728]{1,0:T(8,128)(2,1)S(1)} %copy-done.2, bf16[432,640]{1,0:T(8,128)(2,1)S(1)} %collective-permute-done.17.packw_ref, bf16[432,640]{1,0:T(8,128)(2,1)S(1)} %collective-permute-done.18.packe_ref, f32[128,640]{1,0:T(8,128)S(1)} %get-tuple-element.19.gk0_ref, ...), custom_call_target="tpu_custom_call" | custom-call | tf_op jit(solution)/shard_map/pallas_call | solution.py:387
  (76 shorter events, 7.6 us)
Async XLA Ops:
  7.2 106.9 %all-gather.2.cloned.1.call-start = ((), (), s32[]{:S(2)}) async-start(), calls=%async_computation | async-start | bytes 1492992 | tf_op jit(solution)/shard_map/all_gather | solution.py:328
  7.2 47.6 %collective-permute-start = (bf16[128,1152]{1,0:T(8,128)(2,1)}, bf16[128,1152]{1,0:T(8,128)(2,1)}, u32[]{:S(2)}, u32[]{:S(2)}) collective-permute-start(bf16[128,1152]{1,0:T(8,128)(2,1)} %bitcast.6), channel_id=1, source_target_pairs={{0,32},{32,64},{64,96},{96,128},{128,160},{160,192},{192,224},{224... | collective-permute-start | bytes 884744 | tf_op jit(solution)/shard_map/ppermute | solution.py:319
  11.2 43.6 %collective-permute-start.1 = (bf16[128,1152]{1,0:T(8,128)(2,1)}, bf16[128,1152]{1,0:T(8,128)(2,1)}, u32[]{:S(2)}, u32[]{:S(2)}) collective-permute-start(bf16[128,1152]{1,0:T(8,128)(2,1)} %bitcast.7), channel_id=1, source_target_pairs={{32,0},{64,32},{96,64},{128,96},{160,128},{192,160},{224,192},{256... | collective-permute-start | bytes 884744 | tf_op jit(solution)/shard_map/ppermute | solution.py:320
  20.5 25.7 %collective-permute-start.4 = (bf16[72,1728]{1,0:T(8,128)(2,1)S(1)}, bf16[72,1728]{1,0:T(8,128)(2,1)}, u32[]{:S(2)}, u32[]{:S(2)}) collective-permute-start(bf16[72,1728]{1,0:T(8,128)(2,1)S(1)} %concatenate.19), channel_id=1, source_target_pairs={{224,0},{33,1},{194,2},{67,3},{164,4},{101,5},{134,6},{415,7},{232... | collective-permute-start | bytes 746504 | tf_op jit(solution)/shard_map/ppermute | solution.py:333
  25.4 22.5 %collective-permute-start.5 = (bf16[72,1728]{1,0:T(8,128)(2,1)S(1)}, bf16[72,1728]{1,0:T(8,128)(2,1)S(1)}, u32[]{:S(2)}, u32[]{:S(2)}) collective-permute-start(bf16[72,1728]{1,0:T(8,128)(2,1)S(1)} %concatenate.19), channel_id=1, source_target_pairs={{504,0},{313,1},{474,2},{347,3},{444,4},{381,5},{286,6},{7,7},{496... | collective-permute-start | bytes 746504 | tf_op jit(solution)/shard_map/ppermute | solution.py:333
  26.0 27.8 %collective-permute-start.14 = (bf16[36,1152]{1,0:T(8,128)(2,1)}, bf16[36,1152]{1,0:T(8,128)(2,1)}, u32[]{:S(2)}, u32[]{:S(2)}) collective-permute-start(bf16[36,1152]{1,0:T(8,128)(2,1)} %param.20), channel_id=1, source_target_pairs={{280,0},{281,1},{282,2},{283,3},{284,4},{285,5},{286,6},{287,7},{2... | collective-permute-start | bytes 248840 | tf_op jit(solution)/shard_map/ppermute | solution.py:326
  31.3 0.7 copy-start.26
  31.3 0.7 copy-start.27
  31.3 23.5 %copy-start.3 = (bf16[8,16,1152]{2,1,0:T(8,128)(2,1)S(1)}, bf16[8,16,1152]{2,1,0:T(8,128)(2,1)}, u32[]{:S(2)}) copy-start(bf16[8,16,1152]{2,1,0:T(8,128)(2,1)} %param.15) | copy-start | bytes 884740
  48.5 15.7 %collective-permute-start.6 = (bf16[144,1728]{1,0:T(8,128)(2,1)}, bf16[144,1728]{1,0:T(8,128)(2,1)S(1)}, u32[]{:S(2)}, u32[]{:S(2)}) collective-permute-start(bf16[144,1728]{1,0:T(8,128)(2,1)} %constant_dynamic-update-slice_fusion.b0), channel_id=1, source_target_pairs={{0,2},{2,4},{4,6},{6,0},{1,3},{3,5},{5,7},{7,1},{8,10},{10,12},{12... | collective-permute-start | bytes 1493000 | tf_op jit(solution)/shard_map/ppermute | solution.py:316
  50.4 17.3 %collective-permute-start.7 = (bf16[144,1728]{1,0:T(8,128)(2,1)}, bf16[144,1728]{1,0:T(8,128)(2,1)}, u32[]{:S(2)}, u32[]{:S(2)}) collective-permute-start(bf16[144,1728]{1,0:T(8,128)(2,1)} %constant_dynamic-update-slice_fusion.b0), channel_id=1, source_target_pairs={{0,6},{2,0},{4,2},{6,4},{1,7},{3,1},{5,3},{7,5},{8,14},{10,8},{12,... | collective-permute-start | bytes 1493000 | tf_op jit(solution)/shard_map/ppermute | solution.py:316
  56.9 30.1 %collective-permute-start.2 = (bf16[384,1152]{1,0:T(8,128)(2,1)}, bf16[384,1152]{1,0:T(8,128)(2,1)}, u32[]{:S(2)}, u32[]{:S(2)}) collective-permute-start(bf16[384,1152]{1,0:T(8,128)(2,1)} %pad_maximum_fusion.x_ref), channel_id=1, source_target_pairs={{0,1},{1,2},{2,3},{3,4},{4,5},{5,6},{6,7},{7,8},{8,9},{9,10},{10,1... | collective-permute-start | bytes 2654216 | tf_op jit(solution)/shard_map/ppermute | solution.py:324
  59.5 34.0 %collective-permute-start.10 = (bf16[144,1728]{1,0:T(8,128)(2,1)}, bf16[144,1728]{1,0:T(8,128)(2,1)S(1)}, u32[]{:S(2)}, u32[]{:S(2)}) collective-permute-start(bf16[144,1728]{1,0:T(8,128)(2,1)} %constant_dynamic-update-slice_fusion.b0), channel_id=1, source_target_pairs={{0,1},{1,0},{2,3},{3,2},{4,5},{5,4},{6,7},{7,6},{8,9},{9,8},{10,11... | collective-permute-start | bytes 1493000 | tf_op jit(solution)/shard_map/ppermute | solution.py:313
  61.9 29.9 %collective-permute-start.3 = (bf16[384,1152]{1,0:T(8,128)(2,1)}, bf16[384,1152]{1,0:T(8,128)(2,1)S(1)}, u32[]{:S(2)}, u32[]{:S(2)}) collective-permute-start(bf16[384,1152]{1,0:T(8,128)(2,1)} %pad_maximum_fusion.x_ref), channel_id=1, source_target_pairs={{1,0},{2,1},{3,2},{4,3},{5,4},{6,5},{7,6},{8,7},{9,8},{10,9},{11,1... | collective-permute-start | bytes 2654216 | tf_op jit(solution)/shard_map/ppermute | solution.py:324
  64.2 15.1 %collective-permute-start.8 = (bf16[72,1728]{1,0:T(8,128)(2,1)S(1)}, bf16[72,1728]{1,0:T(8,128)(2,1)S(1)}, u32[]{:S(2)}, u32[]{:S(2)}) collective-permute-start(bf16[72,1728]{1,0:T(8,128)(2,1)S(1)} %slice.8), channel_id=1, source_target_pairs={{0,2},{2,4},{4,6},{6,0},{1,3},{3,5},{5,7},{7,1},{8,10},{10,12},{12... | collective-permute-start | bytes 746504 | tf_op jit(solution)/shard_map/ppermute | solution.py:316
  68.7 15.2 %collective-permute-start.9 = (bf16[72,1728]{1,0:T(8,128)(2,1)S(1)}, bf16[72,1728]{1,0:T(8,128)(2,1)S(1)}, u32[]{:S(2)}, u32[]{:S(2)}) collective-permute-start(bf16[72,1728]{1,0:T(8,128)(2,1)S(1)} %slice.9), channel_id=1, source_target_pairs={{0,6},{2,0},{4,2},{6,4},{1,7},{3,1},{5,3},{7,5},{8,14},{10,8},{12,... | collective-permute-start | bytes 746504 | tf_op jit(solution)/shard_map/ppermute | solution.py:316
  79.3 14.3 %collective-permute-start.11 = (bf16[144,1728]{1,0:T(8,128)(2,1)S(1)}, bf16[144,1728]{1,0:T(8,128)(2,1)S(1)}, u32[]{:S(2)}, u32[]{:S(2)}) collective-permute-start(bf16[144,1728]{1,0:T(8,128)(2,1)S(1)} %collective-permute-done.6.b1), channel_id=1, source_target_pairs={{0,1},{1,0},{2,3},{3,2},{4,5},{5,4},{6,7},{7,6},{8,9},{9,8},{10,11... | collective-permute-start | bytes 1493000 | tf_op jit(solution)/shard_map/ppermute | solution.py:313
  83.9 9.7 %collective-permute-start.12 = (bf16[144,1728]{1,0:T(8,128)(2,1)}, bf16[144,1728]{1,0:T(8,128)(2,1)S(1)}, u32[]{:S(2)}, u32[]{:S(2)}) collective-permute-start(bf16[144,1728]{1,0:T(8,128)(2,1)} %collective-permute-done.7.b2), channel_id=1, source_target_pairs={{0,1},{1,0},{2,3},{3,2},{4,5},{5,4},{6,7},{7,6},{8,9},{9,8},{10,11... | collective-permute-start | bytes 1493000 | tf_op jit(solution)/shard_map/ppermute | solution.py:313
  87.0 6.6 %copy-start.5 = (bf16[144,1728]{1,0:T(8,128)(2,1)}, bf16[144,1728]{1,0:T(8,128)(2,1)S(1)}, u32[]{:S(2)}) copy-start(bf16[144,1728]{1,0:T(8,128)(2,1)S(1)} %constant_dynamic-update-slice_fusion.2.b3) | copy-start | bytes 1492996
  87.0 6.6 %collective-permute-start.13 = (bf16[144,1728]{1,0:T(8,128)(2,1)S(1)}, bf16[144,1728]{1,0:T(8,128)(2,1)S(1)}, u32[]{:S(2)}, u32[]{:S(2)}) collective-permute-start(bf16[144,1728]{1,0:T(8,128)(2,1)S(1)} %constant_dynamic-update-slice_fusion.2.b3), channel_id=1, source_target_pairs={{0,1},{1,0},{2,3},{3,2},{4,5},{5,4},{6,7},{7,6},{8,9},{9,8},{10,11... | collective-permute-start | bytes 1493000 | tf_op jit(solution)/shard_map/ppermute | solution.py:313
  91.8 1.8 %copy-start.23 = (s32[30]{0:T(128)S(1)}, s32[30]{0:T(128)}, u32[]{:S(2)}) copy-start(s32[30]{0:T(128)} %reshape.28.blocks_ref) | copy-start | bytes 364
  93.6 20.5 %copy-start.18 = (f32[8,16,64]{2,1,0:T(8,128)S(1)}, f32[8,16,64]{2,1,0:T(8,128)}, u32[]{:S(2)}) copy-start(f32[8,16,64]{2,1,0:T(8,128)} %param.22) | copy-start | bytes 98308
  106.2 1.9 %copy-start = (bf16[1152,1728]{1,0:T(8,128)(2,1)}, bf16[1152,1728]{1,0:T(8,128)(2,1)S(1)}, u32[]{:S(2)}) copy-start(bf16[1152,1728]{1,0:T(8,128)(2,1)S(1)} %get-tuple-element.17.win_ref) | copy-start | bytes 11943940
  108.1 0.8 copy-start.7
  108.9 0.8 copy-start.9
  109.7 0.8 copy-start.11
  110.5 0.8 copy-start.13
  111.3 0.7 copy-start.16
  112.0 0.6 copy-start.20
  112.6 1.4 copy-start.24
  114.1 1.3 copy-start.4
  115.4 1.0 copy-start.15
  116.4 0.9 copy-start.17
  117.3 0.8 copy-start.19
  118.2 0.8 copy-start.21
  119.0 0.7 copy-start.22
  119.7 28.0 %copy-start.25 = (bf16[1024,1152]{1,0:T(8,128)(2,1)S(1)}, bf16[1024,1152]{1,0:T(8,128)(2,1)}, u32[]{:S(2)}) copy-start(bf16[1024,1152]{1,0:T(8,128)(2,1)} %copy-done.24) | copy-start | bytes 7077892
  121.9 13.6 %collective-permute-start.15 = (bf16[144,640]{1,0:T(8,128)(2,1)S(1)}, bf16[144,640]{1,0:T(8,128)(2,1)S(1)}, u32[]{:S(2)}, u32[]{:S(2)}) collective-permute-start(bf16[144,640]{1,0:T(8,128)(2,1)S(1)} %get-tuple-element.18.up_ref), channel_id=1, source_target_pairs={{0,32},{32,64},{64,96},{96,128},{128,160},{160,192},{192,224},{224... | collective-permute-start | bytes 552968 | tf_op jit(solution)/shard_map/ppermute | solution.py:319
  125.1 11.3 %collective-permute-start.16 = (bf16[144,640]{1,0:T(8,128)(2,1)S(1)}, bf16[144,640]{1,0:T(8,128)(2,1)S(1)}, u32[]{:S(2)}, u32[]{:S(2)}) collective-permute-start(bf16[144,640]{1,0:T(8,128)(2,1)S(1)} %get-tuple-element.18.up_ref), channel_id=1, source_target_pairs={{32,0},{64,32},{96,64},{128,96},{160,128},{192,160},{224,192},{256... | collective-permute-start | bytes 552968 | tf_op jit(solution)/shard_map/ppermute | solution.py:320
  136.4 17.9 %collective-permute-start.17 = (bf16[432,640]{1,0:T(8,128)(2,1)S(1)}, bf16[432,640]{1,0:T(8,128)(2,1)S(1)}, u32[]{:S(2)}, u32[]{:S(2)}) collective-permute-start(bf16[432,640]{1,0:T(8,128)(2,1)S(1)} %constant_dynamic-update-slice_fusion.4.pack_ref), channel_id=1, source_target_pairs={{0,1},{1,2},{2,3},{3,4},{4,5},{5,6},{6,7},{7,8},{8,9},{9,10},{10,1... | collective-permute-start | bytes 1658888 | tf_op jit(solution)/shard_map/ppermute | solution.py:324
  145.6 12.9 %collective-permute-start.18 = (bf16[432,640]{1,0:T(8,128)(2,1)S(1)}, bf16[432,640]{1,0:T(8,128)(2,1)S(1)}, u32[]{:S(2)}, u32[]{:S(2)}) collective-permute-start(bf16[432,640]{1,0:T(8,128)(2,1)S(1)} %constant_dynamic-update-slice_fusion.4.pack_ref), channel_id=1, source_target_pairs={{1,0},{2,1},{3,2},{4,3},{5,4},{6,5},{7,6},{8,7},{9,8},{10,9},{11,1... | collective-permute-start | bytes 1658888 | tf_op jit(solution)/shard_map/ppermute | solution.py:324
  147.7 2.2 %copy-start.1 = (bf16[1152,1728]{1,0:T(8,128)(2,1)S(1)}, bf16[1152,1728]{1,0:T(8,128)(2,1)}, u32[]{:S(2)}) copy-start(bf16[1152,1728]{1,0:T(8,128)(2,1)} %copy-done) | copy-start | bytes 11943940
  152.2 6.3 %copy-start.2 = (bf16[1152,1728]{1,0:T(8,128)(2,1)S(1)}, bf16[1152,1728]{1,0:T(8,128)(2,1)}, u32[]{:S(2)}) copy-start(bf16[1152,1728]{1,0:T(8,128)(2,1)} %copy-done) | copy-start | bytes 11943940
  152.2 6.3 %copy-start.6 = (bf16[144,1728]{1,0:T(8,128)(2,1)S(1)}, bf16[144,1728]{1,0:T(8,128)(2,1)}, u32[]{:S(2)}) copy-start(bf16[144,1728]{1,0:T(8,128)(2,1)} %copy-done.5) | copy-start | bytes 1492996
  152.2 6.3 %copy-start.8 = (bf16[144,1728]{1,0:T(8,128)(2,1)S(1)}, bf16[144,1728]{1,0:T(8,128)(2,1)}, u32[]{:S(2)}) copy-start(bf16[144,1728]{1,0:T(8,128)(2,1)} %copy-done.7) | copy-start | bytes 1492996
  152.2 6.3 %copy-start.10 = (bf16[144,1728]{1,0:T(8,128)(2,1)S(1)}, bf16[144,1728]{1,0:T(8,128)(2,1)}, u32[]{:S(2)}) copy-start(bf16[144,1728]{1,0:T(8,128)(2,1)} %copy-done.9) | copy-start | bytes 1492996
  152.2 6.3 %copy-start.12 = (bf16[144,1728]{1,0:T(8,128)(2,1)S(1)}, bf16[144,1728]{1,0:T(8,128)(2,1)}, u32[]{:S(2)}) copy-start(bf16[144,1728]{1,0:T(8,128)(2,1)} %copy-done.11) | copy-start | bytes 1492996
  152.2 6.3 %copy-start.14 = (bf16[144,1728]{1,0:T(8,128)(2,1)S(1)}, bf16[144,1728]{1,0:T(8,128)(2,1)}, u32[]{:S(2)}) copy-start(bf16[144,1728]{1,0:T(8,128)(2,1)} %copy-done.13) | copy-start | bytes 1492996
Sparse Core Ops, SparseCore 0:
  59.6 40.1 all-gather.1

commit v3 on v2

--- a/solution.py
+++ b/solution.py
@@ -65,9 +65,10 @@
         out_ref[i * T : (i + 1) * T, :] = nn(hidden, order_ref[...]).astype(BF)
 
 
-def collect(blocks, w_ref, sems):
+def collect(blocks, first, rows, w_ref, sems):
     copies = [
-        pltpu.make_async_copy(src, w_ref.at[pl.ds(144 * i, 144)], sems.at[i]) for i, src in enumerate(blocks)
+        pltpu.make_async_copy(src.at[pl.ds(first, rows)], w_ref.at[pl.ds(rows * i, rows)], sems.at[i])
+        for i, src in enumerate(blocks)
     ]
     for c in copies:
         c.start()
@@ -79,7 +80,7 @@
     win_ref, e_ref, att_ref, stat_ref, rows_ref,
     w_ref, bias_ref, acc_ref, sems,
 ):
-    copies = collect((b0, b1, b2, b3, b4, b5, b6, b7), w_ref, sems)
+    copies = collect((b0, b1, b2, b3, b4, b5, b6, b7), 0, 144, w_ref, sems)
     acc_ref[...] = jnp.zeros_like(acc_ref)
 
     qc = (lax.broadcasted_iota(jnp.int32, (T, T), 0) & 8) > 0
@@ -134,13 +135,23 @@
 
 
 def pixel_kernel(
-    att_ref, stat0_ref, rows_ref, place_ref, wout_ref, wpix_ref, x_ref, meas_ref, filt_ref,
+    att_ref, stat0_ref, rows_ref, place_ref, wpix_ref, x_ref, meas_ref, filt_ref, b0, b1, b2, b3, b4, b5, b6, b7,
     den_ref, og_ref, pack_ref, stat_ref,
+    wo_ref, sems,
 ):
-    lane_of = lax.broadcasted_iota(jnp.int32, (640, HW), 0)
-    order = jnp.where(lane_of == place_ref[...], 1.0, 0.0).astype(BF)
+    copies = collect((b0, b1, b2, b3, b4, b5, b6, b7), 144, 48, wo_ref, sems)
+    lane_of = lax.broadcasted_iota(jnp.int32, (640, 384), 0)
+    whole, lower, upper = (
+        jnp.where(lane_of == place_ref[i : i + 1, :], 1.0, 0.0).astype(BF) for i in range(3)
+    )
     att = att_ref[...]
-    den = (x_ref[...].astype(F32) + nn(nn(att, order).astype(BF), wout_ref[...])).astype(BF)
+    att_whole, att_lower, att_upper = (nn(att, g).astype(BF) for g in (whole, lower, upper))
+    for c in copies:
+        c.wait()
+    mixed = nn(att_whole, wo_ref[:, 0:D]) + jnp.concatenate(
+        [nn(att_lower, wo_ref[:, D:QKV]), nn(att_upper, wo_ref[:, D:QKV])], axis=1
+    )
+    den = (x_ref[...].astype(F32) + mixed).astype(BF)
     den_ref[...] = den
     colors = nt(den, wpix_ref[...])
     filt = filt_ref[...]
@@ -150,7 +161,12 @@
     spread = jnp.concatenate([jnp.where(filt == c, misfit, 0.0) for c in range(3)], axis=1).astype(BF)
     og = nn(spread, wpix_ref[...])
     og_ref[...] = og
-    up = nt(nt(og.astype(BF), wout_ref[...]).astype(BF), order).astype(BF)
+    back = og.astype(BF)
+    up = (
+        nt(nt(back, wo_ref[:, 0:D]).astype(BF), whole)
+        + nt(nt(back[:, 0:HW], wo_ref[:, D:QKV]).astype(BF), lower)
+        + nt(nt(back[:, HW:D], wo_ref[:, D:QKV]).astype(BF), upper)
+    ).astype(BF)
     pack_ref[0:T, :] = up
     prod = up.astype(F32) * att.astype(F32)
     lanes = lax.broadcasted_iota(jnp.int32, (T, T), 1)
@@ -231,7 +247,7 @@
     b0, b1, b2, b3, b4, b5, b6, b7,
     out_ref, gk_ref, gv_ref, w_ref, sems,
 ):
-    copies = collect((b0, b1, b2, b3, b4, b5, b6, b7), w_ref, sems)
+    copies = collect((b0, b1, b2, b3, b4, b5, b6, b7), 0, 144, w_ref, sems)
     gk_ref[...] = gk0_ref[...]
     gv_ref[...] = gv0_ref[...]
     key_side(win_ref, ((0, packw_ref), (2, packe_ref)), gk_ref, gv_ref)
@@ -258,17 +274,31 @@
     return jax.ShapeDtypeStruct(shape, dtype)
 
 
+def shards_held(yh, z, x, core, block, second):
+    xs = (x + jnp.asarray(np.array([0, 3, 1, 2] * 2)[block])) & 3
+    cs = core ^ jnp.asarray((block >= 4).astype(np.int32))
+    hops = jnp.where(second, 3 - xs, xs + 1)
+    zs = (z + jnp.where(cs == 0, -hops, hops)) & 7
+    other = jnp.logical_xor(second, (xs == 3) & (cs == 1)).astype(jnp.int32)
+    return (yh ^ other) * 8 + zs
+
+
 def weight_targets(yh, z, x, core):
     place = np.arange(D)
     block, row = place // 144, place % 144
-    second = row >= 72
-    xs = (x + jnp.asarray(np.array([0, 3, 1, 2] * 2)[block])) & 3
-    cs = core ^ jnp.asarray((block >= 4).astype(np.int32))
-    last = xs == 3
-    hops = jnp.where(last & second, 0, xs + 1)
-    zs = (z + jnp.where(cs == 0, -hops, hops)) & 7
-    other = jnp.logical_xor(second, last & (cs == 1)).astype(jnp.int32)
-    return (((yh ^ other) * 8 + zs) * 72 + row % 72).astype(jnp.int32).reshape(1, D)
+    held = shards_held(yh, z, x, core, block, row >= 72)
+    return (held * 72 + row % 72).astype(jnp.int32).reshape(1, D)
+
+
+def out_targets(yh, z, x, core):
+    place = np.arange(384)
+    block, row = place // 48, place % 48
+    held = shards_held(yh, z, x, core, block, row >= 24) * 36 + 64
+    row = row % 24
+    whole = held + row
+    lower = jnp.where(row < 12, held + 24 + row, -1)
+    upper = jnp.where(row >= 12, held + 12 + row, -1)
+    return jnp.stack([whole, lower, upper]).astype(jnp.int32)
 
 
 def device(yh, z, yl, x, core):
@@ -276,26 +306,22 @@
 
 
 def fetch_routes():
-    first, second, mirrored = [], [], []
+    first, second = [], []
     for yh in range(2):
         for z in range(8):
             for yl in range(4):
                 for x in range(4):
                     for core in range(2):
                         me = device(yh, z, yl, x, core)
-                        far = z + (x + 1 if core else -x - 1)
-                        partner = device(1 - yh, z, 3 - yl, x, core)
-                        mirrored.append((partner, me))
-                        if x < 3:
-                            first.append((device(yh, far, yl, x, core), me))
+                        way = 1 if core else -1
+                        near, far = z + way * (x + 1), z + way * (3 - x)
+                        if x == 3 and core == 1:
+                            first.append((device(1 - yh, near, 3 - yl, x, core), me))
+                            second.append((me, me))
+                        else:
+                            first.append((device(yh, near, yl, x, core), me))
                             second.append((device(1 - yh, far, 3 - yl, x, core), me))
-                        elif core == 0:
-                            first.append((device(yh, far, yl, x, core), me))
-                            second.append((partner, me))
-                        else:
-                            first.append((device(1 - yh, far, 3 - yl, x, core), me))
-                            second.append((me, me))
-    return first, second, mirrored
+    return first, second
 
 
 def on_device(tokens, gain, w_query, w_key, w_value, w_out, w_pixel, measured, filter_color, block_mask):
@@ -307,7 +333,7 @@
     east = [(i, (i + 1) % 32) for i in range(32)]
     west = [(j, i) for i, j in east]
     lat, lon = ("yh", "z"), ("yl", "x", "core")
-    first, second, mirrored = fetch_routes()
+    first, second = fetch_routes()
 
     def swap(v):
         return lax.ppermute(v, "core", [(0, 1), (1, 0)])
@@ -323,20 +349,12 @@
     def sides(column):
         return lax.ppermute(column, lon, east), lax.ppermute(column, lon, west)
 
-    out_other = lax.ppermute(w_out, lat + lon, mirrored)
-    out_both = jnp.concatenate([jnp.where(yh == 0, w_out, out_other), jnp.where(yh == 0, out_other, w_out)], axis=0)
-    full_out = lax.all_gather(out_both, "z", axis=0, tiled=True)
-    place = np.arange(HW)
-    place = (64 + (place // 36 % 2 * 8 + place // 72) * 36 + place % 36).astype(np.int32).reshape(1, HW)
-    mine = jnp.concatenate([w_key, w_value, w_query], axis=1)
-    fetched = jnp.concatenate(
-        [lax.ppermute(mine, lat + lon, first), lax.ppermute(mine, lat + lon, second)], axis=0
-    )
-    right, left = along(fetched, 1), along(fetched, 3)
-    across = jnp.concatenate([along(right[:72], 1), along(left[72:], 3)], axis=0)
-    held = (fetched, right, left, across)
-    blocks = held + tuple(swap(v) for v in held)
-
+    out_rows = jnp.concatenate(
+        [w_out[:24], jnp.concatenate([w_out[24:, :HW], w_out[24:, HW:]], axis=0)], axis=1
+    )
+    mine = jnp.concatenate([jnp.concatenate([w_key, w_value, w_query], axis=1), out_rows], axis=0)
+    one, two = lax.ppermute(mine, lat + lon, first), lax.ppermute(mine, lat + lon, second)
+    fetched = jnp.concatenate([one[:72], two[:72], one[72:], two[72:]], axis=0)
     column = columns(x)
     from_west, from_east = sides(column)
     order = pl.pallas_call(
@@ -351,7 +369,13 @@
             cost_estimate=pl.CostEstimate(flops=3_000_000_000, bytes_accessed=5_000_000, transcendentals=0),
         )(v, gain, order)
 
-    hw, hc, he = hidden(from_west), hidden(column), hidden(from_east)
+    fetched, hc = lax.optimization_barrier((fetched, hidden(column)))
+    right, left = along(fetched, 1), along(fetched, 3)
+    right, left, hw, he = lax.optimization_barrier((right, left, hidden(from_west), hidden(from_east)))
+    across = jnp.concatenate([along(right[:96], 1), along(left[96:], 3)], axis=0)
+    held = (fetched, right, left, across)
+    blocks = held + tuple(swap(v) for v in held)
+
     win, e, att, stat0, rows = pl.pallas_call(
         forward_kernel,
         out_shape=(
@@ -363,21 +387,26 @@
             pltpu.VMEM((D, QKV), BF), pltpu.VMEM((T, 9 * T), F32), pltpu.VMEM((T, 640), F32),
             pltpu.SemaphoreType.DMA((8,)),
         ],
-        compiler_params=params(28),
+        compiler_params=params(20),
         cost_estimate=pl.CostEstimate(flops=12_000_000_000, bytes_accessed=8_000_000, transcendentals=1_000_000),
     )(block_mask.reshape(30), hw, hc, he, *blocks)
     den, og, pack, stat = pl.pallas_call(
         pixel_kernel,
         out_shape=(shaped((T, D)), shaped((T, D), F32), shaped((144, 640)), shaped((T, T), F32)),
-        in_specs=[VMEM] * 9, out_specs=(VMEM,) * 4,
-        compiler_params=params(16),
-    )(att, stat0, rows, jnp.asarray(place), full_out, w_pixel.T, x, measured.reshape(T, 64), filter_color.reshape(T, 64))
+        in_specs=[VMEM] * 8 + [ANY] * 8, out_specs=(VMEM,) * 4,
+        scratch_shapes=[pltpu.VMEM((384, QKV), BF), pltpu.SemaphoreType.DMA((8,))],
+        compiler_params=params(14),
+    )(
+        att, stat0, rows, out_targets(yh, z, xi, core), w_pixel.T, x, measured.reshape(T, 64),
+        filter_color.reshape(T, 64), *blocks,
+    )
     packs = columns(pack)
     gq = pl.pallas_call(
         query_kernel, out_shape=shaped((T, HW)), in_specs=[VMEM] * 4, out_specs=VMEM,
         scratch_shapes=[pltpu.VMEM((T, 640), F32)], compiler_params=params(16),
         cost_estimate=pl.CostEstimate(flops=4_000_000_000, bytes_accessed=6_000_000, transcendentals=0),
     )(win, e, pack, stat)
+    packs, gq = lax.optimization_barrier((packs, gq))
     packs_west, packs_east = sides(packs)
     gk, gv = pl.pallas_call(
         key_centre_kernel, out_shape=(shaped((T, 640), F32),) * 2, in_specs=[VMEM] * 2, out_specs=(VMEM,) * 2,
@@ -387,7 +416,7 @@
     guidance = pl.pallas_call(
         finish_kernel, out_shape=shaped((T, D), F32), in_specs=[VMEM] * 10 + [ANY] * 8, out_specs=VMEM,
         scratch_shapes=[pltpu.VMEM((T, 640), F32)] * 2 + [pltpu.VMEM((D, QKV), BF), pltpu.SemaphoreType.DMA((8,))],
-        compiler_params=params(24),
+        compiler_params=params(20),
     )(win, packs_west, packs_east, gk, gv, gq, order, x, gain, og, *blocks)
     return den.reshape(tokens.shape), guidance.reshape(tokens.shape)
 

time: 177 us -> 162 us (0.915)
  the two profiles are of different devices: /device:TPU:39 before, /device:TPU:463 now
where the time goes in v3:
time: 162 us; the launch traced here: 161 us
  waiting for transfers between devices  61.7 us (38%)
  starting transfers between devices  50.8 us (31%)
  Pallas kernels  38.9 us (24%)
  local copies, waits for them, and re-layouts  7.65 us (5%)
    ppermute x2, waiting for transfers between devices, columns(): after = lax.ppermute(own, lat, north)  30.5 us
    ppermute x4, waiting for transfers between devices, along(): return lax.ppermute(v, 'x', [(i, (i + shift) % 4) for i in range(4)])  14.4 us
    ppermute x4, waiting for transfers between devices, sides(): return (lax.ppermute(column, lon, east), lax.ppermute(column, lon, west))  13.1 us
    pallas_call x1, Pallas kernels, on_device(): pl.pallas_call(forward_kernel, out_shape=(shaped((9 * T, QKV)), shaped((H...  12.8 us
    ppermute x4, starting transfers between devices, sides(): return (lax.ppermute(column, lon, east), lax.ppermute(column, lon, west))  11.2 us
    ppermute x4, starting transfers between devices, swap(): return lax.ppermute(v, 'core', [(0, 1), (1, 0)])  10.7 us
    pallas_call x1, Pallas kernels, on_device(): pl.pallas_call(finish_kernel, out_shape=shaped((T, D), F32), in_specs=[VM...  10.6 us
    ppermute x4, starting transfers between devices, along(): return lax.ppermute(v, 'x', [(i, (i + shift) % 4) for i in range(4)])  10.6 us
  transfers between devices with their start and end apart: 18, of which 10 were waited for; matrix products, arithmetic and copies ran while one was open for 2% of the time, Pallas kernels for 6%

profile of v3, /device:TPU:463, one launch (start us, length us, event | category | flops | bytes accessed | tf_op | source)
XLA Modules:
  0.0 160.9 jit_solution(1261265364776173008)
XLA Ops:
  0.6 2.1 %collective-permute-start.2 = (bf16[128,1152]{1,0:T(8,128)(2,1)}, bf16[128,1152]{1,0:T(8,128)(2,1)S(1)}, u32[]{:S(2)}, u32[]{:S(2)}) collective-permute-start(bf16[128,1152]{1,0:T(8,128)(2,1)} %bitcast.6), channel_id=1, source_target_pairs={{0,32},{32,64},{64,96},{96,128},{128,160},{160,192},{192,224},{224... | collective-permute-start | bytes 884744 | tf_op jit(solution)/shard_map/ppermute | solution.py:345
  2.7 3.4 %collective-permute-start.3 = (bf16[128,1152]{1,0:T(8,128)(2,1)}, bf16[128,1152]{1,0:T(8,128)(2,1)S(1)}, u32[]{:S(2)}, u32[]{:S(2)}) collective-permute-start(bf16[128,1152]{1,0:T(8,128)(2,1)} %bitcast.7), channel_id=1, source_target_pairs={{32,0},{64,32},{96,64},{128,96},{160,128},{192,160},{224,192},{256... | collective-permute-start | bytes 884744 | tf_op jit(solution)/shard_map/ppermute | solution.py:346
  6.1 0.9 fusion.16
  7.0 0.8 slice.27
  7.8 1.1 concatenate.24
  9.0 6.7 %collective-permute-start = (bf16[96,1728]{1,0:T(8,128)(2,1)S(1)}, bf16[96,1728]{1,0:T(8,128)(2,1)S(1)}, u32[]{:S(2)}, u32[]{:S(2)}) collective-permute-start(bf16[96,1728]{1,0:T(8,128)(2,1)S(1)} %maximum_maximum_fusion), channel_id=1, source_target_pairs={{224,0},{33,1},{194,2},{67,3},{164,4},{101,5},{134,6},{415,7},{232... | collective-permute-start | bytes 995336 | tf_op jit(solution)/shard_map/ppermute | solution.py:356
  15.7 0.7 collective-permute-start.1
  16.4 14.4 %collective-permute-done.3 = bf16[128,1152]{1,0:T(8,128)(2,1)S(1)} collective-permute-done((bf16[128,1152]{1,0:T(8,128)(2,1)}, bf16[128,1152]{1,0:T(8,128)(2,1)S(1)}, u32[]{:S(2)}, u32[]{:S(2)}) %collective-permute-start.3) | collective-permute-done | bytes 294944 | tf_op jit(solution)/shard_map/ppermute | solution.py:346
  30.8 0.1 pad_maximum_fusion.x_ref
  30.9 4.9 %collective-permute-start.6 = (bf16[384,1152]{1,0:T(8,128)(2,1)S(1)}, bf16[384,1152]{1,0:T(8,128)(2,1)S(1)}, u32[]{:S(2)}, u32[]{:S(2)}) collective-permute-start(bf16[384,1152]{1,0:T(8,128)(2,1)S(1)} %pad_maximum_fusion.x_ref), channel_id=1, source_target_pairs={{0,1},{1,2},{2,3},{3,4},{4,5},{5,6},{6,7},{7,8},{8,9},{9,10},{10,1... | collective-permute-start | bytes 2654216 | tf_op jit(solution)/shard_map/ppermute | solution.py:350
  35.9 0.5 shard_map.203.order_ref
  36.3 0.2 copy-done.13
  36.6 2.0 %collective-permute-start.7 = (bf16[384,1152]{1,0:T(8,128)(2,1)S(1)}, bf16[384,1152]{1,0:T(8,128)(2,1)S(1)}, u32[]{:S(2)}, u32[]{:S(2)}) collective-permute-start(bf16[384,1152]{1,0:T(8,128)(2,1)S(1)} %pad_maximum_fusion.x_ref), channel_id=1, source_target_pairs={{1,0},{2,1},{3,2},{4,3},{5,4},{6,5},{7,6},{8,7},{9,8},{10,9},{11,1... | collective-permute-start | bytes 2654216 | tf_op jit(solution)/shard_map/ppermute | solution.py:350
  38.6 1.8 %shard_map.204.hc_ref = bf16[384,1152]{1,0:T(8,128)(2,1)S(1)} custom-call(bf16[384,1152]{1,0:T(8,128)(2,1)S(1)} %pad_maximum_fusion.x_ref, f32[1,1152]{1,0:T(1,128)S(1)} %reshape.30.gain_ref, bf16[1152,1152]{1,0:T(8,128)(2,1)S(1)} %shard_map.203.order_ref), custom_call_target="tpu_custom_call" | custom-call | flops 3000000000 | bytes 5000000 | tf_op jit(solution)/shard_map/pallas_call | solution.py:366
  40.5 0.1 pad_maximum_fusion.1.b0
  40.6 0.8 copy-done.7
  41.3 1.9 %collective-permute-start.4 = (bf16[192,1728]{1,0:T(8,128)(2,1)S(1)}, bf16[192,1728]{1,0:T(8,128)(2,1)S(1)}, u32[]{:S(2)}, u32[]{:S(2)}) collective-permute-start(bf16[192,1728]{1,0:T(8,128)(2,1)S(1)} %pad_maximum_fusion.1.b0), channel_id=1, source_target_pairs={{0,2},{2,4},{4,6},{6,0},{1,3},{3,5},{5,7},{7,1},{8,10},{10,12},{12... | collective-permute-start | bytes 1990664 | tf_op jit(solution)/shard_map/ppermute | solution.py:342
  43.2 3.4 %collective-permute-start.5 = (bf16[192,1728]{1,0:T(8,128)(2,1)S(1)}, bf16[192,1728]{1,0:T(8,128)(2,1)S(1)}, u32[]{:S(2)}, u32[]{:S(2)}) collective-permute-start(bf16[192,1728]{1,0:T(8,128)(2,1)S(1)} %pad_maximum_fusion.1.b0), channel_id=1, source_target_pairs={{0,6},{2,0},{4,2},{6,4},{1,7},{3,1},{5,3},{7,5},{8,14},{10,8},{12,... | collective-permute-start | bytes 1990664 | tf_op jit(solution)/shard_map/ppermute | solution.py:342
  46.6 1.8 %shard_map.205.hw_ref = bf16[384,1152]{1,0:T(8,128)(2,1)S(1)} custom-call(bf16[384,1152]{1,0:T(8,128)(2,1)S(1)} %collective-permute-done.6.x_ref, f32[1,1152]{1,0:T(1,128)S(1)} %reshape.30.gain_ref, bf16[1152,1152]{1,0:T(8,128)(2,1)S(1)} %shard_map.203.order_ref), custom_call_target="tpu_custom_call" | custom-call | flops 3000000000 | bytes 5000000 | tf_op jit(solution)/shard_map/pallas_call | solution.py:366
  48.4 4.7 %collective-permute-done.7.x_ref = bf16[384,1152]{1,0:T(8,128)(2,1)S(1)} collective-permute-done((bf16[384,1152]{1,0:T(8,128)(2,1)S(1)}, bf16[384,1152]{1,0:T(8,128)(2,1)S(1)}, u32[]{:S(2)}, u32[]{:S(2)}) %collective-permute-start.7) | collective-permute-done | bytes 884768 | tf_op jit(solution)/shard_map/ppermute | solution.py:350
  53.1 1.8 %shard_map.206.he_ref = bf16[384,1152]{1,0:T(8,128)(2,1)S(1)} custom-call(bf16[384,1152]{1,0:T(8,128)(2,1)S(1)} %collective-permute-done.7.x_ref, f32[1,1152]{1,0:T(1,128)S(1)} %reshape.30.gain_ref, bf16[1152,1152]{1,0:T(8,128)(2,1)S(1)} %shard_map.203.order_ref), custom_call_target="tpu_custom_call" | custom-call | flops 3000000000 | bytes 5000000 | tf_op jit(solution)/shard_map/pallas_call | solution.py:366
  55.1 7.3 %collective-permute-done.4.b1 = bf16[192,1728]{1,0:T(8,128)(2,1)S(1)} collective-permute-done((bf16[192,1728]{1,0:T(8,128)(2,1)S(1)}, bf16[192,1728]{1,0:T(8,128)(2,1)S(1)}, u32[]{:S(2)}, u32[]{:S(2)}) %collective-permute-start.4) | collective-permute-done | bytes 663584 | tf_op jit(solution)/shard_map/ppermute | solution.py:342
  62.4 5.6 %collective-permute-done.5.b2 = bf16[192,1728]{1,0:T(8,128)(2,1)S(1)} collective-permute-done((bf16[192,1728]{1,0:T(8,128)(2,1)S(1)}, bf16[192,1728]{1,0:T(8,128)(2,1)S(1)}, u32[]{:S(2)}, u32[]{:S(2)}) %collective-permute-start.5) | collective-permute-done | bytes 663584 | tf_op jit(solution)/shard_map/ppermute | solution.py:342
  68.0 1.9 %collective-permute-start.8 = (bf16[96,1728]{1,0:T(8,128)(2,1)S(1)}, bf16[96,1728]{1,0:T(8,128)(2,1)S(1)}, u32[]{:S(2)}, u32[]{:S(2)}) collective-permute-start(bf16[96,1728]{1,0:T(8,128)(2,1)S(1)} %slice.34), channel_id=1, source_target_pairs={{0,2},{2,4},{4,6},{6,0},{1,3},{3,5},{5,7},{7,1},{8,10},{10,12},{12... | collective-permute-start | bytes 995336 | tf_op jit(solution)/shard_map/ppermute | solution.py:342
  70.0 3.4 %collective-permute-start.9 = (bf16[96,1728]{1,0:T(8,128)(2,1)S(1)}, bf16[96,1728]{1,0:T(8,128)(2,1)S(1)}, u32[]{:S(2)}, u32[]{:S(2)}) collective-permute-start(bf16[96,1728]{1,0:T(8,128)(2,1)S(1)} %slice.35), channel_id=1, source_target_pairs={{0,6},{2,0},{4,2},{6,4},{1,7},{3,1},{5,3},{7,5},{8,14},{10,8},{12,... | collective-permute-start | bytes 995336 | tf_op jit(solution)/shard_map/ppermute | solution.py:342
  73.3 3.0 %collective-permute-start.10 = (bf16[192,1728]{1,0:T(8,128)(2,1)S(1)}, bf16[192,1728]{1,0:T(8,128)(2,1)S(1)}, u32[]{:S(2)}, u32[]{:S(2)}) collective-permute-start(bf16[192,1728]{1,0:T(8,128)(2,1)S(1)} %pad_maximum_fusion.1.b0), channel_id=1, source_target_pairs={{0,1},{1,0},{2,3},{3,2},{4,5},{5,4},{6,7},{7,6},{8,9},{9,8},{10,11... | collective-permute-start | bytes 1990664 | tf_op jit(solution)/shard_map/ppermute | solution.py:339
  76.3 1.9 %collective-permute-start.11 = (bf16[192,1728]{1,0:T(8,128)(2,1)S(1)}, bf16[192,1728]{1,0:T(8,128)(2,1)}, u32[]{:S(2)}, u32[]{:S(2)}) collective-permute-start(bf16[192,1728]{1,0:T(8,128)(2,1)S(1)} %collective-permute-done.4.b1), channel_id=1, source_target_pairs={{0,1},{1,0},{2,3},{3,2},{4,5},{5,4},{6,7},{7,6},{8,9},{9,8},{10,11... | collective-permute-start | bytes 1990664 | tf_op jit(solution)/shard_map/ppermute | solution.py:339
  78.2 2.4 %collective-permute-start.12 = (bf16[192,1728]{1,0:T(8,128)(2,1)S(1)}, bf16[192,1728]{1,0:T(8,128)(2,1)}, u32[]{:S(2)}, u32[]{:S(2)}) collective-permute-start(bf16[192,1728]{1,0:T(8,128)(2,1)S(1)} %collective-permute-done.5.b2), channel_id=1, source_target_pairs={{0,1},{1,0},{2,3},{3,2},{4,5},{5,4},{6,7},{7,6},{8,9},{9,8},{10,11... | collective-permute-start | bytes 1990664 | tf_op jit(solution)/shard_map/ppermute | solution.py:339
  80.7 1.5 collective-permute-done.9
  82.2 3.4 %collective-permute-start.13 = (bf16[192,1728]{1,0:T(8,128)(2,1)S(1)}, bf16[192,1728]{1,0:T(8,128)(2,1)}, u32[]{:S(2)}, u32[]{:S(2)}) collective-permute-start(bf16[192,1728]{1,0:T(8,128)(2,1)S(1)} %constant_dynamic-update-slice_fusion.b3), channel_id=1, source_target_pairs={{0,1},{1,0},{2,3},{3,2},{4,5},{5,4},{6,7},{7,6},{8,9},{9,8},{10,11... | collective-permute-start | bytes 1990664 | tf_op jit(solution)/shard_map/ppermute | solution.py:339
  85.7 0.1 reshape.28.blocks_ref
  86.0 1.4 collective-permute-done.13.b7
  87.4 1.2 copy-done.8
  88.5 1.2 copy-done.10
  89.7 1.2 copy-done.12
  90.9 12.8 %shard_map.207 = (bf16[1152,1728]{1,0:T(8,128)(2,1)S(1)}, bf16[1024,1152]{1,0:T(8,128)(2,1)S(1)}, bf16[128,640]{1,0:T(8,128)(2,1)S(1)}, f32[128,128]{1,0:T(8,128)S(1)}, f32[32,128]{1,0:T(8,128)S(1)}) custom-call(s32[30]{0:T(128)S(1)} %reshape.28.blocks_ref, bf16[384,1152]{1,0:T(8,128)(2,1)S(1)} %copy-done.10, bf16[384,1152]{1,0:T(8,128)(2,1)S(1)} %copy-done.8, ...), custom_call_target="tpu_custom_call" | custom-call | flops 12000000000 | bytes 8000000 | tf_op jit(solution)/shard_map/pallas_call | solution.py:379
  103.7 5.2 %shard_map.208 = (bf16[128,1152]{1,0:T(8,128)(2,1)}, f32[128,1152]{1,0:T(8,128)S(1)}, bf16[144,640]{1,0:T(8,128)(2,1)S(1)}, f32[128,128]{1,0:T(8,128)S(1)}) custom-call(bf16[128,640]{1,0:T(8,128)(2,1)S(1)} %get-tuple-element.27.att_ref, f32[128,128]{1,0:T(8,128)S(1)} %get-tuple-element.28.stat0_ref, f32[32,128]{1,0:T(8,128)S(1)} %get-tuple-element.29.rows_ref, ...), custom_call_target="tpu_custom_call" | custom-call | tf_op jit(solution)/shard_map/pallas_call | solution.py:393
  109.0 1.9 %collective-permute-start.14 = (bf16[144,640]{1,0:T(8,128)(2,1)S(1)}, bf16[144,640]{1,0:T(8,128)(2,1)S(1)}, u32[]{:S(2)}, u32[]{:S(2)}) collective-permute-start(bf16[144,640]{1,0:T(8,128)(2,1)S(1)} %get-tuple-element.32.up_ref), channel_id=1, source_target_pairs={{0,32},{32,64},{64,96},{96,128},{128,160},{160,192},{192,224},{224... | collective-permute-start | bytes 552968 | tf_op jit(solution)/shard_map/ppermute | solution.py:345
  110.9 3.6 %collective-permute-start.15 = (bf16[144,640]{1,0:T(8,128)(2,1)S(1)}, bf16[144,640]{1,0:T(8,128)(2,1)S(1)}, u32[]{:S(2)}, u32[]{:S(2)}) collective-permute-start(bf16[144,640]{1,0:T(8,128)(2,1)S(1)} %get-tuple-element.32.up_ref), channel_id=1, source_target_pairs={{32,0},{64,32},{96,64},{128,96},{160,128},{192,160},{224,192},{256... | collective-permute-start | bytes 552968 | tf_op jit(solution)/shard_map/ppermute | solution.py:346
  114.5 2.3 %shard_map.209.gq_ref = bf16[128,576]{1,0:T(8,128)(2,1)S(1)} custom-call(bf16[1152,1728]{1,0:T(8,128)(2,1)S(1)} %get-tuple-element.31.win_ref, bf16[1024,1152]{1,0:T(8,128)(2,1)S(1)} %get-tuple-element.33.e_ref, bf16[144,640]{1,0:T(8,128)(2,1)S(1)} %get-tuple-element.32.up_ref, f32[128,128]{1,0:T(8,128)S(1)} %get-tuple-element.34.stat_ref), custom_call_target="tpu_custom_call" | custom-call | flops 4000000000 | bytes 6000000 | tf_op jit(solution)/shard_map/pallas_call | solution.py:404
  116.8 2.4 %collective-permute-done.14 = bf16[144,640]{1,0:T(8,128)(2,1)S(1)} collective-permute-done((bf16[144,640]{1,0:T(8,128)(2,1)S(1)}, bf16[144,640]{1,0:T(8,128)(2,1)S(1)}, u32[]{:S(2)}, u32[]{:S(2)}) %collective-permute-start.14) | collective-permute-done | bytes 184352 | tf_op jit(solution)/shard_map/ppermute | solution.py:345
  119.2 16.0 %collective-permute-done.15 = bf16[144,640]{1,0:T(8,128)(2,1)S(1)} collective-permute-done((bf16[144,640]{1,0:T(8,128)(2,1)S(1)}, bf16[144,640]{1,0:T(8,128)(2,1)S(1)}, u32[]{:S(2)}, u32[]{:S(2)}) %collective-permute-start.15) | collective-permute-done | bytes 184352 | tf_op jit(solution)/shard_map/ppermute | solution.py:346
  135.3 1.9 %collective-permute-start.16 = (bf16[432,640]{1,0:T(8,128)(2,1)S(1)}, bf16[432,640]{1,0:T(8,128)(2,1)S(1)}, u32[]{:S(2)}, u32[]{:S(2)}) collective-permute-start(bf16[432,640]{1,0:T(8,128)(2,1)S(1)} %pad_maximum_fusion.2.pack_ref), channel_id=1, source_target_pairs={{0,1},{1,2},{2,3},{3,4},{4,5},{5,6},{6,7},{7,8},{8,9},{9,10},{10,1... | collective-permute-start | bytes 1658888 | tf_op jit(solution)/shard_map/ppermute | solution.py:350
  137.2 2.4 %collective-permute-start.17 = (bf16[432,640]{1,0:T(8,128)(2,1)S(1)}, bf16[432,640]{1,0:T(8,128)(2,1)S(1)}, u32[]{:S(2)}, u32[]{:S(2)}) collective-permute-start(bf16[432,640]{1,0:T(8,128)(2,1)S(1)} %pad_maximum_fusion.2.pack_ref), channel_id=1, source_target_pairs={{1,0},{2,1},{3,2},{4,3},{5,4},{6,5},{7,6},{8,7},{9,8},{10,9},{11,1... | collective-permute-start | bytes 1658888 | tf_op jit(solution)/shard_map/ppermute | solution.py:350
  139.6 2.1 %shard_map.210 = (f32[128,640]{1,0:T(8,128)S(1)}, f32[128,640]{1,0:T(8,128)S(1)}) custom-call(bf16[1152,1728]{1,0:T(8,128)(2,1)S(1)} %get-tuple-element.31.win_ref, bf16[432,640]{1,0:T(8,128)(2,1)S(1)} %pad_maximum_fusion.2.pack_ref), custom_call_target="tpu_custom_call" | custom-call | flops 4000000000 | bytes 6000000 | tf_op jit(solution)/shard_map/pallas_call | solution.py:411
  141.7 1.9 %collective-permute-done.16.packw_ref = bf16[432,640]{1,0:T(8,128)(2,1)S(1)} collective-permute-done((bf16[432,640]{1,0:T(8,128)(2,1)S(1)}, bf16[432,640]{1,0:T(8,128)(2,1)S(1)}, u32[]{:S(2)}, u32[]{:S(2)}) %collective-permute-start.16) | collective-permute-done | bytes 552992 | tf_op jit(solution)/shard_map/ppermute | solution.py:350
  143.6 6.5 %collective-permute-done.17.packe_ref = bf16[432,640]{1,0:T(8,128)(2,1)S(1)} collective-permute-done((bf16[432,640]{1,0:T(8,128)(2,1)S(1)}, bf16[432,640]{1,0:T(8,128)(2,1)S(1)}, u32[]{:S(2)}, u32[]{:S(2)}) %collective-permute-start.17) | collective-permute-done | bytes 552992 | tf_op jit(solution)/shard_map/ppermute | solution.py:350
  150.1 10.6 %shard_map.211 = f32[128,1152]{1,0:T(8,128)} custom-call(bf16[1152,1728]{1,0:T(8,128)(2,1)S(1)} %get-tuple-element.31.win_ref, bf16[432,640]{1,0:T(8,128)(2,1)S(1)} %collective-permute-done.16.packw_ref, bf16[432,640]{1,0:T(8,128)(2,1)S(1)} %collective-permute-done.17.packe_ref, f32[128,640]{1,0:T(8,128)S(1)} %get-tuple-element.36.gk0_ref, ...), custom_call_target="tpu_custom_call" | custom-call | tf_op jit(solution)/shard_map/pallas_call | solution.py:416
  (73 shorter events, 0.5 us)
Async XLA Ops:
  0.6 30.2 %copy-start.2 = (bf16[8,16,1152]{2,1,0:T(8,128)(2,1)S(1)}, bf16[8,16,1152]{2,1,0:T(8,128)(2,1)}, u32[]{:S(2)}) copy-start(bf16[8,16,1152]{2,1,0:T(8,128)(2,1)} %param.20) | copy-start | bytes 884740
  0.6 15.7 %collective-permute-start.2 = (bf16[128,1152]{1,0:T(8,128)(2,1)}, bf16[128,1152]{1,0:T(8,128)(2,1)S(1)}, u32[]{:S(2)}, u32[]{:S(2)}) collective-permute-start(bf16[128,1152]{1,0:T(8,128)(2,1)} %bitcast.6), channel_id=1, source_target_pairs={{0,32},{32,64},{64,96},{96,128},{128,160},{160,192},{192,224},{224... | collective-permute-start | bytes 884744 | tf_op jit(solution)/shard_map/ppermute | solution.py:345
  2.7 28.1 %collective-permute-start.3 = (bf16[128,1152]{1,0:T(8,128)(2,1)}, bf16[128,1152]{1,0:T(8,128)(2,1)S(1)}, u32[]{:S(2)}, u32[]{:S(2)}) collective-permute-start(bf16[128,1152]{1,0:T(8,128)(2,1)} %bitcast.7), channel_id=1, source_target_pairs={{32,0},{64,32},{96,64},{128,96},{160,128},{192,160},{224,192},{256... | collective-permute-start | bytes 884744 | tf_op jit(solution)/shard_map/ppermute | solution.py:346
  8.9 26.9 %copy-start.15 = (s32[1152]{0:T(1024)S(1)}, s32[1152]{0:T(1024)}, u32[]{:S(2)}) copy-start(s32[1152]{0:T(1024)} %constant.67.clone) | copy-start | bytes 13828
  8.9 26.9 %copy-start.16 = (s32[1152]{0:T(1024)S(1)}, s32[1152]{0:T(1024)}, u32[]{:S(2)}) copy-start(s32[1152]{0:T(1024)} %constant.68.clone) | copy-start | bytes 13828
  8.9 26.9 %copy-start.17 = (s32[1152]{0:T(1024)S(1)}, s32[1152]{0:T(1024)}, u32[]{:S(2)}) copy-start(s32[1152]{0:T(1024)} %constant.70.clone) | copy-start | bytes 13828
  8.9 26.9 %copy-start.21 = (pred[1152]{0:T(1024)(128)(4,1)S(1)}, pred[1152]{0:T(1024)(128)(4,1)}, u32[]{:S(2)}) copy-start(pred[1152]{0:T(1024)(128)(4,1)} %constant.69.clone) | copy-start | bytes 3460
  9.0 31.4 %collective-permute-start = (bf16[96,1728]{1,0:T(8,128)(2,1)S(1)}, bf16[96,1728]{1,0:T(8,128)(2,1)S(1)}, u32[]{:S(2)}, u32[]{:S(2)}) collective-permute-start(bf16[96,1728]{1,0:T(8,128)(2,1)S(1)} %maximum_maximum_fusion), channel_id=1, source_target_pairs={{224,0},{33,1},{194,2},{67,3},{164,4},{101,5},{134,6},{415,7},{232... | collective-permute-start | bytes 995336 | tf_op jit(solution)/shard_map/ppermute | solution.py:356
  15.7 24.8 %collective-permute-start.1 = (bf16[96,1728]{1,0:T(8,128)(2,1)S(1)}, bf16[96,1728]{1,0:T(8,128)(2,1)S(1)}, u32[]{:S(2)}, u32[]{:S(2)}) collective-permute-start(bf16[96,1728]{1,0:T(8,128)(2,1)S(1)} %maximum_maximum_fusion), channel_id=1, source_target_pairs={{440,0},{377,1},{474,2},{347,3},{508,4},{317,5},{286,6},{7,7},{432... | collective-permute-start | bytes 995336 | tf_op jit(solution)/shard_map/ppermute | solution.py:356
  30.9 15.7 %collective-permute-start.6 = (bf16[384,1152]{1,0:T(8,128)(2,1)S(1)}, bf16[384,1152]{1,0:T(8,128)(2,1)S(1)}, u32[]{:S(2)}, u32[]{:S(2)}) collective-permute-start(bf16[384,1152]{1,0:T(8,128)(2,1)S(1)} %pad_maximum_fusion.x_ref), channel_id=1, source_target_pairs={{0,1},{1,2},{2,3},{3,4},{4,5},{5,6},{6,7},{7,8},{8,9},{9,10},{10,1... | collective-permute-start | bytes 2654216 | tf_op jit(solution)/shard_map/ppermute | solution.py:350
  35.9 0.7 copy-start.13
  36.6 16.6 %copy-start = (bf16[1152,1152]{1,0:T(8,128)(2,1)}, bf16[1152,1152]{1,0:T(8,128)(2,1)S(1)}, u32[]{:S(2)}) copy-start(bf16[1152,1152]{1,0:T(8,128)(2,1)S(1)} %shard_map.203.order_ref) | copy-start | bytes 7962628
  36.6 16.6 %collective-permute-start.7 = (bf16[384,1152]{1,0:T(8,128)(2,1)S(1)}, bf16[384,1152]{1,0:T(8,128)(2,1)S(1)}, u32[]{:S(2)}, u32[]{:S(2)}) collective-permute-start(bf16[384,1152]{1,0:T(8,128)(2,1)S(1)} %pad_maximum_fusion.x_ref), channel_id=1, source_target_pairs={{1,0},{2,1},{3,2},{4,3},{5,4},{6,5},{7,6},{8,7},{9,8},{10,9},{11,1... | collective-permute-start | bytes 2654216 | tf_op jit(solution)/shard_map/ppermute | solution.py:350
  40.4 0.9 copy-start.7
  41.3 21.1 %collective-permute-start.4 = (bf16[192,1728]{1,0:T(8,128)(2,1)S(1)}, bf16[192,1728]{1,0:T(8,128)(2,1)S(1)}, u32[]{:S(2)}, u32[]{:S(2)}) collective-permute-start(bf16[192,1728]{1,0:T(8,128)(2,1)S(1)} %pad_maximum_fusion.1.b0), channel_id=1, source_target_pairs={{0,2},{2,4},{4,6},{6,0},{1,3},{3,5},{5,7},{7,1},{8,10},{10,12},{12... | collective-permute-start | bytes 1990664 | tf_op jit(solution)/shard_map/ppermute | solution.py:342
  43.2 24.7 %collective-permute-start.5 = (bf16[192,1728]{1,0:T(8,128)(2,1)S(1)}, bf16[192,1728]{1,0:T(8,128)(2,1)S(1)}, u32[]{:S(2)}, u32[]{:S(2)}) collective-permute-start(bf16[192,1728]{1,0:T(8,128)(2,1)S(1)} %pad_maximum_fusion.1.b0), channel_id=1, source_target_pairs={{0,6},{2,0},{4,2},{6,4},{1,7},{3,1},{5,3},{7,5},{8,14},{10,8},{12,... | collective-permute-start | bytes 1990664 | tf_op jit(solution)/shard_map/ppermute | solution.py:342
  48.4 6.5 %copy-start.9 = (bf16[384,1152]{1,0:T(8,128)(2,1)}, bf16[384,1152]{1,0:T(8,128)(2,1)S(1)}, u32[]{:S(2)}) copy-start(bf16[384,1152]{1,0:T(8,128)(2,1)S(1)} %shard_map.205.hw_ref) | copy-start | bytes 2654212
  55.0 30.7 %copy-start.11 = (bf16[384,1152]{1,0:T(8,128)(2,1)}, bf16[384,1152]{1,0:T(8,128)(2,1)S(1)}, u32[]{:S(2)}) copy-start(bf16[384,1152]{1,0:T(8,128)(2,1)S(1)} %shard_map.206.he_ref) | copy-start | bytes 2654212
  55.0 30.7 %copy-start.18 = (s32[1,2,3,5]{3,1,2,0:T(2,128)S(1)}, s32[1,2,3,5]{3,1,2,0:T(2,128)}, u32[]{:S(2)}) copy-start(s32[1,2,3,5]{3,1,2,0:T(2,128)} %param.29) | copy-start | bytes 364
  55.0 30.8 %copy-start.14 = (s32[384]{0:T(512)S(1)}, s32[384]{0:T(512)}, u32[]{:S(2)}) copy-start(s32[384]{0:T(512)} %constant.74.clone) | copy-start | bytes 4612
  55.0 30.8 %copy-start.19 = (s32[384]{0:T(512)S(1)}, s32[384]{0:T(512)}, u32[]{:S(2)}) copy-start(s32[384]{0:T(512)} %constant.71.clone) | copy-start | bytes 4612
  55.0 30.8 %copy-start.20 = (s32[384]{0:T(512)S(1)}, s32[384]{0:T(512)}, u32[]{:S(2)}) copy-start(s32[384]{0:T(512)} %constant.72.clone) | copy-start | bytes 4612
  55.0 30.8 %copy-start.24 = (pred[384]{0:T(512)(128)(4,1)S(1)}, pred[384]{0:T(512)(128)(4,1)}, u32[]{:S(2)}) copy-start(pred[384]{0:T(512)(128)(4,1)} %constant.73.clone) | copy-start | bytes 1156
  55.0 30.8 %copy-start.22 = (pred[384]{0:T(512)(128)(4,1)S(1)}, pred[384]{0:T(512)(128)(4,1)}, u32[]{:S(2)}) copy-start(pred[384]{0:T(512)(128)(4,1)} %constant.75.clone) | copy-start | bytes 1156
  55.1 30.8 %copy-start.23 = (pred[384]{0:T(512)(128)(4,1)S(1)}, pred[384]{0:T(512)(128)(4,1)}, u32[]{:S(2)}) copy-start(pred[384]{0:T(512)(128)(4,1)} %constant.76.clone) | copy-start | bytes 1156
  68.0 12.6 %collective-permute-start.8 = (bf16[96,1728]{1,0:T(8,128)(2,1)S(1)}, bf16[96,1728]{1,0:T(8,128)(2,1)S(1)}, u32[]{:S(2)}, u32[]{:S(2)}) collective-permute-start(bf16[96,1728]{1,0:T(8,128)(2,1)S(1)} %slice.34), channel_id=1, source_target_pairs={{0,2},{2,4},{4,6},{6,0},{1,3},{3,5},{5,7},{7,1},{8,10},{10,12},{12... | collective-permute-start | bytes 995336 | tf_op jit(solution)/shard_map/ppermute | solution.py:342
  70.0 12.2 %collective-permute-start.9 = (bf16[96,1728]{1,0:T(8,128)(2,1)S(1)}, bf16[96,1728]{1,0:T(8,128)(2,1)S(1)}, u32[]{:S(2)}, u32[]{:S(2)}) collective-permute-start(bf16[96,1728]{1,0:T(8,128)(2,1)S(1)} %slice.35), channel_id=1, source_target_pairs={{0,6},{2,0},{4,2},{6,4},{1,7},{3,1},{5,3},{7,5},{8,14},{10,8},{12,... | collective-permute-start | bytes 995336 | tf_op jit(solution)/shard_map/ppermute | solution.py:342
  73.3 12.6 %collective-permute-start.10 = (bf16[192,1728]{1,0:T(8,128)(2,1)S(1)}, bf16[192,1728]{1,0:T(8,128)(2,1)S(1)}, u32[]{:S(2)}, u32[]{:S(2)}) collective-permute-start(bf16[192,1728]{1,0:T(8,128)(2,1)S(1)} %pad_maximum_fusion.1.b0), channel_id=1, source_target_pairs={{0,1},{1,0},{2,3},{3,2},{4,5},{5,4},{6,7},{7,6},{8,9},{9,8},{10,11... | collective-permute-start | bytes 1990664 | tf_op jit(solution)/shard_map/ppermute | solution.py:339
  76.3 9.7 %collective-permute-start.11 = (bf16[192,1728]{1,0:T(8,128)(2,1)S(1)}, bf16[192,1728]{1,0:T(8,128)(2,1)}, u32[]{:S(2)}, u32[]{:S(2)}) collective-permute-start(bf16[192,1728]{1,0:T(8,128)(2,1)S(1)} %collective-permute-done.4.b1), channel_id=1, source_target_pairs={{0,1},{1,0},{2,3},{3,2},{4,5},{5,4},{6,7},{7,6},{8,9},{9,8},{10,11... | collective-permute-start | bytes 1990664 | tf_op jit(solution)/shard_map/ppermute | solution.py:339
  78.2 7.8 %collective-permute-start.12 = (bf16[192,1728]{1,0:T(8,128)(2,1)S(1)}, bf16[192,1728]{1,0:T(8,128)(2,1)}, u32[]{:S(2)}, u32[]{:S(2)}) collective-permute-start(bf16[192,1728]{1,0:T(8,128)(2,1)S(1)} %collective-permute-done.5.b2), channel_id=1, source_target_pairs={{0,1},{1,0},{2,3},{3,2},{4,5},{5,4},{6,7},{7,6},{8,9},{9,8},{10,11... | collective-permute-start | bytes 1990664 | tf_op jit(solution)/shard_map/ppermute | solution.py:339
  82.2 5.1 %collective-permute-start.13 = (bf16[192,1728]{1,0:T(8,128)(2,1)S(1)}, bf16[192,1728]{1,0:T(8,128)(2,1)}, u32[]{:S(2)}, u32[]{:S(2)}) collective-permute-start(bf16[192,1728]{1,0:T(8,128)(2,1)S(1)} %constant_dynamic-update-slice_fusion.b3), channel_id=1, source_target_pairs={{0,1},{1,0},{2,3},{3,2},{4,5},{5,4},{6,7},{7,6},{8,9},{9,8},{10,11... | collective-permute-start | bytes 1990664 | tf_op jit(solution)/shard_map/ppermute | solution.py:339
  85.9 17.8 %copy-start.3 = (bf16[8,16,1152]{2,1,0:T(8,128)(2,1)S(1)}, bf16[8,16,1152]{2,1,0:T(8,128)(2,1)}, u32[]{:S(2)}) copy-start(bf16[8,16,1152]{2,1,0:T(8,128)(2,1)} %param.20) | copy-start | bytes 884740
  85.9 17.8 %copy-start.4 = (bf16[1152,192]{0,1:T(8,128)(2,1)S(1)}, bf16[1152,192]{0,1:T(8,128)(2,1)}, u32[]{:S(2)}) copy-start(bf16[1152,192]{0,1:T(8,128)(2,1)} %param.26) | copy-start | bytes 1327108
  85.9 17.8 %copy-start.5 = (f32[8,16,64]{2,1,0:T(8,128)S(1)}, f32[8,16,64]{2,1,0:T(8,128)}, u32[]{:S(2)}) copy-start(f32[8,16,64]{2,1,0:T(8,128)} %param.27) | copy-start | bytes 98308
  85.9 17.8 %copy-start.6 = (s32[8,16,64]{2,1,0:T(8,128)S(1)}, s32[8,16,64]{2,1,0:T(8,128)}, u32[]{:S(2)}) copy-start(s32[8,16,64]{2,1,0:T(8,128)} %param.28) | copy-start | bytes 98308
  87.4 1.2 copy-start.8
  88.5 1.2 copy-start.10
  89.7 1.2 copy-start.12
  109.0 10.2 %collective-permute-start.14 = (bf16[144,640]{1,0:T(8,128)(2,1)S(1)}, bf16[144,640]{1,0:T(8,128)(2,1)S(1)}, u32[]{:S(2)}, u32[]{:S(2)}) collective-permute-start(bf16[144,640]{1,0:T(8,128)(2,1)S(1)} %get-tuple-element.32.up_ref), channel_id=1, source_target_pairs={{0,32},{32,64},{64,96},{96,128},{128,160},{160,192},{192,224},{224... | collective-permute-start | bytes 552968 | tf_op jit(solution)/shard_map/ppermute | solution.py:345
  110.9 24.3 %collective-permute-start.15 = (bf16[144,640]{1,0:T(8,128)(2,1)S(1)}, bf16[144,640]{1,0:T(8,128)(2,1)S(1)}, u32[]{:S(2)}, u32[]{:S(2)}) collective-permute-start(bf16[144,640]{1,0:T(8,128)(2,1)S(1)} %get-tuple-element.32.up_ref), channel_id=1, source_target_pairs={{32,0},{64,32},{96,64},{128,96},{160,128},{192,160},{224,192},{256... | collective-permute-start | bytes 552968 | tf_op jit(solution)/shard_map/ppermute | solution.py:346
  135.3 8.3 %collective-permute-start.16 = (bf16[432,640]{1,0:T(8,128)(2,1)S(1)}, bf16[432,640]{1,0:T(8,128)(2,1)S(1)}, u32[]{:S(2)}, u32[]{:S(2)}) collective-permute-start(bf16[432,640]{1,0:T(8,128)(2,1)S(1)} %pad_maximum_fusion.2.pack_ref), channel_id=1, source_target_pairs={{0,1},{1,2},{2,3},{3,4},{4,5},{5,6},{6,7},{7,8},{8,9},{9,10},{10,1... | collective-permute-start | bytes 1658888 | tf_op jit(solution)/shard_map/ppermute | solution.py:350
  137.2 12.9 %collective-permute-start.17 = (bf16[432,640]{1,0:T(8,128)(2,1)S(1)}, bf16[432,640]{1,0:T(8,128)(2,1)S(1)}, u32[]{:S(2)}, u32[]{:S(2)}) collective-permute-start(bf16[432,640]{1,0:T(8,128)(2,1)S(1)} %pad_maximum_fusion.2.pack_ref), channel_id=1, source_target_pairs={{1,0},{2,1},{3,2},{4,3},{5,4},{6,5},{7,6},{8,7},{9,8},{10,9},{11,1... | collective-permute-start | bytes 1658888 | tf_op jit(solution)/shard_map/ppermute | solution.py:350
  139.6 10.5 %copy-start.1 = (bf16[1152,1152]{1,0:T(8,128)(2,1)S(1)}, bf16[1152,1152]{1,0:T(8,128)(2,1)}, u32[]{:S(2)}) copy-start(bf16[1152,1152]{1,0:T(8,128)(2,1)} %copy-done) | copy-start | bytes 7962628

commit v4 on v3

--- a/solution.py
+++ b/solution.py
@@ -22,6 +22,7 @@
 VMEM = pl.BlockSpec(memory_space=pltpu.VMEM)
 SMEM = pl.BlockSpec(memory_space=pltpu.SMEM)
 ANY = pl.BlockSpec(memory_space=pl.ANY)
+HBM = pl.BlockSpec(memory_space=pltpu.HBM)
 K0, V0, Q0 = 0, HW, 2 * HW
 VB = 512
 
@@ -63,6 +64,20 @@
         center, rstd = norm_parts(x_ref[i * T : (i + 1) * T, :].astype(F32))
         hidden = (center * rstd * gain_ref[...]).astype(BF)
         out_ref[i * T : (i + 1) * T, :] = nn(hidden, order_ref[...]).astype(BF)
+
+
+def gather_kernel(k_any, v_any, q_any, o_any, out_ref, k_ref, v_ref, q_ref, o_ref, sems):
+    pairs = ((k_any, k_ref), (v_any, v_ref), (q_any, q_ref), (o_any, o_ref))
+    copies = [pltpu.make_async_copy(a, b, sems.at[i]) for i, (a, b) in enumerate(pairs)]
+    for c in copies:
+        c.start()
+    for c in copies:
+        c.wait()
+    lasts = jnp.concatenate([o_ref[24:36, 0:HW], o_ref[24:36, HW:D]], axis=0)
+    rows = jnp.concatenate([o_ref[0:24, :], lasts], axis=1)
+    out_ref[...] = jnp.concatenate(
+        [jnp.concatenate([k_ref[...], v_ref[...], q_ref[...]], axis=1), rows], axis=0
+    )
 
 
 def collect(blocks, first, rows, w_ref, sems):
@@ -75,12 +90,20 @@
     return copies
 
 
+def table_kernel(blocks_ref, hw_any, hc_any, he_any, out_ref):
+    for i in range(30):
+        out_ref[i] = blocks_ref[i]
+
+
 def forward_kernel(
-    blocks_ref, hw_ref, hc_ref, he_ref, b0, b1, b2, b3, b4, b5, b6, b7,
-    win_ref, e_ref, att_ref, stat_ref, rows_ref,
-    w_ref, bias_ref, acc_ref, sems,
+    blocks_ref, hw_any, hc_any, he_any, place_ref, wpix_ref, x_ref, meas_ref, filt_ref,
+    b0, b1, b2, b3, b4, b5, b6, b7,
+    win_ref, e_ref, den_ref, og_ref, pack_ref, stat_ref,
+    wo_ref, w_ref, wn_ref, h_ref, bias_ref, acc_ref, sems_o, sems, sems_h,
 ):
+    copies_o = collect((b0, b1, b2, b3, b4, b5, b6, b7), 144, 48, wo_ref, sems_o)
     copies = collect((b0, b1, b2, b3, b4, b5, b6, b7), 0, 144, w_ref, sems)
+    copies += collect((hw_any, hc_any, he_any), 0, 3 * T, h_ref, sems_h)
     acc_ref[...] = jnp.zeros_like(acc_ref)
 
     qc = (lax.broadcasted_iota(jnp.int32, (T, T), 0) & 8) > 0
@@ -94,7 +117,6 @@
     for r in range(3):
         for w in range(6):
             rows.append(jnp.where(lane_c, allowed(1, r, w), allowed(0, r, w)))
-    rows_ref[...] = jnp.concatenate(rows + [jnp.zeros((14, T), F32)], axis=0)
     for t in range(3):
         for r in range(3):
             seen = jnp.where(
@@ -104,12 +126,21 @@
             )
             j = 3 * t + r
             bias_ref[:, j * T : (j + 1) * T] = (1.0 - seen) * OFF
+    lane_of = lax.broadcasted_iota(jnp.int32, (640, 384), 0)
+    whole, lower, upper = (
+        jnp.where(lane_of == place_ref[i : i + 1, :], 1.0, 0.0).astype(BF) for i in range(3)
+    )
+    for c in copies_o:
+        c.wait()
+    halves = wo_ref[:, D:QKV]
+    wn_ref[...] = (
+        nn(whole, wo_ref[:, 0:D]) + jnp.concatenate([nn(lower, halves), nn(upper, halves)], axis=1)
+    ).astype(BF)
     for c in copies:
         c.wait()
-    for g, h_ref in enumerate((hw_ref, hc_ref, he_ref)):
-        for part in range(3):
-            s = slice(part * T, (part + 1) * T)
-            win_ref[(g * 3 + part) * T : (g * 3 + part + 1) * T, :] = nn(h_ref[s, :], w_ref[...]).astype(BF)
+    for i in range(9):
+        s = slice(i * T, (i + 1) * T)
+        win_ref[s, :] = nn(h_ref[s, :], w_ref[...]).astype(BF)
 
     own = slice(4 * T, 5 * T)
     lanes = lax.broadcasted_iota(jnp.int32, (T, T), 1)
@@ -130,28 +161,9 @@
         a, b = window(V0 + HD * e)
         o = nn(low, win_ref[:, a:b]) * inv
         acc_ref[:, a - VB : b - VB] += head_only(o, V0 + HD * e, a)
-    att_ref[...] = acc_ref[...].astype(BF)
-    stat_ref[...] = stats
-
-
-def pixel_kernel(
-    att_ref, stat0_ref, rows_ref, place_ref, wpix_ref, x_ref, meas_ref, filt_ref, b0, b1, b2, b3, b4, b5, b6, b7,
-    den_ref, og_ref, pack_ref, stat_ref,
-    wo_ref, sems,
-):
-    copies = collect((b0, b1, b2, b3, b4, b5, b6, b7), 144, 48, wo_ref, sems)
-    lane_of = lax.broadcasted_iota(jnp.int32, (640, 384), 0)
-    whole, lower, upper = (
-        jnp.where(lane_of == place_ref[i : i + 1, :], 1.0, 0.0).astype(BF) for i in range(3)
-    )
-    att = att_ref[...]
-    att_whole, att_lower, att_upper = (nn(att, g).astype(BF) for g in (whole, lower, upper))
-    for c in copies:
-        c.wait()
-    mixed = nn(att_whole, wo_ref[:, 0:D]) + jnp.concatenate(
-        [nn(att_lower, wo_ref[:, D:QKV]), nn(att_upper, wo_ref[:, D:QKV])], axis=1
-    )
-    den = (x_ref[...].astype(F32) + mixed).astype(BF)
+
+    att = acc_ref[...].astype(BF)
+    den = (x_ref[...].astype(F32) + nn(att, wn_ref[...])).astype(BF)
     den_ref[...] = den
     colors = nt(den, wpix_ref[...])
     filt = filt_ref[...]
@@ -161,16 +173,9 @@
     spread = jnp.concatenate([jnp.where(filt == c, misfit, 0.0) for c in range(3)], axis=1).astype(BF)
     og = nn(spread, wpix_ref[...])
     og_ref[...] = og
-    back = og.astype(BF)
-    up = (
-        nt(nt(back, wo_ref[:, 0:D]).astype(BF), whole)
-        + nt(nt(back[:, 0:HW], wo_ref[:, D:QKV]).astype(BF), lower)
-        + nt(nt(back[:, HW:D], wo_ref[:, D:QKV]).astype(BF), upper)
-    ).astype(BF)
+    up = nt(og.astype(BF), wn_ref[...]).astype(BF)
     pack_ref[0:T, :] = up
     prod = up.astype(F32) * att.astype(F32)
-    lanes = lax.broadcasted_iota(jnp.int32, (T, T), 1)
-    stats = stat0_ref[...]
     for e in range(H):
         a, b = window(V0 + HD * e)
         inner = jnp.sum(head_only(prod[:, a - VB : b - VB], V0 + HD * e, a), axis=1, keepdims=True)
@@ -182,7 +187,11 @@
     mid = rest.astype(BF)
     low = (rest - mid.astype(F32)).astype(BF)
     pack_ref[T : T + 16, :] = jnp.concatenate(
-        [high, mid, low, rows_ref[0:16, :].astype(BF), rows_ref[16:32, :].astype(BF)], axis=1
+        [
+            high, mid, low, jnp.concatenate(rows[:16], axis=0).astype(BF),
+            jnp.concatenate(rows[16:] + [jnp.zeros((14, T), F32)], axis=0).astype(BF),
+        ],
+        axis=1,
     )
 
 
@@ -258,11 +267,9 @@
         c.wait()
     moved = nt(grads, w_ref[...])
     high = moved.astype(BF)
-    rest = moved - high.astype(F32)
-    mid = rest.astype(BF)
-    low = (rest - mid.astype(F32)).astype(BF)
-    order = order_ref[...]
-    grad = (nt(high, order) + nt(mid, order) + nt(low, order)) * gain_ref[...]
+    low = (moved - high.astype(F32)).astype(BF)
+    both = nt(jnp.concatenate([high, low], axis=0), order_ref[...])
+    grad = (both[0:T, :] + both[T : 2 * T, :]) * gain_ref[...]
     center, rstd = norm_parts(x_ref[...].astype(F32))
     xhat = center * rstd
     mean_g = jnp.mean(grad, axis=-1, keepdims=True)
@@ -349,18 +356,24 @@
     def sides(column):
         return lax.ppermute(column, lon, east), lax.ppermute(column, lon, west)
 
-    out_rows = jnp.concatenate(
-        [w_out[:24], jnp.concatenate([w_out[24:, :HW], w_out[24:, HW:]], axis=0)], axis=1
-    )
-    mine = jnp.concatenate([jnp.concatenate([w_key, w_value, w_query], axis=1), out_rows], axis=0)
+    mine = pl.pallas_call(
+        gather_kernel, out_shape=shaped((96, QKV)), in_specs=[HBM] * 4, out_specs=VMEM,
+        scratch_shapes=[pltpu.VMEM((72, HW), BF)] * 3 + [pltpu.VMEM((36, D), BF), pltpu.SemaphoreType.DMA((4,))],
+        compiler_params=params(8),
+    )(w_key, w_value, w_query, w_out)
     one, two = lax.ppermute(mine, lat + lon, first), lax.ppermute(mine, lat + lon, second)
     fetched = jnp.concatenate([one[:72], two[:72], one[72:], two[72:]], axis=0)
     column = columns(x)
     from_west, from_east = sides(column)
-    order = pl.pallas_call(
-        order_kernel, out_shape=shaped((D, D)), in_specs=[VMEM], out_specs=VMEM, compiler_params=params(16),
-        cost_estimate=pl.CostEstimate(flops=2_000_000_000, bytes_accessed=3_000_000, transcendentals=0),
-    )(weight_targets(yh, z, xi, core))
+    target = weight_targets(yh, z, xi, core)
+
+    def ordering(target):
+        return pl.pallas_call(
+            order_kernel, out_shape=shaped((D, D)), in_specs=[VMEM], out_specs=VMEM, compiler_params=params(8),
+            cost_estimate=pl.CostEstimate(flops=2_000_000_000, bytes_accessed=3_000_000, transcendentals=0),
+        )(target)
+
+    order = ordering(target)
 
     def hidden(v):
         return pl.pallas_call(
@@ -376,28 +389,28 @@
     held = (fetched, right, left, across)
     blocks = held + tuple(swap(v) for v in held)
 
-    win, e, att, stat0, rows = pl.pallas_call(
+    table = pl.pallas_call(
+        table_kernel, out_shape=shaped((30,), jnp.int32), in_specs=[SMEM] + [ANY] * 3, out_specs=SMEM,
+        compiler_params=params(4),
+        cost_estimate=pl.CostEstimate(flops=2_000_000_000, bytes_accessed=3_000_000, transcendentals=0),
+    )(block_mask.reshape(30), hw, hc, he)
+    win, e, den, og, pack, stat = pl.pallas_call(
         forward_kernel,
         out_shape=(
-            shaped((9 * T, QKV)), shaped((H * T, 9 * T)), shaped((T, 640)), shaped((T, T), F32), shaped((32, T), F32),
+            shaped((9 * T, QKV)), shaped((H * T, 9 * T)), shaped((T, D)), shaped((T, D), F32), shaped((144, 640)),
+            shaped((T, T), F32),
         ),
-        in_specs=[SMEM] + [VMEM] * 3 + [ANY] * 8,
-        out_specs=(VMEM,) * 5,
+        in_specs=[SMEM] + [HBM] * 3 + [VMEM] * 5 + [ANY] * 8,
+        out_specs=(VMEM,) * 6,
         scratch_shapes=[
-            pltpu.VMEM((D, QKV), BF), pltpu.VMEM((T, 9 * T), F32), pltpu.VMEM((T, 640), F32),
-            pltpu.SemaphoreType.DMA((8,)),
+            pltpu.VMEM((384, QKV), BF), pltpu.VMEM((D, QKV), BF), pltpu.VMEM((640, D), BF),
+            pltpu.VMEM((9 * T, D), BF), pltpu.VMEM((T, 9 * T), F32), pltpu.VMEM((T, 640), F32),
+            pltpu.SemaphoreType.DMA((8,)), pltpu.SemaphoreType.DMA((8,)), pltpu.SemaphoreType.DMA((3,)),
         ],
-        compiler_params=params(20),
+        compiler_params=params(22),
         cost_estimate=pl.CostEstimate(flops=12_000_000_000, bytes_accessed=8_000_000, transcendentals=1_000_000),
-    )(block_mask.reshape(30), hw, hc, he, *blocks)
-    den, og, pack, stat = pl.pallas_call(
-        pixel_kernel,
-        out_shape=(shaped((T, D)), shaped((T, D), F32), shaped((144, 640)), shaped((T, T), F32)),
-        in_specs=[VMEM] * 8 + [ANY] * 8, out_specs=(VMEM,) * 4,
-        scratch_shapes=[pltpu.VMEM((384, QKV), BF), pltpu.SemaphoreType.DMA((8,))],
-        compiler_params=params(14),
     )(
-        att, stat0, rows, out_targets(yh, z, xi, core), w_pixel.T, x, measured.reshape(T, 64),
+        table, hw, hc, he, out_targets(yh, z, xi, core), w_pixel.T, x, measured.reshape(T, 64),
         filter_color.reshape(T, 64), *blocks,
     )
     packs = columns(pack)
@@ -406,7 +419,7 @@
         scratch_shapes=[pltpu.VMEM((T, 640), F32)], compiler_params=params(16),
         cost_estimate=pl.CostEstimate(flops=4_000_000_000, bytes_accessed=6_000_000, transcendentals=0),
     )(win, e, pack, stat)
-    packs, gq = lax.optimization_barrier((packs, gq))
+    packs, gq, target = lax.optimization_barrier((packs, gq, target))
     packs_west, packs_east = sides(packs)
     gk, gv = pl.pallas_call(
         key_centre_kernel, out_shape=(shaped((T, 640), F32),) * 2, in_specs=[VMEM] * 2, out_specs=(VMEM,) * 2,
@@ -417,7 +430,7 @@
         finish_kernel, out_shape=shaped((T, D), F32), in_specs=[VMEM] * 10 + [ANY] * 8, out_specs=VMEM,
         scratch_shapes=[pltpu.VMEM((T, 640), F32)] * 2 + [pltpu.VMEM((D, QKV), BF), pltpu.SemaphoreType.DMA((8,))],
         compiler_params=params(20),
-    )(win, packs_west, packs_east, gk, gv, gq, order, x, gain, og, *blocks)
+    )(win, packs_west, packs_east, gk, gv, gq, ordering(target), x, gain, og, *blocks)
     return den.reshape(tokens.shape), guidance.reshape(tokens.shape)
 
 

time: 162 us -> 168 us (1.037)
  the two profiles are of different devices: /device:TPU:463 before, /device:TPU:32 now
where the time goes in v4:
time: 168 us; the launch traced here: 167 us
  starting transfers between devices  63.7 us (38%)
  waiting for transfers between devices  51.2 us (30%)
  Pallas kernels  41.9 us (25%)
  local copies, waits for them, and re-layouts  7.76 us (5%)
    ppermute x2, waiting for transfers between devices, columns(): before = lax.ppermute(own, lat, south)  21.9 us
    pallas_call x1, Pallas kernels, on_device(): pl.pallas_call(forward_kernel, out_shape=(shaped((9 * T, QKV)), shaped((H...  19.2 us
    ppermute x4, starting transfers between devices, sides(): return (lax.ppermute(column, lon, east), lax.ppermute(column, lon, west))  16.7 us
    ppermute x4, waiting for transfers between devices, sides(): return (lax.ppermute(column, lon, east), lax.ppermute(column, lon, west))  16.5 us
    ppermute x2, starting transfers between devices, columns(): after = lax.ppermute(own, lat, north)  13.2 us
    ppermute x4, starting transfers between devices, along(): return lax.ppermute(v, 'x', [(i, (i + shift) % 4) for i in range(4)])  12.9 us
    ppermute x4, waiting for transfers between devices, along(): return lax.ppermute(v, 'x', [(i, (i + shift) % 4) for i in range(4)])  12.7 us
    pallas_call x1, Pallas kernels, on_device(): pl.pallas_call(finish_kernel, out_shape=shaped((T, D), F32), in_specs=[VM...  10.2 us
  transfers between devices with their start and end apart: 18, of which 7 were waited for; matrix products, arithmetic and copies ran while one was open for 2% of the time, Pallas kernels for 7%

profile of v4, /device:TPU:32, one launch (start us, length us, event | category | flops | bytes accessed | tf_op | source)
XLA Modules:
  0.0 167.2 jit_solution(12031270564395460751)
XLA Ops:
  0.7 10.6 %collective-permute-start.3 = (bf16[128,1152]{1,0:T(8,128)(2,1)}, bf16[128,1152]{1,0:T(8,128)(2,1)S(1)}, u32[]{:S(2)}, u32[]{:S(2)}) collective-permute-start(bf16[128,1152]{1,0:T(8,128)(2,1)} %bitcast.6), channel_id=1, source_target_pairs={{32,0},{64,32},{96,64},{128,96},{160,128},{192,160},{224,192},{256... | collective-permute-start | bytes 884744 | tf_op jit(solution)/shard_map/ppermute | solution.py:353
  11.3 1.9 %collective-permute-start.2 = (bf16[128,1152]{1,0:T(8,128)(2,1)}, bf16[128,1152]{1,0:T(8,128)(2,1)S(1)}, u32[]{:S(2)}, u32[]{:S(2)}) collective-permute-start(bf16[128,1152]{1,0:T(8,128)(2,1)} %bitcast.7), channel_id=1, source_target_pairs={{0,32},{32,64},{64,96},{96,128},{128,160},{160,192},{192,224},{224... | collective-permute-start | bytes 884744 | tf_op jit(solution)/shard_map/ppermute | solution.py:352
  13.2 0.9 copy-done.1
  14.1 0.9 copy-done.2
  15.0 0.9 copy-done.3
  15.9 0.9 copy-done.4
  16.8 0.6 shard_map.203
  17.4 2.8 %collective-permute-start.1 = (bf16[96,1728]{1,0:T(8,128)(2,1)S(1)}, bf16[96,1728]{1,0:T(8,128)(2,1)S(1)}, u32[]{:S(2)}, u32[]{:S(2)}) collective-permute-start(bf16[96,1728]{1,0:T(8,128)(2,1)S(1)} %shard_map.203), channel_id=1, source_target_pairs={{440,0},{377,1},{474,2},{347,3},{508,4},{317,5},{286,6},{7,7},{432... | collective-permute-start | bytes 995336 | tf_op jit(solution)/shard_map/ppermute | solution.py:364
  20.2 3.9 %collective-permute-start = (bf16[96,1728]{1,0:T(8,128)(2,1)S(1)}, bf16[96,1728]{1,0:T(8,128)(2,1)S(1)}, u32[]{:S(2)}, u32[]{:S(2)}) collective-permute-start(bf16[96,1728]{1,0:T(8,128)(2,1)S(1)} %shard_map.203), channel_id=1, source_target_pairs={{224,0},{33,1},{194,2},{67,3},{164,4},{101,5},{134,6},{415,7},{232... | collective-permute-start | bytes 995336 | tf_op jit(solution)/shard_map/ppermute | solution.py:364
  24.1 13.2 %collective-permute-done.2 = bf16[128,1152]{1,0:T(8,128)(2,1)S(1)} collective-permute-done((bf16[128,1152]{1,0:T(8,128)(2,1)}, bf16[128,1152]{1,0:T(8,128)(2,1)S(1)}, u32[]{:S(2)}, u32[]{:S(2)}) %collective-permute-start.2) | collective-permute-done | bytes 294944 | tf_op jit(solution)/shard_map/ppermute | solution.py:352
  37.4 1.0 pad_maximum_fusion.x_ref
  38.4 1.9 %collective-permute-start.7 = (bf16[384,1152]{1,0:T(8,128)(2,1)S(1)}, bf16[384,1152]{1,0:T(8,128)(2,1)S(1)}, u32[]{:S(2)}, u32[]{:S(2)}) collective-permute-start(bf16[384,1152]{1,0:T(8,128)(2,1)S(1)} %pad_maximum_fusion.x_ref), channel_id=1, source_target_pairs={{1,0},{2,1},{3,2},{4,3},{5,4},{6,5},{7,6},{8,7},{9,8},{10,9},{11,1... | collective-permute-start | bytes 2654216 | tf_op jit(solution)/shard_map/ppermute | solution.py:357
  40.4 0.5 shard_map.204.order_ref
  40.9 0.2 copy-done.12
  41.1 2.4 %collective-permute-start.6 = (bf16[384,1152]{1,0:T(8,128)(2,1)S(1)}, bf16[384,1152]{1,0:T(8,128)(2,1)S(1)}, u32[]{:S(2)}, u32[]{:S(2)}) collective-permute-start(bf16[384,1152]{1,0:T(8,128)(2,1)S(1)} %pad_maximum_fusion.x_ref), channel_id=1, source_target_pairs={{0,1},{1,2},{2,3},{3,4},{4,5},{5,6},{6,7},{7,8},{8,9},{9,10},{10,1... | collective-permute-start | bytes 2654216 | tf_op jit(solution)/shard_map/ppermute | solution.py:357
  43.5 1.8 %shard_map.205.hc_any = bf16[384,1152]{1,0:T(8,128)(2,1)S(1)} custom-call(bf16[384,1152]{1,0:T(8,128)(2,1)S(1)} %pad_maximum_fusion.x_ref, f32[1,1152]{1,0:T(1,128)S(1)} %reshape.30.gain_ref, bf16[1152,1152]{1,0:T(8,128)(2,1)S(1)} %shard_map.204.order_ref), custom_call_target="tpu_custom_call" | custom-call | flops 3000000000 | bytes 5000000 | tf_op jit(solution)/shard_map/pallas_call | solution.py:379
  45.4 0.1 pad_maximum_fusion.1.b0
  45.5 2.5 %collective-permute-start.5 = (bf16[192,1728]{1,0:T(8,128)(2,1)S(1)}, bf16[192,1728]{1,0:T(8,128)(2,1)S(1)}, u32[]{:S(2)}, u32[]{:S(2)}) collective-permute-start(bf16[192,1728]{1,0:T(8,128)(2,1)S(1)} %pad_maximum_fusion.1.b0), channel_id=1, source_target_pairs={{0,6},{2,0},{4,2},{6,4},{1,7},{3,1},{5,3},{7,5},{8,14},{10,8},{12,... | collective-permute-start | bytes 1990664 | tf_op jit(solution)/shard_map/ppermute | solution.py:349
  48.0 3.3 %collective-permute-start.4 = (bf16[192,1728]{1,0:T(8,128)(2,1)S(1)}, bf16[192,1728]{1,0:T(8,128)(2,1)S(1)}, u32[]{:S(2)}, u32[]{:S(2)}) collective-permute-start(bf16[192,1728]{1,0:T(8,128)(2,1)S(1)} %pad_maximum_fusion.1.b0), channel_id=1, source_target_pairs={{0,2},{2,4},{4,6},{6,0},{1,3},{3,5},{5,7},{7,1},{8,10},{10,12},{12... | collective-permute-start | bytes 1990664 | tf_op jit(solution)/shard_map/ppermute | solution.py:349
  51.4 1.8 %shard_map.207.he_any = bf16[384,1152]{1,0:T(8,128)(2,1)S(1)} custom-call(bf16[384,1152]{1,0:T(8,128)(2,1)S(1)} %collective-permute-done.7.x_ref, f32[1,1152]{1,0:T(1,128)S(1)} %reshape.30.gain_ref, bf16[1152,1152]{1,0:T(8,128)(2,1)S(1)} %shard_map.204.order_ref), custom_call_target="tpu_custom_call" | custom-call | flops 3000000000 | bytes 5000000 | tf_op jit(solution)/shard_map/pallas_call | solution.py:379
  53.2 6.3 %collective-permute-done.6.x_ref = bf16[384,1152]{1,0:T(8,128)(2,1)S(1)} collective-permute-done((bf16[384,1152]{1,0:T(8,128)(2,1)S(1)}, bf16[384,1152]{1,0:T(8,128)(2,1)S(1)}, u32[]{:S(2)}, u32[]{:S(2)}) %collective-permute-start.6) | collective-permute-done | bytes 884768 | tf_op jit(solution)/shard_map/ppermute | solution.py:357
  59.5 1.8 %shard_map.206.hw_any = bf16[384,1152]{1,0:T(8,128)(2,1)S(1)} custom-call(bf16[384,1152]{1,0:T(8,128)(2,1)S(1)} %collective-permute-done.6.x_ref, f32[1,1152]{1,0:T(1,128)S(1)} %reshape.30.gain_ref, bf16[1152,1152]{1,0:T(8,128)(2,1)S(1)} %shard_map.204.order_ref), custom_call_target="tpu_custom_call" | custom-call | flops 3000000000 | bytes 5000000 | tf_op jit(solution)/shard_map/pallas_call | solution.py:379
  61.4 5.1 %collective-permute-done.5.b2 = bf16[192,1728]{1,0:T(8,128)(2,1)S(1)} collective-permute-done((bf16[192,1728]{1,0:T(8,128)(2,1)S(1)}, bf16[192,1728]{1,0:T(8,128)(2,1)S(1)}, u32[]{:S(2)}, u32[]{:S(2)}) %collective-permute-start.5) | collective-permute-done | bytes 663584 | tf_op jit(solution)/shard_map/ppermute | solution.py:349
  66.5 7.6 %collective-permute-done.4.b1 = bf16[192,1728]{1,0:T(8,128)(2,1)S(1)} collective-permute-done((bf16[192,1728]{1,0:T(8,128)(2,1)S(1)}, bf16[192,1728]{1,0:T(8,128)(2,1)S(1)}, u32[]{:S(2)}, u32[]{:S(2)}) %collective-permute-start.4) | collective-permute-done | bytes 663584 | tf_op jit(solution)/shard_map/ppermute | solution.py:349
  74.1 0.8 slice.22
  74.9 1.9 %collective-permute-start.8 = (bf16[96,1728]{1,0:T(8,128)(2,1)}, bf16[96,1728]{1,0:T(8,128)(2,1)}, u32[]{:S(2)}, u32[]{:S(2)}) collective-permute-start(bf16[96,1728]{1,0:T(8,128)(2,1)} %slice.22), channel_id=1, source_target_pairs={{0,2},{2,4},{4,6},{6,0},{1,3},{3,5},{5,7},{7,1},{8,10},{10,12},{12... | collective-permute-start | bytes 995336 | tf_op jit(solution)/shard_map/ppermute | solution.py:349
  76.8 0.8 slice.23
  77.6 5.1 %collective-permute-start.9 = (bf16[96,1728]{1,0:T(8,128)(2,1)}, bf16[96,1728]{1,0:T(8,128)(2,1)S(1)}, u32[]{:S(2)}, u32[]{:S(2)}) collective-permute-start(bf16[96,1728]{1,0:T(8,128)(2,1)} %slice.23), channel_id=1, source_target_pairs={{0,6},{2,0},{4,2},{6,4},{1,7},{3,1},{5,3},{7,5},{8,14},{10,8},{12,... | collective-permute-start | bytes 995336 | tf_op jit(solution)/shard_map/ppermute | solution.py:349
  82.7 0.1 reshape.28.blocks_ref
  82.8 2.0 %collective-permute-start.10 = (bf16[192,1728]{1,0:T(8,128)(2,1)S(1)}, bf16[192,1728]{1,0:T(8,128)(2,1)S(1)}, u32[]{:S(2)}, u32[]{:S(2)}) collective-permute-start(bf16[192,1728]{1,0:T(8,128)(2,1)S(1)} %pad_maximum_fusion.1.b0), channel_id=1, source_target_pairs={{0,1},{1,0},{2,3},{3,2},{4,5},{5,4},{6,7},{7,6},{8,9},{9,8},{10,11... | collective-permute-start | bytes 1990664 | tf_op jit(solution)/shard_map/ppermute | solution.py:346
  84.9 2.4 %collective-permute-start.11 = (bf16[192,1728]{1,0:T(8,128)(2,1)S(1)}, bf16[192,1728]{1,0:T(8,128)(2,1)S(1)}, u32[]{:S(2)}, u32[]{:S(2)}) collective-permute-start(bf16[192,1728]{1,0:T(8,128)(2,1)S(1)} %collective-permute-done.4.b1), channel_id=1, source_target_pairs={{0,1},{1,0},{2,3},{3,2},{4,5},{5,4},{6,7},{7,6},{8,9},{9,8},{10,11... | collective-permute-start | bytes 1990664 | tf_op jit(solution)/shard_map/ppermute | solution.py:346
  87.3 1.9 %collective-permute-start.12 = (bf16[192,1728]{1,0:T(8,128)(2,1)S(1)}, bf16[192,1728]{1,0:T(8,128)(2,1)S(1)}, u32[]{:S(2)}, u32[]{:S(2)}) collective-permute-start(bf16[192,1728]{1,0:T(8,128)(2,1)S(1)} %collective-permute-done.5.b2), channel_id=1, source_target_pairs={{0,1},{1,0},{2,3},{3,2},{4,5},{5,4},{6,7},{7,6},{8,9},{9,8},{10,11... | collective-permute-start | bytes 1990664 | tf_op jit(solution)/shard_map/ppermute | solution.py:346
  89.2 1.0 constant_dynamic-update-slice_fusion.1
  90.3 2.4 %collective-permute-start.13 = (bf16[192,1728]{1,0:T(8,128)(2,1)S(1)}, bf16[192,1728]{1,0:T(8,128)(2,1)S(1)}, u32[]{:S(2)}, u32[]{:S(2)}) collective-permute-start(bf16[192,1728]{1,0:T(8,128)(2,1)S(1)} %constant_dynamic-update-slice_fusion.b3), channel_id=1, source_target_pairs={{0,1},{1,0},{2,3},{3,2},{4,5},{5,4},{6,7},{7,6},{8,9},{9,8},{10,11... | collective-permute-start | bytes 1990664 | tf_op jit(solution)/shard_map/ppermute | solution.py:346
  92.9 1.2 copy-done.11
  94.0 1.2 shard_map.208.blocks_ref
  95.3 19.2 %shard_map.209 = (bf16[1152,1728]{1,0:T(8,128)(2,1)S(1)}, bf16[1024,1152]{1,0:T(8,128)(2,1)S(1)}, bf16[128,1152]{1,0:T(8,128)(2,1)}, f32[128,1152]{1,0:T(8,128)S...) custom-call(s32[30]{0:T(128)S(1)} %shard_map.208.blocks_ref, bf16[384,1152]{1,0:T(8,128)(2,1)S(1)} %copy-done.11, ...), custom_call_target="tpu_custom_call" | custom-call | flops 12000000000 | bytes 8000000 | tf_op jit(solution)/shard_map/pallas_call | solution.py:397
  114.5 2.6 %collective-permute-start.15 = (bf16[144,640]{1,0:T(8,128)(2,1)S(1)}, bf16[144,640]{1,0:T(8,128)(2,1)S(1)}, u32[]{:S(2)}, u32[]{:S(2)}) collective-permute-start(bf16[144,640]{1,0:T(8,128)(2,1)S(1)} %get-tuple-element.27.up_ref), channel_id=1, source_target_pairs={{32,0},{64,32},{96,64},{128,96},{160,128},{192,160},{224,192},{256... | collective-permute-start | bytes 552968 | tf_op jit(solution)/shard_map/ppermute | solution.py:353
  117.1 3.5 %collective-permute-start.14 = (bf16[144,640]{1,0:T(8,128)(2,1)S(1)}, bf16[144,640]{1,0:T(8,128)(2,1)S(1)}, u32[]{:S(2)}, u32[]{:S(2)}) collective-permute-start(bf16[144,640]{1,0:T(8,128)(2,1)S(1)} %get-tuple-element.27.up_ref), channel_id=1, source_target_pairs={{0,32},{32,64},{64,96},{96,128},{128,160},{160,192},{192,224},{224... | collective-permute-start | bytes 552968 | tf_op jit(solution)/shard_map/ppermute | solution.py:352
  120.6 2.4 %shard_map.210.gq_ref = bf16[128,576]{1,0:T(8,128)(2,1)S(1)} custom-call(bf16[1152,1728]{1,0:T(8,128)(2,1)S(1)} %get-tuple-element.26.win_ref, bf16[1024,1152]{1,0:T(8,128)(2,1)S(1)} %get-tuple-element.28.e_ref, bf16[144,640]{1,0:T(8,128)(2,1)S(1)} %get-tuple-element.27.up_ref, f32[128,128]{1,0:T(8,128)S(1)} %get-tuple-element.29.stat_ref), custom_call_target="tpu_custom_call" | custom-call | flops 4000000000 | bytes 6000000 | tf_op jit(solution)/shard_map/pallas_call | solution.py:417
  123.0 8.6 %collective-permute-done.14 = bf16[144,640]{1,0:T(8,128)(2,1)S(1)} collective-permute-done((bf16[144,640]{1,0:T(8,128)(2,1)S(1)}, bf16[144,640]{1,0:T(8,128)(2,1)S(1)}, u32[]{:S(2)}, u32[]{:S(2)}) %collective-permute-start.14) | collective-permute-done | bytes 184352 | tf_op jit(solution)/shard_map/ppermute | solution.py:352
  131.6 10.5 %collective-permute-start.17 = (bf16[432,640]{1,0:T(8,128)(2,1)S(1)}, bf16[432,640]{1,0:T(8,128)(2,1)S(1)}, u32[]{:S(2)}, u32[]{:S(2)}) collective-permute-start(bf16[432,640]{1,0:T(8,128)(2,1)S(1)} %pad_maximum_fusion.2.pack_ref), channel_id=1, source_target_pairs={{1,0},{2,1},{3,2},{4,3},{5,4},{6,5},{7,6},{8,7},{9,8},{10,9},{11,1... | collective-permute-start | bytes 1658888 | tf_op jit(solution)/shard_map/ppermute | solution.py:357
  142.1 1.9 %collective-permute-start.16 = (bf16[432,640]{1,0:T(8,128)(2,1)S(1)}, bf16[432,640]{1,0:T(8,128)(2,1)S(1)}, u32[]{:S(2)}, u32[]{:S(2)}) collective-permute-start(bf16[432,640]{1,0:T(8,128)(2,1)S(1)} %pad_maximum_fusion.2.pack_ref), channel_id=1, source_target_pairs={{0,1},{1,2},{2,3},{3,4},{4,5},{5,6},{6,7},{7,8},{8,9},{9,10},{10,1... | collective-permute-start | bytes 1658888 | tf_op jit(solution)/shard_map/ppermute | solution.py:357
  144.0 0.5 shard_map.212.order_ref
  144.5 2.1 %shard_map.211 = (f32[128,640]{1,0:T(8,128)S(1)}, f32[128,640]{1,0:T(8,128)S(1)}) custom-call(bf16[1152,1728]{1,0:T(8,128)(2,1)S(1)} %get-tuple-element.26.win_ref, bf16[432,640]{1,0:T(8,128)(2,1)S(1)} %pad_maximum_fusion.2.pack_ref), custom_call_target="tpu_custom_call" | custom-call | flops 4000000000 | bytes 6000000 | tf_op jit(solution)/shard_map/pallas_call | solution.py:424
  146.6 2.5 %collective-permute-done.17.packe_ref = bf16[432,640]{1,0:T(8,128)(2,1)S(1)} collective-permute-done((bf16[432,640]{1,0:T(8,128)(2,1)S(1)}, bf16[432,640]{1,0:T(8,128)(2,1)S(1)}, u32[]{:S(2)}, u32[]{:S(2)}) %collective-permute-start.17) | collective-permute-done | bytes 552992 | tf_op jit(solution)/shard_map/ppermute | solution.py:357
  149.1 7.7 %collective-permute-done.16.packw_ref = bf16[432,640]{1,0:T(8,128)(2,1)S(1)} collective-permute-done((bf16[432,640]{1,0:T(8,128)(2,1)S(1)}, bf16[432,640]{1,0:T(8,128)(2,1)S(1)}, u32[]{:S(2)}, u32[]{:S(2)}) %collective-permute-start.16) | collective-permute-done | bytes 552992 | tf_op jit(solution)/shard_map/ppermute | solution.py:357
  156.8 10.2 %shard_map.213 = f32[128,1152]{1,0:T(8,128)} custom-call(bf16[1152,1728]{1,0:T(8,128)(2,1)S(1)} %get-tuple-element.26.win_ref, bf16[432,640]{1,0:T(8,128)(2,1)S(1)} %collective-permute-done.16.packw_ref, bf16[432,640]{1,0:T(8,128)(2,1)S(1)} %collective-permute-done.17.packe_ref, f32[128,640]{1,0:T(8,128)S(1)} %get-tuple-element.31.gk0_ref, ...), custom_call_target="tpu_custom_call" | custom-call | tf_op jit(solution)/shard_map/pallas_call | solution.py:429
  (69 shorter events, 0.4 us)
Async XLA Ops:
  0.6 39.7 %copy-start.14 = (s32[1152]{0:T(1024)S(1)}, s32[1152]{0:T(1024)}, u32[]{:S(2)}) copy-start(s32[1152]{0:T(1024)} %constant.70.clone) | copy-start | bytes 13828
  0.6 39.7 %copy-start.20 = (pred[1152]{0:T(1024)(128)(4,1)S(1)}, pred[1152]{0:T(1024)(128)(4,1)}, u32[]{:S(2)}) copy-start(pred[1152]{0:T(1024)(128)(4,1)} %constant.69.clone) | copy-start | bytes 3460
  0.7 39.7 %copy-start.15 = (s32[1152]{0:T(1024)S(1)}, s32[1152]{0:T(1024)}, u32[]{:S(2)}) copy-start(s32[1152]{0:T(1024)} %constant.68.clone) | copy-start | bytes 13828
  0.7 23.5 %collective-permute-start.3 = (bf16[128,1152]{1,0:T(8,128)(2,1)}, bf16[128,1152]{1,0:T(8,128)(2,1)S(1)}, u32[]{:S(2)}, u32[]{:S(2)}) collective-permute-start(bf16[128,1152]{1,0:T(8,128)(2,1)} %bitcast.6), channel_id=1, source_target_pairs={{32,0},{64,32},{96,64},{128,96},{160,128},{192,160},{224,192},{256... | collective-permute-start | bytes 884744 | tf_op jit(solution)/shard_map/ppermute | solution.py:353
  11.3 26.1 %collective-permute-start.2 = (bf16[128,1152]{1,0:T(8,128)(2,1)}, bf16[128,1152]{1,0:T(8,128)(2,1)S(1)}, u32[]{:S(2)}, u32[]{:S(2)}) collective-permute-start(bf16[128,1152]{1,0:T(8,128)(2,1)} %bitcast.7), channel_id=1, source_target_pairs={{0,32},{32,64},{64,96},{96,128},{128,160},{160,192},{192,224},{224... | collective-permute-start | bytes 884744 | tf_op jit(solution)/shard_map/ppermute | solution.py:352
  13.2 0.9 copy-start.1
  14.1 0.9 copy-start.2
  15.0 0.9 copy-start.3
  15.9 0.9 copy-start.4
  16.8 23.6 %copy-start.16 = (s32[1152]{0:T(1024)S(1)}, s32[1152]{0:T(1024)}, u32[]{:S(2)}) copy-start(s32[1152]{0:T(1024)} %constant.67.clone) | copy-start | bytes 13828
  17.4 28.0 %collective-permute-start.1 = (bf16[96,1728]{1,0:T(8,128)(2,1)S(1)}, bf16[96,1728]{1,0:T(8,128)(2,1)S(1)}, u32[]{:S(2)}, u32[]{:S(2)}) collective-permute-start(bf16[96,1728]{1,0:T(8,128)(2,1)S(1)} %shard_map.203), channel_id=1, source_target_pairs={{440,0},{377,1},{474,2},{347,3},{508,4},{317,5},{286,6},{7,7},{432... | collective-permute-start | bytes 995336 | tf_op jit(solution)/shard_map/ppermute | solution.py:364
  20.2 25.2 %collective-permute-start = (bf16[96,1728]{1,0:T(8,128)(2,1)S(1)}, bf16[96,1728]{1,0:T(8,128)(2,1)S(1)}, u32[]{:S(2)}, u32[]{:S(2)}) collective-permute-start(bf16[96,1728]{1,0:T(8,128)(2,1)S(1)} %shard_map.203), channel_id=1, source_target_pairs={{224,0},{33,1},{194,2},{67,3},{164,4},{101,5},{134,6},{415,7},{232... | collective-permute-start | bytes 995336 | tf_op jit(solution)/shard_map/ppermute | solution.py:364
  38.4 13.0 %collective-permute-start.7 = (bf16[384,1152]{1,0:T(8,128)(2,1)S(1)}, bf16[384,1152]{1,0:T(8,128)(2,1)S(1)}, u32[]{:S(2)}, u32[]{:S(2)}) collective-permute-start(bf16[384,1152]{1,0:T(8,128)(2,1)S(1)} %pad_maximum_fusion.x_ref), channel_id=1, source_target_pairs={{1,0},{2,1},{3,2},{4,3},{5,4},{6,5},{7,6},{8,7},{9,8},{10,9},{11,1... | collective-permute-start | bytes 2654216 | tf_op jit(solution)/shard_map/ppermute | solution.py:357
  40.4 0.7 copy-start.12
  41.1 18.4 %collective-permute-start.6 = (bf16[384,1152]{1,0:T(8,128)(2,1)S(1)}, bf16[384,1152]{1,0:T(8,128)(2,1)S(1)}, u32[]{:S(2)}, u32[]{:S(2)}) collective-permute-start(bf16[384,1152]{1,0:T(8,128)(2,1)S(1)} %pad_maximum_fusion.x_ref), channel_id=1, source_target_pairs={{0,1},{1,2},{2,3},{3,4},{4,5},{5,6},{6,7},{7,8},{8,9},{9,10},{10,1... | collective-permute-start | bytes 2654216 | tf_op jit(solution)/shard_map/ppermute | solution.py:357
  45.5 21.0 %collective-permute-start.5 = (bf16[192,1728]{1,0:T(8,128)(2,1)S(1)}, bf16[192,1728]{1,0:T(8,128)(2,1)S(1)}, u32[]{:S(2)}, u32[]{:S(2)}) collective-permute-start(bf16[192,1728]{1,0:T(8,128)(2,1)S(1)} %pad_maximum_fusion.1.b0), channel_id=1, source_target_pairs={{0,6},{2,0},{4,2},{6,4},{1,7},{3,1},{5,3},{7,5},{8,14},{10,8},{12,... | collective-permute-start | bytes 1990664 | tf_op jit(solution)/shard_map/ppermute | solution.py:349
  48.0 26.1 %collective-permute-start.4 = (bf16[192,1728]{1,0:T(8,128)(2,1)S(1)}, bf16[192,1728]{1,0:T(8,128)(2,1)S(1)}, u32[]{:S(2)}, u32[]{:S(2)}) collective-permute-start(bf16[192,1728]{1,0:T(8,128)(2,1)S(1)} %pad_maximum_fusion.1.b0), channel_id=1, source_target_pairs={{0,2},{2,4},{4,6},{6,0},{1,3},{3,5},{5,7},{7,1},{8,10},{10,12},{12... | collective-permute-start | bytes 1990664 | tf_op jit(solution)/shard_map/ppermute | solution.py:349
  53.2 8.1 %copy-start.8 = (bf16[384,1152]{1,0:T(8,128)(2,1)}, bf16[384,1152]{1,0:T(8,128)(2,1)S(1)}, u32[]{:S(2)}) copy-start(bf16[384,1152]{1,0:T(8,128)(2,1)S(1)} %shard_map.207.he_any) | copy-start | bytes 2654212
  61.3 21.4 %copy-start.10 = (bf16[384,1152]{1,0:T(8,128)(2,1)}, bf16[384,1152]{1,0:T(8,128)(2,1)S(1)}, u32[]{:S(2)}) copy-start(bf16[384,1152]{1,0:T(8,128)(2,1)S(1)} %shard_map.206.hw_any) | copy-start | bytes 2654212
  61.3 21.4 %copy-start.17 = (s32[1,2,3,5]{3,1,2,0:T(2,128)S(1)}, s32[1,2,3,5]{3,1,2,0:T(2,128)}, u32[]{:S(2)}) copy-start(s32[1,2,3,5]{3,1,2,0:T(2,128)} %param.29) | copy-start | bytes 364
  61.3 31.4 %copy-start.13 = (s32[384]{0:T(512)S(1)}, s32[384]{0:T(512)}, u32[]{:S(2)}) copy-start(s32[384]{0:T(512)} %constant.74.clone) | copy-start | bytes 4612
  61.3 31.4 %copy-start.18 = (s32[384]{0:T(512)S(1)}, s32[384]{0:T(512)}, u32[]{:S(2)}) copy-start(s32[384]{0:T(512)} %constant.72.clone) | copy-start | bytes 4612
  61.4 31.4 %copy-start.19 = (s32[384]{0:T(512)S(1)}, s32[384]{0:T(512)}, u32[]{:S(2)}) copy-start(s32[384]{0:T(512)} %constant.71.clone) | copy-start | bytes 4612
  61.4 31.4 %copy-start.23 = (pred[384]{0:T(512)(128)(4,1)S(1)}, pred[384]{0:T(512)(128)(4,1)}, u32[]{:S(2)}) copy-start(pred[384]{0:T(512)(128)(4,1)} %constant.73.clone) | copy-start | bytes 1156
  61.4 31.4 %copy-start.21 = (pred[384]{0:T(512)(128)(4,1)S(1)}, pred[384]{0:T(512)(128)(4,1)}, u32[]{:S(2)}) copy-start(pred[384]{0:T(512)(128)(4,1)} %constant.76.clone) | copy-start | bytes 1156
  61.4 31.4 %copy-start.22 = (pred[384]{0:T(512)(128)(4,1)S(1)}, pred[384]{0:T(512)(128)(4,1)}, u32[]{:S(2)}) copy-start(pred[384]{0:T(512)(128)(4,1)} %constant.75.clone) | copy-start | bytes 1156
  74.9 14.3 %collective-permute-start.8 = (bf16[96,1728]{1,0:T(8,128)(2,1)}, bf16[96,1728]{1,0:T(8,128)(2,1)}, u32[]{:S(2)}, u32[]{:S(2)}) collective-permute-start(bf16[96,1728]{1,0:T(8,128)(2,1)} %slice.22), channel_id=1, source_target_pairs={{0,2},{2,4},{4,6},{6,0},{1,3},{3,5},{5,7},{7,1},{8,10},{10,12},{12... | collective-permute-start | bytes 995336 | tf_op jit(solution)/shard_map/ppermute | solution.py:349
  77.6 12.7 %collective-permute-start.9 = (bf16[96,1728]{1,0:T(8,128)(2,1)}, bf16[96,1728]{1,0:T(8,128)(2,1)S(1)}, u32[]{:S(2)}, u32[]{:S(2)}) collective-permute-start(bf16[96,1728]{1,0:T(8,128)(2,1)} %slice.23), channel_id=1, source_target_pairs={{0,6},{2,0},{4,2},{6,4},{1,7},{3,1},{5,3},{7,5},{8,14},{10,8},{12,... | collective-permute-start | bytes 995336 | tf_op jit(solution)/shard_map/ppermute | solution.py:349
  82.8 10.0 %copy-start.9 = (bf16[384,1152]{1,0:T(8,128)(2,1)S(1)}, bf16[384,1152]{1,0:T(8,128)(2,1)}, u32[]{:S(2)}) copy-start(bf16[384,1152]{1,0:T(8,128)(2,1)} %copy-done.8) | copy-start | bytes 2654212
  82.8 12.4 %collective-permute-start.10 = (bf16[192,1728]{1,0:T(8,128)(2,1)S(1)}, bf16[192,1728]{1,0:T(8,128)(2,1)S(1)}, u32[]{:S(2)}, u32[]{:S(2)}) collective-permute-start(bf16[192,1728]{1,0:T(8,128)(2,1)S(1)} %pad_maximum_fusion.1.b0), channel_id=1, source_target_pairs={{0,1},{1,0},{2,3},{3,2},{4,5},{5,4},{6,7},{7,6},{8,9},{9,8},{10,11... | collective-permute-start | bytes 1990664 | tf_op jit(solution)/shard_map/ppermute | solution.py:346
  84.9 10.3 %collective-permute-start.11 = (bf16[192,1728]{1,0:T(8,128)(2,1)S(1)}, bf16[192,1728]{1,0:T(8,128)(2,1)S(1)}, u32[]{:S(2)}, u32[]{:S(2)}) collective-permute-start(bf16[192,1728]{1,0:T(8,128)(2,1)S(1)} %collective-permute-done.4.b1), channel_id=1, source_target_pairs={{0,1},{1,0},{2,3},{3,2},{4,5},{5,4},{6,7},{7,6},{8,9},{9,8},{10,11... | collective-permute-start | bytes 1990664 | tf_op jit(solution)/shard_map/ppermute | solution.py:346
  87.3 7.9 %collective-permute-start.12 = (bf16[192,1728]{1,0:T(8,128)(2,1)S(1)}, bf16[192,1728]{1,0:T(8,128)(2,1)S(1)}, u32[]{:S(2)}, u32[]{:S(2)}) collective-permute-start(bf16[192,1728]{1,0:T(8,128)(2,1)S(1)} %collective-permute-done.5.b2), channel_id=1, source_target_pairs={{0,1},{1,0},{2,3},{3,2},{4,5},{5,4},{6,7},{7,6},{8,9},{9,8},{10,11... | collective-permute-start | bytes 1990664 | tf_op jit(solution)/shard_map/ppermute | solution.py:346
  90.3 5.0 %collective-permute-start.13 = (bf16[192,1728]{1,0:T(8,128)(2,1)S(1)}, bf16[192,1728]{1,0:T(8,128)(2,1)S(1)}, u32[]{:S(2)}, u32[]{:S(2)}) collective-permute-start(bf16[192,1728]{1,0:T(8,128)(2,1)S(1)} %constant_dynamic-update-slice_fusion.b3), channel_id=1, source_target_pairs={{0,1},{1,0},{2,3},{3,2},{4,5},{5,4},{6,7},{7,6},{8,9},{9,8},{10,11... | collective-permute-start | bytes 1990664 | tf_op jit(solution)/shard_map/ppermute | solution.py:346
  92.9 1.2 copy-start.11
  94.0 1.2 copy-start
  94.0 1.2 copy-start.5
  94.0 1.2 copy-start.6
  94.0 1.2 copy-start.7
  114.5 8.4 %collective-permute-start.15 = (bf16[144,640]{1,0:T(8,128)(2,1)S(1)}, bf16[144,640]{1,0:T(8,128)(2,1)S(1)}, u32[]{:S(2)}, u32[]{:S(2)}) collective-permute-start(bf16[144,640]{1,0:T(8,128)(2,1)S(1)} %get-tuple-element.27.up_ref), channel_id=1, source_target_pairs={{32,0},{64,32},{96,64},{128,96},{160,128},{192,160},{224,192},{256... | collective-permute-start | bytes 552968 | tf_op jit(solution)/shard_map/ppermute | solution.py:353
  117.1 14.5 %collective-permute-start.14 = (bf16[144,640]{1,0:T(8,128)(2,1)S(1)}, bf16[144,640]{1,0:T(8,128)(2,1)S(1)}, u32[]{:S(2)}, u32[]{:S(2)}) collective-permute-start(bf16[144,640]{1,0:T(8,128)(2,1)S(1)} %get-tuple-element.27.up_ref), channel_id=1, source_target_pairs={{0,32},{32,64},{64,96},{96,128},{128,160},{160,192},{192,224},{224... | collective-permute-start | bytes 552968 | tf_op jit(solution)/shard_map/ppermute | solution.py:352
  131.6 17.4 %collective-permute-start.17 = (bf16[432,640]{1,0:T(8,128)(2,1)S(1)}, bf16[432,640]{1,0:T(8,128)(2,1)S(1)}, u32[]{:S(2)}, u32[]{:S(2)}) collective-permute-start(bf16[432,640]{1,0:T(8,128)(2,1)S(1)} %pad_maximum_fusion.2.pack_ref), channel_id=1, source_target_pairs={{1,0},{2,1},{3,2},{4,3},{5,4},{6,5},{7,6},{8,7},{9,8},{10,9},{11,1... | collective-permute-start | bytes 1658888 | tf_op jit(solution)/shard_map/ppermute | solution.py:357
  142.1 14.7 %collective-permute-start.16 = (bf16[432,640]{1,0:T(8,128)(2,1)S(1)}, bf16[432,640]{1,0:T(8,128)(2,1)S(1)}, u32[]{:S(2)}, u32[]{:S(2)}) collective-permute-start(bf16[432,640]{1,0:T(8,128)(2,1)S(1)} %pad_maximum_fusion.2.pack_ref), channel_id=1, source_target_pairs={{0,1},{1,2},{2,3},{3,4},{4,5},{5,6},{6,7},{7,8},{8,9},{9,10},{10,1... | collective-permute-start | bytes 1658888 | tf_op jit(solution)/shard_map/ppermute | solution.py:357

commit v5 on v4

--- a/solution.py
+++ b/solution.py
@@ -80,68 +80,68 @@
     )
 
 
-def collect(blocks, first, rows, w_ref, sems):
-    copies = [
-        pltpu.make_async_copy(src.at[pl.ds(first, rows)], w_ref.at[pl.ds(rows * i, rows)], sems.at[i])
-        for i, src in enumerate(blocks)
-    ]
-    for c in copies:
-        c.start()
-    return copies
-
-
-def table_kernel(blocks_ref, hw_any, hc_any, he_any, out_ref):
-    for i in range(30):
-        out_ref[i] = blocks_ref[i]
+def collect(blocks, first, rows, w_ref):
+    for i, block in enumerate(blocks):
+        w_ref[rows * i : rows * (i + 1), :] = block[first : first + rows, :]
+
+
+def position(slot_t, slot_r):
+    turned = 2 - slot_r
+    return (slot_r if slot_t == 1 else turned, slot_t), (turned if slot_t == 1 else slot_r, 2 - slot_t)
+
+
+def project_kernel(
+    place_ref, hw_ref, hc_ref, he_ref, b0, b1, b2, b3, b4, b5, b6, b7, win_ref, wn_ref, wo_ref, w_ref
+):
+    collect((b0, b1, b2, b3, b4, b5, b6, b7), 144, 48, wo_ref)
+    collect((b0, b1, b2, b3, b4, b5, b6, b7), 0, 144, w_ref)
+    for g, h_ref in enumerate((hw_ref, hc_ref, he_ref)):
+        for part in range(3):
+            s = slice(part * T, (part + 1) * T)
+            win_ref[(g * 3 + part) * T : (g * 3 + part + 1) * T, :] = nn(h_ref[s, :], w_ref[...]).astype(BF)
+    lane_of = lax.broadcasted_iota(jnp.int32, (640, 384), 0)
+    whole, lower, upper = (
+        jnp.where(lane_of == place_ref[i : i + 1, :], 1.0, 0.0).astype(BF) for i in range(3)
+    )
+    halves = wo_ref[:, D:QKV]
+    wn_ref[...] = (
+        nn(whole, wo_ref[:, 0:D]) + jnp.concatenate([nn(lower, halves), nn(upper, halves)], axis=1)
+    ).astype(BF)
 
 
 def forward_kernel(
-    blocks_ref, hw_any, hc_any, he_any, place_ref, wpix_ref, x_ref, meas_ref, filt_ref,
-    b0, b1, b2, b3, b4, b5, b6, b7,
-    win_ref, e_ref, den_ref, og_ref, pack_ref, stat_ref,
-    wo_ref, w_ref, wn_ref, h_ref, bias_ref, acc_ref, sems_o, sems, sems_h,
+    blocks_ref, win_ref, wn_ref, wpix_ref, x_ref, meas_ref, filt_ref,
+    e_ref, den_ref, og_ref, pack_ref, stat_ref,
+    bias_ref, acc_ref,
 ):
-    copies_o = collect((b0, b1, b2, b3, b4, b5, b6, b7), 144, 48, wo_ref, sems_o)
-    copies = collect((b0, b1, b2, b3, b4, b5, b6, b7), 0, 144, w_ref, sems)
-    copies += collect((hw_any, hc_any, he_any), 0, 3 * T, h_ref, sems_h)
     acc_ref[...] = jnp.zeros_like(acc_ref)
 
     qc = (lax.broadcasted_iota(jnp.int32, (T, T), 0) & 8) > 0
     kc = (lax.broadcasted_iota(jnp.int32, (T, T), 1) & 8) > 0
 
+    core = blocks_ref[30]
+
     def allowed(c, r, w):
-        return blocks_ref[(c * 3 + r) * 5 + w - c].astype(F32) if 0 <= w - c < 5 else jnp.float32(0.0)
+        there = jnp.logical_and(w - c >= 0, w - c < 5)
+        value = blocks_ref[(c * 3 + r) * 5 + jnp.clip(w - c, 0, 4)]
+        return jnp.where(there, value, 0).astype(F32)
 
     lane_c = (lax.broadcasted_iota(jnp.int32, (1, T), 1) & 8) > 0
     rows = []
     for r in range(3):
         for w in range(6):
-            rows.append(jnp.where(lane_c, allowed(1, r, w), allowed(0, r, w)))
-    for t in range(3):
-        for r in range(3):
+            rows.append(jnp.where(lane_c, allowed(1, r, jnp.int32(w)), allowed(0, r, jnp.int32(w))))
+    for slot_t in range(3):
+        for slot_r in range(3):
+            (r0, t0), (r1, t1) = position(slot_t, slot_r)
+            r, t = jnp.where(core == 0, r0, r1), jnp.where(core == 0, t0, t1)
             seen = jnp.where(
                 qc,
                 jnp.where(kc, allowed(1, r, 2 * t + 1), allowed(1, r, 2 * t)),
                 jnp.where(kc, allowed(0, r, 2 * t + 1), allowed(0, r, 2 * t)),
             )
-            j = 3 * t + r
+            j = 3 * slot_t + slot_r
             bias_ref[:, j * T : (j + 1) * T] = (1.0 - seen) * OFF
-    lane_of = lax.broadcasted_iota(jnp.int32, (640, 384), 0)
-    whole, lower, upper = (
-        jnp.where(lane_of == place_ref[i : i + 1, :], 1.0, 0.0).astype(BF) for i in range(3)
-    )
-    for c in copies_o:
-        c.wait()
-    halves = wo_ref[:, D:QKV]
-    wn_ref[...] = (
-        nn(whole, wo_ref[:, 0:D]) + jnp.concatenate([nn(lower, halves), nn(upper, halves)], axis=1)
-    ).astype(BF)
-    for c in copies:
-        c.wait()
-    for i in range(9):
-        s = slice(i * T, (i + 1) * T)
-        win_ref[s, :] = nn(h_ref[s, :], w_ref[...]).astype(BF)
-
     own = slice(4 * T, 5 * T)
     lanes = lax.broadcasted_iota(jnp.int32, (T, T), 1)
     stats = jnp.zeros((T, T), F32)
@@ -209,9 +209,10 @@
     gq_ref[...] = acc_ref[:, 0:HW].astype(BF)
 
 
-def key_side(win_ref, groups, gk_ref, gv_ref):
+def key_side(core_ref, win_ref, groups, gk_ref, gv_ref):
     own = slice(4 * T, 5 * T)
     kc = (lax.broadcasted_iota(jnp.int32, (T, T), 0) & 8) > 0
+    second = core_ref[0].astype(F32)
     for t, pack_ref in groups:
         bias, stats, ups = [], [], []
         for r in range(3):
@@ -221,8 +222,11 @@
             stats.append(extra[:, 0:128] + extra[:, 128:256] + extra[:, 256:384])
             seen = []
             for w in range(2):
-                i = (2 - r) * 6 + (2 - t) * 2 + w
-                seen.append(extra[i : i + 1, 384:512] if i < 16 else extra[i - 16 : i - 15, 512:640])
+                on = []
+                for row, col in position(t, r):
+                    i = (2 - row) * 6 + (2 - col) * 2 + w
+                    on.append(extra[i : i + 1, 384:512] if i < 16 else extra[i - 16 : i - 15, 512:640])
+                seen.append(on[0] * (1.0 - second) + on[1] * second)
             bias.append((1.0 - jnp.where(kc, seen[1], seen[0])) * OFF)
         bias = jnp.concatenate(bias, axis=1)
         stats = jnp.concatenate(stats, axis=1)
@@ -245,26 +249,24 @@
             gv_ref[:, c - VB : d - VB] += head_only(nn(p.astype(BF), up), V0 + HD * e, c)
 
 
-def key_centre_kernel(win_ref, pack_ref, gk_ref, gv_ref):
+def key_centre_kernel(core_ref, win_ref, pack_ref, gk_ref, gv_ref):
     gk_ref[...] = jnp.zeros_like(gk_ref)
     gv_ref[...] = jnp.zeros_like(gv_ref)
-    key_side(win_ref, ((1, pack_ref),), gk_ref, gv_ref)
+    key_side(core_ref, win_ref, ((1, pack_ref),), gk_ref, gv_ref)
 
 
 def finish_kernel(
-    win_ref, packw_ref, packe_ref, gk0_ref, gv0_ref, gq_ref, order_ref, x_ref, gain_ref, og_ref,
+    core_ref, win_ref, packo_ref, packi_ref, gk0_ref, gv0_ref, gq_ref, order_ref, x_ref, gain_ref, og_ref,
     b0, b1, b2, b3, b4, b5, b6, b7,
-    out_ref, gk_ref, gv_ref, w_ref, sems,
+    out_ref, gk_ref, gv_ref, w_ref,
 ):
-    copies = collect((b0, b1, b2, b3, b4, b5, b6, b7), 0, 144, w_ref, sems)
+    collect((b0, b1, b2, b3, b4, b5, b6, b7), 0, 144, w_ref)
     gk_ref[...] = gk0_ref[...]
     gv_ref[...] = gv0_ref[...]
-    key_side(win_ref, ((0, packw_ref), (2, packe_ref)), gk_ref, gv_ref)
+    key_side(core_ref, win_ref, ((0, packo_ref), (2, packi_ref)), gk_ref, gv_ref)
     gk = (gk_ref[:, 0:HW] * FACTOR).astype(BF)
     gv = gv_ref[:, 64:640].astype(BF)
     grads = jnp.concatenate([gk, gv, gq_ref[...]], axis=1)
-    for c in copies:
-        c.wait()
     moved = nt(grads, w_ref[...])
     high = moved.astype(BF)
     low = (moved - high.astype(F32)).astype(BF)
@@ -282,8 +284,9 @@
 
 
 def shards_held(yh, z, x, core, block, second):
-    xs = (x + jnp.asarray(np.array([0, 3, 1, 2] * 2)[block])) & 3
     cs = core ^ jnp.asarray((block >= 4).astype(np.int32))
+    shift = np.array([0, 3, 1, 2] * 2)[block]
+    xs = (x + jnp.where(cs == 0, jnp.asarray(shift), jnp.asarray(-shift))) & 3
     hops = jnp.where(second, 3 - xs, xs + 1)
     zs = (z + jnp.where(cs == 0, -hops, hops)) & 7
     other = jnp.logical_xor(second, (xs == 3) & (cs == 1)).astype(jnp.int32)
@@ -333,28 +336,31 @@
 
 def on_device(tokens, gain, w_query, w_key, w_value, w_out, w_pixel, measured, filter_color, block_mask):
     yh, z, xi, core = (lax.axis_index(n) for n in ("yh", "z", "x", "core"))
+    which = core.reshape(1).astype(jnp.int32)
     x = tokens.reshape(T, D)
     gain = gain.reshape(1, D)
-    south = [(i, i + 1) for i in range(15)]
+    south = [(2 * i, 2 * i + 2) for i in range(15)] + [(2 * i + 3, 2 * i + 1) for i in range(15)]
     north = [(j, i) for i, j in south]
-    east = [(i, (i + 1) % 32) for i in range(32)]
-    west = [(j, i) for i, j in east]
+    ring = [(2 * i, (2 * i + 2) % 8) for i in range(4)] + [((2 * i + 3) % 8, 2 * i + 1) for i in range(4)]
+    back = [(j, i) for i, j in ring]
+    border = [(2 * i + 1, (2 * i + 2) % 32) for i in range(16)]
+    border = border + [(j, i) for i, j in border]
     lat, lon = ("yh", "z"), ("yl", "x", "core")
     first, second = fetch_routes()
 
     def swap(v):
         return lax.ppermute(v, "core", [(0, 1), (1, 0)])
 
-    def along(v, shift):
-        return lax.ppermute(v, "x", [(i, (i + shift) % 4) for i in range(4)])
+    def along(v, perm):
+        return lax.ppermute(v, ("x", "core"), perm)
 
     def columns(own):
-        before = lax.ppermute(own, lat, south)
-        after = lax.ppermute(own, lat, north)
+        before = lax.ppermute(own, lat + ("core",), south)
+        after = lax.ppermute(own, lat + ("core",), north)
         return jnp.concatenate([before, own, after], axis=0)
 
     def sides(column):
-        return lax.ppermute(column, lon, east), lax.ppermute(column, lon, west)
+        return lax.ppermute(column, lon, border), swap(column)
 
     mine = pl.pallas_call(
         gather_kernel, out_shape=shaped((96, QKV)), in_specs=[HBM] * 4, out_specs=VMEM,
@@ -364,7 +370,7 @@
     one, two = lax.ppermute(mine, lat + lon, first), lax.ppermute(mine, lat + lon, second)
     fetched = jnp.concatenate([one[:72], two[:72], one[72:], two[72:]], axis=0)
     column = columns(x)
-    from_west, from_east = sides(column)
+    outer, inner = sides(column)
     target = weight_targets(yh, z, xi, core)
 
     def ordering(target):
@@ -383,36 +389,31 @@
         )(v, gain, order)
 
     fetched, hc = lax.optimization_barrier((fetched, hidden(column)))
-    right, left = along(fetched, 1), along(fetched, 3)
-    right, left, hw, he = lax.optimization_barrier((right, left, hidden(from_west), hidden(from_east)))
-    across = jnp.concatenate([along(right[:96], 1), along(left[96:], 3)], axis=0)
-    held = (fetched, right, left, across)
-    blocks = held + tuple(swap(v) for v in held)
-
-    table = pl.pallas_call(
-        table_kernel, out_shape=shaped((30,), jnp.int32), in_specs=[SMEM] + [ANY] * 3, out_specs=SMEM,
-        compiler_params=params(4),
-        cost_estimate=pl.CostEstimate(flops=2_000_000_000, bytes_accessed=3_000_000, transcendentals=0),
-    )(block_mask.reshape(30), hw, hc, he)
-    win, e, den, og, pack, stat = pl.pallas_call(
+    right, left = along(fetched, ring), along(fetched, back)
+    fetched_too = swap(fetched)
+    right, left, hw, he, fetched_too = lax.optimization_barrier(
+        (right, left, hidden(outer), hidden(inner), fetched_too)
+    )
+    across = jnp.concatenate([along(right[:96], ring), along(left[96:], back)], axis=0)
+    blocks = (fetched, right, left, across, fetched_too, swap(right), swap(left), swap(across))
+
+    win, wn = pl.pallas_call(
+        project_kernel, out_shape=(shaped((9 * T, QKV)), shaped((640, D))),
+        in_specs=[VMEM] * 12, out_specs=(VMEM,) * 2,
+        scratch_shapes=[pltpu.VMEM((384, QKV), BF), pltpu.VMEM((D, QKV), BF)],
+        compiler_params=params(24),
+        cost_estimate=pl.CostEstimate(flops=6_000_000_000, bytes_accessed=8_000_000, transcendentals=0),
+    )(out_targets(yh, z, xi, core), hw, hc, he, *blocks)
+    e, den, og, pack, stat = pl.pallas_call(
         forward_kernel,
         out_shape=(
-            shaped((9 * T, QKV)), shaped((H * T, 9 * T)), shaped((T, D)), shaped((T, D), F32), shaped((144, 640)),
-            shaped((T, T), F32),
+            shaped((H * T, 9 * T)), shaped((T, D)), shaped((T, D), F32), shaped((144, 640)), shaped((T, T), F32),
         ),
-        in_specs=[SMEM] + [HBM] * 3 + [VMEM] * 5 + [ANY] * 8,
-        out_specs=(VMEM,) * 6,
-        scratch_shapes=[
-            pltpu.VMEM((384, QKV), BF), pltpu.VMEM((D, QKV), BF), pltpu.VMEM((640, D), BF),
-            pltpu.VMEM((9 * T, D), BF), pltpu.VMEM((T, 9 * T), F32), pltpu.VMEM((T, 640), F32),
-            pltpu.SemaphoreType.DMA((8,)), pltpu.SemaphoreType.DMA((8,)), pltpu.SemaphoreType.DMA((3,)),
-        ],
-        compiler_params=params(22),
-        cost_estimate=pl.CostEstimate(flops=12_000_000_000, bytes_accessed=8_000_000, transcendentals=1_000_000),
-    )(
-        table, hw, hc, he, out_targets(yh, z, xi, core), w_pixel.T, x, measured.reshape(T, 64),
-        filter_color.reshape(T, 64), *blocks,
-    )
+        in_specs=[SMEM] + [VMEM] * 6, out_specs=(VMEM,) * 5,
+        scratch_shapes=[pltpu.VMEM((T, 9 * T), F32), pltpu.VMEM((T, 640), F32)],
+        compiler_params=params(18),
+        cost_estimate=pl.CostEstimate(flops=6_000_000_000, bytes_accessed=8_000_000, transcendentals=1_000_000),
+    )(jnp.concatenate([block_mask.reshape(30), which]), win, wn, w_pixel.T, x, measured.reshape(T, 64), filter_color.reshape(T, 64))
     packs = columns(pack)
     gq = pl.pallas_call(
         query_kernel, out_shape=shaped((T, HW)), in_specs=[VMEM] * 4, out_specs=VMEM,
@@ -420,17 +421,17 @@
         cost_estimate=pl.CostEstimate(flops=4_000_000_000, bytes_accessed=6_000_000, transcendentals=0),
     )(win, e, pack, stat)
     packs, gq, target = lax.optimization_barrier((packs, gq, target))
-    packs_west, packs_east = sides(packs)
+    packs_outer, packs_inner = sides(packs)
     gk, gv = pl.pallas_call(
-        key_centre_kernel, out_shape=(shaped((T, 640), F32),) * 2, in_specs=[VMEM] * 2, out_specs=(VMEM,) * 2,
+        key_centre_kernel, out_shape=(shaped((T, 640), F32),) * 2, in_specs=[SMEM] + [VMEM] * 2, out_specs=(VMEM,) * 2,
         compiler_params=params(16),
         cost_estimate=pl.CostEstimate(flops=4_000_000_000, bytes_accessed=6_000_000, transcendentals=0),
-    )(win, packs)
+    )(which, win, packs)
     guidance = pl.pallas_call(
-        finish_kernel, out_shape=shaped((T, D), F32), in_specs=[VMEM] * 10 + [ANY] * 8, out_specs=VMEM,
-        scratch_shapes=[pltpu.VMEM((T, 640), F32)] * 2 + [pltpu.VMEM((D, QKV), BF), pltpu.SemaphoreType.DMA((8,))],
+        finish_kernel, out_shape=shaped((T, D), F32), in_specs=[SMEM] + [VMEM] * 18, out_specs=VMEM,
+        scratch_shapes=[pltpu.VMEM((T, 640), F32)] * 2 + [pltpu.VMEM((D, QKV), BF)],
         compiler_params=params(20),
-    )(win, packs_west, packs_east, gk, gv, gq, ordering(target), x, gain, og, *blocks)
+    )(which, win, packs_outer, packs_inner, gk, gv, gq, ordering(target), x, gain, og, *blocks)
     return den.reshape(tokens.shape), guidance.reshape(tokens.shape)
 
 

time: 168 us -> 149 us (0.89)
  the two profiles are of different devices: /device:TPU:32 before, /device:TPU:47 now
where the time goes in v5:
time: 149 us; the launch traced here: 148 us
  starting transfers between devices  75.7 us (51%)
  Pallas kernels  31.9 us (21%)
  waiting for transfers between devices  27.8 us (19%)
  local copies, waits for them, and re-layouts  9.76 us (7%)
    ppermute x6, starting transfers between devices, swap(): return lax.ppermute(v, 'core', [(0, 1), (1, 0)])  29.4 us
    ppermute x2, starting transfers between devices, columns(): before = lax.ppermute(own, lat + ('core',), south)  18.6 us
    ppermute x4, waiting for transfers between devices, along(): return lax.ppermute(v, ('x', 'core'), perm)  13.2 us
    ppermute x4, starting transfers between devices, along(): return lax.ppermute(v, ('x', 'core'), perm)  11.8 us
    ppermute x2, waiting for transfers between devices, sides(): return (lax.ppermute(column, lon, border), swap(column))  9.45 us
    unnamed x58, local copies, waits for them, and re-layouts  8.07 us
    pallas_call x1, Pallas kernels, on_device(): pl.pallas_call(project_kernel, out_shape=(shaped((9 * T, QKV)), shaped((6...  7.37 us
    pallas_call x1, Pallas kernels, on_device(): pl.pallas_call(finish_kernel, out_shape=shaped((T, D), F32), in_specs=[SM...  7.04 us
  transfers between devices with their start and end apart: 18, of which 7 were waited for; matrix products, arithmetic and copies ran while one was open for 1% of the time, Pallas kernels for 8%

profile of v5, /device:TPU:47, one launch (start us, length us, event | category | flops | bytes accessed | tf_op | source)
XLA Modules:
  0.0 147.8 jit_solution(17413657438593993158)
XLA Ops:
  0.7 4.1 %collective-permute-start.3 = (bf16[128,1152]{1,0:T(8,128)(2,1)}, bf16[128,1152]{1,0:T(8,128)(2,1)S(1)}, u32[]{:S(2)}, u32[]{:S(2)}) collective-permute-start(bf16[128,1152]{1,0:T(8,128)(2,1)} %bitcast.7), channel_id=1, source_target_pairs={{32,0},{64,32},{96,64},{128,96},{160,128},{192,160},{224,192},{256... | collective-permute-start | bytes 884744 | tf_op jit(solution)/shard_map/ppermute | solution.py:359
  4.8 9.0 %collective-permute-start.2 = (bf16[128,1152]{1,0:T(8,128)(2,1)}, bf16[128,1152]{1,0:T(8,128)(2,1)S(1)}, u32[]{:S(2)}, u32[]{:S(2)}) collective-permute-start(bf16[128,1152]{1,0:T(8,128)(2,1)} %bitcast.8), channel_id=1, source_target_pairs={{0,32},{32,64},{64,96},{96,128},{128,160},{160,192},{192,224},{224... | collective-permute-start | bytes 884744 | tf_op jit(solution)/shard_map/ppermute | solution.py:358
  13.9 0.9 copy-done.1
  14.7 0.9 copy-done.2
  15.6 0.9 copy-done.3
  16.5 0.9 copy-done.4
  17.4 0.6 shard_map.221
  18.0 0.7 collective-permute-start.1
  18.7 4.7 %collective-permute-start = (bf16[96,1728]{1,0:T(8,128)(2,1)S(1)}, bf16[96,1728]{1,0:T(8,128)(2,1)S(1)}, u32[]{:S(2)}, u32[]{:S(2)}) collective-permute-start(bf16[96,1728]{1,0:T(8,128)(2,1)S(1)} %shard_map.221), channel_id=1, source_target_pairs={{224,0},{33,1},{194,2},{67,3},{164,4},{101,5},{134,6},{415,7},{232... | collective-permute-start | bytes 995336 | tf_op jit(solution)/shard_map/ppermute | solution.py:370
  23.4 3.9 %collective-permute-done.2 = bf16[128,1152]{1,0:T(8,128)(2,1)S(1)} collective-permute-done((bf16[128,1152]{1,0:T(8,128)(2,1)}, bf16[128,1152]{1,0:T(8,128)(2,1)S(1)}, u32[]{:S(2)}, u32[]{:S(2)}) %collective-permute-start.2) | collective-permute-done | bytes 294944 | tf_op jit(solution)/shard_map/ppermute | solution.py:358
  27.3 1.0 pad_maximum_fusion.x_ref
  28.3 8.6 %collective-permute-start.7 = (bf16[384,1152]{1,0:T(8,128)(2,1)S(1)}, bf16[384,1152]{1,0:T(8,128)(2,1)S(1)}, u32[]{:S(2)}, u32[]{:S(2)}) collective-permute-start(bf16[384,1152]{1,0:T(8,128)(2,1)S(1)} %pad_maximum_fusion.x_ref), channel_id=1, source_target_pairs={{0,1},{1,0},{2,3},{3,2},{4,5},{5,4},{6,7},{7,6},{8,9},{9,8},{10,11... | collective-permute-start | bytes 2654216 | tf_op jit(solution)/shard_map/ppermute | solution.py:352
  37.0 0.5 shard_map.222.order_ref
  37.5 0.2 copy-done.14
  37.7 1.9 %collective-permute-start.6 = (bf16[384,1152]{1,0:T(8,128)(2,1)S(1)}, bf16[384,1152]{1,0:T(8,128)(2,1)S(1)}, u32[]{:S(2)}, u32[]{:S(2)}) collective-permute-start(bf16[384,1152]{1,0:T(8,128)(2,1)S(1)} %pad_maximum_fusion.x_ref), channel_id=1, source_target_pairs={{1,2},{3,4},{5,6},{7,8},{9,10},{11,12},{13,14},{15,16},{17,18},{19... | collective-permute-start | bytes 2654216 | tf_op jit(solution)/shard_map/ppermute | solution.py:363
  39.6 1.8 %shard_map.223.hc_ref = bf16[384,1152]{1,0:T(8,128)(2,1)S(1)} custom-call(bf16[384,1152]{1,0:T(8,128)(2,1)S(1)} %pad_maximum_fusion.x_ref, f32[1,1152]{1,0:T(1,128)S(1)} %reshape.34.gain_ref, bf16[1152,1152]{1,0:T(8,128)(2,1)S(1)} %shard_map.222.order_ref), custom_call_target="tpu_custom_call" | custom-call | flops 3000000000 | bytes 5000000 | tf_op jit(solution)/shard_map/pallas_call | solution.py:385
  41.4 0.9 copy-done.8
  42.5 2.9 %collective-permute-start.8 = (bf16[192,1728]{1,0:T(8,128)(2,1)S(1)}, bf16[192,1728]{1,0:T(8,128)(2,1)S(1)}, u32[]{:S(2)}, u32[]{:S(2)}) collective-permute-start(bf16[192,1728]{1,0:T(8,128)(2,1)S(1)} %pad_maximum_fusion.1.b0), channel_id=1, source_target_pairs={{0,1},{1,0},{2,3},{3,2},{4,5},{5,4},{6,7},{7,6},{8,9},{9,8},{10,11... | collective-permute-start | bytes 1990664 | tf_op jit(solution)/shard_map/ppermute | solution.py:352
  45.4 1.9 %collective-permute-start.5 = (bf16[192,1728]{1,0:T(8,128)(2,1)S(1)}, bf16[192,1728]{1,0:T(8,128)(2,1)S(1)}, u32[]{:S(2)}, u32[]{:S(2)}) collective-permute-start(bf16[192,1728]{1,0:T(8,128)(2,1)S(1)} %pad_maximum_fusion.1.b0), channel_id=1, source_target_pairs={{2,0},{4,2},{6,4},{0,6},{1,3},{3,5},{5,7},{7,1},{10,8},{12,10},{14... | collective-permute-start | bytes 1990664 | tf_op jit(solution)/shard_map/ppermute | solution.py:355
  47.3 3.4 %collective-permute-start.4 = (bf16[192,1728]{1,0:T(8,128)(2,1)S(1)}, bf16[192,1728]{1,0:T(8,128)(2,1)S(1)}, u32[]{:S(2)}, u32[]{:S(2)}) collective-permute-start(bf16[192,1728]{1,0:T(8,128)(2,1)S(1)} %pad_maximum_fusion.1.b0), channel_id=1, source_target_pairs={{0,2},{2,4},{4,6},{6,0},{3,1},{5,3},{7,5},{1,7},{8,10},{10,12},{12... | collective-permute-start | bytes 1990664 | tf_op jit(solution)/shard_map/ppermute | solution.py:355
  50.7 1.8 %shard_map.225.he_ref = bf16[384,1152]{1,0:T(8,128)(2,1)S(1)} custom-call(bf16[384,1152]{1,0:T(8,128)(2,1)S(1)} %collective-permute-done.7.x_ref, f32[1,1152]{1,0:T(1,128)S(1)} %reshape.34.gain_ref, bf16[1152,1152]{1,0:T(8,128)(2,1)S(1)} %shard_map.222.order_ref), custom_call_target="tpu_custom_call" | custom-call | flops 3000000000 | bytes 5000000 | tf_op jit(solution)/shard_map/pallas_call | solution.py:385
  52.5 1.8 %collective-permute-done.6.x_ref = bf16[384,1152]{1,0:T(8,128)(2,1)S(1)} collective-permute-done((bf16[384,1152]{1,0:T(8,128)(2,1)S(1)}, bf16[384,1152]{1,0:T(8,128)(2,1)S(1)}, u32[]{:S(2)}, u32[]{:S(2)}) %collective-permute-start.6) | collective-permute-done | bytes 884768 | tf_op jit(solution)/shard_map/ppermute | solution.py:363
  54.3 1.8 %shard_map.224.hw_ref = bf16[384,1152]{1,0:T(8,128)(2,1)S(1)} custom-call(bf16[384,1152]{1,0:T(8,128)(2,1)S(1)} %collective-permute-done.6.x_ref, f32[1,1152]{1,0:T(1,128)S(1)} %reshape.34.gain_ref, bf16[1152,1152]{1,0:T(8,128)(2,1)S(1)} %shard_map.222.order_ref), custom_call_target="tpu_custom_call" | custom-call | flops 3000000000 | bytes 5000000 | tf_op jit(solution)/shard_map/pallas_call | solution.py:385
  56.1 0.9 copy-done.12
  57.1 7.4 %collective-permute-done.5.b2 = bf16[192,1728]{1,0:T(8,128)(2,1)S(1)} collective-permute-done((bf16[192,1728]{1,0:T(8,128)(2,1)S(1)}, bf16[192,1728]{1,0:T(8,128)(2,1)S(1)}, u32[]{:S(2)}, u32[]{:S(2)}) %collective-permute-start.5) | collective-permute-done | bytes 663584 | tf_op jit(solution)/shard_map/ppermute | solution.py:355
  64.5 4.6 %collective-permute-done.4.b1 = bf16[192,1728]{1,0:T(8,128)(2,1)S(1)} collective-permute-done((bf16[192,1728]{1,0:T(8,128)(2,1)S(1)}, bf16[192,1728]{1,0:T(8,128)(2,1)S(1)}, u32[]{:S(2)}, u32[]{:S(2)}) %collective-permute-start.4) | collective-permute-done | bytes 663584 | tf_op jit(solution)/shard_map/ppermute | solution.py:355
  69.1 0.8 slice.22
  69.8 1.9 %collective-permute-start.9 = (bf16[96,1728]{1,0:T(8,128)(2,1)}, bf16[96,1728]{1,0:T(8,128)(2,1)S(1)}, u32[]{:S(2)}, u32[]{:S(2)}) collective-permute-start(bf16[96,1728]{1,0:T(8,128)(2,1)} %slice.22), channel_id=1, source_target_pairs={{0,2},{2,4},{4,6},{6,0},{3,1},{5,3},{7,5},{1,7},{8,10},{10,12},{12... | collective-permute-start | bytes 995336 | tf_op jit(solution)/shard_map/ppermute | solution.py:355
  71.8 0.8 slice.23
  72.5 4.6 %collective-permute-start.10 = (bf16[96,1728]{1,0:T(8,128)(2,1)}, bf16[96,1728]{1,0:T(8,128)(2,1)S(1)}, u32[]{:S(2)}, u32[]{:S(2)}) collective-permute-start(bf16[96,1728]{1,0:T(8,128)(2,1)} %slice.23), channel_id=1, source_target_pairs={{2,0},{4,2},{6,4},{0,6},{1,3},{3,5},{5,7},{7,1},{10,8},{12,10},{14... | collective-permute-start | bytes 995336 | tf_op jit(solution)/shard_map/ppermute | solution.py:355
  77.2 2.0 %collective-permute-start.11 = (bf16[192,1728]{1,0:T(8,128)(2,1)S(1)}, bf16[192,1728]{1,0:T(8,128)(2,1)S(1)}, u32[]{:S(2)}, u32[]{:S(2)}) collective-permute-start(bf16[192,1728]{1,0:T(8,128)(2,1)S(1)} %collective-permute-done.4.b1), channel_id=1, source_target_pairs={{0,1},{1,0},{2,3},{3,2},{4,5},{5,4},{6,7},{7,6},{8,9},{9,8},{10,11... | collective-permute-start | bytes 1990664 | tf_op jit(solution)/shard_map/ppermute | solution.py:352
  79.3 2.4 %collective-permute-start.12 = (bf16[192,1728]{1,0:T(8,128)(2,1)S(1)}, bf16[192,1728]{1,0:T(8,128)(2,1)S(1)}, u32[]{:S(2)}, u32[]{:S(2)}) collective-permute-start(bf16[192,1728]{1,0:T(8,128)(2,1)S(1)} %collective-permute-done.5.b2), channel_id=1, source_target_pairs={{0,1},{1,0},{2,3},{3,2},{4,5},{5,4},{6,7},{7,6},{8,9},{9,8},{10,11... | collective-permute-start | bytes 1990664 | tf_op jit(solution)/shard_map/ppermute | solution.py:352
  81.7 1.2 collective-permute-done.10
  82.9 2.8 %collective-permute-start.13 = (bf16[192,1728]{1,0:T(8,128)(2,1)S(1)}, bf16[192,1728]{1,0:T(8,128)(2,1)S(1)}, u32[]{:S(2)}, u32[]{:S(2)}) collective-permute-start(bf16[192,1728]{1,0:T(8,128)(2,1)S(1)} %constant_dynamic-update-slice_fusion.b3), channel_id=1, source_target_pairs={{0,1},{1,0},{2,3},{3,2},{4,5},{5,4},{6,7},{7,6},{8,9},{9,8},{10,11... | collective-permute-start | bytes 1990664 | tf_op jit(solution)/shard_map/ppermute | solution.py:352
  86.1 1.3 collective-permute-done.13.b7
  87.3 1.2 copy-done.11
  88.5 1.2 copy-done.13
  89.7 7.4 %shard_map.226 = (bf16[1152,1728]{1,0:T(8,128)(2,1)S(1)}, bf16[640,1152]{1,0:T(8,128)(2,1)S(1)}) custom-call(s32[3,384]{1,0:T(4,128)S(1)} %pad_add_fusion.place_ref, bf16[384,1152]{1,0:T(8,128)(2,1)S(1)} %copy-done.13, bf16[384,1152]{1,0:T(8,128)(2,1)S(1)} %copy-done.9, bf16[384,1152]{1,0:T(8,128)(2,1)S(1)} %copy-done.11, ...), custom_call_target="tpu_custom_call" | custom-call | flops 6000000000 | bytes 8000000 | tf_op jit(solution)/shard_map/pallas_call | solution.py:400
  97.1 6.1 %shard_map.227 = (bf16[1024,1152]{1,0:T(8,128)(2,1)S(1)}, bf16[128,1152]{1,0:T(8,128)(2,1)}, f32[128,1152]{1,0:T(8,128)S(1)}, bf16[144,640]{1,0:T(8,128)(2,1)S(1)}, f32[128,128]{1,0:T(8,128)S(1)}) custom-call(s32[31]{0:T(128)S(1)} %pad_add_fusion.1.blocks_ref, bf16[1152,1728]{1,0:T(8,128)(2,1)S(1)} %get-tuple-element.28.win_ref, ...), custom_call_target="tpu_custom_call" | custom-call | flops 6000000000 | bytes 8000000 | tf_op jit(solution)/shard_map/pallas_call | solution.py:407
  103.1 1.9 %collective-permute-start.15 = (bf16[144,640]{1,0:T(8,128)(2,1)S(1)}, bf16[144,640]{1,0:T(8,128)(2,1)S(1)}, u32[]{:S(2)}, u32[]{:S(2)}) collective-permute-start(bf16[144,640]{1,0:T(8,128)(2,1)S(1)} %get-tuple-element.31.up_ref), channel_id=1, source_target_pairs={{32,0},{64,32},{96,64},{128,96},{160,128},{192,160},{224,192},{256... | collective-permute-start | bytes 552968 | tf_op jit(solution)/shard_map/ppermute | solution.py:359
  105.1 9.6 %collective-permute-start.14 = (bf16[144,640]{1,0:T(8,128)(2,1)S(1)}, bf16[144,640]{1,0:T(8,128)(2,1)S(1)}, u32[]{:S(2)}, u32[]{:S(2)}) collective-permute-start(bf16[144,640]{1,0:T(8,128)(2,1)S(1)} %get-tuple-element.31.up_ref), channel_id=1, source_target_pairs={{0,32},{32,64},{64,96},{96,128},{128,160},{160,192},{192,224},{224... | collective-permute-start | bytes 552968 | tf_op jit(solution)/shard_map/ppermute | solution.py:358
  114.7 2.4 %shard_map.228.gq_ref = bf16[128,576]{1,0:T(8,128)(2,1)S(1)} custom-call(bf16[1152,1728]{1,0:T(8,128)(2,1)S(1)} %get-tuple-element.28.win_ref, bf16[1024,1152]{1,0:T(8,128)(2,1)S(1)} %get-tuple-element.32.e_ref, bf16[144,640]{1,0:T(8,128)(2,1)S(1)} %get-tuple-element.31.up_ref, f32[128,128]{1,0:T(8,128)S(1)} %get-tuple-element.33.stat_ref), custom_call_target="tpu_custom_call" | custom-call | flops 4000000000 | bytes 6000000 | tf_op jit(solution)/shard_map/pallas_call | solution.py:418
  117.2 10.7 %collective-permute-start.17 = (bf16[432,640]{1,0:T(8,128)(2,1)S(1)}, bf16[432,640]{1,0:T(8,128)(2,1)S(1)}, u32[]{:S(2)}, u32[]{:S(2)}) collective-permute-start(bf16[432,640]{1,0:T(8,128)(2,1)S(1)} %pad_maximum_fusion.2.pack_ref), channel_id=1, source_target_pairs={{0,1},{1,0},{2,3},{3,2},{4,5},{5,4},{6,7},{7,6},{8,9},{9,8},{10,11... | collective-permute-start | bytes 1658888 | tf_op jit(solution)/shard_map/ppermute | solution.py:352
  127.9 2.7 %collective-permute-start.16 = (bf16[432,640]{1,0:T(8,128)(2,1)S(1)}, bf16[432,640]{1,0:T(8,128)(2,1)S(1)}, u32[]{:S(2)}, u32[]{:S(2)}) collective-permute-start(bf16[432,640]{1,0:T(8,128)(2,1)S(1)} %pad_maximum_fusion.2.pack_ref), channel_id=1, source_target_pairs={{1,2},{3,4},{5,6},{7,8},{9,10},{11,12},{13,14},{15,16},{17,18},{19... | collective-permute-start | bytes 1658888 | tf_op jit(solution)/shard_map/ppermute | solution.py:363
  130.5 0.5 shard_map.230.order_ref
  131.0 2.1 %shard_map.229 = (f32[128,640]{1,0:T(8,128)S(1)}, f32[128,640]{1,0:T(8,128)S(1)}) custom-call(s32[1]{0:T(128)} %bitcast.core_ref, bf16[1152,1728]{1,0:T(8,128)(2,1)S(1)} %get-tuple-element.28.win_ref, bf16[432,640]{1,0:T(8,128)(2,1)S(1)} %pad_maximum_fusion.2.pack_ref), custom_call_target="tpu_custom_call" | custom-call | flops 4000000000 | bytes 6000000 | tf_op jit(solution)/shard_map/pallas_call | solution.py:425
  133.1 7.7 %collective-permute-done.16.packo_ref = bf16[432,640]{1,0:T(8,128)(2,1)S(1)} collective-permute-done((bf16[432,640]{1,0:T(8,128)(2,1)S(1)}, bf16[432,640]{1,0:T(8,128)(2,1)S(1)}, u32[]{:S(2)}, u32[]{:S(2)}) %collective-permute-start.16) | collective-permute-done | bytes 552992 | tf_op jit(solution)/shard_map/ppermute | solution.py:363
  140.8 7.0 %shard_map.231 = f32[128,1152]{1,0:T(8,128)} custom-call(s32[1]{0:T(128)} %bitcast.core_ref, bf16[1152,1728]{1,0:T(8,128)(2,1)S(1)} %get-tuple-element.28.win_ref, bf16[432,640]{1,0:T(8,128)(2,1)S(1)} %collective-permute-done.16.packo_ref, bf16[432,640]{1,0:T(8,128)(2,1)S(1)} %collective-permute-done.17.packi_ref, f32[128,640]{1,0:T(8,128)S(1)} %get-tuple-element.35.gk0_ref, ...), custom_call_target="tpu_custom_call" | custom-call | tf_op jit(solution)/shard_map/pallas_call | solution.py:430
  (78 shorter events, 0.6 us)
Async XLA Ops:
  0.6 36.3 %copy-start.15 = (s32[1152]{0:T(1024)S(1)}, s32[1152]{0:T(1024)}, u32[]{:S(2)}) copy-start(s32[1152]{0:T(1024)} %constant.75.clone) | copy-start | bytes 13828
  0.6 36.3 %copy-start.21 = (pred[1152]{0:T(1024)(128)(4,1)S(1)}, pred[1152]{0:T(1024)(128)(4,1)}, u32[]{:S(2)}) copy-start(pred[1152]{0:T(1024)(128)(4,1)} %constant.74.clone) | copy-start | bytes 3460
  0.7 36.3 %copy-start.16 = (s32[1152]{0:T(1024)S(1)}, s32[1152]{0:T(1024)}, u32[]{:S(2)}) copy-start(s32[1152]{0:T(1024)} %constant.73.clone) | copy-start | bytes 13828
  0.7 22.7 %collective-permute-start.3 = (bf16[128,1152]{1,0:T(8,128)(2,1)}, bf16[128,1152]{1,0:T(8,128)(2,1)S(1)}, u32[]{:S(2)}, u32[]{:S(2)}) collective-permute-start(bf16[128,1152]{1,0:T(8,128)(2,1)} %bitcast.7), channel_id=1, source_target_pairs={{32,0},{64,32},{96,64},{128,96},{160,128},{192,160},{224,192},{256... | collective-permute-start | bytes 884744 | tf_op jit(solution)/shard_map/ppermute | solution.py:359
  4.8 22.5 %collective-permute-start.2 = (bf16[128,1152]{1,0:T(8,128)(2,1)}, bf16[128,1152]{1,0:T(8,128)(2,1)S(1)}, u32[]{:S(2)}, u32[]{:S(2)}) collective-permute-start(bf16[128,1152]{1,0:T(8,128)(2,1)} %bitcast.8), channel_id=1, source_target_pairs={{0,32},{32,64},{64,96},{96,128},{128,160},{160,192},{192,224},{224... | collective-permute-start | bytes 884744 | tf_op jit(solution)/shard_map/ppermute | solution.py:358
  13.9 0.9 copy-start.1
  14.7 0.9 copy-start.2
  15.6 0.9 copy-start.3
  16.5 0.9 copy-start.4
  17.4 19.5 %copy-start.17 = (s32[1152]{0:T(1024)S(1)}, s32[1152]{0:T(1024)}, u32[]{:S(2)}) copy-start(s32[1152]{0:T(1024)} %constant.72.clone) | copy-start | bytes 13828
  17.4 19.5 %copy-start.18 = (s32[1152]{0:T(1024)S(1)}, s32[1152]{0:T(1024)}, u32[]{:S(2)}) copy-start(s32[1152]{0:T(1024)} %constant.71.clone) | copy-start | bytes 13828
  18.0 24.3 %collective-permute-start.1 = (bf16[96,1728]{1,0:T(8,128)(2,1)S(1)}, bf16[96,1728]{1,0:T(8,128)(2,1)S(1)}, u32[]{:S(2)}, u32[]{:S(2)}) collective-permute-start(bf16[96,1728]{1,0:T(8,128)(2,1)S(1)} %shard_map.221), channel_id=1, source_target_pairs={{440,0},{377,1},{474,2},{347,3},{508,4},{317,5},{286,6},{7,7},{432... | collective-permute-start | bytes 995336 | tf_op jit(solution)/shard_map/ppermute | solution.py:370
  18.7 23.7 %collective-permute-start = (bf16[96,1728]{1,0:T(8,128)(2,1)S(1)}, bf16[96,1728]{1,0:T(8,128)(2,1)S(1)}, u32[]{:S(2)}, u32[]{:S(2)}) collective-permute-start(bf16[96,1728]{1,0:T(8,128)(2,1)S(1)} %shard_map.221), channel_id=1, source_target_pairs={{224,0},{33,1},{194,2},{67,3},{164,4},{101,5},{134,6},{415,7},{232... | collective-permute-start | bytes 995336 | tf_op jit(solution)/shard_map/ppermute | solution.py:370
  28.3 22.3 %collective-permute-start.7 = (bf16[384,1152]{1,0:T(8,128)(2,1)S(1)}, bf16[384,1152]{1,0:T(8,128)(2,1)S(1)}, u32[]{:S(2)}, u32[]{:S(2)}) collective-permute-start(bf16[384,1152]{1,0:T(8,128)(2,1)S(1)} %pad_maximum_fusion.x_ref), channel_id=1, source_target_pairs={{0,1},{1,0},{2,3},{3,2},{4,5},{5,4},{6,7},{7,6},{8,9},{9,8},{10,11... | collective-permute-start | bytes 2654216 | tf_op jit(solution)/shard_map/ppermute | solution.py:352
  37.0 0.7 copy-start.14
  37.7 16.6 %collective-permute-start.6 = (bf16[384,1152]{1,0:T(8,128)(2,1)S(1)}, bf16[384,1152]{1,0:T(8,128)(2,1)S(1)}, u32[]{:S(2)}, u32[]{:S(2)}) collective-permute-start(bf16[384,1152]{1,0:T(8,128)(2,1)S(1)} %pad_maximum_fusion.x_ref), channel_id=1, source_target_pairs={{1,2},{3,4},{5,6},{7,8},{9,10},{11,12},{13,14},{15,16},{17,18},{19... | collective-permute-start | bytes 2654216 | tf_op jit(solution)/shard_map/ppermute | solution.py:363
  41.4 0.9 copy-start.8
  42.5 14.6 %collective-permute-start.8 = (bf16[192,1728]{1,0:T(8,128)(2,1)S(1)}, bf16[192,1728]{1,0:T(8,128)(2,1)S(1)}, u32[]{:S(2)}, u32[]{:S(2)}) collective-permute-start(bf16[192,1728]{1,0:T(8,128)(2,1)S(1)} %pad_maximum_fusion.1.b0), channel_id=1, source_target_pairs={{0,1},{1,0},{2,3},{3,2},{4,5},{5,4},{6,7},{7,6},{8,9},{9,8},{10,11... | collective-permute-start | bytes 1990664 | tf_op jit(solution)/shard_map/ppermute | solution.py:352
  45.4 19.1 %collective-permute-start.5 = (bf16[192,1728]{1,0:T(8,128)(2,1)S(1)}, bf16[192,1728]{1,0:T(8,128)(2,1)S(1)}, u32[]{:S(2)}, u32[]{:S(2)}) collective-permute-start(bf16[192,1728]{1,0:T(8,128)(2,1)S(1)} %pad_maximum_fusion.1.b0), channel_id=1, source_target_pairs={{2,0},{4,2},{6,4},{0,6},{1,3},{3,5},{5,7},{7,1},{10,8},{12,10},{14... | collective-permute-start | bytes 1990664 | tf_op jit(solution)/shard_map/ppermute | solution.py:355
  47.3 21.8 %collective-permute-start.4 = (bf16[192,1728]{1,0:T(8,128)(2,1)S(1)}, bf16[192,1728]{1,0:T(8,128)(2,1)S(1)}, u32[]{:S(2)}, u32[]{:S(2)}) collective-permute-start(bf16[192,1728]{1,0:T(8,128)(2,1)S(1)} %pad_maximum_fusion.1.b0), channel_id=1, source_target_pairs={{0,2},{2,4},{4,6},{6,0},{3,1},{5,3},{7,5},{1,7},{8,10},{10,12},{12... | collective-permute-start | bytes 1990664 | tf_op jit(solution)/shard_map/ppermute | solution.py:355
  52.5 3.6 %copy-start.10 = (bf16[384,1152]{1,0:T(8,128)(2,1)}, bf16[384,1152]{1,0:T(8,128)(2,1)S(1)}, u32[]{:S(2)}) copy-start(bf16[384,1152]{1,0:T(8,128)(2,1)S(1)} %shard_map.225.he_ref) | copy-start | bytes 2654212
  56.1 0.9 copy-start.12
  57.0 20.1 %copy-start.20 = (s32[1,2,3,5]{3,1,2,0:T(2,128)S(1)}, s32[1,2,3,5]{3,1,2,0:T(2,128)}, u32[]{:S(2)}) copy-start(s32[1,2,3,5]{3,1,2,0:T(2,128)} %param.31) | copy-start | bytes 364
  57.0 28.7 %copy-start.19 = (s32[384]{0:T(512)S(1)}, s32[384]{0:T(512)}, u32[]{:S(2)}) copy-start(s32[384]{0:T(512)} %constant.80.clone) | copy-start | bytes 4612
  57.0 28.8 %copy-start.22 = (s32[384]{0:T(512)S(1)}, s32[384]{0:T(512)}, u32[]{:S(2)}) copy-start(s32[384]{0:T(512)} %constant.78.clone) | copy-start | bytes 4612
  57.0 28.8 %copy-start.23 = (s32[384]{0:T(512)S(1)}, s32[384]{0:T(512)}, u32[]{:S(2)}) copy-start(s32[384]{0:T(512)} %constant.77.clone) | copy-start | bytes 4612
  57.0 28.8 %copy-start.24 = (s32[384]{0:T(512)S(1)}, s32[384]{0:T(512)}, u32[]{:S(2)}) copy-start(s32[384]{0:T(512)} %constant.76.clone) | copy-start | bytes 4612
  57.0 28.8 %copy-start.27 = (pred[384]{0:T(512)(128)(4,1)S(1)}, pred[384]{0:T(512)(128)(4,1)}, u32[]{:S(2)}) copy-start(pred[384]{0:T(512)(128)(4,1)} %constant.79.clone) | copy-start | bytes 1156
  57.0 28.8 %copy-start.25 = (pred[384]{0:T(512)(128)(4,1)S(1)}, pred[384]{0:T(512)(128)(4,1)}, u32[]{:S(2)}) copy-start(pred[384]{0:T(512)(128)(4,1)} %constant.82.clone) | copy-start | bytes 1156
  57.1 28.8 %copy-start.26 = (pred[384]{0:T(512)(128)(4,1)S(1)}, pred[384]{0:T(512)(128)(4,1)}, u32[]{:S(2)}) copy-start(pred[384]{0:T(512)(128)(4,1)} %constant.81.clone) | copy-start | bytes 1156
  69.8 11.8 %collective-permute-start.9 = (bf16[96,1728]{1,0:T(8,128)(2,1)}, bf16[96,1728]{1,0:T(8,128)(2,1)S(1)}, u32[]{:S(2)}, u32[]{:S(2)}) collective-permute-start(bf16[96,1728]{1,0:T(8,128)(2,1)} %slice.22), channel_id=1, source_target_pairs={{0,2},{2,4},{4,6},{6,0},{3,1},{5,3},{7,5},{1,7},{8,10},{10,12},{12... | collective-permute-start | bytes 995336 | tf_op jit(solution)/shard_map/ppermute | solution.py:355
  72.5 10.4 %collective-permute-start.10 = (bf16[96,1728]{1,0:T(8,128)(2,1)}, bf16[96,1728]{1,0:T(8,128)(2,1)S(1)}, u32[]{:S(2)}, u32[]{:S(2)}) collective-permute-start(bf16[96,1728]{1,0:T(8,128)(2,1)} %slice.23), channel_id=1, source_target_pairs={{2,0},{4,2},{6,4},{0,6},{1,3},{3,5},{5,7},{7,1},{10,8},{12,10},{14... | collective-permute-start | bytes 995336 | tf_op jit(solution)/shard_map/ppermute | solution.py:355
  77.2 10.1 %copy-start.9 = (bf16[384,1152]{1,0:T(8,128)(2,1)S(1)}, bf16[384,1152]{1,0:T(8,128)(2,1)}, u32[]{:S(2)}) copy-start(bf16[384,1152]{1,0:T(8,128)(2,1)} %copy-done.8) | copy-start | bytes 2654212
  77.2 8.8 %collective-permute-start.11 = (bf16[192,1728]{1,0:T(8,128)(2,1)S(1)}, bf16[192,1728]{1,0:T(8,128)(2,1)S(1)}, u32[]{:S(2)}, u32[]{:S(2)}) collective-permute-start(bf16[192,1728]{1,0:T(8,128)(2,1)S(1)} %collective-permute-done.4.b1), channel_id=1, source_target_pairs={{0,1},{1,0},{2,3},{3,2},{4,5},{5,4},{6,7},{7,6},{8,9},{9,8},{10,11... | collective-permute-start | bytes 1990664 | tf_op jit(solution)/shard_map/ppermute | solution.py:352
  79.3 6.8 %collective-permute-start.12 = (bf16[192,1728]{1,0:T(8,128)(2,1)S(1)}, bf16[192,1728]{1,0:T(8,128)(2,1)S(1)}, u32[]{:S(2)}, u32[]{:S(2)}) collective-permute-start(bf16[192,1728]{1,0:T(8,128)(2,1)S(1)} %collective-permute-done.5.b2), channel_id=1, source_target_pairs={{0,1},{1,0},{2,3},{3,2},{4,5},{5,4},{6,7},{7,6},{8,9},{9,8},{10,11... | collective-permute-start | bytes 1990664 | tf_op jit(solution)/shard_map/ppermute | solution.py:352
  82.9 4.4 %collective-permute-start.13 = (bf16[192,1728]{1,0:T(8,128)(2,1)S(1)}, bf16[192,1728]{1,0:T(8,128)(2,1)S(1)}, u32[]{:S(2)}, u32[]{:S(2)}) collective-permute-start(bf16[192,1728]{1,0:T(8,128)(2,1)S(1)} %constant_dynamic-update-slice_fusion.b3), channel_id=1, source_target_pairs={{0,1},{1,0},{2,3},{3,2},{4,5},{5,4},{6,7},{7,6},{8,9},{9,8},{10,11... | collective-permute-start | bytes 1990664 | tf_op jit(solution)/shard_map/ppermute | solution.py:352
  86.0 11.1 %copy-start = (bf16[8,16,1152]{2,1,0:T(8,128)(2,1)S(1)}, bf16[8,16,1152]{2,1,0:T(8,128)(2,1)}, u32[]{:S(2)}) copy-start(bf16[8,16,1152]{2,1,0:T(8,128)(2,1)} %param.22) | copy-start | bytes 884740
  86.0 11.0 %copy-start.5 = (bf16[1152,192]{0,1:T(8,128)(2,1)S(1)}, bf16[1152,192]{0,1:T(8,128)(2,1)}, u32[]{:S(2)}) copy-start(bf16[1152,192]{0,1:T(8,128)(2,1)} %param.28) | copy-start | bytes 1327108
  86.0 11.0 %copy-start.6 = (f32[8,16,64]{2,1,0:T(8,128)S(1)}, f32[8,16,64]{2,1,0:T(8,128)}, u32[]{:S(2)}) copy-start(f32[8,16,64]{2,1,0:T(8,128)} %param.29) | copy-start | bytes 98308
  86.0 11.0 %copy-start.7 = (s32[8,16,64]{2,1,0:T(8,128)S(1)}, s32[8,16,64]{2,1,0:T(8,128)}, u32[]{:S(2)}) copy-start(s32[8,16,64]{2,1,0:T(8,128)} %param.30) | copy-start | bytes 98308
  87.3 1.2 copy-start.11
  88.5 1.2 copy-start.13
  103.1 13.9 %collective-permute-start.15 = (bf16[144,640]{1,0:T(8,128)(2,1)S(1)}, bf16[144,640]{1,0:T(8,128)(2,1)S(1)}, u32[]{:S(2)}, u32[]{:S(2)}) collective-permute-start(bf16[144,640]{1,0:T(8,128)(2,1)S(1)} %get-tuple-element.31.up_ref), channel_id=1, source_target_pairs={{32,0},{64,32},{96,64},{128,96},{160,128},{192,160},{224,192},{256... | collective-permute-start | bytes 552968 | tf_op jit(solution)/shard_map/ppermute | solution.py:359
  105.1 12.0 %collective-permute-start.14 = (bf16[144,640]{1,0:T(8,128)(2,1)S(1)}, bf16[144,640]{1,0:T(8,128)(2,1)S(1)}, u32[]{:S(2)}, u32[]{:S(2)}) collective-permute-start(bf16[144,640]{1,0:T(8,128)(2,1)S(1)} %get-tuple-element.31.up_ref), channel_id=1, source_target_pairs={{0,32},{32,64},{64,96},{96,128},{128,160},{160,192},{192,224},{224... | collective-permute-start | bytes 552968 | tf_op jit(solution)/shard_map/ppermute | solution.py:358
  117.2 15.9 %collective-permute-start.17 = (bf16[432,640]{1,0:T(8,128)(2,1)S(1)}, bf16[432,640]{1,0:T(8,128)(2,1)S(1)}, u32[]{:S(2)}, u32[]{:S(2)}) collective-permute-start(bf16[432,640]{1,0:T(8,128)(2,1)S(1)} %pad_maximum_fusion.2.pack_ref), channel_id=1, source_target_pairs={{0,1},{1,0},{2,3},{3,2},{4,5},{5,4},{6,7},{7,6},{8,9},{9,8},{10,11... | collective-permute-start | bytes 1658888 | tf_op jit(solution)/shard_map/ppermute | solution.py:352
  127.9 12.9 %collective-permute-start.16 = (bf16[432,640]{1,0:T(8,128)(2,1)S(1)}, bf16[432,640]{1,0:T(8,128)(2,1)S(1)}, u32[]{:S(2)}, u32[]{:S(2)}) collective-permute-start(bf16[432,640]{1,0:T(8,128)(2,1)S(1)} %pad_maximum_fusion.2.pack_ref), channel_id=1, source_target_pairs={{1,2},{3,4},{5,6},{7,8},{9,10},{11,12},{13,14},{15,16},{17,18},{19... | collective-permute-start | bytes 1658888 | tf_op jit(solution)/shard_map/ppermute | solution.py:363

commit v6 on v5

--- a/solution.py
+++ b/solution.py
@@ -59,25 +59,12 @@
     order_ref[...] = jnp.where(rows == target_ref[...], 1.0, 0.0).astype(BF)
 
 
-def hidden_kernel(x_ref, gain_ref, order_ref, out_ref):
+def hidden_kernel(x_ref, gain_ref, target_ref, out_ref, order_ref):
+    order_kernel(target_ref, order_ref)
     for i in range(x_ref.shape[0] // T):
         center, rstd = norm_parts(x_ref[i * T : (i + 1) * T, :].astype(F32))
         hidden = (center * rstd * gain_ref[...]).astype(BF)
         out_ref[i * T : (i + 1) * T, :] = nn(hidden, order_ref[...]).astype(BF)
-
-
-def gather_kernel(k_any, v_any, q_any, o_any, out_ref, k_ref, v_ref, q_ref, o_ref, sems):
-    pairs = ((k_any, k_ref), (v_any, v_ref), (q_any, q_ref), (o_any, o_ref))
-    copies = [pltpu.make_async_copy(a, b, sems.at[i]) for i, (a, b) in enumerate(pairs)]
-    for c in copies:
-        c.start()
-    for c in copies:
-        c.wait()
-    lasts = jnp.concatenate([o_ref[24:36, 0:HW], o_ref[24:36, HW:D]], axis=0)
-    rows = jnp.concatenate([o_ref[0:24, :], lasts], axis=1)
-    out_ref[...] = jnp.concatenate(
-        [jnp.concatenate([k_ref[...], v_ref[...], q_ref[...]], axis=1), rows], axis=0
-    )
 
 
 def collect(blocks, first, rows, w_ref):
@@ -209,50 +196,57 @@
     gq_ref[...] = acc_ref[:, 0:HW].astype(BF)
 
 
-def key_side(core_ref, win_ref, groups, gk_ref, gv_ref):
+def key_side(core_ref, win_ref, tiles, gk_ref, gv_ref):
     own = slice(4 * T, 5 * T)
     kc = (lax.broadcasted_iota(jnp.int32, (T, T), 0) & 8) > 0
     second = core_ref[0].astype(F32)
-    for t, pack_ref in groups:
-        bias, stats, ups = [], [], []
-        for r in range(3):
-            base = r * 144
-            ups.append(pack_ref[base : base + T, :])
-            extra = pack_ref[base + T : base + T + 16, :].astype(F32)
-            stats.append(extra[:, 0:128] + extra[:, 128:256] + extra[:, 256:384])
-            seen = []
-            for w in range(2):
-                on = []
-                for row, col in position(t, r):
-                    i = (2 - row) * 6 + (2 - col) * 2 + w
-                    on.append(extra[i : i + 1, 384:512] if i < 16 else extra[i - 16 : i - 15, 512:640])
-                seen.append(on[0] * (1.0 - second) + on[1] * second)
-            bias.append((1.0 - jnp.where(kc, seen[1], seen[0])) * OFF)
-        bias = jnp.concatenate(bias, axis=1)
-        stats = jnp.concatenate(stats, axis=1)
-        ups = jnp.concatenate(ups, axis=0)
-        q_rows = slice(t * 3 * T, (t + 1) * 3 * T)
-        for e in range(H):
-            a, b = window(K0 + HD * e)
-            if Q0 + b <= QKV:
-                q = win_ref[q_rows, Q0 + a : Q0 + b]
-            else:
-                q = jnp.concatenate([win_ref[q_rows, Q0 + a : QKV], jnp.zeros((3 * T, Q0 + b - QKV), BF)], axis=1)
-            k = head_only(win_ref[own, a:b], HD * e, a)
-            s = nt(k, q) * SCALE2 + bias
-            p = jnp.exp2(s - stats[e : e + 1, :])
-            c, d = window(V0 + HD * e)
-            v = head_only(win_ref[own, c:d], V0 + HD * e, c)
-            up = ups[:, c - VB : d - VB]
-            ds = (p * (nt(v, up) - stats[8 + e : 9 + e, :])).astype(BF)
-            gk_ref[:, a:b] += head_only(nn(ds, q), HD * e, a)
-            gv_ref[:, c - VB : d - VB] += head_only(nn(p.astype(BF), up), V0 + HD * e, c)
-
-
-def key_centre_kernel(core_ref, win_ref, pack_ref, gk_ref, gv_ref):
+    bias, stats, ups = [], [], []
+    for t, r, pack_ref, base in tiles:
+        ups.append(pack_ref[base : base + T, :])
+        extra = pack_ref[base + T : base + T + 16, :].astype(F32)
+        stats.append(extra[:, 0:128] + extra[:, 128:256] + extra[:, 256:384])
+        seen = []
+        for w in range(2):
+            on = []
+            for row, col in position(t, r):
+                i = (2 - row) * 6 + (2 - col) * 2 + w
+                on.append(extra[i : i + 1, 384:512] if i < 16 else extra[i - 16 : i - 15, 512:640])
+            seen.append(on[0] * (1.0 - second) + on[1] * second)
+        bias.append((1.0 - jnp.where(kc, seen[1], seen[0])) * OFF)
+    bias = jnp.concatenate(bias, axis=1)
+    stats = jnp.concatenate(stats, axis=1)
+    ups = jnp.concatenate(ups, axis=0)
+    count = len(tiles) * T
+
+    def queries(a, b):
+        return jnp.concatenate(
+            [win_ref[(3 * t + r) * T : (3 * t + r + 1) * T, Q0 + a : Q0 + b] for t, r, _, _ in tiles], axis=0
+        )
+
+    for e in range(H):
+        a, b = window(K0 + HD * e)
+        if Q0 + b <= QKV:
+            q = queries(a, b)
+        else:
+            q = jnp.concatenate([queries(a, HW), jnp.zeros((count, b - HW), BF)], axis=1)
+        k = head_only(win_ref[own, a:b], HD * e, a)
+        s = nt(k, q) * SCALE2 + bias
+        p = jnp.exp2(s - stats[e : e + 1, :])
+        c, d = window(V0 + HD * e)
+        v = head_only(win_ref[own, c:d], V0 + HD * e, c)
+        up = ups[:, c - VB : d - VB]
+        ds = (p * (nt(v, up) - stats[8 + e : 9 + e, :])).astype(BF)
+        gk_ref[:, a:b] += head_only(nn(ds, q), HD * e, a)
+        gv_ref[:, c - VB : d - VB] += head_only(nn(p.astype(BF), up), V0 + HD * e, c)
+
+
+def key_near_kernel(core_ref, win_ref, own_ref, before_ref, after_ref, outer_ref, inner_ref, gk_ref, gv_ref):
     gk_ref[...] = jnp.zeros_like(gk_ref)
     gv_ref[...] = jnp.zeros_like(gv_ref)
-    key_side(core_ref, win_ref, ((1, pack_ref),), gk_ref, gv_ref)
+    tiles = (
+        (1, 0, before_ref, 0), (1, 1, own_ref, 0), (1, 2, after_ref, 0), (0, 1, outer_ref, 0), (2, 1, inner_ref, 0)
+    )
+    key_side(core_ref, win_ref, tiles, gk_ref, gv_ref)
 
 
 def finish_kernel(
@@ -263,7 +257,8 @@
     collect((b0, b1, b2, b3, b4, b5, b6, b7), 0, 144, w_ref)
     gk_ref[...] = gk0_ref[...]
     gv_ref[...] = gv0_ref[...]
-    key_side(core_ref, win_ref, ((0, packo_ref), (2, packi_ref)), gk_ref, gv_ref)
+    tiles = ((0, 0, packo_ref, 0), (0, 2, packo_ref, 144), (2, 0, packi_ref, 0), (2, 2, packi_ref, 144))
+    key_side(core_ref, win_ref, tiles, gk_ref, gv_ref)
     gk = (gk_ref[:, 0:HW] * FACTOR).astype(BF)
     gv = gv_ref[:, 64:640].astype(BF)
     grads = jnp.concatenate([gk, gv, gq_ref[...]], axis=1)
@@ -354,22 +349,28 @@
     def along(v, perm):
         return lax.ppermute(v, ("x", "core"), perm)
 
-    def columns(own):
-        before = lax.ppermute(own, lat + ("core",), south)
-        after = lax.ppermute(own, lat + ("core",), north)
-        return jnp.concatenate([before, own, after], axis=0)
+    def rows_beside(own):
+        return lax.ppermute(own, lat + ("core",), south), lax.ppermute(own, lat + ("core",), north)
 
     def sides(column):
         return lax.ppermute(column, lon, border), swap(column)
 
-    mine = pl.pallas_call(
-        gather_kernel, out_shape=shaped((96, QKV)), in_specs=[HBM] * 4, out_specs=VMEM,
-        scratch_shapes=[pltpu.VMEM((72, HW), BF)] * 3 + [pltpu.VMEM((36, D), BF), pltpu.SemaphoreType.DMA((4,))],
-        compiler_params=params(8),
-    )(w_key, w_value, w_query, w_out)
+    def placed(v, rows, cols):
+        return lax.pad(v, jnp.zeros((), BF), ((*rows, 0), (*cols, 0)))
+
+    at_row = lax.broadcasted_iota(jnp.int32, (96, QKV), 0)
+    at_col = lax.broadcasted_iota(jnp.int32, (96, QKV), 1)
+    lefts = placed(w_out, (48, 12), (D, -HW))
+    rights = placed(w_out, (60, 0), (HW, 0))
+    mine = (
+        placed(w_key, (0, 24), (0, 2 * HW)) + placed(w_value, (0, 24), (HW, HW))
+        + placed(w_query, (0, 24), (2 * HW, 0)) + placed(w_out, (72, -12), (0, HW))
+        + jnp.where(at_row >= 72, lefts, 0) + jnp.where((at_row >= 84) & (at_col >= D), rights, 0)
+    )
     one, two = lax.ppermute(mine, lat + lon, first), lax.ppermute(mine, lat + lon, second)
     fetched = jnp.concatenate([one[:72], two[:72], one[72:], two[72:]], axis=0)
-    column = columns(x)
+    before, after = rows_beside(x)
+    column = jnp.concatenate([before, x, after], axis=0)
     outer, inner = sides(column)
     target = weight_targets(yh, z, xi, core)
 
@@ -379,22 +380,20 @@
             cost_estimate=pl.CostEstimate(flops=2_000_000_000, bytes_accessed=3_000_000, transcendentals=0),
         )(target)
 
-    order = ordering(target)
 
     def hidden(v):
         return pl.pallas_call(
             hidden_kernel, out_shape=shaped((3 * T, D)), in_specs=[VMEM] * 3, out_specs=VMEM,
-            compiler_params=params(16),
+            scratch_shapes=[pltpu.VMEM((D, D), BF)], compiler_params=params(16),
             cost_estimate=pl.CostEstimate(flops=3_000_000_000, bytes_accessed=5_000_000, transcendentals=0),
-        )(v, gain, order)
+        )(v, gain, target)
 
     fetched, hc = lax.optimization_barrier((fetched, hidden(column)))
     right, left = along(fetched, ring), along(fetched, back)
+    right, left, he = lax.optimization_barrier((right, left, hidden(inner)))
     fetched_too = swap(fetched)
-    right, left, hw, he, fetched_too = lax.optimization_barrier(
-        (right, left, hidden(outer), hidden(inner), fetched_too)
-    )
-    across = jnp.concatenate([along(right[:96], ring), along(left[96:], back)], axis=0)
+    upper, lower, hw = lax.optimization_barrier((along(right[:96], ring), along(left[96:], back), hidden(outer)))
+    across = jnp.concatenate([upper, lower], axis=0)
     blocks = (fetched, right, left, across, fetched_too, swap(right), swap(left), swap(across))
 
     win, wn = pl.pallas_call(
@@ -414,19 +413,21 @@
         compiler_params=params(18),
         cost_estimate=pl.CostEstimate(flops=6_000_000_000, bytes_accessed=8_000_000, transcendentals=1_000_000),
     )(jnp.concatenate([block_mask.reshape(30), which]), win, wn, w_pixel.T, x, measured.reshape(T, 64), filter_color.reshape(T, 64))
-    packs = columns(pack)
+    before, after = rows_beside(pack)
     gq = pl.pallas_call(
         query_kernel, out_shape=shaped((T, HW)), in_specs=[VMEM] * 4, out_specs=VMEM,
         scratch_shapes=[pltpu.VMEM((T, 640), F32)], compiler_params=params(16),
         cost_estimate=pl.CostEstimate(flops=4_000_000_000, bytes_accessed=6_000_000, transcendentals=0),
     )(win, e, pack, stat)
-    packs, gq, target = lax.optimization_barrier((packs, gq, target))
-    packs_outer, packs_inner = sides(packs)
+    pack_late, gq = lax.optimization_barrier((pack, gq))
+    near_outer, near_inner = sides(pack_late)
+    corners, target = lax.optimization_barrier((jnp.concatenate([before, after], axis=0), target))
+    packs_outer, packs_inner = sides(corners)
     gk, gv = pl.pallas_call(
-        key_centre_kernel, out_shape=(shaped((T, 640), F32),) * 2, in_specs=[SMEM] + [VMEM] * 2, out_specs=(VMEM,) * 2,
+        key_near_kernel, out_shape=(shaped((T, 640), F32),) * 2, in_specs=[SMEM] + [VMEM] * 6, out_specs=(VMEM,) * 2,
         compiler_params=params(16),
         cost_estimate=pl.CostEstimate(flops=4_000_000_000, bytes_accessed=6_000_000, transcendentals=0),
-    )(which, win, packs)
+    )(which, win, pack, before, after, near_outer, near_inner)
     guidance = pl.pallas_call(
         finish_kernel, out_shape=shaped((T, D), F32), in_specs=[SMEM] + [VMEM] * 18, out_specs=VMEM,
         scratch_shapes=[pltpu.VMEM((T, 640), F32)] * 2 + [pltpu.VMEM((D, QKV), BF)],

time: 149 us -> 147 us (0.987)
  the two profiles are of different devices: /device:TPU:47 before, /device:TPU:63 now
where the time goes in v6:
time: 147 us; the launch traced here: 146 us
  starting transfers between devices  82.7 us (56%)
  Pallas kernels  32.2 us (22%)
  waiting for transfers between devices  21.5 us (15%)
  local copies, waits for them, and re-layouts  5.3 us (4%)
  other arithmetic  3.25 us (2%)
    ppermute x3, starting transfers between devices, sides(): return (lax.ppermute(column, lon, border), swap(column))  27 us
    ppermute x2, starting transfers between devices, rows_beside(): lax.ppermute(own, lat + ('core',), south)  20.4 us
    ppermute x7, starting transfers between devices, swap(): return lax.ppermute(v, 'core', [(0, 1), (1, 0)])  16.2 us
    ppermute x4, waiting for transfers between devices, along(): return lax.ppermute(v, ('x', 'core'), perm)  12.9 us
    ppermute x4, starting transfers between devices, along(): return lax.ppermute(v, ('x', 'core'), perm)  10.6 us
    pallas_call x3, Pallas kernels, hidden(): pl.pallas_call(hidden_kernel, out_shape=shaped((3 * T, D)), in_specs=[VME...  7.49 us
    pallas_call x1, Pallas kernels, on_device(): pl.pallas_call(project_kernel, out_shape=(shaped((9 * T, QKV)), shaped((6...  7.39 us
    pallas_call x1, Pallas kernels, on_device(): pl.pallas_call(forward_kernel, out_shape=(shaped((H * T, 9 * T)), shaped(...  6.11 us
  transfers between devices with their start and end apart: 20, of which 5 were waited for; matrix products, arithmetic and copies ran while one was open for 5% of the time, Pallas kernels for 9%

profile of v6, /device:TPU:63, one launch (start us, length us, event | category | flops | bytes accessed | tf_op | source)
XLA Modules:
  0.0 146.3 jit_solution(6658116429818418606)
XLA Ops:
  0.6 4.0 %collective-permute-start.3 = (bf16[128,1152]{1,0:T(8,128)(2,1)}, bf16[128,1152]{1,0:T(8,128)(2,1)S(1)}, u32[]{:S(2)}, u32[]{:S(2)}) collective-permute-start(bf16[128,1152]{1,0:T(8,128)(2,1)} %bitcast.7), channel_id=1, source_target_pairs={{32,0},{64,32},{96,64},{128,96},{160,128},{192,160},{224,192},{256... | collective-permute-start | bytes 884744 | tf_op jit(solution)/shard_map/ppermute | solution.py:353
  4.6 10.8 %collective-permute-start.2 = (bf16[128,1152]{1,0:T(8,128)(2,1)}, bf16[128,1152]{1,0:T(8,128)(2,1)S(1)}, u32[]{:S(2)}, u32[]{:S(2)}) collective-permute-start(bf16[128,1152]{1,0:T(8,128)(2,1)} %bitcast.8), channel_id=1, source_target_pairs={{0,32},{32,64},{64,96},{96,128},{128,160},{160,192},{192,224},{224... | collective-permute-start | bytes 884744 | tf_op jit(solution)/shard_map/ppermute | solution.py:353
  15.5 1.2 fusion.2
  16.7 0.7 collective-permute-start.1
  17.4 1.9 %collective-permute-start = (bf16[96,1728]{1,0:T(8,128)(2,1)S(1)}, bf16[96,1728]{1,0:T(8,128)(2,1)S(1)}, u32[]{:S(2)}, u32[]{:S(2)}) collective-permute-start(bf16[96,1728]{1,0:T(8,128)(2,1)S(1)} %fusion.2), channel_id=1, source_target_pairs={{224,0},{33,1},{194,2},{67,3},{164,4},{101,5},{134,6},{415,7},{232... | collective-permute-start | bytes 995336 | tf_op jit(solution)/shard_map/ppermute | solution.py:370
  19.4 0.7 reshape.34.gain_ref
  20.1 0.8 fusion.15
  20.9 1.0 collective-permute-done.2
  21.8 1.0 pad_maximum_fusion.x_ref
  22.9 17.5 %collective-permute-start.9 = (bf16[384,1152]{1,0:T(8,128)(2,1)S(1)}, bf16[384,1152]{1,0:T(8,128)(2,1)}, u32[]{:S(2)}, u32[]{:S(2)}) collective-permute-start(bf16[384,1152]{1,0:T(8,128)(2,1)S(1)} %pad_maximum_fusion.x_ref), channel_id=1, source_target_pairs={{1,2},{3,4},{5,6},{7,8},{9,10},{11,12},{13,14},{15,16},{17,18},{19... | collective-permute-start | bytes 2654216 | tf_op jit(solution)/shard_map/ppermute | solution.py:356
  40.4 1.9 %collective-permute-start.6 = (bf16[384,1152]{1,0:T(8,128)(2,1)S(1)}, bf16[384,1152]{1,0:T(8,128)(2,1)S(1)}, u32[]{:S(2)}, u32[]{:S(2)}) collective-permute-start(bf16[384,1152]{1,0:T(8,128)(2,1)S(1)} %pad_maximum_fusion.x_ref), channel_id=1, source_target_pairs={{0,1},{1,0},{2,3},{3,2},{4,5},{5,4},{6,7},{7,6},{8,9},{9,8},{10,11... | collective-permute-start | bytes 2654216 | tf_op jit(solution)/shard_map/ppermute | solution.py:347
  42.3 2.1 %shard_map.221.hc_ref = bf16[384,1152]{1,0:T(8,128)(2,1)S(1)} custom-call(bf16[384,1152]{1,0:T(8,128)(2,1)S(1)} %pad_maximum_fusion.x_ref, f32[1,1152]{1,0:T(1,128)S(1)} %reshape.34.gain_ref, s32[1,1152]{1,0:T(1,128)S(1)} %reshape.35.target_ref), custom_call_target="tpu_custom_call" | custom-call | flops 3000000000 | bytes 5000000 | tf_op jit(solution)/shard_map/pallas_call | solution.py:385
  44.5 0.9 copy-done.4
  45.5 0.1 pad_maximum_fusion.1.b0
  45.6 1.9 %collective-permute-start.5 = (bf16[192,1728]{1,0:T(8,128)(2,1)S(1)}, bf16[192,1728]{1,0:T(8,128)(2,1)S(1)}, u32[]{:S(2)}, u32[]{:S(2)}) collective-permute-start(bf16[192,1728]{1,0:T(8,128)(2,1)S(1)} %pad_maximum_fusion.1.b0), channel_id=1, source_target_pairs={{2,0},{4,2},{6,4},{0,6},{1,3},{3,5},{5,7},{7,1},{10,8},{12,10},{14... | collective-permute-start | bytes 1990664 | tf_op jit(solution)/shard_map/ppermute | solution.py:350
  47.5 3.4 %collective-permute-start.4 = (bf16[192,1728]{1,0:T(8,128)(2,1)S(1)}, bf16[192,1728]{1,0:T(8,128)(2,1)S(1)}, u32[]{:S(2)}, u32[]{:S(2)}) collective-permute-start(bf16[192,1728]{1,0:T(8,128)(2,1)S(1)} %pad_maximum_fusion.1.b0), channel_id=1, source_target_pairs={{0,2},{2,4},{4,6},{6,0},{3,1},{5,3},{7,5},{1,7},{8,10},{10,12},{12... | collective-permute-start | bytes 1990664 | tf_op jit(solution)/shard_map/ppermute | solution.py:350
  50.9 2.1 %shard_map.222.he_ref = bf16[384,1152]{1,0:T(8,128)(2,1)S(1)} custom-call(bf16[384,1152]{1,0:T(8,128)(2,1)S(1)} %collective-permute-done.6.x_ref, f32[1,1152]{1,0:T(1,128)S(1)} %reshape.34.gain_ref, s32[1,1152]{1,0:T(1,128)S(1)} %reshape.35.target_ref), custom_call_target="tpu_custom_call" | custom-call | flops 3000000000 | bytes 5000000 | tf_op jit(solution)/shard_map/pallas_call | solution.py:385
  53.0 0.9 copy-done.6
  53.9 10.4 %collective-permute-done.5.b2 = bf16[192,1728]{1,0:T(8,128)(2,1)S(1)} collective-permute-done((bf16[192,1728]{1,0:T(8,128)(2,1)S(1)}, bf16[192,1728]{1,0:T(8,128)(2,1)S(1)}, u32[]{:S(2)}, u32[]{:S(2)}) %collective-permute-start.5) | collective-permute-done | bytes 663584 | tf_op jit(solution)/shard_map/ppermute | solution.py:350
  64.3 2.5 %collective-permute-done.4.b1 = bf16[192,1728]{1,0:T(8,128)(2,1)S(1)} collective-permute-done((bf16[192,1728]{1,0:T(8,128)(2,1)S(1)}, bf16[192,1728]{1,0:T(8,128)(2,1)S(1)}, u32[]{:S(2)}, u32[]{:S(2)}) %collective-permute-start.4) | collective-permute-done | bytes 663584 | tf_op jit(solution)/shard_map/ppermute | solution.py:350
  66.8 0.8 slice.24
  67.5 0.7 slice.25
  68.3 1.9 %collective-permute-start.8 = (bf16[96,1728]{1,0:T(8,128)(2,1)}, bf16[96,1728]{1,0:T(8,128)(2,1)S(1)}, u32[]{:S(2)}, u32[]{:S(2)}) collective-permute-start(bf16[96,1728]{1,0:T(8,128)(2,1)} %slice.25), channel_id=1, source_target_pairs={{2,0},{4,2},{6,4},{0,6},{1,3},{3,5},{5,7},{7,1},{10,8},{12,10},{14... | collective-permute-start | bytes 995336 | tf_op jit(solution)/shard_map/ppermute | solution.py:350
  70.2 3.4 %collective-permute-start.7 = (bf16[96,1728]{1,0:T(8,128)(2,1)}, bf16[96,1728]{1,0:T(8,128)(2,1)}, u32[]{:S(2)}, u32[]{:S(2)}) collective-permute-start(bf16[96,1728]{1,0:T(8,128)(2,1)} %slice.24), channel_id=1, source_target_pairs={{0,2},{2,4},{4,6},{6,0},{3,1},{5,3},{7,5},{1,7},{8,10},{10,12},{12... | collective-permute-start | bytes 995336 | tf_op jit(solution)/shard_map/ppermute | solution.py:350
  73.6 0.1 reshape.31
  73.7 0.0 copy-start.12
  73.7 0.0 copy-start.15
  73.8 4.0 %collective-permute-start.10 = (bf16[192,1728]{1,0:T(8,128)(2,1)S(1)}, bf16[192,1728]{1,0:T(8,128)(2,1)S(1)}, u32[]{:S(2)}, u32[]{:S(2)}) collective-permute-start(bf16[192,1728]{1,0:T(8,128)(2,1)S(1)} %pad_maximum_fusion.1.b0), channel_id=1, source_target_pairs={{0,1},{1,0},{2,3},{3,2},{4,5},{5,4},{6,7},{7,6},{8,9},{9,8},{10,11... | collective-permute-start | bytes 1990664 | tf_op jit(solution)/shard_map/ppermute | solution.py:347
  77.8 1.9 %collective-permute-start.11 = (bf16[192,1728]{1,0:T(8,128)(2,1)S(1)}, bf16[192,1728]{1,0:T(8,128)(2,1)S(1)}, u32[]{:S(2)}, u32[]{:S(2)}) collective-permute-start(bf16[192,1728]{1,0:T(8,128)(2,1)S(1)} %collective-permute-done.4.b1), channel_id=1, source_target_pairs={{0,1},{1,0},{2,3},{3,2},{4,5},{5,4},{6,7},{7,6},{8,9},{9,8},{10,11... | collective-permute-start | bytes 1990664 | tf_op jit(solution)/shard_map/ppermute | solution.py:347
  79.7 2.4 %collective-permute-start.12 = (bf16[192,1728]{1,0:T(8,128)(2,1)S(1)}, bf16[192,1728]{1,0:T(8,128)(2,1)S(1)}, u32[]{:S(2)}, u32[]{:S(2)}) collective-permute-start(bf16[192,1728]{1,0:T(8,128)(2,1)S(1)} %collective-permute-done.5.b2), channel_id=1, source_target_pairs={{0,1},{1,0},{2,3},{3,2},{4,5},{5,4},{6,7},{7,6},{8,9},{9,8},{10,11... | collective-permute-start | bytes 1990664 | tf_op jit(solution)/shard_map/ppermute | solution.py:347
  82.1 3.3 %shard_map.223.hw_ref = bf16[384,1152]{1,0:T(8,128)(2,1)S(1)} custom-call(bf16[384,1152]{1,0:T(8,128)(2,1)} %collective-permute-done.9.x_ref, f32[1,1152]{1,0:T(1,128)S(1)} %reshape.34.gain_ref, s32[1,1152]{1,0:T(1,128)S(1)} %reshape.35.target_ref), custom_call_target="tpu_custom_call" | custom-call | flops 3000000000 | bytes 5000000 | tf_op jit(solution)/shard_map/pallas_call | solution.py:385
  85.4 1.0 constant_dynamic-update-slice_fusion.1
  86.5 2.1 %collective-permute-start.13 = (bf16[192,1728]{1,0:T(8,128)(2,1)S(1)}, bf16[192,1728]{1,0:T(8,128)(2,1)S(1)}, u32[]{:S(2)}, u32[]{:S(2)}) collective-permute-start(bf16[192,1728]{1,0:T(8,128)(2,1)S(1)} %constant_dynamic-update-slice_fusion.b3), channel_id=1, source_target_pairs={{0,1},{1,0},{2,3},{3,2},{4,5},{5,4},{6,7},{7,6},{8,9},{9,8},{10,11... | collective-permute-start | bytes 1990664 | tf_op jit(solution)/shard_map/ppermute | solution.py:347
  88.7 0.1 pad_add_fusion.1.blocks_ref
  88.9 1.6 %collective-permute-done.13.b7 = bf16[192,1728]{1,0:T(8,128)(2,1)S(1)} collective-permute-done((bf16[192,1728]{1,0:T(8,128)(2,1)S(1)}, bf16[192,1728]{1,0:T(8,128)(2,1)S(1)}, u32[]{:S(2)}, u32[]{:S(2)}) %collective-permute-start.13) | collective-permute-done | bytes 663584 | tf_op jit(solution)/shard_map/ppermute | solution.py:347
  90.5 7.4 %shard_map.224 = (bf16[1152,1728]{1,0:T(8,128)(2,1)S(1)}, bf16[640,1152]{1,0:T(8,128)(2,1)S(1)}) custom-call(s32[3,384]{1,0:T(4,128)S(1)} %pad_add_fusion.place_ref, bf16[384,1152]{1,0:T(8,128)(2,1)S(1)} %shard_map.223.hw_ref, bf16[384,1152]{1,0:T(8,128)(2,1)S(1)} %copy-done.5, bf16[384,1152]{1,0:T(8,128)(2,1)S(1)} %copy-done.7, ...), custom_call_target="tpu_custom_call" | custom-call | flops 6000000000 | bytes 8000000 | tf_op jit(solution)/shard_map/pallas_call | solution.py:399
  97.9 6.1 %shard_map.225 = (bf16[1024,1152]{1,0:T(8,128)(2,1)S(1)}, bf16[128,1152]{1,0:T(8,128)(2,1)}, f32[128,1152]{1,0:T(8,128)S(1)}, bf16[144,640]{1,0:T(8,128)(2,1)S(1)}, f32[128,128]{1,0:T(8,128)S(1)}) custom-call(s32[31]{0:T(128)S(1)} %pad_add_fusion.1.blocks_ref, bf16[1152,1728]{1,0:T(8,128)(2,1)S(1)} %get-tuple-element.31.win_ref, ...), custom_call_target="tpu_custom_call" | custom-call | flops 6000000000 | bytes 8000000 | tf_op jit(solution)/shard_map/pallas_call | solution.py:406
  104.0 1.9 %collective-permute-start.15 = (bf16[144,640]{1,0:T(8,128)(2,1)S(1)}, bf16[144,640]{1,0:T(8,128)(2,1)S(1)}, u32[]{:S(2)}, u32[]{:S(2)}) collective-permute-start(bf16[144,640]{1,0:T(8,128)(2,1)S(1)} %get-tuple-element.38.up_ref.own_ref), channel_id=1, source_target_pairs={{32,0},{64,32},{96,64},{128,96},{160,128},{192,160},{224,192},{256... | collective-permute-start | bytes 552968 | tf_op jit(solution)/shard_map/ppermute | solution.py:353
  106.0 9.6 %collective-permute-start.14 = (bf16[144,640]{1,0:T(8,128)(2,1)S(1)}, bf16[144,640]{1,0:T(8,128)(2,1)S(1)}, u32[]{:S(2)}, u32[]{:S(2)}) collective-permute-start(bf16[144,640]{1,0:T(8,128)(2,1)S(1)} %get-tuple-element.38.up_ref.own_ref), channel_id=1, source_target_pairs={{0,32},{32,64},{64,96},{96,128},{128,160},{160,192},{192,224},{224... | collective-permute-start | bytes 552968 | tf_op jit(solution)/shard_map/ppermute | solution.py:353
  115.6 2.4 %shard_map.226.gq_ref = bf16[128,576]{1,0:T(8,128)(2,1)S(1)} custom-call(bf16[1152,1728]{1,0:T(8,128)(2,1)S(1)} %get-tuple-element.31.win_ref, bf16[1024,1152]{1,0:T(8,128)(2,1)S(1)} %get-tuple-element.36.e_ref, bf16[144,640]{1,0:T(8,128)(2,1)S(1)} %get-tuple-element.38.up_ref.own_ref, f32[128,128]{1,0:T(8,128)S(1)} %get-tuple-element.37.stat_ref), custom_call_target="tpu_custom_call" | custom-call | flops 4000000000 | bytes 6000000 | tf_op jit(solution)/shard_map/pallas_call | solution.py:417
  118.0 1.9 %collective-permute-start.19 = (bf16[144,640]{1,0:T(8,128)(2,1)S(1)}, bf16[144,640]{1,0:T(8,128)(2,1)S(1)}, u32[]{:S(2)}, u32[]{:S(2)}) collective-permute-start(bf16[144,640]{1,0:T(8,128)(2,1)S(1)} %get-tuple-element.38.up_ref.own_ref), channel_id=1, source_target_pairs={{0,1},{1,0},{2,3},{3,2},{4,5},{5,4},{6,7},{7,6},{8,9},{9,8},{10,11... | collective-permute-start | bytes 552968 | tf_op jit(solution)/shard_map/ppermute | solution.py:347
  119.9 6.0 %collective-permute-start.18 = (bf16[144,640]{1,0:T(8,128)(2,1)S(1)}, bf16[144,640]{1,0:T(8,128)(2,1)S(1)}, u32[]{:S(2)}, u32[]{:S(2)}) collective-permute-start(bf16[144,640]{1,0:T(8,128)(2,1)S(1)} %get-tuple-element.38.up_ref.own_ref), channel_id=1, source_target_pairs={{1,2},{3,4},{5,6},{7,8},{9,10},{11,12},{13,14},{15,16},{17,18},{19... | collective-permute-start | bytes 552968 | tf_op jit(solution)/shard_map/ppermute | solution.py:356
  126.0 1.9 %collective-permute-start.17 = (bf16[288,640]{1,0:T(8,128)(2,1)S(1)}, bf16[288,640]{1,0:T(8,128)(2,1)S(1)}, u32[]{:S(2)}, u32[]{:S(2)}) collective-permute-start(bf16[288,640]{1,0:T(8,128)(2,1)S(1)} %pad_maximum_fusion.2), channel_id=1, source_target_pairs={{0,1},{1,0},{2,3},{3,2},{4,5},{5,4},{6,7},{7,6},{8,9},{9,8},{10,11... | collective-permute-start | bytes 1105928 | tf_op jit(solution)/shard_map/ppermute | solution.py:347
  128.0 3.4 %collective-permute-start.16 = (bf16[288,640]{1,0:T(8,128)(2,1)S(1)}, bf16[288,640]{1,0:T(8,128)(2,1)S(1)}, u32[]{:S(2)}, u32[]{:S(2)}) collective-permute-start(bf16[288,640]{1,0:T(8,128)(2,1)S(1)} %pad_maximum_fusion.2), channel_id=1, source_target_pairs={{1,2},{3,4},{5,6},{7,8},{9,10},{11,12},{13,14},{15,16},{17,18},{19... | collective-permute-start | bytes 1105928 | tf_op jit(solution)/shard_map/ppermute | solution.py:356
  131.4 0.5 shard_map.228.order_ref
  131.9 2.8 %shard_map.227 = (f32[128,640]{1,0:T(8,128)S(1)}, f32[128,640]{1,0:T(8,128)S(1)}) custom-call(s32[1]{0:T(128)} %bitcast.core_ref, bf16[1152,1728]{1,0:T(8,128)(2,1)S(1)} %get-tuple-element.31.win_ref, bf16[144,640]{1,0:T(8,128)(2,1)S(1)} %get-tuple-element.38.up_ref.own_ref, bf16[144,640]{1,0:T(8,128)(2,1)S(1)} %collective-permute-done.14.before_ref, ...), custom_call_target="tpu_custom_call" | custom-call | flops 4000000000 | bytes 6000000 | tf_op jit(solution)/shard_map/pallas_call | solution.py:426
  134.7 6.0 %collective-permute-done.16.packo_ref = bf16[288,640]{1,0:T(8,128)(2,1)S(1)} collective-permute-done((bf16[288,640]{1,0:T(8,128)(2,1)S(1)}, bf16[288,640]{1,0:T(8,128)(2,1)S(1)}, u32[]{:S(2)}, u32[]{:S(2)}) %collective-permute-start.16) | collective-permute-done | bytes 368672 | tf_op jit(solution)/shard_map/ppermute | solution.py:356
  140.7 5.6 %shard_map.229 = f32[128,1152]{1,0:T(8,128)} custom-call(s32[1]{0:T(128)} %bitcast.core_ref, bf16[1152,1728]{1,0:T(8,128)(2,1)S(1)} %get-tuple-element.31.win_ref, bf16[288,640]{1,0:T(8,128)(2,1)S(1)} %collective-permute-done.16.packo_ref, bf16[288,640]{1,0:T(8,128)(2,1)S(1)} %collective-permute-done.17.packi_ref, f32[128,640]{1,0:T(8,128)S(1)} %get-tuple-element.39.gk0_ref, ...), custom_call_target="tpu_custom_call" | custom-call | tf_op jit(solution)/shard_map/pallas_call | solution.py:431
  (59 shorter events, 0.3 us)
Async XLA Ops:
  0.6 20.2 %collective-permute-start.3 = (bf16[128,1152]{1,0:T(8,128)(2,1)}, bf16[128,1152]{1,0:T(8,128)(2,1)S(1)}, u32[]{:S(2)}, u32[]{:S(2)}) collective-permute-start(bf16[128,1152]{1,0:T(8,128)(2,1)} %bitcast.7), channel_id=1, source_target_pairs={{32,0},{64,32},{96,64},{128,96},{160,128},{192,160},{224,192},{256... | collective-permute-start | bytes 884744 | tf_op jit(solution)/shard_map/ppermute | solution.py:353
  4.6 17.2 %collective-permute-start.2 = (bf16[128,1152]{1,0:T(8,128)(2,1)}, bf16[128,1152]{1,0:T(8,128)(2,1)S(1)}, u32[]{:S(2)}, u32[]{:S(2)}) collective-permute-start(bf16[128,1152]{1,0:T(8,128)(2,1)} %bitcast.8), channel_id=1, source_target_pairs={{0,32},{32,64},{64,96},{96,128},{128,160},{160,192},{192,224},{224... | collective-permute-start | bytes 884744 | tf_op jit(solution)/shard_map/ppermute | solution.py:353
  16.7 28.7 %collective-permute-start.1 = (bf16[96,1728]{1,0:T(8,128)(2,1)S(1)}, bf16[96,1728]{1,0:T(8,128)(2,1)S(1)}, u32[]{:S(2)}, u32[]{:S(2)}) collective-permute-start(bf16[96,1728]{1,0:T(8,128)(2,1)S(1)} %fusion.2), channel_id=1, source_target_pairs={{440,0},{377,1},{474,2},{347,3},{508,4},{317,5},{286,6},{7,7},{432... | collective-permute-start | bytes 995336 | tf_op jit(solution)/shard_map/ppermute | solution.py:370
  17.4 28.0 %collective-permute-start = (bf16[96,1728]{1,0:T(8,128)(2,1)S(1)}, bf16[96,1728]{1,0:T(8,128)(2,1)S(1)}, u32[]{:S(2)}, u32[]{:S(2)}) collective-permute-start(bf16[96,1728]{1,0:T(8,128)(2,1)S(1)} %fusion.2), channel_id=1, source_target_pairs={{224,0},{33,1},{194,2},{67,3},{164,4},{101,5},{134,6},{415,7},{232... | collective-permute-start | bytes 995336 | tf_op jit(solution)/shard_map/ppermute | solution.py:370
  22.9 56.8 %collective-permute-start.9 = (bf16[384,1152]{1,0:T(8,128)(2,1)S(1)}, bf16[384,1152]{1,0:T(8,128)(2,1)}, u32[]{:S(2)}, u32[]{:S(2)}) collective-permute-start(bf16[384,1152]{1,0:T(8,128)(2,1)S(1)} %pad_maximum_fusion.x_ref), channel_id=1, source_target_pairs={{1,2},{3,4},{5,6},{7,8},{9,10},{11,12},{13,14},{15,16},{17,18},{19... | collective-permute-start | bytes 2654216 | tf_op jit(solution)/shard_map/ppermute | solution.py:356
  40.4 10.4 %collective-permute-start.6 = (bf16[384,1152]{1,0:T(8,128)(2,1)S(1)}, bf16[384,1152]{1,0:T(8,128)(2,1)S(1)}, u32[]{:S(2)}, u32[]{:S(2)}) collective-permute-start(bf16[384,1152]{1,0:T(8,128)(2,1)S(1)} %pad_maximum_fusion.x_ref), channel_id=1, source_target_pairs={{0,1},{1,0},{2,3},{3,2},{4,5},{5,4},{6,7},{7,6},{8,9},{9,8},{10,11... | collective-permute-start | bytes 2654216 | tf_op jit(solution)/shard_map/ppermute | solution.py:347
  44.5 0.9 copy-start.4
  45.6 28.0 %copy-start.9 = (s32[1,2,3,5]{3,1,2,0:T(2,128)S(1)}, s32[1,2,3,5]{3,1,2,0:T(2,128)}, u32[]{:S(2)}) copy-start(s32[1,2,3,5]{3,1,2,0:T(2,128)} %param.31) | copy-start | bytes 364
  45.6 18.7 %collective-permute-start.5 = (bf16[192,1728]{1,0:T(8,128)(2,1)S(1)}, bf16[192,1728]{1,0:T(8,128)(2,1)S(1)}, u32[]{:S(2)}, u32[]{:S(2)}) collective-permute-start(bf16[192,1728]{1,0:T(8,128)(2,1)S(1)} %pad_maximum_fusion.1.b0), channel_id=1, source_target_pairs={{2,0},{4,2},{6,4},{0,6},{1,3},{3,5},{5,7},{7,1},{10,8},{12,10},{14... | collective-permute-start | bytes 1990664 | tf_op jit(solution)/shard_map/ppermute | solution.py:350
  47.5 19.3 %collective-permute-start.4 = (bf16[192,1728]{1,0:T(8,128)(2,1)S(1)}, bf16[192,1728]{1,0:T(8,128)(2,1)S(1)}, u32[]{:S(2)}, u32[]{:S(2)}) collective-permute-start(bf16[192,1728]{1,0:T(8,128)(2,1)S(1)} %pad_maximum_fusion.1.b0), channel_id=1, source_target_pairs={{0,2},{2,4},{4,6},{6,0},{3,1},{5,3},{7,5},{1,7},{8,10},{10,12},{12... | collective-permute-start | bytes 1990664 | tf_op jit(solution)/shard_map/ppermute | solution.py:350
  53.0 0.9 copy-start.6
  68.3 17.1 %collective-permute-start.8 = (bf16[96,1728]{1,0:T(8,128)(2,1)}, bf16[96,1728]{1,0:T(8,128)(2,1)S(1)}, u32[]{:S(2)}, u32[]{:S(2)}) collective-permute-start(bf16[96,1728]{1,0:T(8,128)(2,1)} %slice.25), channel_id=1, source_target_pairs={{2,0},{4,2},{6,4},{0,6},{1,3},{3,5},{5,7},{7,1},{10,8},{12,10},{14... | collective-permute-start | bytes 995336 | tf_op jit(solution)/shard_map/ppermute | solution.py:350
  70.2 15.2 %collective-permute-start.7 = (bf16[96,1728]{1,0:T(8,128)(2,1)}, bf16[96,1728]{1,0:T(8,128)(2,1)}, u32[]{:S(2)}, u32[]{:S(2)}) collective-permute-start(bf16[96,1728]{1,0:T(8,128)(2,1)} %slice.24), channel_id=1, source_target_pairs={{0,2},{2,4},{4,6},{6,0},{3,1},{5,3},{7,5},{1,7},{8,10},{10,12},{12... | collective-permute-start | bytes 995336 | tf_op jit(solution)/shard_map/ppermute | solution.py:350
  73.7 14.9 %copy-start.8 = (s32[384]{0:T(512)S(1)}, s32[384]{0:T(512)}, u32[]{:S(2)}) copy-start(s32[384]{0:T(512)} %constant.89.clone) | copy-start | bytes 4612
  73.7 14.9 %copy-start.10 = (s32[384]{0:T(512)S(1)}, s32[384]{0:T(512)}, u32[]{:S(2)}) copy-start(s32[384]{0:T(512)} %constant.87.clone) | copy-start | bytes 4612
  73.7 14.9 %copy-start.11 = (s32[384]{0:T(512)S(1)}, s32[384]{0:T(512)}, u32[]{:S(2)}) copy-start(s32[384]{0:T(512)} %constant.86.clone) | copy-start | bytes 4612
  73.7 14.9 %copy-start.12 = (s32[384]{0:T(512)S(1)}, s32[384]{0:T(512)}, u32[]{:S(2)}) copy-start(s32[384]{0:T(512)} %constant.85.clone) | copy-start | bytes 4612
  73.7 14.9 %copy-start.15 = (pred[384]{0:T(512)(128)(4,1)S(1)}, pred[384]{0:T(512)(128)(4,1)}, u32[]{:S(2)}) copy-start(pred[384]{0:T(512)(128)(4,1)} %constant.88.clone) | copy-start | bytes 1156
  73.7 14.9 %copy-start.13 = (pred[384]{0:T(512)(128)(4,1)S(1)}, pred[384]{0:T(512)(128)(4,1)}, u32[]{:S(2)}) copy-start(pred[384]{0:T(512)(128)(4,1)} %constant.91.clone) | copy-start | bytes 1156
  73.7 14.9 %copy-start.14 = (pred[384]{0:T(512)(128)(4,1)S(1)}, pred[384]{0:T(512)(128)(4,1)}, u32[]{:S(2)}) copy-start(pred[384]{0:T(512)(128)(4,1)} %constant.90.clone) | copy-start | bytes 1156
  73.7 16.8 %copy-start.5 = (bf16[384,1152]{1,0:T(8,128)(2,1)S(1)}, bf16[384,1152]{1,0:T(8,128)(2,1)}, u32[]{:S(2)}) copy-start(bf16[384,1152]{1,0:T(8,128)(2,1)} %copy-done.4) | copy-start | bytes 2654212
  73.7 16.7 %copy-start.7 = (bf16[384,1152]{1,0:T(8,128)(2,1)S(1)}, bf16[384,1152]{1,0:T(8,128)(2,1)}, u32[]{:S(2)}) copy-start(bf16[384,1152]{1,0:T(8,128)(2,1)} %copy-done.6) | copy-start | bytes 2654212
  73.8 15.1 %collective-permute-start.10 = (bf16[192,1728]{1,0:T(8,128)(2,1)S(1)}, bf16[192,1728]{1,0:T(8,128)(2,1)S(1)}, u32[]{:S(2)}, u32[]{:S(2)}) collective-permute-start(bf16[192,1728]{1,0:T(8,128)(2,1)S(1)} %pad_maximum_fusion.1.b0), channel_id=1, source_target_pairs={{0,1},{1,0},{2,3},{3,2},{4,5},{5,4},{6,7},{7,6},{8,9},{9,8},{10,11... | collective-permute-start | bytes 1990664 | tf_op jit(solution)/shard_map/ppermute | solution.py:347
  77.8 11.1 %collective-permute-start.11 = (bf16[192,1728]{1,0:T(8,128)(2,1)S(1)}, bf16[192,1728]{1,0:T(8,128)(2,1)S(1)}, u32[]{:S(2)}, u32[]{:S(2)}) collective-permute-start(bf16[192,1728]{1,0:T(8,128)(2,1)S(1)} %collective-permute-done.4.b1), channel_id=1, source_target_pairs={{0,1},{1,0},{2,3},{3,2},{4,5},{5,4},{6,7},{7,6},{8,9},{9,8},{10,11... | collective-permute-start | bytes 1990664 | tf_op jit(solution)/shard_map/ppermute | solution.py:347
  79.7 9.2 %collective-permute-start.12 = (bf16[192,1728]{1,0:T(8,128)(2,1)S(1)}, bf16[192,1728]{1,0:T(8,128)(2,1)S(1)}, u32[]{:S(2)}, u32[]{:S(2)}) collective-permute-start(bf16[192,1728]{1,0:T(8,128)(2,1)S(1)} %collective-permute-done.5.b2), channel_id=1, source_target_pairs={{0,1},{1,0},{2,3},{3,2},{4,5},{5,4},{6,7},{7,6},{8,9},{9,8},{10,11... | collective-permute-start | bytes 1990664 | tf_op jit(solution)/shard_map/ppermute | solution.py:347
  86.5 4.0 %collective-permute-start.13 = (bf16[192,1728]{1,0:T(8,128)(2,1)S(1)}, bf16[192,1728]{1,0:T(8,128)(2,1)S(1)}, u32[]{:S(2)}, u32[]{:S(2)}) collective-permute-start(bf16[192,1728]{1,0:T(8,128)(2,1)S(1)} %constant_dynamic-update-slice_fusion.b3), channel_id=1, source_target_pairs={{0,1},{1,0},{2,3},{3,2},{4,5},{5,4},{6,7},{7,6},{8,9},{9,8},{10,11... | collective-permute-start | bytes 1990664 | tf_op jit(solution)/shard_map/ppermute | solution.py:347
  88.8 9.1 %copy-start = (bf16[8,16,1152]{2,1,0:T(8,128)(2,1)S(1)}, bf16[8,16,1152]{2,1,0:T(8,128)(2,1)}, u32[]{:S(2)}) copy-start(bf16[8,16,1152]{2,1,0:T(8,128)(2,1)} %param.22) | copy-start | bytes 884740
  88.8 9.1 %copy-start.1 = (bf16[1152,192]{0,1:T(8,128)(2,1)S(1)}, bf16[1152,192]{0,1:T(8,128)(2,1)}, u32[]{:S(2)}) copy-start(bf16[1152,192]{0,1:T(8,128)(2,1)} %param.28) | copy-start | bytes 1327108
  88.8 9.1 %copy-start.2 = (f32[8,16,64]{2,1,0:T(8,128)S(1)}, f32[8,16,64]{2,1,0:T(8,128)}, u32[]{:S(2)}) copy-start(f32[8,16,64]{2,1,0:T(8,128)} %param.29) | copy-start | bytes 98308
  88.8 9.1 %copy-start.3 = (s32[8,16,64]{2,1,0:T(8,128)S(1)}, s32[8,16,64]{2,1,0:T(8,128)}, u32[]{:S(2)}) copy-start(s32[8,16,64]{2,1,0:T(8,128)} %param.30) | copy-start | bytes 98308
  104.0 21.9 %collective-permute-start.15 = (bf16[144,640]{1,0:T(8,128)(2,1)S(1)}, bf16[144,640]{1,0:T(8,128)(2,1)S(1)}, u32[]{:S(2)}, u32[]{:S(2)}) collective-permute-start(bf16[144,640]{1,0:T(8,128)(2,1)S(1)} %get-tuple-element.38.up_ref.own_ref), channel_id=1, source_target_pairs={{32,0},{64,32},{96,64},{128,96},{160,128},{192,160},{224,192},{256... | collective-permute-start | bytes 552968 | tf_op jit(solution)/shard_map/ppermute | solution.py:353
  106.0 20.0 %collective-permute-start.14 = (bf16[144,640]{1,0:T(8,128)(2,1)S(1)}, bf16[144,640]{1,0:T(8,128)(2,1)S(1)}, u32[]{:S(2)}, u32[]{:S(2)}) collective-permute-start(bf16[144,640]{1,0:T(8,128)(2,1)S(1)} %get-tuple-element.38.up_ref.own_ref), channel_id=1, source_target_pairs={{0,32},{32,64},{64,96},{96,128},{128,160},{160,192},{192,224},{224... | collective-permute-start | bytes 552968 | tf_op jit(solution)/shard_map/ppermute | solution.py:353
  118.0 13.9 %collective-permute-start.19 = (bf16[144,640]{1,0:T(8,128)(2,1)S(1)}, bf16[144,640]{1,0:T(8,128)(2,1)S(1)}, u32[]{:S(2)}, u32[]{:S(2)}) collective-permute-start(bf16[144,640]{1,0:T(8,128)(2,1)S(1)} %get-tuple-element.38.up_ref.own_ref), channel_id=1, source_target_pairs={{0,1},{1,0},{2,3},{3,2},{4,5},{5,4},{6,7},{7,6},{8,9},{9,8},{10,11... | collective-permute-start | bytes 552968 | tf_op jit(solution)/shard_map/ppermute | solution.py:347
  119.9 12.0 %collective-permute-start.18 = (bf16[144,640]{1,0:T(8,128)(2,1)S(1)}, bf16[144,640]{1,0:T(8,128)(2,1)S(1)}, u32[]{:S(2)}, u32[]{:S(2)}) collective-permute-start(bf16[144,640]{1,0:T(8,128)(2,1)S(1)} %get-tuple-element.38.up_ref.own_ref), channel_id=1, source_target_pairs={{1,2},{3,4},{5,6},{7,8},{9,10},{11,12},{13,14},{15,16},{17,18},{19... | collective-permute-start | bytes 552968 | tf_op jit(solution)/shard_map/ppermute | solution.py:356
  126.0 8.6 %collective-permute-start.17 = (bf16[288,640]{1,0:T(8,128)(2,1)S(1)}, bf16[288,640]{1,0:T(8,128)(2,1)S(1)}, u32[]{:S(2)}, u32[]{:S(2)}) collective-permute-start(bf16[288,640]{1,0:T(8,128)(2,1)S(1)} %pad_maximum_fusion.2), channel_id=1, source_target_pairs={{0,1},{1,0},{2,3},{3,2},{4,5},{5,4},{6,7},{7,6},{8,9},{9,8},{10,11... | collective-permute-start | bytes 1105928 | tf_op jit(solution)/shard_map/ppermute | solution.py:347
  128.0 12.7 %collective-permute-start.16 = (bf16[288,640]{1,0:T(8,128)(2,1)S(1)}, bf16[288,640]{1,0:T(8,128)(2,1)S(1)}, u32[]{:S(2)}, u32[]{:S(2)}) collective-permute-start(bf16[288,640]{1,0:T(8,128)(2,1)S(1)} %pad_maximum_fusion.2), channel_id=1, source_target_pairs={{1,2},{3,4},{5,6},{7,8},{9,10},{11,12},{13,14},{15,16},{17,18},{19... | collective-permute-start | bytes 1105928 | tf_op jit(solution)/shard_map/ppermute | solution.py:356

commit v7 on v6

--- a/solution.py
+++ b/solution.py
@@ -390,10 +390,9 @@
 
     fetched, hc = lax.optimization_barrier((fetched, hidden(column)))
     right, left = along(fetched, ring), along(fetched, back)
-    right, left, he = lax.optimization_barrier((right, left, hidden(inner)))
+    right, left, he, outer = lax.optimization_barrier((right, left, hidden(inner), outer))
     fetched_too = swap(fetched)
-    upper, lower, hw = lax.optimization_barrier((along(right[:96], ring), along(left[96:], back), hidden(outer)))
-    across = jnp.concatenate([upper, lower], axis=0)
+    across, hw = lax.optimization_barrier((along(right, ring), hidden(outer)))
     blocks = (fetched, right, left, across, fetched_too, swap(right), swap(left), swap(across))
 
     win, wn = pl.pallas_call(
@@ -414,15 +413,14 @@
         cost_estimate=pl.CostEstimate(flops=6_000_000_000, bytes_accessed=8_000_000, transcendentals=1_000_000),
     )(jnp.concatenate([block_mask.reshape(30), which]), win, wn, w_pixel.T, x, measured.reshape(T, 64), filter_color.reshape(T, 64))
     before, after = rows_beside(pack)
+    near_outer, near_inner = sides(pack)
+    corners, target, stat_late = lax.optimization_barrier((jnp.concatenate([before, after], axis=0), target, stat))
+    packs_outer, packs_inner = sides(corners)
     gq = pl.pallas_call(
         query_kernel, out_shape=shaped((T, HW)), in_specs=[VMEM] * 4, out_specs=VMEM,
         scratch_shapes=[pltpu.VMEM((T, 640), F32)], compiler_params=params(16),
         cost_estimate=pl.CostEstimate(flops=4_000_000_000, bytes_accessed=6_000_000, transcendentals=0),
-    )(win, e, pack, stat)
-    pack_late, gq = lax.optimization_barrier((pack, gq))
-    near_outer, near_inner = sides(pack_late)
-    corners, target = lax.optimization_barrier((jnp.concatenate([before, after], axis=0), target))
-    packs_outer, packs_inner = sides(corners)
+    )(win, e, pack, stat_late)
     gk, gv = pl.pallas_call(
         key_near_kernel, out_shape=(shaped((T, 640), F32),) * 2, in_specs=[SMEM] + [VMEM] * 6, out_specs=(VMEM,) * 2,
         compiler_params=params(16),

time: 147 us -> 144 us (0.980)
  the two profiles are of different devices: /device:TPU:63 before, /device:TPU:47 now
where the time goes in v7:
time: 144 us; the launch traced here: 143 us
  starting transfers between devices  79.2 us (55%)
  Pallas kernels  31.1 us (22%)
  waiting for transfers between devices  23.1 us (16%)
  local copies, waits for them, and re-layouts  4.86 us (3%)
  other arithmetic  3.25 us (2%)
    ppermute x7, starting transfers between devices, swap(): return lax.ppermute(v, 'core', [(0, 1), (1, 0)])  23.1 us
    ppermute x2, starting transfers between devices, rows_beside(): lax.ppermute(own, lat + ('core',), south)  20.9 us
    ppermute x3, starting transfers between devices, sides(): return (lax.ppermute(column, lon, border), swap(column))  16.7 us
    ppermute x3, waiting for transfers between devices, along(): return lax.ppermute(v, ('x', 'core'), perm)  13.1 us
    pallas_call x1, Pallas kernels, on_device(): pl.pallas_call(project_kernel, out_shape=(shaped((9 * T, QKV)), shaped((6...  7.38 us
    ppermute x3, starting transfers between devices, along(): return lax.ppermute(v, ('x', 'core'), perm)  7.19 us
    pallas_call x3, Pallas kernels, hidden(): pl.pallas_call(hidden_kernel, out_shape=shaped((3 * T, D)), in_specs=[VME...  6.33 us
    pallas_call x1, Pallas kernels, on_device(): pl.pallas_call(forward_kernel, out_shape=(shaped((H * T, 9 * T)), shaped(...  6.12 us
  transfers between devices with their start and end apart: 19, of which 6 were waited for; matrix products, arithmetic and copies ran while one was open for 3% of the time, Pallas kernels for 8%

profile of v7, /device:TPU:47, one launch (start us, length us, event | category | flops | bytes accessed | tf_op | source)
XLA Modules:
  0.0 142.7 jit_solution(14027971853210574081)
XLA Ops:
  0.6 4.0 %collective-permute-start.3 = (bf16[128,1152]{1,0:T(8,128)(2,1)}, bf16[128,1152]{1,0:T(8,128)(2,1)S(1)}, u32[]{:S(2)}, u32[]{:S(2)}) collective-permute-start(bf16[128,1152]{1,0:T(8,128)(2,1)} %bitcast.7), channel_id=1, source_target_pairs={{32,0},{64,32},{96,64},{128,96},{160,128},{192,160},{224,192},{256... | collective-permute-start | bytes 884744 | tf_op jit(solution)/shard_map/ppermute | solution.py:353
  4.6 9.0 %collective-permute-start.2 = (bf16[128,1152]{1,0:T(8,128)(2,1)}, bf16[128,1152]{1,0:T(8,128)(2,1)S(1)}, u32[]{:S(2)}, u32[]{:S(2)}) collective-permute-start(bf16[128,1152]{1,0:T(8,128)(2,1)} %bitcast.8), channel_id=1, source_target_pairs={{0,32},{32,64},{64,96},{96,128},{128,160},{160,192},{192,224},{224... | collective-permute-start | bytes 884744 | tf_op jit(solution)/shard_map/ppermute | solution.py:353
  13.7 1.2 fusion.2
  14.9 0.7 collective-permute-start.1
  15.6 4.7 %collective-permute-start = (bf16[96,1728]{1,0:T(8,128)(2,1)S(1)}, bf16[96,1728]{1,0:T(8,128)(2,1)S(1)}, u32[]{:S(2)}, u32[]{:S(2)}) collective-permute-start(bf16[96,1728]{1,0:T(8,128)(2,1)S(1)} %fusion.2), channel_id=1, source_target_pairs={{224,0},{33,1},{194,2},{67,3},{164,4},{101,5},{134,6},{415,7},{232... | collective-permute-start | bytes 995336 | tf_op jit(solution)/shard_map/ppermute | solution.py:370
  20.3 0.7 reshape.34.gain_ref
  21.0 0.8 fusion.15
  21.8 5.3 %collective-permute-done.2 = bf16[128,1152]{1,0:T(8,128)(2,1)S(1)} collective-permute-done((bf16[128,1152]{1,0:T(8,128)(2,1)}, bf16[128,1152]{1,0:T(8,128)(2,1)S(1)}, u32[]{:S(2)}, u32[]{:S(2)}) %collective-permute-start.2) | collective-permute-done | bytes 294944 | tf_op jit(solution)/shard_map/ppermute | solution.py:353
  27.1 1.0 pad_maximum_fusion.x_ref
  28.2 8.6 %collective-permute-start.7 = (bf16[384,1152]{1,0:T(8,128)(2,1)S(1)}, bf16[384,1152]{1,0:T(8,128)(2,1)S(1)}, u32[]{:S(2)}, u32[]{:S(2)}) collective-permute-start(bf16[384,1152]{1,0:T(8,128)(2,1)S(1)} %pad_maximum_fusion.x_ref), channel_id=1, source_target_pairs={{1,2},{3,4},{5,6},{7,8},{9,10},{11,12},{13,14},{15,16},{17,18},{19... | collective-permute-start | bytes 2654216 | tf_op jit(solution)/shard_map/ppermute | solution.py:356
  36.8 1.9 %collective-permute-start.6 = (bf16[384,1152]{1,0:T(8,128)(2,1)S(1)}, bf16[384,1152]{1,0:T(8,128)(2,1)S(1)}, u32[]{:S(2)}, u32[]{:S(2)}) collective-permute-start(bf16[384,1152]{1,0:T(8,128)(2,1)S(1)} %pad_maximum_fusion.x_ref), channel_id=1, source_target_pairs={{0,1},{1,0},{2,3},{3,2},{4,5},{5,4},{6,7},{7,6},{8,9},{9,8},{10,11... | collective-permute-start | bytes 2654216 | tf_op jit(solution)/shard_map/ppermute | solution.py:347
  38.7 2.1 %shard_map.221.hc_ref = bf16[384,1152]{1,0:T(8,128)(2,1)S(1)} custom-call(bf16[384,1152]{1,0:T(8,128)(2,1)S(1)} %pad_maximum_fusion.x_ref, f32[1,1152]{1,0:T(1,128)S(1)} %reshape.34.gain_ref, s32[1,1152]{1,0:T(1,128)S(1)} %reshape.35.target_ref), custom_call_target="tpu_custom_call" | custom-call | flops 3000000000 | bytes 5000000 | tf_op jit(solution)/shard_map/pallas_call | solution.py:385
  40.8 0.9 copy-done.6
  41.8 0.1 pad_maximum_fusion.1.b0
  41.9 1.9 %collective-permute-start.5 = (bf16[192,1728]{1,0:T(8,128)(2,1)S(1)}, bf16[192,1728]{1,0:T(8,128)(2,1)S(1)}, u32[]{:S(2)}, u32[]{:S(2)}) collective-permute-start(bf16[192,1728]{1,0:T(8,128)(2,1)S(1)} %pad_maximum_fusion.1.b0), channel_id=1, source_target_pairs={{2,0},{4,2},{6,4},{0,6},{1,3},{3,5},{5,7},{7,1},{10,8},{12,10},{14... | collective-permute-start | bytes 1990664 | tf_op jit(solution)/shard_map/ppermute | solution.py:350
  43.9 3.4 %collective-permute-start.4 = (bf16[192,1728]{1,0:T(8,128)(2,1)S(1)}, bf16[192,1728]{1,0:T(8,128)(2,1)S(1)}, u32[]{:S(2)}, u32[]{:S(2)}) collective-permute-start(bf16[192,1728]{1,0:T(8,128)(2,1)S(1)} %pad_maximum_fusion.1.b0), channel_id=1, source_target_pairs={{0,2},{2,4},{4,6},{6,0},{3,1},{5,3},{7,5},{1,7},{8,10},{10,12},{12... | collective-permute-start | bytes 1990664 | tf_op jit(solution)/shard_map/ppermute | solution.py:350
  47.2 2.1 %shard_map.222.he_ref = bf16[384,1152]{1,0:T(8,128)(2,1)S(1)} custom-call(bf16[384,1152]{1,0:T(8,128)(2,1)S(1)} %collective-permute-done.6.x_ref, f32[1,1152]{1,0:T(1,128)S(1)} %reshape.34.gain_ref, s32[1,1152]{1,0:T(1,128)S(1)} %reshape.35.target_ref), custom_call_target="tpu_custom_call" | custom-call | flops 3000000000 | bytes 5000000 | tf_op jit(solution)/shard_map/pallas_call | solution.py:385
  49.4 0.9 copy-done.8
  50.3 9.7 %collective-permute-done.5.b2 = bf16[192,1728]{1,0:T(8,128)(2,1)S(1)} collective-permute-done((bf16[192,1728]{1,0:T(8,128)(2,1)S(1)}, bf16[192,1728]{1,0:T(8,128)(2,1)S(1)}, u32[]{:S(2)}, u32[]{:S(2)}) %collective-permute-start.5) | collective-permute-done | bytes 663584 | tf_op jit(solution)/shard_map/ppermute | solution.py:350
  60.0 3.1 %collective-permute-done.4.b1 = bf16[192,1728]{1,0:T(8,128)(2,1)S(1)} collective-permute-done((bf16[192,1728]{1,0:T(8,128)(2,1)S(1)}, bf16[192,1728]{1,0:T(8,128)(2,1)S(1)}, u32[]{:S(2)}, u32[]{:S(2)}) %collective-permute-start.4) | collective-permute-done | bytes 663584 | tf_op jit(solution)/shard_map/ppermute | solution.py:350
  63.1 0.9 copy-done.1
  64.1 1.9 %collective-permute-start.8 = (bf16[192,1728]{1,0:T(8,128)(2,1)S(1)}, bf16[192,1728]{1,0:T(8,128)(2,1)S(1)}, u32[]{:S(2)}, u32[]{:S(2)}) collective-permute-start(bf16[192,1728]{1,0:T(8,128)(2,1)S(1)} %collective-permute-done.4.b1), channel_id=1, source_target_pairs={{0,2},{2,4},{4,6},{6,0},{3,1},{5,3},{7,5},{1,7},{8,10},{10,12},{12... | collective-permute-start | bytes 1990664 | tf_op jit(solution)/shard_map/ppermute | solution.py:350
  66.0 0.0 copy-start.14
  66.0 0.0 copy-start.17
  66.0 0.0 copy-start.16
  66.1 0.1 reshape.31
  66.2 2.9 %collective-permute-start.9 = (bf16[192,1728]{1,0:T(8,128)(2,1)S(1)}, bf16[192,1728]{1,0:T(8,128)(2,1)S(1)}, u32[]{:S(2)}, u32[]{:S(2)}) collective-permute-start(bf16[192,1728]{1,0:T(8,128)(2,1)S(1)} %pad_maximum_fusion.1.b0), channel_id=1, source_target_pairs={{0,1},{1,0},{2,3},{3,2},{4,5},{5,4},{6,7},{7,6},{8,9},{9,8},{10,11... | collective-permute-start | bytes 1990664 | tf_op jit(solution)/shard_map/ppermute | solution.py:347
  69.1 1.9 %collective-permute-start.10 = (bf16[192,1728]{1,0:T(8,128)(2,1)S(1)}, bf16[192,1728]{1,0:T(8,128)(2,1)S(1)}, u32[]{:S(2)}, u32[]{:S(2)}) collective-permute-start(bf16[192,1728]{1,0:T(8,128)(2,1)S(1)} %collective-permute-done.4.b1), channel_id=1, source_target_pairs={{0,1},{1,0},{2,3},{3,2},{4,5},{5,4},{6,7},{7,6},{8,9},{9,8},{10,11... | collective-permute-start | bytes 1990664 | tf_op jit(solution)/shard_map/ppermute | solution.py:347
  71.0 2.4 %collective-permute-start.11 = (bf16[192,1728]{1,0:T(8,128)(2,1)S(1)}, bf16[192,1728]{1,0:T(8,128)(2,1)S(1)}, u32[]{:S(2)}, u32[]{:S(2)}) collective-permute-start(bf16[192,1728]{1,0:T(8,128)(2,1)S(1)} %collective-permute-done.5.b2), channel_id=1, source_target_pairs={{0,1},{1,0},{2,3},{3,2},{4,5},{5,4},{6,7},{7,6},{8,9},{9,8},{10,11... | collective-permute-start | bytes 1990664 | tf_op jit(solution)/shard_map/ppermute | solution.py:347
  73.4 1.2 copy-done.2
  74.6 2.1 %shard_map.223.hw_ref = bf16[384,1152]{1,0:T(8,128)(2,1)S(1)} custom-call(bf16[384,1152]{1,0:T(8,128)(2,1)S(1)} %copy-done.2, f32[1,1152]{1,0:T(1,128)S(1)} %reshape.34.gain_ref, s32[1,1152]{1,0:T(1,128)S(1)} %reshape.35.target_ref), custom_call_target="tpu_custom_call" | custom-call | flops 3000000000 | bytes 5000000 | tf_op jit(solution)/shard_map/pallas_call | solution.py:385
  76.7 0.2 collective-permute-done.8.b3
  76.9 2.1 %collective-permute-start.12 = (bf16[192,1728]{1,0:T(8,128)(2,1)S(1)}, bf16[192,1728]{1,0:T(8,128)(2,1)S(1)}, u32[]{:S(2)}, u32[]{:S(2)}) collective-permute-start(bf16[192,1728]{1,0:T(8,128)(2,1)S(1)} %collective-permute-done.8.b3), channel_id=1, source_target_pairs={{0,1},{1,0},{2,3},{3,2},{4,5},{5,4},{6,7},{7,6},{8,9},{9,8},{10,11... | collective-permute-start | bytes 1990664 | tf_op jit(solution)/shard_map/ppermute | solution.py:347
  79.2 0.1 pad_add_fusion.1.blocks_ref
  79.4 1.6 %collective-permute-done.12.b7 = bf16[192,1728]{1,0:T(8,128)(2,1)S(1)} collective-permute-done((bf16[192,1728]{1,0:T(8,128)(2,1)S(1)}, bf16[192,1728]{1,0:T(8,128)(2,1)S(1)}, u32[]{:S(2)}, u32[]{:S(2)}) %collective-permute-start.12) | collective-permute-done | bytes 663584 | tf_op jit(solution)/shard_map/ppermute | solution.py:347
  81.0 7.4 %shard_map.224 = (bf16[1152,1728]{1,0:T(8,128)(2,1)S(1)}, bf16[640,1152]{1,0:T(8,128)(2,1)S(1)}) custom-call(s32[3,384]{1,0:T(4,128)S(1)} %pad_add_fusion.place_ref, bf16[384,1152]{1,0:T(8,128)(2,1)S(1)} %shard_map.223.hw_ref, bf16[384,1152]{1,0:T(8,128)(2,1)S(1)} %copy-done.7, bf16[384,1152]{1,0:T(8,128)(2,1)S(1)} %copy-done.9, ...), custom_call_target="tpu_custom_call" | custom-call | flops 6000000000 | bytes 8000000 | tf_op jit(solution)/shard_map/pallas_call | solution.py:398
  88.4 6.1 %shard_map.225 = (bf16[1024,1152]{1,0:T(8,128)(2,1)S(1)}, bf16[128,1152]{1,0:T(8,128)(2,1)}, f32[128,1152]{1,0:T(8,128)S(1)}, bf16[144,640]{1,0:T(8,128)(2,1)S(1)}, f32[128,128]{1,0:T(8,128)S(1)}) custom-call(s32[31]{0:T(128)S(1)} %pad_add_fusion.1.blocks_ref, bf16[1152,1728]{1,0:T(8,128)(2,1)S(1)} %get-tuple-element.30.win_ref, ...), custom_call_target="tpu_custom_call" | custom-call | flops 6000000000 | bytes 8000000 | tf_op jit(solution)/shard_map/pallas_call | solution.py:405
  94.5 1.9 %collective-permute-start.14 = (bf16[144,640]{1,0:T(8,128)(2,1)S(1)}, bf16[144,640]{1,0:T(8,128)(2,1)S(1)}, u32[]{:S(2)}, u32[]{:S(2)}) collective-permute-start(bf16[144,640]{1,0:T(8,128)(2,1)S(1)} %get-tuple-element.33.own_ref.up_ref), channel_id=1, source_target_pairs={{32,0},{64,32},{96,64},{128,96},{160,128},{192,160},{224,192},{256... | collective-permute-start | bytes 552968 | tf_op jit(solution)/shard_map/ppermute | solution.py:353
  96.4 11.9 %collective-permute-start.13 = (bf16[144,640]{1,0:T(8,128)(2,1)S(1)}, bf16[144,640]{1,0:T(8,128)(2,1)S(1)}, u32[]{:S(2)}, u32[]{:S(2)}) collective-permute-start(bf16[144,640]{1,0:T(8,128)(2,1)S(1)} %get-tuple-element.33.own_ref.up_ref), channel_id=1, source_target_pairs={{0,32},{32,64},{64,96},{96,128},{128,160},{160,192},{192,224},{224... | collective-permute-start | bytes 552968 | tf_op jit(solution)/shard_map/ppermute | solution.py:353
  108.3 2.3 %collective-permute-start.18 = (bf16[144,640]{1,0:T(8,128)(2,1)S(1)}, bf16[144,640]{1,0:T(8,128)(2,1)S(1)}, u32[]{:S(2)}, u32[]{:S(2)}) collective-permute-start(bf16[144,640]{1,0:T(8,128)(2,1)S(1)} %get-tuple-element.33.own_ref.up_ref), channel_id=1, source_target_pairs={{0,1},{1,0},{2,3},{3,2},{4,5},{5,4},{6,7},{7,6},{8,9},{9,8},{10,11... | collective-permute-start | bytes 552968 | tf_op jit(solution)/shard_map/ppermute | solution.py:347
  110.7 5.9 %collective-permute-start.17 = (bf16[144,640]{1,0:T(8,128)(2,1)S(1)}, bf16[144,640]{1,0:T(8,128)(2,1)S(1)}, u32[]{:S(2)}, u32[]{:S(2)}) collective-permute-start(bf16[144,640]{1,0:T(8,128)(2,1)S(1)} %get-tuple-element.33.own_ref.up_ref), channel_id=1, source_target_pairs={{1,2},{3,4},{5,6},{7,8},{9,10},{11,12},{13,14},{15,16},{17,18},{19... | collective-permute-start | bytes 552968 | tf_op jit(solution)/shard_map/ppermute | solution.py:356
  116.6 9.6 %collective-permute-start.16 = (bf16[288,640]{1,0:T(8,128)(2,1)S(1)}, bf16[288,640]{1,0:T(8,128)(2,1)S(1)}, u32[]{:S(2)}, u32[]{:S(2)}) collective-permute-start(bf16[288,640]{1,0:T(8,128)(2,1)S(1)} %pad_maximum_fusion.2), channel_id=1, source_target_pairs={{0,1},{1,0},{2,3},{3,2},{4,5},{5,4},{6,7},{7,6},{8,9},{9,8},{10,11... | collective-permute-start | bytes 1105928 | tf_op jit(solution)/shard_map/ppermute | solution.py:347
  126.2 2.2 %collective-permute-start.15 = (bf16[288,640]{1,0:T(8,128)(2,1)S(1)}, bf16[288,640]{1,0:T(8,128)(2,1)S(1)}, u32[]{:S(2)}, u32[]{:S(2)}) collective-permute-start(bf16[288,640]{1,0:T(8,128)(2,1)S(1)} %pad_maximum_fusion.2), channel_id=1, source_target_pairs={{1,2},{3,4},{5,6},{7,8},{9,10},{11,12},{13,14},{15,16},{17,18},{19... | collective-permute-start | bytes 1105928 | tf_op jit(solution)/shard_map/ppermute | solution.py:356
  128.4 2.4 %shard_map.227.gq_ref = bf16[128,576]{1,0:T(8,128)(2,1)S(1)} custom-call(bf16[1152,1728]{1,0:T(8,128)(2,1)S(1)} %get-tuple-element.30.win_ref, bf16[1024,1152]{1,0:T(8,128)(2,1)S(1)} %get-tuple-element.38.e_ref, bf16[144,640]{1,0:T(8,128)(2,1)S(1)} %get-tuple-element.33.own_ref.up_ref, f32[128,128]{1,0:T(8,128)S(1)} %get-tuple-element.39.stat_ref), custom_call_target="tpu_custom_call" | custom-call | flops 4000000000 | bytes 6000000 | tf_op jit(solution)/shard_map/pallas_call | solution.py:419
  130.8 0.5 shard_map.228.order_ref
  131.3 2.8 %shard_map.226 = (f32[128,640]{1,0:T(8,128)S(1)}, f32[128,640]{1,0:T(8,128)S(1)}) custom-call(s32[1]{0:T(128)} %bitcast.core_ref, bf16[1152,1728]{1,0:T(8,128)(2,1)S(1)} %get-tuple-element.30.win_ref, bf16[144,640]{1,0:T(8,128)(2,1)S(1)} %get-tuple-element.33.own_ref.up_ref, bf16[144,640]{1,0:T(8,128)(2,1)S(1)} %collective-permute-done.13.before_ref, ...), custom_call_target="tpu_custom_call" | custom-call | flops 4000000000 | bytes 6000000 | tf_op jit(solution)/shard_map/pallas_call | solution.py:424
  134.1 3.0 %collective-permute-done.15.packo_ref = bf16[288,640]{1,0:T(8,128)(2,1)S(1)} collective-permute-done((bf16[288,640]{1,0:T(8,128)(2,1)S(1)}, bf16[288,640]{1,0:T(8,128)(2,1)S(1)}, u32[]{:S(2)}, u32[]{:S(2)}) %collective-permute-start.15) | collective-permute-done | bytes 368672 | tf_op jit(solution)/shard_map/ppermute | solution.py:356
  137.1 5.6 %shard_map.229 = f32[128,1152]{1,0:T(8,128)} custom-call(s32[1]{0:T(128)} %bitcast.core_ref, bf16[1152,1728]{1,0:T(8,128)(2,1)S(1)} %get-tuple-element.30.win_ref, bf16[288,640]{1,0:T(8,128)(2,1)S(1)} %collective-permute-done.15.packo_ref, bf16[288,640]{1,0:T(8,128)(2,1)S(1)} %collective-permute-done.16.packi_ref, f32[128,640]{1,0:T(8,128)S(1)} %get-tuple-element.36.gk0_ref, ...), custom_call_target="tpu_custom_call" | custom-call | tf_op jit(solution)/shard_map/pallas_call | solution.py:429
  (57 shorter events, 0.3 us)
Async XLA Ops:
  0.6 21.2 %collective-permute-start.3 = (bf16[128,1152]{1,0:T(8,128)(2,1)}, bf16[128,1152]{1,0:T(8,128)(2,1)S(1)}, u32[]{:S(2)}, u32[]{:S(2)}) collective-permute-start(bf16[128,1152]{1,0:T(8,128)(2,1)} %bitcast.7), channel_id=1, source_target_pairs={{32,0},{64,32},{96,64},{128,96},{160,128},{192,160},{224,192},{256... | collective-permute-start | bytes 884744 | tf_op jit(solution)/shard_map/ppermute | solution.py:353
  4.6 22.5 %collective-permute-start.2 = (bf16[128,1152]{1,0:T(8,128)(2,1)}, bf16[128,1152]{1,0:T(8,128)(2,1)S(1)}, u32[]{:S(2)}, u32[]{:S(2)}) collective-permute-start(bf16[128,1152]{1,0:T(8,128)(2,1)} %bitcast.8), channel_id=1, source_target_pairs={{0,32},{32,64},{64,96},{96,128},{128,160},{160,192},{192,224},{224... | collective-permute-start | bytes 884744 | tf_op jit(solution)/shard_map/ppermute | solution.py:353
  14.9 26.8 %collective-permute-start.1 = (bf16[96,1728]{1,0:T(8,128)(2,1)S(1)}, bf16[96,1728]{1,0:T(8,128)(2,1)S(1)}, u32[]{:S(2)}, u32[]{:S(2)}) collective-permute-start(bf16[96,1728]{1,0:T(8,128)(2,1)S(1)} %fusion.2), channel_id=1, source_target_pairs={{440,0},{377,1},{474,2},{347,3},{508,4},{317,5},{286,6},{7,7},{432... | collective-permute-start | bytes 995336 | tf_op jit(solution)/shard_map/ppermute | solution.py:370
  15.6 26.2 %collective-permute-start = (bf16[96,1728]{1,0:T(8,128)(2,1)S(1)}, bf16[96,1728]{1,0:T(8,128)(2,1)S(1)}, u32[]{:S(2)}, u32[]{:S(2)}) collective-permute-start(bf16[96,1728]{1,0:T(8,128)(2,1)S(1)} %fusion.2), channel_id=1, source_target_pairs={{224,0},{33,1},{194,2},{67,3},{164,4},{101,5},{134,6},{415,7},{232... | collective-permute-start | bytes 995336 | tf_op jit(solution)/shard_map/ppermute | solution.py:370
  28.2 35.0 %collective-permute-start.7 = (bf16[384,1152]{1,0:T(8,128)(2,1)S(1)}, bf16[384,1152]{1,0:T(8,128)(2,1)S(1)}, u32[]{:S(2)}, u32[]{:S(2)}) collective-permute-start(bf16[384,1152]{1,0:T(8,128)(2,1)S(1)} %pad_maximum_fusion.x_ref), channel_id=1, source_target_pairs={{1,2},{3,4},{5,6},{7,8},{9,10},{11,12},{13,14},{15,16},{17,18},{19... | collective-permute-start | bytes 2654216 | tf_op jit(solution)/shard_map/ppermute | solution.py:356
  36.8 10.4 %collective-permute-start.6 = (bf16[384,1152]{1,0:T(8,128)(2,1)S(1)}, bf16[384,1152]{1,0:T(8,128)(2,1)S(1)}, u32[]{:S(2)}, u32[]{:S(2)}) collective-permute-start(bf16[384,1152]{1,0:T(8,128)(2,1)S(1)} %pad_maximum_fusion.x_ref), channel_id=1, source_target_pairs={{0,1},{1,0},{2,3},{3,2},{4,5},{5,4},{6,7},{7,6},{8,9},{9,8},{10,11... | collective-permute-start | bytes 2654216 | tf_op jit(solution)/shard_map/ppermute | solution.py:347
  40.8 0.9 copy-start.6
  41.9 24.1 %copy-start.11 = (s32[1,2,3,5]{3,1,2,0:T(2,128)S(1)}, s32[1,2,3,5]{3,1,2,0:T(2,128)}, u32[]{:S(2)}) copy-start(s32[1,2,3,5]{3,1,2,0:T(2,128)} %param.31) | copy-start | bytes 364
  41.9 18.1 %collective-permute-start.5 = (bf16[192,1728]{1,0:T(8,128)(2,1)S(1)}, bf16[192,1728]{1,0:T(8,128)(2,1)S(1)}, u32[]{:S(2)}, u32[]{:S(2)}) collective-permute-start(bf16[192,1728]{1,0:T(8,128)(2,1)S(1)} %pad_maximum_fusion.1.b0), channel_id=1, source_target_pairs={{2,0},{4,2},{6,4},{0,6},{1,3},{3,5},{5,7},{7,1},{10,8},{12,10},{14... | collective-permute-start | bytes 1990664 | tf_op jit(solution)/shard_map/ppermute | solution.py:350
  43.9 19.3 %collective-permute-start.4 = (bf16[192,1728]{1,0:T(8,128)(2,1)S(1)}, bf16[192,1728]{1,0:T(8,128)(2,1)S(1)}, u32[]{:S(2)}, u32[]{:S(2)}) collective-permute-start(bf16[192,1728]{1,0:T(8,128)(2,1)S(1)} %pad_maximum_fusion.1.b0), channel_id=1, source_target_pairs={{0,2},{2,4},{4,6},{6,0},{3,1},{5,3},{7,5},{1,7},{8,10},{10,12},{12... | collective-permute-start | bytes 1990664 | tf_op jit(solution)/shard_map/ppermute | solution.py:350
  49.3 0.9 copy-start.8
  63.1 0.9 copy-start.1
  64.1 12.9 %collective-permute-start.8 = (bf16[192,1728]{1,0:T(8,128)(2,1)S(1)}, bf16[192,1728]{1,0:T(8,128)(2,1)S(1)}, u32[]{:S(2)}, u32[]{:S(2)}) collective-permute-start(bf16[192,1728]{1,0:T(8,128)(2,1)S(1)} %collective-permute-done.4.b1), channel_id=1, source_target_pairs={{0,2},{2,4},{4,6},{6,0},{3,1},{5,3},{7,5},{1,7},{8,10},{10,12},{12... | collective-permute-start | bytes 1990664 | tf_op jit(solution)/shard_map/ppermute | solution.py:350
  66.0 13.1 %copy-start.13 = (s32[384]{0:T(512)S(1)}, s32[384]{0:T(512)}, u32[]{:S(2)}) copy-start(s32[384]{0:T(512)} %constant.86.clone) | copy-start | bytes 4612
  66.0 13.1 %copy-start.14 = (s32[384]{0:T(512)S(1)}, s32[384]{0:T(512)}, u32[]{:S(2)}) copy-start(s32[384]{0:T(512)} %constant.85.clone) | copy-start | bytes 4612
  66.0 13.0 %copy-start.17 = (pred[384]{0:T(512)(128)(4,1)S(1)}, pred[384]{0:T(512)(128)(4,1)}, u32[]{:S(2)}) copy-start(pred[384]{0:T(512)(128)(4,1)} %constant.88.clone) | copy-start | bytes 1156
  66.0 13.1 %copy-start.16 = (pred[384]{0:T(512)(128)(4,1)S(1)}, pred[384]{0:T(512)(128)(4,1)}, u32[]{:S(2)}) copy-start(pred[384]{0:T(512)(128)(4,1)} %constant.90.clone) | copy-start | bytes 1156
  66.1 13.0 %copy-start.10 = (s32[384]{0:T(512)S(1)}, s32[384]{0:T(512)}, u32[]{:S(2)}) copy-start(s32[384]{0:T(512)} %constant.89.clone) | copy-start | bytes 4612
  66.1 13.0 %copy-start.12 = (s32[384]{0:T(512)S(1)}, s32[384]{0:T(512)}, u32[]{:S(2)}) copy-start(s32[384]{0:T(512)} %constant.87.clone) | copy-start | bytes 4612
  66.1 13.1 %copy-start.15 = (pred[384]{0:T(512)(128)(4,1)S(1)}, pred[384]{0:T(512)(128)(4,1)}, u32[]{:S(2)}) copy-start(pred[384]{0:T(512)(128)(4,1)} %constant.91.clone) | copy-start | bytes 1156
  66.2 13.2 %collective-permute-start.9 = (bf16[192,1728]{1,0:T(8,128)(2,1)S(1)}, bf16[192,1728]{1,0:T(8,128)(2,1)S(1)}, u32[]{:S(2)}, u32[]{:S(2)}) collective-permute-start(bf16[192,1728]{1,0:T(8,128)(2,1)S(1)} %pad_maximum_fusion.1.b0), channel_id=1, source_target_pairs={{0,1},{1,0},{2,3},{3,2},{4,5},{5,4},{6,7},{7,6},{8,9},{9,8},{10,11... | collective-permute-start | bytes 1990664 | tf_op jit(solution)/shard_map/ppermute | solution.py:347
  69.1 10.3 %collective-permute-start.10 = (bf16[192,1728]{1,0:T(8,128)(2,1)S(1)}, bf16[192,1728]{1,0:T(8,128)(2,1)S(1)}, u32[]{:S(2)}, u32[]{:S(2)}) collective-permute-start(bf16[192,1728]{1,0:T(8,128)(2,1)S(1)} %collective-permute-done.4.b1), channel_id=1, source_target_pairs={{0,1},{1,0},{2,3},{3,2},{4,5},{5,4},{6,7},{7,6},{8,9},{9,8},{10,11... | collective-permute-start | bytes 1990664 | tf_op jit(solution)/shard_map/ppermute | solution.py:347
  71.0 8.3 %collective-permute-start.11 = (bf16[192,1728]{1,0:T(8,128)(2,1)S(1)}, bf16[192,1728]{1,0:T(8,128)(2,1)S(1)}, u32[]{:S(2)}, u32[]{:S(2)}) collective-permute-start(bf16[192,1728]{1,0:T(8,128)(2,1)S(1)} %collective-permute-done.5.b2), channel_id=1, source_target_pairs={{0,1},{1,0},{2,3},{3,2},{4,5},{5,4},{6,7},{7,6},{8,9},{9,8},{10,11... | collective-permute-start | bytes 1990664 | tf_op jit(solution)/shard_map/ppermute | solution.py:347
  73.4 1.2 copy-start.2
  74.6 6.4 %copy-start.7 = (bf16[384,1152]{1,0:T(8,128)(2,1)S(1)}, bf16[384,1152]{1,0:T(8,128)(2,1)}, u32[]{:S(2)}) copy-start(bf16[384,1152]{1,0:T(8,128)(2,1)} %copy-done.6) | copy-start | bytes 2654212
  74.6 6.4 %copy-start.9 = (bf16[384,1152]{1,0:T(8,128)(2,1)S(1)}, bf16[384,1152]{1,0:T(8,128)(2,1)}, u32[]{:S(2)}) copy-start(bf16[384,1152]{1,0:T(8,128)(2,1)} %copy-done.8) | copy-start | bytes 2654212
  76.9 4.0 %collective-permute-start.12 = (bf16[192,1728]{1,0:T(8,128)(2,1)S(1)}, bf16[192,1728]{1,0:T(8,128)(2,1)S(1)}, u32[]{:S(2)}, u32[]{:S(2)}) collective-permute-start(bf16[192,1728]{1,0:T(8,128)(2,1)S(1)} %collective-permute-done.8.b3), channel_id=1, source_target_pairs={{0,1},{1,0},{2,3},{3,2},{4,5},{5,4},{6,7},{7,6},{8,9},{9,8},{10,11... | collective-permute-start | bytes 1990664 | tf_op jit(solution)/shard_map/ppermute | solution.py:347
  79.3 9.1 %copy-start = (bf16[8,16,1152]{2,1,0:T(8,128)(2,1)S(1)}, bf16[8,16,1152]{2,1,0:T(8,128)(2,1)}, u32[]{:S(2)}) copy-start(bf16[8,16,1152]{2,1,0:T(8,128)(2,1)} %param.22) | copy-start | bytes 884740
  79.3 9.1 %copy-start.3 = (bf16[1152,192]{0,1:T(8,128)(2,1)S(1)}, bf16[1152,192]{0,1:T(8,128)(2,1)}, u32[]{:S(2)}) copy-start(bf16[1152,192]{0,1:T(8,128)(2,1)} %param.28) | copy-start | bytes 1327108
  79.3 9.1 %copy-start.4 = (f32[8,16,64]{2,1,0:T(8,128)S(1)}, f32[8,16,64]{2,1,0:T(8,128)}, u32[]{:S(2)}) copy-start(f32[8,16,64]{2,1,0:T(8,128)} %param.29) | copy-start | bytes 98308
  79.3 9.1 %copy-start.5 = (s32[8,16,64]{2,1,0:T(8,128)S(1)}, s32[8,16,64]{2,1,0:T(8,128)}, u32[]{:S(2)}) copy-start(s32[8,16,64]{2,1,0:T(8,128)} %param.30) | copy-start | bytes 98308
  94.5 22.0 %collective-permute-start.14 = (bf16[144,640]{1,0:T(8,128)(2,1)S(1)}, bf16[144,640]{1,0:T(8,128)(2,1)S(1)}, u32[]{:S(2)}, u32[]{:S(2)}) collective-permute-start(bf16[144,640]{1,0:T(8,128)(2,1)S(1)} %get-tuple-element.33.own_ref.up_ref), channel_id=1, source_target_pairs={{32,0},{64,32},{96,64},{128,96},{160,128},{192,160},{224,192},{256... | collective-permute-start | bytes 552968 | tf_op jit(solution)/shard_map/ppermute | solution.py:353
  96.4 20.1 %collective-permute-start.13 = (bf16[144,640]{1,0:T(8,128)(2,1)S(1)}, bf16[144,640]{1,0:T(8,128)(2,1)S(1)}, u32[]{:S(2)}, u32[]{:S(2)}) collective-permute-start(bf16[144,640]{1,0:T(8,128)(2,1)S(1)} %get-tuple-element.33.own_ref.up_ref), channel_id=1, source_target_pairs={{0,32},{32,64},{64,96},{96,128},{128,160},{160,192},{192,224},{224... | collective-permute-start | bytes 552968 | tf_op jit(solution)/shard_map/ppermute | solution.py:353
  108.3 23.0 %collective-permute-start.18 = (bf16[144,640]{1,0:T(8,128)(2,1)S(1)}, bf16[144,640]{1,0:T(8,128)(2,1)S(1)}, u32[]{:S(2)}, u32[]{:S(2)}) collective-permute-start(bf16[144,640]{1,0:T(8,128)(2,1)S(1)} %get-tuple-element.33.own_ref.up_ref), channel_id=1, source_target_pairs={{0,1},{1,0},{2,3},{3,2},{4,5},{5,4},{6,7},{7,6},{8,9},{9,8},{10,11... | collective-permute-start | bytes 552968 | tf_op jit(solution)/shard_map/ppermute | solution.py:347
  110.7 20.6 %collective-permute-start.17 = (bf16[144,640]{1,0:T(8,128)(2,1)S(1)}, bf16[144,640]{1,0:T(8,128)(2,1)S(1)}, u32[]{:S(2)}, u32[]{:S(2)}) collective-permute-start(bf16[144,640]{1,0:T(8,128)(2,1)S(1)} %get-tuple-element.33.own_ref.up_ref), channel_id=1, source_target_pairs={{1,2},{3,4},{5,6},{7,8},{9,10},{11,12},{13,14},{15,16},{17,18},{19... | collective-permute-start | bytes 552968 | tf_op jit(solution)/shard_map/ppermute | solution.py:356
  116.6 17.5 %collective-permute-start.16 = (bf16[288,640]{1,0:T(8,128)(2,1)S(1)}, bf16[288,640]{1,0:T(8,128)(2,1)S(1)}, u32[]{:S(2)}, u32[]{:S(2)}) collective-permute-start(bf16[288,640]{1,0:T(8,128)(2,1)S(1)} %pad_maximum_fusion.2), channel_id=1, source_target_pairs={{0,1},{1,0},{2,3},{3,2},{4,5},{5,4},{6,7},{7,6},{8,9},{9,8},{10,11... | collective-permute-start | bytes 1105928 | tf_op jit(solution)/shard_map/ppermute | solution.py:347
  126.2 10.9 %collective-permute-start.15 = (bf16[288,640]{1,0:T(8,128)(2,1)S(1)}, bf16[288,640]{1,0:T(8,128)(2,1)S(1)}, u32[]{:S(2)}, u32[]{:S(2)}) collective-permute-start(bf16[288,640]{1,0:T(8,128)(2,1)S(1)} %pad_maximum_fusion.2), channel_id=1, source_target_pairs={{1,2},{3,4},{5,6},{7,8},{9,10},{11,12},{13,14},{15,16},{17,18},{19... | collective-permute-start | bytes 1105928 | tf_op jit(solution)/shard_map/ppermute | solution.py:356

commit v8 on v7

--- a/solution.py
+++ b/solution.py
@@ -368,7 +368,6 @@
         + jnp.where(at_row >= 72, lefts, 0) + jnp.where((at_row >= 84) & (at_col >= D), rights, 0)
     )
     one, two = lax.ppermute(mine, lat + lon, first), lax.ppermute(mine, lat + lon, second)
-    fetched = jnp.concatenate([one[:72], two[:72], one[72:], two[72:]], axis=0)
     before, after = rows_beside(x)
     column = jnp.concatenate([before, x, after], axis=0)
     outer, inner = sides(column)
@@ -388,12 +387,18 @@
             cost_estimate=pl.CostEstimate(flops=3_000_000_000, bytes_accessed=5_000_000, transcendentals=0),
         )(v, gain, target)
 
-    fetched, hc = lax.optimization_barrier((fetched, hidden(column)))
-    right, left = along(fetched, ring), along(fetched, back)
-    right, left, he, outer = lax.optimization_barrier((right, left, hidden(inner), outer))
-    fetched_too = swap(fetched)
-    across, hw = lax.optimization_barrier((along(right, ring), hidden(outer)))
-    blocks = (fetched, right, left, across, fetched_too, swap(right), swap(left), swap(across))
+    two, hc = lax.optimization_barrier((two, hidden(column)))
+
+    def block(p, q):
+        return jnp.concatenate([p[:72], q[:72], p[72:], q[72:]], axis=0)
+
+    right_one, left_one = along(one, ring), along(one, back)
+    right_two, left_two = along(two, ring), along(two, back)
+    across_one = along(right_one, ring)
+    right_two, left_two, he, outer = lax.optimization_barrier((right_two, left_two, hidden(inner), outer))
+    across_two, hw = lax.optimization_barrier((along(right_two, ring), hidden(outer)))
+    held = (block(one, two), block(right_one, right_two), block(left_one, left_two), block(across_one, across_two))
+    blocks = held + tuple(swap(v) for v in held)
 
     win, wn = pl.pallas_call(
         project_kernel, out_shape=(shaped((9 * T, QKV)), shaped((640, D))),

time: 144 us -> 158 us (1.097)
  the two profiles are of different devices: /device:TPU:47 before, /device:TPU:48 now
where the time goes in v8:
time: 158 us; the launch traced here: 157 us
  starting transfers between devices  75.4 us (48%)
  waiting for transfers between devices  40.7 us (26%)
  Pallas kernels  31.1 us (20%)
  local copies, waits for them, and re-layouts  5.92 us (4%)
  other arithmetic  2.67 us (2%)
    ppermute x2, starting transfers between devices, rows_beside(): lax.ppermute(own, lat + ('core',), north)  21.5 us
    ppermute x6, starting transfers between devices, along(): return lax.ppermute(v, ('x', 'core'), perm)  20.6 us
    ppermute x6, waiting for transfers between devices, along(): return lax.ppermute(v, ('x', 'core'), perm)  15.3 us
    ppermute x7, starting transfers between devices, swap(): return lax.ppermute(v, 'core', [(0, 1), (1, 0)])  15.2 us
    ppermute x2, waiting for transfers between devices, rows_beside(): lax.ppermute(own, lat + ('core',), south)  12 us
    ppermute x3, starting transfers between devices, sides(): return (lax.ppermute(column, lon, border), swap(column))  10.5 us
    ppermute x2, waiting for transfers between devices, rows_beside(): lax.ppermute(own, lat + ('core',), north)  8.6 us
    pallas_call x1, Pallas kernels, on_device(): pl.pallas_call(project_kernel, out_shape=(shaped((9 * T, QKV)), shaped((6...  7.43 us
  transfers between devices with their start and end apart: 22, of which 8 were waited for; matrix products, arithmetic and copies ran while one was open for 5% of the time, Pallas kernels for 8%

profile of v8, /device:TPU:48, one launch (start us, length us, event | category | flops | bytes accessed | tf_op | source)
XLA Modules:
  0.0 157.3 jit_solution(15435361827089878245)
XLA Ops:
  0.7 12.4 %collective-permute-start.2 = (bf16[128,1152]{1,0:T(8,128)(2,1)}, bf16[128,1152]{1,0:T(8,128)(2,1)S(1)}, u32[]{:S(2)}, u32[]{:S(2)}) collective-permute-start(bf16[128,1152]{1,0:T(8,128)(2,1)} %bitcast.7), channel_id=1, source_target_pairs={{32,0},{64,32},{96,64},{128,96},{160,128},{192,160},{224,192},{256... | collective-permute-start | bytes 884744 | tf_op jit(solution)/shard_map/ppermute | solution.py:353
  13.1 1.9 %collective-permute-start.1 = (bf16[128,1152]{1,0:T(8,128)(2,1)}, bf16[128,1152]{1,0:T(8,128)(2,1)S(1)}, u32[]{:S(2)}, u32[]{:S(2)}) collective-permute-start(bf16[128,1152]{1,0:T(8,128)(2,1)} %bitcast.8), channel_id=1, source_target_pairs={{0,32},{32,64},{64,96},{96,128},{128,160},{160,192},{192,224},{224... | collective-permute-start | bytes 884744 | tf_op jit(solution)/shard_map/ppermute | solution.py:353
  15.1 1.2 fusion.2
  16.3 1.9 %collective-permute-start.8 = (bf16[96,1728]{1,0:T(8,128)(2,1)S(1)}, bf16[96,1728]{1,0:T(8,128)(2,1)}, u32[]{:S(2)}, u32[]{:S(2)}) collective-permute-start(bf16[96,1728]{1,0:T(8,128)(2,1)S(1)} %fusion.2), channel_id=1, source_target_pairs={{224,0},{33,1},{194,2},{67,3},{164,4},{101,5},{134,6},{415,7},{232... | collective-permute-start | bytes 995336 | tf_op jit(solution)/shard_map/ppermute | solution.py:370
  18.3 8.6 %collective-permute-done.2 = bf16[128,1152]{1,0:T(8,128)(2,1)S(1)} collective-permute-done((bf16[128,1152]{1,0:T(8,128)(2,1)}, bf16[128,1152]{1,0:T(8,128)(2,1)S(1)}, u32[]{:S(2)}, u32[]{:S(2)}) %collective-permute-start.2) | collective-permute-done | bytes 294944 | tf_op jit(solution)/shard_map/ppermute | solution.py:353
  26.9 4.1 %collective-permute-done.1 = bf16[128,1152]{1,0:T(8,128)(2,1)S(1)} collective-permute-done((bf16[128,1152]{1,0:T(8,128)(2,1)}, bf16[128,1152]{1,0:T(8,128)(2,1)S(1)}, u32[]{:S(2)}, u32[]{:S(2)}) %collective-permute-start.1) | collective-permute-done | bytes 294944 | tf_op jit(solution)/shard_map/ppermute | solution.py:353
  30.9 1.0 pad_maximum_fusion.x_ref
  32.0 1.9 %collective-permute-start.5 = (bf16[384,1152]{1,0:T(8,128)(2,1)S(1)}, bf16[384,1152]{1,0:T(8,128)(2,1)S(1)}, u32[]{:S(2)}, u32[]{:S(2)}) collective-permute-start(bf16[384,1152]{1,0:T(8,128)(2,1)S(1)} %pad_maximum_fusion.x_ref), channel_id=1, source_target_pairs={{0,1},{1,0},{2,3},{3,2},{4,5},{5,4},{6,7},{7,6},{8,9},{9,8},{10,11... | collective-permute-start | bytes 2654216 | tf_op jit(solution)/shard_map/ppermute | solution.py:347
  33.9 4.6 %collective-permute-start.9 = (bf16[96,1728]{1,0:T(8,128)(2,1)}, bf16[96,1728]{1,0:T(8,128)(2,1)}, u32[]{:S(2)}, u32[]{:S(2)}) collective-permute-start(bf16[96,1728]{1,0:T(8,128)(2,1)} %collective-permute-done.8), channel_id=1, source_target_pairs={{0,2},{2,4},{4,6},{6,0},{3,1},{5,3},{7,5},{1,7},{8,10},{10,12},{12... | collective-permute-start | bytes 995336 | tf_op jit(solution)/shard_map/ppermute | solution.py:350
  38.5 1.9 %collective-permute-start = (bf16[96,1728]{1,0:T(8,128)(2,1)S(1)}, bf16[96,1728]{1,0:T(8,128)(2,1)}, u32[]{:S(2)}, u32[]{:S(2)}) collective-permute-start(bf16[96,1728]{1,0:T(8,128)(2,1)S(1)} %fusion.2), channel_id=1, source_target_pairs={{440,0},{377,1},{474,2},{347,3},{508,4},{317,5},{286,6},{7,7},{432... | collective-permute-start | bytes 995336 | tf_op jit(solution)/shard_map/ppermute | solution.py:370
  40.5 5.1 %collective-permute-start.6 = (bf16[384,1152]{1,0:T(8,128)(2,1)S(1)}, bf16[384,1152]{1,0:T(8,128)(2,1)S(1)}, u32[]{:S(2)}, u32[]{:S(2)}) collective-permute-start(bf16[384,1152]{1,0:T(8,128)(2,1)S(1)} %pad_maximum_fusion.x_ref), channel_id=1, source_target_pairs={{1,2},{3,4},{5,6},{7,8},{9,10},{11,12},{13,14},{15,16},{17,18},{19... | collective-permute-start | bytes 2654216 | tf_op jit(solution)/shard_map/ppermute | solution.py:356
  45.6 5.0 %collective-permute-start.10 = (bf16[96,1728]{1,0:T(8,128)(2,1)}, bf16[96,1728]{1,0:T(8,128)(2,1)S(1)}, u32[]{:S(2)}, u32[]{:S(2)}) collective-permute-start(bf16[96,1728]{1,0:T(8,128)(2,1)} %collective-permute-done.8), channel_id=1, source_target_pairs={{2,0},{4,2},{6,4},{0,6},{1,3},{3,5},{5,7},{7,1},{10,8},{12,10},{14... | collective-permute-start | bytes 995336 | tf_op jit(solution)/shard_map/ppermute | solution.py:350
  50.7 0.1 reshape.31
  50.8 11.7 %collective-permute-done.9 = bf16[96,1728]{1,0:T(8,128)(2,1)} collective-permute-done((bf16[96,1728]{1,0:T(8,128)(2,1)}, bf16[96,1728]{1,0:T(8,128)(2,1)}, u32[]{:S(2)}, u32[]{:S(2)}) %collective-permute-start.9) | collective-permute-done | bytes 331808 | tf_op jit(solution)/shard_map/ppermute | solution.py:350
  62.5 1.9 %collective-permute-start.11 = (bf16[96,1728]{1,0:T(8,128)(2,1)}, bf16[96,1728]{1,0:T(8,128)(2,1)S(1)}, u32[]{:S(2)}, u32[]{:S(2)}) collective-permute-start(bf16[96,1728]{1,0:T(8,128)(2,1)} %collective-permute-done.9), channel_id=1, source_target_pairs={{0,2},{2,4},{4,6},{6,0},{3,1},{5,3},{7,5},{1,7},{8,10},{10,12},{12... | collective-permute-start | bytes 995336 | tf_op jit(solution)/shard_map/ppermute | solution.py:350
  64.4 2.1 %shard_map.221.hc_ref = bf16[384,1152]{1,0:T(8,128)(2,1)S(1)} custom-call(bf16[384,1152]{1,0:T(8,128)(2,1)S(1)} %pad_maximum_fusion.x_ref, f32[1,1152]{1,0:T(1,128)S(1)} %reshape.34.gain_ref, s32[1,1152]{1,0:T(1,128)S(1)} %reshape.35.target_ref), custom_call_target="tpu_custom_call" | custom-call | flops 3000000000 | bytes 5000000 | tf_op jit(solution)/shard_map/pallas_call | solution.py:384
  66.6 0.9 slice.53
  67.4 1.0 slice.51
  68.4 5.1 %collective-permute-start.4 = (bf16[96,1728]{1,0:T(8,128)(2,1)}, bf16[96,1728]{1,0:T(8,128)(2,1)S(1)}, u32[]{:S(2)}, u32[]{:S(2)}) collective-permute-start(bf16[96,1728]{1,0:T(8,128)(2,1)} %collective-permute-done), channel_id=1, source_target_pairs={{2,0},{4,2},{6,4},{0,6},{1,3},{3,5},{5,7},{7,1},{10,8},{12,10},{14... | collective-permute-start | bytes 995336 | tf_op jit(solution)/shard_map/ppermute | solution.py:350
  73.6 0.9 slice.67
  74.5 1.0 slice.66
  75.4 1.9 %collective-permute-start.3 = (bf16[96,1728]{1,0:T(8,128)(2,1)}, bf16[96,1728]{1,0:T(8,128)(2,1)S(1)}, u32[]{:S(2)}, u32[]{:S(2)}) collective-permute-start(bf16[96,1728]{1,0:T(8,128)(2,1)} %collective-permute-done), channel_id=1, source_target_pairs={{0,2},{2,4},{4,6},{6,0},{3,1},{5,3},{7,5},{1,7},{8,10},{10,12},{12... | collective-permute-start | bytes 995336 | tf_op jit(solution)/shard_map/ppermute | solution.py:350
  77.4 0.9 slice.69
  78.3 1.0 slice.68
  79.3 1.9 %collective-permute-start.12 = (bf16[192,1728]{1,0:T(8,128)(2,1)S(1)}, bf16[192,1728]{1,0:T(8,128)(2,1)S(1)}, u32[]{:S(2)}, u32[]{:S(2)}) collective-permute-start(bf16[192,1728]{1,0:T(8,128)(2,1)S(1)} %pad_maximum_fusion.1.b0), channel_id=1, source_target_pairs={{0,1},{1,0},{2,3},{3,2},{4,5},{5,4},{6,7},{7,6},{8,9},{9,8},{10,11... | collective-permute-start | bytes 1990664 | tf_op jit(solution)/shard_map/ppermute | solution.py:347
  81.3 2.1 %shard_map.222.he_ref = bf16[384,1152]{1,0:T(8,128)(2,1)S(1)} custom-call(bf16[384,1152]{1,0:T(8,128)(2,1)S(1)} %collective-permute-done.5.x_ref, f32[1,1152]{1,0:T(1,128)S(1)} %reshape.34.gain_ref, s32[1,1152]{1,0:T(1,128)S(1)} %reshape.35.target_ref), custom_call_target="tpu_custom_call" | custom-call | flops 3000000000 | bytes 5000000 | tf_op jit(solution)/shard_map/pallas_call | solution.py:384
  83.4 2.6 %collective-permute-done.3 = bf16[96,1728]{1,0:T(8,128)(2,1)S(1)} collective-permute-done((bf16[96,1728]{1,0:T(8,128)(2,1)}, bf16[96,1728]{1,0:T(8,128)(2,1)S(1)}, u32[]{:S(2)}, u32[]{:S(2)}) %collective-permute-start.3) | collective-permute-done | bytes 331808 | tf_op jit(solution)/shard_map/ppermute | solution.py:350
  86.1 1.9 %collective-permute-start.7 = (bf16[96,1728]{1,0:T(8,128)(2,1)S(1)}, bf16[96,1728]{1,0:T(8,128)(2,1)S(1)}, u32[]{:S(2)}, u32[]{:S(2)}) collective-permute-start(bf16[96,1728]{1,0:T(8,128)(2,1)S(1)} %collective-permute-done.3), channel_id=1, source_target_pairs={{0,2},{2,4},{4,6},{6,0},{3,1},{5,3},{7,5},{1,7},{8,10},{10,12},{12... | collective-permute-start | bytes 995336 | tf_op jit(solution)/shard_map/ppermute | solution.py:350
  88.1 2.9 %collective-permute-start.13 = (bf16[192,1728]{1,0:T(8,128)(2,1)S(1)}, bf16[192,1728]{1,0:T(8,128)(2,1)S(1)}, u32[]{:S(2)}, u32[]{:S(2)}) collective-permute-start(bf16[192,1728]{1,0:T(8,128)(2,1)S(1)} %pad_maximum_fusion.2.b1), channel_id=1, source_target_pairs={{0,1},{1,0},{2,3},{3,2},{4,5},{5,4},{6,7},{7,6},{8,9},{9,8},{10,11... | collective-permute-start | bytes 1990664 | tf_op jit(solution)/shard_map/ppermute | solution.py:347
  91.1 2.1 %collective-permute-start.14 = (bf16[192,1728]{1,0:T(8,128)(2,1)S(1)}, bf16[192,1728]{1,0:T(8,128)(2,1)S(1)}, u32[]{:S(2)}, u32[]{:S(2)}) collective-permute-start(bf16[192,1728]{1,0:T(8,128)(2,1)S(1)} %pad_maximum_fusion.3.b2), channel_id=1, source_target_pairs={{0,1},{1,0},{2,3},{3,2},{4,5},{5,4},{6,7},{7,6},{8,9},{9,8},{10,11... | collective-permute-start | bytes 1990664 | tf_op jit(solution)/shard_map/ppermute | solution.py:347
  93.2 2.1 %shard_map.223.hw_ref = bf16[384,1152]{1,0:T(8,128)(2,1)S(1)} custom-call(bf16[384,1152]{1,0:T(8,128)(2,1)S(1)} %collective-permute-done.6.x_ref, f32[1,1152]{1,0:T(1,128)S(1)} %reshape.34.gain_ref, s32[1,1152]{1,0:T(1,128)S(1)} %reshape.35.target_ref), custom_call_target="tpu_custom_call" | custom-call | flops 3000000000 | bytes 5000000 | tf_op jit(solution)/shard_map/pallas_call | solution.py:384
  95.4 1.1 collective-permute-done.7
  96.6 2.1 %collective-permute-start.15 = (bf16[192,1728]{1,0:T(8,128)(2,1)S(1)}, bf16[192,1728]{1,0:T(8,128)(2,1)S(1)}, u32[]{:S(2)}, u32[]{:S(2)}) collective-permute-start(bf16[192,1728]{1,0:T(8,128)(2,1)S(1)} %pad_maximum_fusion.4.b3), channel_id=1, source_target_pairs={{0,1},{1,0},{2,3},{3,2},{4,5},{5,4},{6,7},{7,6},{8,9},{9,8},{10,11... | collective-permute-start | bytes 1990664 | tf_op jit(solution)/shard_map/ppermute | solution.py:347
  99.0 1.6 %collective-permute-done.15.b7 = bf16[192,1728]{1,0:T(8,128)(2,1)S(1)} collective-permute-done((bf16[192,1728]{1,0:T(8,128)(2,1)S(1)}, bf16[192,1728]{1,0:T(8,128)(2,1)S(1)}, u32[]{:S(2)}, u32[]{:S(2)}) %collective-permute-start.15) | collective-permute-done | bytes 663584 | tf_op jit(solution)/shard_map/ppermute | solution.py:347
  100.6 7.4 %shard_map.224 = (bf16[1152,1728]{1,0:T(8,128)(2,1)S(1)}, bf16[640,1152]{1,0:T(8,128)(2,1)S(1)}) custom-call(s32[3,384]{1,0:T(4,128)S(1)} %pad_add_fusion.place_ref, bf16[384,1152]{1,0:T(8,128)(2,1)S(1)} %shard_map.223.hw_ref, bf16[384,1152]{1,0:T(8,128)(2,1)S(1)} %shard_map.221.hc_ref, bf16[384,1152]{1,0:T(8,128)(2,1)S(1)} %shard_map.222.he_ref, ...), custom_call_target="tpu_custom_call" | custom-call | flops 6000000000 | bytes 8000000 | tf_op jit(solution)/shard_map/pallas_call | solution.py:403
  108.1 6.1 %shard_map.225 = (bf16[1024,1152]{1,0:T(8,128)(2,1)S(1)}, bf16[128,1152]{1,0:T(8,128)(2,1)}, f32[128,1152]{1,0:T(8,128)S(1)}, bf16[144,640]{1,0:T(8,128)(2,1)S(1)}, f32[128,128]{1,0:T(8,128)S(1)}) custom-call(s32[31]{0:T(128)S(1)} %pad_add_fusion.1.blocks_ref, bf16[1152,1728]{1,0:T(8,128)(2,1)S(1)} %get-tuple-element.30.win_ref, ...), custom_call_target="tpu_custom_call" | custom-call | flops 6000000000 | bytes 8000000 | tf_op jit(solution)/shard_map/pallas_call | solution.py:410
  114.2 9.0 %collective-permute-start.17 = (bf16[144,640]{1,0:T(8,128)(2,1)S(1)}, bf16[144,640]{1,0:T(8,128)(2,1)S(1)}, u32[]{:S(2)}, u32[]{:S(2)}) collective-permute-start(bf16[144,640]{1,0:T(8,128)(2,1)S(1)} %get-tuple-element.33.own_ref.up_ref), channel_id=1, source_target_pairs={{32,0},{64,32},{96,64},{128,96},{160,128},{192,160},{224,192},{256... | collective-permute-start | bytes 552968 | tf_op jit(solution)/shard_map/ppermute | solution.py:353
  123.2 1.9 %collective-permute-start.16 = (bf16[144,640]{1,0:T(8,128)(2,1)S(1)}, bf16[144,640]{1,0:T(8,128)(2,1)S(1)}, u32[]{:S(2)}, u32[]{:S(2)}) collective-permute-start(bf16[144,640]{1,0:T(8,128)(2,1)S(1)} %get-tuple-element.33.own_ref.up_ref), channel_id=1, source_target_pairs={{0,32},{32,64},{64,96},{96,128},{128,160},{160,192},{192,224},{224... | collective-permute-start | bytes 552968 | tf_op jit(solution)/shard_map/ppermute | solution.py:353
  125.2 2.4 %collective-permute-start.21 = (bf16[144,640]{1,0:T(8,128)(2,1)S(1)}, bf16[144,640]{1,0:T(8,128)(2,1)S(1)}, u32[]{:S(2)}, u32[]{:S(2)}) collective-permute-start(bf16[144,640]{1,0:T(8,128)(2,1)S(1)} %get-tuple-element.33.own_ref.up_ref), channel_id=1, source_target_pairs={{0,1},{1,0},{2,3},{3,2},{4,5},{5,4},{6,7},{7,6},{8,9},{9,8},{10,11... | collective-permute-start | bytes 552968 | tf_op jit(solution)/shard_map/ppermute | solution.py:347
  127.6 3.2 %collective-permute-start.20 = (bf16[144,640]{1,0:T(8,128)(2,1)S(1)}, bf16[144,640]{1,0:T(8,128)(2,1)S(1)}, u32[]{:S(2)}, u32[]{:S(2)}) collective-permute-start(bf16[144,640]{1,0:T(8,128)(2,1)S(1)} %get-tuple-element.33.own_ref.up_ref), channel_id=1, source_target_pairs={{1,2},{3,4},{5,6},{7,8},{9,10},{11,12},{13,14},{15,16},{17,18},{19... | collective-permute-start | bytes 552968 | tf_op jit(solution)/shard_map/ppermute | solution.py:356
  130.8 8.0 %collective-permute-done.16.before_ref = bf16[144,640]{1,0:T(8,128)(2,1)S(1)} collective-permute-done((bf16[144,640]{1,0:T(8,128)(2,1)S(1)}, bf16[144,640]{1,0:T(8,128)(2,1)S(1)}, u32[]{:S(2)}, u32[]{:S(2)}) %collective-permute-start.16) | collective-permute-done | bytes 184352 | tf_op jit(solution)/shard_map/ppermute | solution.py:353
  138.8 1.9 %collective-permute-start.19 = (bf16[288,640]{1,0:T(8,128)(2,1)S(1)}, bf16[288,640]{1,0:T(8,128)(2,1)S(1)}, u32[]{:S(2)}, u32[]{:S(2)}) collective-permute-start(bf16[288,640]{1,0:T(8,128)(2,1)S(1)} %pad_maximum_fusion.5), channel_id=1, source_target_pairs={{0,1},{1,0},{2,3},{3,2},{4,5},{5,4},{6,7},{7,6},{8,9},{9,8},{10,11... | collective-permute-start | bytes 1105928 | tf_op jit(solution)/shard_map/ppermute | solution.py:347
  140.7 2.1 %collective-permute-start.18 = (bf16[288,640]{1,0:T(8,128)(2,1)S(1)}, bf16[288,640]{1,0:T(8,128)(2,1)S(1)}, u32[]{:S(2)}, u32[]{:S(2)}) collective-permute-start(bf16[288,640]{1,0:T(8,128)(2,1)S(1)} %pad_maximum_fusion.5), channel_id=1, source_target_pairs={{1,2},{3,4},{5,6},{7,8},{9,10},{11,12},{13,14},{15,16},{17,18},{19... | collective-permute-start | bytes 1105928 | tf_op jit(solution)/shard_map/ppermute | solution.py:356
  142.9 2.4 %shard_map.227.gq_ref = bf16[128,576]{1,0:T(8,128)(2,1)S(1)} custom-call(bf16[1152,1728]{1,0:T(8,128)(2,1)S(1)} %get-tuple-element.30.win_ref, bf16[1024,1152]{1,0:T(8,128)(2,1)S(1)} %get-tuple-element.38.e_ref, bf16[144,640]{1,0:T(8,128)(2,1)S(1)} %get-tuple-element.33.own_ref.up_ref, f32[128,128]{1,0:T(8,128)S(1)} %get-tuple-element.39.stat_ref), custom_call_target="tpu_custom_call" | custom-call | flops 4000000000 | bytes 6000000 | tf_op jit(solution)/shard_map/pallas_call | solution.py:424
  145.2 0.5 shard_map.228.order_ref
  145.7 2.8 %shard_map.226 = (f32[128,640]{1,0:T(8,128)S(1)}, f32[128,640]{1,0:T(8,128)S(1)}) custom-call(s32[1]{0:T(128)} %bitcast.core_ref, bf16[1152,1728]{1,0:T(8,128)(2,1)S(1)} %get-tuple-element.30.win_ref, bf16[144,640]{1,0:T(8,128)(2,1)S(1)} %get-tuple-element.33.own_ref.up_ref, bf16[144,640]{1,0:T(8,128)(2,1)S(1)} %collective-permute-done.16.before_ref, ...), custom_call_target="tpu_custom_call" | custom-call | flops 4000000000 | bytes 6000000 | tf_op jit(solution)/shard_map/pallas_call | solution.py:429
  148.5 3.1 %collective-permute-done.18.packo_ref = bf16[288,640]{1,0:T(8,128)(2,1)S(1)} collective-permute-done((bf16[288,640]{1,0:T(8,128)(2,1)S(1)}, bf16[288,640]{1,0:T(8,128)(2,1)S(1)}, u32[]{:S(2)}, u32[]{:S(2)}) %collective-permute-start.18) | collective-permute-done | bytes 368672 | tf_op jit(solution)/shard_map/ppermute | solution.py:356
  151.7 5.6 %shard_map.229 = f32[128,1152]{1,0:T(8,128)} custom-call(s32[1]{0:T(128)} %bitcast.core_ref, bf16[1152,1728]{1,0:T(8,128)(2,1)S(1)} %get-tuple-element.30.win_ref, bf16[288,640]{1,0:T(8,128)(2,1)S(1)} %collective-permute-done.18.packo_ref, bf16[288,640]{1,0:T(8,128)(2,1)S(1)} %collective-permute-done.19.packi_ref, f32[128,640]{1,0:T(8,128)S(1)} %get-tuple-element.36.gk0_ref, ...), custom_call_target="tpu_custom_call" | custom-call | tf_op jit(solution)/shard_map/pallas_call | solution.py:434
  (86 shorter events, 0.7 us)
Async XLA Ops:
  0.6 50.0 %copy-start.7 = (s32[1152]{0:T(1024)S(1)}, s32[1152]{0:T(1024)}, u32[]{:S(2)}) copy-start(s32[1152]{0:T(1024)} %constant.84.clone) | copy-start | bytes 13828
  0.6 50.0 %copy-start.13 = (pred[1152]{0:T(1024)(128)(4,1)S(1)}, pred[1152]{0:T(1024)(128)(4,1)}, u32[]{:S(2)}) copy-start(pred[1152]{0:T(1024)(128)(4,1)} %constant.83.clone) | copy-start | bytes 3460
  0.7 50.0 %copy-start.8 = (s32[1152]{0:T(1024)S(1)}, s32[1152]{0:T(1024)}, u32[]{:S(2)}) copy-start(s32[1152]{0:T(1024)} %constant.82.clone) | copy-start | bytes 13828
  0.7 50.0 %copy-start.9 = (s32[1152]{0:T(1024)S(1)}, s32[1152]{0:T(1024)}, u32[]{:S(2)}) copy-start(s32[1152]{0:T(1024)} %constant.81.clone) | copy-start | bytes 13828
  0.7 50.0 %copy-start.10 = (s32[1152]{0:T(1024)S(1)}, s32[1152]{0:T(1024)}, u32[]{:S(2)}) copy-start(s32[1152]{0:T(1024)} %constant.80.clone) | copy-start | bytes 13828
  0.7 50.0 %copy-start.12 = (s32[1,2,3,5]{3,1,2,0:T(2,128)S(1)}, s32[1,2,3,5]{3,1,2,0:T(2,128)}, u32[]{:S(2)}) copy-start(s32[1,2,3,5]{3,1,2,0:T(2,128)} %param.31) | copy-start | bytes 364
  0.7 50.1 %copy-start.6 = (f32[1152]{0:T(1024)S(1)}, f32[1152]{0:T(1024)}, u32[]{:S(2)}) copy-start(f32[1152]{0:T(1024)} %param.23) | copy-start | bytes 13828
  0.7 26.1 %collective-permute-start.2 = (bf16[128,1152]{1,0:T(8,128)(2,1)}, bf16[128,1152]{1,0:T(8,128)(2,1)S(1)}, u32[]{:S(2)}, u32[]{:S(2)}) collective-permute-start(bf16[128,1152]{1,0:T(8,128)(2,1)} %bitcast.7), channel_id=1, source_target_pairs={{32,0},{64,32},{96,64},{128,96},{160,128},{192,160},{224,192},{256... | collective-permute-start | bytes 884744 | tf_op jit(solution)/shard_map/ppermute | solution.py:353
  13.1 17.8 %collective-permute-start.1 = (bf16[128,1152]{1,0:T(8,128)(2,1)}, bf16[128,1152]{1,0:T(8,128)(2,1)S(1)}, u32[]{:S(2)}, u32[]{:S(2)}) collective-permute-start(bf16[128,1152]{1,0:T(8,128)(2,1)} %bitcast.8), channel_id=1, source_target_pairs={{0,32},{32,64},{64,96},{96,128},{128,160},{160,192},{192,224},{224... | collective-permute-start | bytes 884744 | tf_op jit(solution)/shard_map/ppermute | solution.py:353
  16.3 17.6 %collective-permute-start.8 = (bf16[96,1728]{1,0:T(8,128)(2,1)S(1)}, bf16[96,1728]{1,0:T(8,128)(2,1)}, u32[]{:S(2)}, u32[]{:S(2)}) collective-permute-start(bf16[96,1728]{1,0:T(8,128)(2,1)S(1)} %fusion.2), channel_id=1, source_target_pairs={{224,0},{33,1},{194,2},{67,3},{164,4},{101,5},{134,6},{415,7},{232... | collective-permute-start | bytes 995336 | tf_op jit(solution)/shard_map/ppermute | solution.py:370
  32.0 49.3 %collective-permute-start.5 = (bf16[384,1152]{1,0:T(8,128)(2,1)S(1)}, bf16[384,1152]{1,0:T(8,128)(2,1)S(1)}, u32[]{:S(2)}, u32[]{:S(2)}) collective-permute-start(bf16[384,1152]{1,0:T(8,128)(2,1)S(1)} %pad_maximum_fusion.x_ref), channel_id=1, source_target_pairs={{0,1},{1,0},{2,3},{3,2},{4,5},{5,4},{6,7},{7,6},{8,9},{9,8},{10,11... | collective-permute-start | bytes 2654216 | tf_op jit(solution)/shard_map/ppermute | solution.py:347
  33.9 28.6 %collective-permute-start.9 = (bf16[96,1728]{1,0:T(8,128)(2,1)}, bf16[96,1728]{1,0:T(8,128)(2,1)}, u32[]{:S(2)}, u32[]{:S(2)}) collective-permute-start(bf16[96,1728]{1,0:T(8,128)(2,1)} %collective-permute-done.8), channel_id=1, source_target_pairs={{0,2},{2,4},{4,6},{6,0},{3,1},{5,3},{7,5},{1,7},{8,10},{10,12},{12... | collective-permute-start | bytes 995336 | tf_op jit(solution)/shard_map/ppermute | solution.py:350
  38.5 28.0 %collective-permute-start = (bf16[96,1728]{1,0:T(8,128)(2,1)S(1)}, bf16[96,1728]{1,0:T(8,128)(2,1)}, u32[]{:S(2)}, u32[]{:S(2)}) collective-permute-start(bf16[96,1728]{1,0:T(8,128)(2,1)S(1)} %fusion.2), channel_id=1, source_target_pairs={{440,0},{377,1},{474,2},{347,3},{508,4},{317,5},{286,6},{7,7},{432... | collective-permute-start | bytes 995336 | tf_op jit(solution)/shard_map/ppermute | solution.py:370
  40.5 45.5 %collective-permute-start.6 = (bf16[384,1152]{1,0:T(8,128)(2,1)S(1)}, bf16[384,1152]{1,0:T(8,128)(2,1)S(1)}, u32[]{:S(2)}, u32[]{:S(2)}) collective-permute-start(bf16[384,1152]{1,0:T(8,128)(2,1)S(1)} %pad_maximum_fusion.x_ref), channel_id=1, source_target_pairs={{1,2},{3,4},{5,6},{7,8},{9,10},{11,12},{13,14},{15,16},{17,18},{19... | collective-permute-start | bytes 2654216 | tf_op jit(solution)/shard_map/ppermute | solution.py:356
  45.6 29.8 %collective-permute-start.10 = (bf16[96,1728]{1,0:T(8,128)(2,1)}, bf16[96,1728]{1,0:T(8,128)(2,1)S(1)}, u32[]{:S(2)}, u32[]{:S(2)}) collective-permute-start(bf16[96,1728]{1,0:T(8,128)(2,1)} %collective-permute-done.8), channel_id=1, source_target_pairs={{2,0},{4,2},{6,4},{0,6},{1,3},{3,5},{5,7},{7,1},{10,8},{12,10},{14... | collective-permute-start | bytes 995336 | tf_op jit(solution)/shard_map/ppermute | solution.py:350
  62.5 16.8 %collective-permute-start.11 = (bf16[96,1728]{1,0:T(8,128)(2,1)}, bf16[96,1728]{1,0:T(8,128)(2,1)S(1)}, u32[]{:S(2)}, u32[]{:S(2)}) collective-permute-start(bf16[96,1728]{1,0:T(8,128)(2,1)} %collective-permute-done.9), channel_id=1, source_target_pairs={{0,2},{2,4},{4,6},{6,0},{3,1},{5,3},{7,5},{1,7},{8,10},{10,12},{12... | collective-permute-start | bytes 995336 | tf_op jit(solution)/shard_map/ppermute | solution.py:350
  68.4 15.0 %collective-permute-start.4 = (bf16[96,1728]{1,0:T(8,128)(2,1)}, bf16[96,1728]{1,0:T(8,128)(2,1)S(1)}, u32[]{:S(2)}, u32[]{:S(2)}) collective-permute-start(bf16[96,1728]{1,0:T(8,128)(2,1)} %collective-permute-done), channel_id=1, source_target_pairs={{2,0},{4,2},{6,4},{0,6},{1,3},{3,5},{5,7},{7,1},{10,8},{12,10},{14... | collective-permute-start | bytes 995336 | tf_op jit(solution)/shard_map/ppermute | solution.py:350
  75.4 3.9 %copy-start.5 = (bf16[96,1728]{1,0:T(8,128)(2,1)}, bf16[96,1728]{1,0:T(8,128)(2,1)S(1)}, u32[]{:S(2)}) copy-start(bf16[96,1728]{1,0:T(8,128)(2,1)S(1)} %collective-permute-done.10) | copy-start | bytes 995332
  75.4 10.6 %collective-permute-start.3 = (bf16[96,1728]{1,0:T(8,128)(2,1)}, bf16[96,1728]{1,0:T(8,128)(2,1)S(1)}, u32[]{:S(2)}, u32[]{:S(2)}) collective-permute-start(bf16[96,1728]{1,0:T(8,128)(2,1)} %collective-permute-done), channel_id=1, source_target_pairs={{0,2},{2,4},{4,6},{6,0},{3,1},{5,3},{7,5},{1,7},{8,10},{10,12},{12... | collective-permute-start | bytes 995336 | tf_op jit(solution)/shard_map/ppermute | solution.py:350
  79.3 4.1 %copy-start.4 = (bf16[96,1728]{1,0:T(8,128)(2,1)}, bf16[96,1728]{1,0:T(8,128)(2,1)S(1)}, u32[]{:S(2)}) copy-start(bf16[96,1728]{1,0:T(8,128)(2,1)S(1)} %collective-permute-done.11) | copy-start | bytes 995332
  79.3 19.6 %collective-permute-start.12 = (bf16[192,1728]{1,0:T(8,128)(2,1)S(1)}, bf16[192,1728]{1,0:T(8,128)(2,1)S(1)}, u32[]{:S(2)}, u32[]{:S(2)}) collective-permute-start(bf16[192,1728]{1,0:T(8,128)(2,1)S(1)} %pad_maximum_fusion.1.b0), channel_id=1, source_target_pairs={{0,1},{1,0},{2,3},{3,2},{4,5},{5,4},{6,7},{7,6},{8,9},{9,8},{10,11... | collective-permute-start | bytes 1990664 | tf_op jit(solution)/shard_map/ppermute | solution.py:347
  83.4 7.6 %slice-start.2 = ((bf16[96,1728]{1,0:T(8,128)(2,1)}), bf16[24,1728]{1,0:T(8,128)(2,1)S(1)}, s32[]{:S(2)}) async-start(bf16[96,1728]{1,0:T(8,128)(2,1)} %copy-done.5), calls=%async_computation.2 | async-start | bytes 172032 | tf_op jit(solution)/shard_map/slice | solution.py:393
  83.4 7.6 %slice-start.3 = ((bf16[96,1728]{1,0:T(8,128)(2,1)}), bf16[72,1728]{1,0:T(8,128)(2,1)S(1)}, s32[]{:S(2)}) async-start(bf16[96,1728]{1,0:T(8,128)(2,1)} %copy-done.5), calls=%async_computation.3 | async-start | bytes 516096 | tf_op jit(solution)/shard_map/slice | solution.py:393
  86.1 10.4 %collective-permute-start.7 = (bf16[96,1728]{1,0:T(8,128)(2,1)S(1)}, bf16[96,1728]{1,0:T(8,128)(2,1)S(1)}, u32[]{:S(2)}, u32[]{:S(2)}) collective-permute-start(bf16[96,1728]{1,0:T(8,128)(2,1)S(1)} %collective-permute-done.3), channel_id=1, source_target_pairs={{0,2},{2,4},{4,6},{6,0},{3,1},{5,3},{7,5},{1,7},{8,10},{10,12},{12... | collective-permute-start | bytes 995336 | tf_op jit(solution)/shard_map/ppermute | solution.py:350
  88.1 10.9 %collective-permute-start.13 = (bf16[192,1728]{1,0:T(8,128)(2,1)S(1)}, bf16[192,1728]{1,0:T(8,128)(2,1)S(1)}, u32[]{:S(2)}, u32[]{:S(2)}) collective-permute-start(bf16[192,1728]{1,0:T(8,128)(2,1)S(1)} %pad_maximum_fusion.2.b1), channel_id=1, source_target_pairs={{0,1},{1,0},{2,3},{3,2},{4,5},{5,4},{6,7},{7,6},{8,9},{9,8},{10,11... | collective-permute-start | bytes 1990664 | tf_op jit(solution)/shard_map/ppermute | solution.py:347
  91.1 5.4 %slice-start = ((bf16[96,1728]{1,0:T(8,128)(2,1)}), bf16[24,1728]{1,0:T(8,128)(2,1)S(1)}, s32[]{:S(2)}) async-start(bf16[96,1728]{1,0:T(8,128)(2,1)} %copy-done.4), calls=%async_computation | async-start | bytes 172032 | tf_op jit(solution)/shard_map/slice | solution.py:393
  91.1 5.4 %slice-start.1 = ((bf16[96,1728]{1,0:T(8,128)(2,1)}), bf16[72,1728]{1,0:T(8,128)(2,1)S(1)}, s32[]{:S(2)}) async-start(bf16[96,1728]{1,0:T(8,128)(2,1)} %copy-done.4), calls=%async_computation.1 | async-start | bytes 516096 | tf_op jit(solution)/shard_map/slice | solution.py:393
  91.1 7.9 %collective-permute-start.14 = (bf16[192,1728]{1,0:T(8,128)(2,1)S(1)}, bf16[192,1728]{1,0:T(8,128)(2,1)S(1)}, u32[]{:S(2)}, u32[]{:S(2)}) collective-permute-start(bf16[192,1728]{1,0:T(8,128)(2,1)S(1)} %pad_maximum_fusion.3.b2), channel_id=1, source_target_pairs={{0,1},{1,0},{2,3},{3,2},{4,5},{5,4},{6,7},{7,6},{8,9},{9,8},{10,11... | collective-permute-start | bytes 1990664 | tf_op jit(solution)/shard_map/ppermute | solution.py:347
  95.3 3.4 %copy-start.11 = (s32[384]{0:T(512)S(1)}, s32[384]{0:T(512)}, u32[]{:S(2)}) copy-start(s32[384]{0:T(512)} %constant.89.clone) | copy-start | bytes 4612
  95.3 3.4 %copy-start.14 = (s32[384]{0:T(512)S(1)}, s32[384]{0:T(512)}, u32[]{:S(2)}) copy-start(s32[384]{0:T(512)} %constant.87.clone) | copy-start | bytes 4612
  95.3 3.4 %copy-start.15 = (s32[384]{0:T(512)S(1)}, s32[384]{0:T(512)}, u32[]{:S(2)}) copy-start(s32[384]{0:T(512)} %constant.86.clone) | copy-start | bytes 4612
  95.3 3.4 %copy-start.16 = (s32[384]{0:T(512)S(1)}, s32[384]{0:T(512)}, u32[]{:S(2)}) copy-start(s32[384]{0:T(512)} %constant.85.clone) | copy-start | bytes 4612
  95.3 3.4 %copy-start.19 = (pred[384]{0:T(512)(128)(4,1)S(1)}, pred[384]{0:T(512)(128)(4,1)}, u32[]{:S(2)}) copy-start(pred[384]{0:T(512)(128)(4,1)} %constant.88.clone) | copy-start | bytes 1156
  95.4 3.4 %copy-start.17 = (pred[384]{0:T(512)(128)(4,1)S(1)}, pred[384]{0:T(512)(128)(4,1)}, u32[]{:S(2)}) copy-start(pred[384]{0:T(512)(128)(4,1)} %constant.91.clone) | copy-start | bytes 1156
  95.4 3.4 %copy-start.18 = (pred[384]{0:T(512)(128)(4,1)S(1)}, pred[384]{0:T(512)(128)(4,1)}, u32[]{:S(2)}) copy-start(pred[384]{0:T(512)(128)(4,1)} %constant.90.clone) | copy-start | bytes 1156
  96.6 4.0 %collective-permute-start.15 = (bf16[192,1728]{1,0:T(8,128)(2,1)S(1)}, bf16[192,1728]{1,0:T(8,128)(2,1)S(1)}, u32[]{:S(2)}, u32[]{:S(2)}) collective-permute-start(bf16[192,1728]{1,0:T(8,128)(2,1)S(1)} %pad_maximum_fusion.4.b3), channel_id=1, source_target_pairs={{0,1},{1,0},{2,3},{3,2},{4,5},{5,4},{6,7},{7,6},{8,9},{9,8},{10,11... | collective-permute-start | bytes 1990664 | tf_op jit(solution)/shard_map/ppermute | solution.py:347
  98.9 9.1 %copy-start = (bf16[8,16,1152]{2,1,0:T(8,128)(2,1)S(1)}, bf16[8,16,1152]{2,1,0:T(8,128)(2,1)}, u32[]{:S(2)}) copy-start(bf16[8,16,1152]{2,1,0:T(8,128)(2,1)} %param.22) | copy-start | bytes 884740
  98.9 9.1 %copy-start.1 = (bf16[1152,192]{0,1:T(8,128)(2,1)S(1)}, bf16[1152,192]{0,1:T(8,128)(2,1)}, u32[]{:S(2)}) copy-start(bf16[1152,192]{0,1:T(8,128)(2,1)} %param.28) | copy-start | bytes 1327108
  98.9 9.1 %copy-start.2 = (f32[8,16,64]{2,1,0:T(8,128)S(1)}, f32[8,16,64]{2,1,0:T(8,128)}, u32[]{:S(2)}) copy-start(f32[8,16,64]{2,1,0:T(8,128)} %param.29) | copy-start | bytes 98308
  98.9 9.1 %copy-start.3 = (s32[8,16,64]{2,1,0:T(8,128)S(1)}, s32[8,16,64]{2,1,0:T(8,128)}, u32[]{:S(2)}) copy-start(s32[8,16,64]{2,1,0:T(8,128)} %param.30) | copy-start | bytes 98308
  114.2 16.6 %collective-permute-start.17 = (bf16[144,640]{1,0:T(8,128)(2,1)S(1)}, bf16[144,640]{1,0:T(8,128)(2,1)S(1)}, u32[]{:S(2)}, u32[]{:S(2)}) collective-permute-start(bf16[144,640]{1,0:T(8,128)(2,1)S(1)} %get-tuple-element.33.own_ref.up_ref), channel_id=1, source_target_pairs={{32,0},{64,32},{96,64},{128,96},{160,128},{192,160},{224,192},{256... | collective-permute-start | bytes 552968 | tf_op jit(solution)/shard_map/ppermute | solution.py:353
  123.2 15.5 %collective-permute-start.16 = (bf16[144,640]{1,0:T(8,128)(2,1)S(1)}, bf16[144,640]{1,0:T(8,128)(2,1)S(1)}, u32[]{:S(2)}, u32[]{:S(2)}) collective-permute-start(bf16[144,640]{1,0:T(8,128)(2,1)S(1)} %get-tuple-element.33.own_ref.up_ref), channel_id=1, source_target_pairs={{0,32},{32,64},{64,96},{96,128},{128,160},{160,192},{192,224},{224... | collective-permute-start | bytes 552968 | tf_op jit(solution)/shard_map/ppermute | solution.py:353
  125.2 20.5 %collective-permute-start.21 = (bf16[144,640]{1,0:T(8,128)(2,1)S(1)}, bf16[144,640]{1,0:T(8,128)(2,1)S(1)}, u32[]{:S(2)}, u32[]{:S(2)}) collective-permute-start(bf16[144,640]{1,0:T(8,128)(2,1)S(1)} %get-tuple-element.33.own_ref.up_ref), channel_id=1, source_target_pairs={{0,1},{1,0},{2,3},{3,2},{4,5},{5,4},{6,7},{7,6},{8,9},{9,8},{10,11... | collective-permute-start | bytes 552968 | tf_op jit(solution)/shard_map/ppermute | solution.py:347
  127.6 18.2 %collective-permute-start.20 = (bf16[144,640]{1,0:T(8,128)(2,1)S(1)}, bf16[144,640]{1,0:T(8,128)(2,1)S(1)}, u32[]{:S(2)}, u32[]{:S(2)}) collective-permute-start(bf16[144,640]{1,0:T(8,128)(2,1)S(1)} %get-tuple-element.33.own_ref.up_ref), channel_id=1, source_target_pairs={{1,2},{3,4},{5,6},{7,8},{9,10},{11,12},{13,14},{15,16},{17,18},{19... | collective-permute-start | bytes 552968 | tf_op jit(solution)/shard_map/ppermute | solution.py:356
  138.8 9.7 %collective-permute-start.19 = (bf16[288,640]{1,0:T(8,128)(2,1)S(1)}, bf16[288,640]{1,0:T(8,128)(2,1)S(1)}, u32[]{:S(2)}, u32[]{:S(2)}) collective-permute-start(bf16[288,640]{1,0:T(8,128)(2,1)S(1)} %pad_maximum_fusion.5), channel_id=1, source_target_pairs={{0,1},{1,0},{2,3},{3,2},{4,5},{5,4},{6,7},{7,6},{8,9},{9,8},{10,11... | collective-permute-start | bytes 1105928 | tf_op jit(solution)/shard_map/ppermute | solution.py:347
  140.7 10.9 %collective-permute-start.18 = (bf16[288,640]{1,0:T(8,128)(2,1)S(1)}, bf16[288,640]{1,0:T(8,128)(2,1)S(1)}, u32[]{:S(2)}, u32[]{:S(2)}) collective-permute-start(bf16[288,640]{1,0:T(8,128)(2,1)S(1)} %pad_maximum_fusion.5), channel_id=1, source_target_pairs={{1,2},{3,4},{5,6},{7,8},{9,10},{11,12},{13,14},{15,16},{17,18},{19... | collective-permute-start | bytes 1105928 | tf_op jit(solution)/shard_map/ppermute | solution.py:356

commit v9 on v7

--- a/solution.py
+++ b/solution.py
@@ -40,7 +40,16 @@
 
 
 def window(first):
-    return first // 128 * 128, -(-(first + HD) // 128) * 128
+    start = first // 128 * 128
+    return start, start + 256
+
+
+def stacked(x, first, start):
+    return jnp.concatenate([head_only(x, first, start), head_only(x, first + HD, start)], axis=0)
+
+
+def unstacked(x, first, start):
+    return head_only(x[0:T, :], first, start) + head_only(x[T : 2 * T, :], first + HD, start)
 
 
 def head_only(x, first, start):
@@ -132,22 +141,28 @@
     own = slice(4 * T, 5 * T)
     lanes = lax.broadcasted_iota(jnp.int32, (T, T), 1)
     stats = jnp.zeros((T, T), F32)
-    for e in range(H):
+    for e in range(0, H, 2):
         a, b = window(K0 + HD * e)
-        q = head_only(win_ref[own, Q0 + a : Q0 + b], HD * e, a) if Q0 + b <= QKV else head_only(
-            jnp.concatenate([win_ref[own, Q0 + a : QKV], jnp.zeros((T, Q0 + b - QKV), BF)], axis=1), HD * e, a)
-        s = nt(q, win_ref[:, a:b]) * SCALE2 + bias_ref[...]
-        peak = jnp.max(s, axis=1, keepdims=True)
-        p = jnp.exp2(s - peak)
-        total = jnp.sum(p, axis=1, keepdims=True)
-        low = p.astype(BF)
-        e_ref[e * T : (e + 1) * T, :] = low
-        inv = 1.0 / total
-        stats = jnp.where(lanes == e, peak + jnp.log2(total), stats)
-        stats = jnp.where(lanes == 16 + e, inv, stats)
+        q = win_ref[own, Q0 + a : min(Q0 + b, QKV)]
+        if Q0 + b > QKV:
+            q = jnp.concatenate([q, jnp.zeros((T, Q0 + b - QKV), BF)], axis=1)
+        scores = nt(stacked(q, HD * e, a), win_ref[:, a:b])
+        lows, invs = [], []
+        for i in range(2):
+            s = scores[i * T : (i + 1) * T, :] * SCALE2 + bias_ref[...]
+            peak = jnp.max(s, axis=1, keepdims=True)
+            p = jnp.exp2(s - peak)
+            total = jnp.sum(p, axis=1, keepdims=True)
+            inv = 1.0 / total
+            stats = jnp.where(lanes == e + i, peak + jnp.log2(total), stats)
+            stats = jnp.where(lanes == 16 + e + i, inv, stats)
+            lows.append(p.astype(BF))
+            invs.append(inv)
+        low = jnp.concatenate(lows, axis=0)
+        e_ref[e * T : (e + 2) * T, :] = low
         a, b = window(V0 + HD * e)
-        o = nn(low, win_ref[:, a:b]) * inv
-        acc_ref[:, a - VB : b - VB] += head_only(o, V0 + HD * e, a)
+        o = nn(low, win_ref[:, a:b]) * jnp.concatenate(invs, axis=0)
+        acc_ref[:, a - VB : b - VB] += unstacked(o, V0 + HD * e, a)
 
     att = acc_ref[...].astype(BF)
     den = (x_ref[...].astype(F32) + nn(att, wn_ref[...])).astype(BF)
@@ -164,7 +179,7 @@
     pack_ref[0:T, :] = up
     prod = up.astype(F32) * att.astype(F32)
     for e in range(H):
-        a, b = window(V0 + HD * e)
+        a, b = window(V0 + HD * (e - e % 2))
         inner = jnp.sum(head_only(prod[:, a - VB : b - VB], V0 + HD * e, a), axis=1, keepdims=True)
         stats = jnp.where(lanes == 8 + e, inner, stats)
     stat_ref[...] = stats
@@ -184,15 +199,17 @@
 
 def query_kernel(win_ref, e_ref, up_ref, stat_ref, gq_ref, acc_ref):
     acc_ref[...] = jnp.zeros_like(acc_ref)
-    for e in range(H):
+    for e in range(0, H, 2):
         a, b = window(V0 + HD * e)
-        up = head_only(up_ref[0:T, a - VB : b - VB], V0 + HD * e, a)
+        up = stacked(up_ref[0:T, a - VB : b - VB], V0 + HD * e, a)
         dprob = nt(up, win_ref[:, a:b])
-        p = e_ref[e * T : (e + 1) * T, :].astype(F32)
-        ds = (p * (dprob - stat_ref[:, 8 + e : 9 + e])).astype(BF)
+        p = e_ref[e * T : (e + 2) * T, :].astype(F32)
+        inner = jnp.concatenate([stat_ref[:, 8 + e : 9 + e], stat_ref[:, 9 + e : 10 + e]], axis=0)
+        inv = jnp.concatenate([stat_ref[:, 16 + e : 17 + e], stat_ref[:, 17 + e : 18 + e]], axis=0)
+        ds = (p * (dprob - inner)).astype(BF)
         a, b = window(K0 + HD * e)
-        dq = nn(ds, win_ref[:, a:b]) * (stat_ref[:, 16 + e : 17 + e] * FACTOR)
-        acc_ref[:, a:b] += head_only(dq, HD * e, a)
+        dq = nn(ds, win_ref[:, a:b]) * (inv * FACTOR)
+        acc_ref[:, a:b] += unstacked(dq, HD * e, a)
     gq_ref[...] = acc_ref[:, 0:HW].astype(BF)
 
 
@@ -223,21 +240,24 @@
             [win_ref[(3 * t + r) * T : (3 * t + r + 1) * T, Q0 + a : Q0 + b] for t, r, _, _ in tiles], axis=0
         )
 
-    for e in range(H):
+    for e in range(0, H, 2):
         a, b = window(K0 + HD * e)
         if Q0 + b <= QKV:
             q = queries(a, b)
         else:
             q = jnp.concatenate([queries(a, HW), jnp.zeros((count, b - HW), BF)], axis=1)
-        k = head_only(win_ref[own, a:b], HD * e, a)
-        s = nt(k, q) * SCALE2 + bias
-        p = jnp.exp2(s - stats[e : e + 1, :])
         c, d = window(V0 + HD * e)
-        v = head_only(win_ref[own, c:d], V0 + HD * e, c)
         up = ups[:, c - VB : d - VB]
-        ds = (p * (nt(v, up) - stats[8 + e : 9 + e, :])).astype(BF)
-        gk_ref[:, a:b] += head_only(nn(ds, q), HD * e, a)
-        gv_ref[:, c - VB : d - VB] += head_only(nn(p.astype(BF), up), V0 + HD * e, c)
+        scores = nt(stacked(win_ref[own, a:b], HD * e, a), q)
+        dprob = nt(stacked(win_ref[own, c:d], V0 + HD * e, c), up)
+        ps, dss = [], []
+        for i in range(2):
+            rows = slice(i * T, (i + 1) * T)
+            p = jnp.exp2(scores[rows, :] * SCALE2 + bias - stats[e + i : e + i + 1, :])
+            ps.append(p.astype(BF))
+            dss.append((p * (dprob[rows, :] - stats[8 + e + i : 9 + e + i, :])).astype(BF))
+        gk_ref[:, a:b] += unstacked(nn(jnp.concatenate(dss, axis=0), q), HD * e, a)
+        gv_ref[:, c - VB : d - VB] += unstacked(nn(jnp.concatenate(ps, axis=0), up), V0 + HD * e, c)
 
 
 def key_near_kernel(core_ref, win_ref, own_ref, before_ref, after_ref, outer_ref, inner_ref, gk_ref, gv_ref):

time: 144 us -> 142 us (0.986)
  Pallas kernels: 31.1 us -> 28.4 us
  transfers between devices with their start and end apart: 19 -> 19, of which waited for: 6 -> 6; matrix products, arithmetic and copies ran while one was open for 3% -> 3% of each run, Pallas kernels for 8% -> 7%
where the time goes in v9:
time: 142 us; the launch traced here: 141 us
  starting transfers between devices  79.2 us (56%)
  Pallas kernels  28.4 us (20%)
  waiting for transfers between devices  24.4 us (17%)
  local copies, waits for them, and re-layouts  4.86 us (3%)
  other arithmetic  3.25 us (2%)
    ppermute x7, starting transfers between devices, swap(): return lax.ppermute(v, 'core', [(0, 1), (1, 0)])  23.1 us
    ppermute x2, starting transfers between devices, rows_beside(): lax.ppermute(own, lat + ('core',), south)  20.9 us
    ppermute x3, starting transfers between devices, sides(): return (lax.ppermute(column, lon, border), swap(column))  16.7 us
    ppermute x3, waiting for transfers between devices, along(): return lax.ppermute(v, ('x', 'core'), perm)  13.1 us
    pallas_call x1, Pallas kernels, on_device(): pl.pallas_call(project_kernel, out_shape=(shaped((9 * T, QKV)), shaped((6...  7.38 us
    ppermute x3, starting transfers between devices, along(): return lax.ppermute(v, ('x', 'core'), perm)  7.19 us
    pallas_call x3, Pallas kernels, hidden(): pl.pallas_call(hidden_kernel, out_shape=shaped((3 * T, D)), in_specs=[VME...  6.33 us
    ppermute x2, starting transfers between devices, rows_beside(): lax.ppermute(own, lat + ('core',), north)  5.91 us
  transfers between devices with their start and end apart: 19, of which 6 were waited for; matrix products, arithmetic and copies ran while one was open for 3% of the time, Pallas kernels for 7%

profile of v9, /device:TPU:47, one launch (start us, length us, event | category | flops | bytes accessed | tf_op | source)
XLA Modules:
  0.0 141.4 jit_solution(9214956047827528193)
XLA Ops:
  0.6 4.0 %collective-permute-start.3 = (bf16[128,1152]{1,0:T(8,128)(2,1)}, bf16[128,1152]{1,0:T(8,128)(2,1)S(1)}, u32[]{:S(2)}, u32[]{:S(2)}) collective-permute-start(bf16[128,1152]{1,0:T(8,128)(2,1)} %bitcast.7), channel_id=1, source_target_pairs={{32,0},{64,32},{96,64},{128,96},{160,128},{192,160},{224,192},{256... | collective-permute-start | bytes 884744 | tf_op jit(solution)/shard_map/ppermute | solution.py:373
  4.6 9.0 %collective-permute-start.2 = (bf16[128,1152]{1,0:T(8,128)(2,1)}, bf16[128,1152]{1,0:T(8,128)(2,1)S(1)}, u32[]{:S(2)}, u32[]{:S(2)}) collective-permute-start(bf16[128,1152]{1,0:T(8,128)(2,1)} %bitcast.8), channel_id=1, source_target_pairs={{0,32},{32,64},{64,96},{96,128},{128,160},{160,192},{192,224},{224... | collective-permute-start | bytes 884744 | tf_op jit(solution)/shard_map/ppermute | solution.py:373
  13.7 1.2 fusion.2
  14.9 0.7 collective-permute-start.1
  15.6 4.7 %collective-permute-start = (bf16[96,1728]{1,0:T(8,128)(2,1)S(1)}, bf16[96,1728]{1,0:T(8,128)(2,1)S(1)}, u32[]{:S(2)}, u32[]{:S(2)}) collective-permute-start(bf16[96,1728]{1,0:T(8,128)(2,1)S(1)} %fusion.2), channel_id=1, source_target_pairs={{224,0},{33,1},{194,2},{67,3},{164,4},{101,5},{134,6},{415,7},{232... | collective-permute-start | bytes 995336 | tf_op jit(solution)/shard_map/ppermute | solution.py:390
  20.3 0.7 reshape.34.gain_ref
  21.0 0.8 fusion.15
  21.8 5.3 %collective-permute-done.2 = bf16[128,1152]{1,0:T(8,128)(2,1)S(1)} collective-permute-done((bf16[128,1152]{1,0:T(8,128)(2,1)}, bf16[128,1152]{1,0:T(8,128)(2,1)S(1)}, u32[]{:S(2)}, u32[]{:S(2)}) %collective-permute-start.2) | collective-permute-done | bytes 294944 | tf_op jit(solution)/shard_map/ppermute | solution.py:373
  27.1 1.0 pad_maximum_fusion.x_ref
  28.2 8.6 %collective-permute-start.7 = (bf16[384,1152]{1,0:T(8,128)(2,1)S(1)}, bf16[384,1152]{1,0:T(8,128)(2,1)S(1)}, u32[]{:S(2)}, u32[]{:S(2)}) collective-permute-start(bf16[384,1152]{1,0:T(8,128)(2,1)S(1)} %pad_maximum_fusion.x_ref), channel_id=1, source_target_pairs={{1,2},{3,4},{5,6},{7,8},{9,10},{11,12},{13,14},{15,16},{17,18},{19... | collective-permute-start | bytes 2654216 | tf_op jit(solution)/shard_map/ppermute | solution.py:376
  36.8 1.9 %collective-permute-start.6 = (bf16[384,1152]{1,0:T(8,128)(2,1)S(1)}, bf16[384,1152]{1,0:T(8,128)(2,1)S(1)}, u32[]{:S(2)}, u32[]{:S(2)}) collective-permute-start(bf16[384,1152]{1,0:T(8,128)(2,1)S(1)} %pad_maximum_fusion.x_ref), channel_id=1, source_target_pairs={{0,1},{1,0},{2,3},{3,2},{4,5},{5,4},{6,7},{7,6},{8,9},{9,8},{10,11... | collective-permute-start | bytes 2654216 | tf_op jit(solution)/shard_map/ppermute | solution.py:367
  38.7 2.1 %shard_map.221.hc_ref = bf16[384,1152]{1,0:T(8,128)(2,1)S(1)} custom-call(bf16[384,1152]{1,0:T(8,128)(2,1)S(1)} %pad_maximum_fusion.x_ref, f32[1,1152]{1,0:T(1,128)S(1)} %reshape.34.gain_ref, s32[1,1152]{1,0:T(1,128)S(1)} %reshape.35.target_ref), custom_call_target="tpu_custom_call" | custom-call | flops 3000000000 | bytes 5000000 | tf_op jit(solution)/shard_map/pallas_call | solution.py:405
  40.8 0.9 copy-done.6
  41.8 0.1 pad_maximum_fusion.1.b0
  41.9 1.9 %collective-permute-start.5 = (bf16[192,1728]{1,0:T(8,128)(2,1)S(1)}, bf16[192,1728]{1,0:T(8,128)(2,1)S(1)}, u32[]{:S(2)}, u32[]{:S(2)}) collective-permute-start(bf16[192,1728]{1,0:T(8,128)(2,1)S(1)} %pad_maximum_fusion.1.b0), channel_id=1, source_target_pairs={{2,0},{4,2},{6,4},{0,6},{1,3},{3,5},{5,7},{7,1},{10,8},{12,10},{14... | collective-permute-start | bytes 1990664 | tf_op jit(solution)/shard_map/ppermute | solution.py:370
  43.9 3.4 %collective-permute-start.4 = (bf16[192,1728]{1,0:T(8,128)(2,1)S(1)}, bf16[192,1728]{1,0:T(8,128)(2,1)S(1)}, u32[]{:S(2)}, u32[]{:S(2)}) collective-permute-start(bf16[192,1728]{1,0:T(8,128)(2,1)S(1)} %pad_maximum_fusion.1.b0), channel_id=1, source_target_pairs={{0,2},{2,4},{4,6},{6,0},{3,1},{5,3},{7,5},{1,7},{8,10},{10,12},{12... | collective-permute-start | bytes 1990664 | tf_op jit(solution)/shard_map/ppermute | solution.py:370
  47.2 2.1 %shard_map.222.he_ref = bf16[384,1152]{1,0:T(8,128)(2,1)S(1)} custom-call(bf16[384,1152]{1,0:T(8,128)(2,1)S(1)} %collective-permute-done.6.x_ref, f32[1,1152]{1,0:T(1,128)S(1)} %reshape.34.gain_ref, s32[1,1152]{1,0:T(1,128)S(1)} %reshape.35.target_ref), custom_call_target="tpu_custom_call" | custom-call | flops 3000000000 | bytes 5000000 | tf_op jit(solution)/shard_map/pallas_call | solution.py:405
  49.4 0.9 copy-done.8
  50.3 9.7 %collective-permute-done.5.b2 = bf16[192,1728]{1,0:T(8,128)(2,1)S(1)} collective-permute-done((bf16[192,1728]{1,0:T(8,128)(2,1)S(1)}, bf16[192,1728]{1,0:T(8,128)(2,1)S(1)}, u32[]{:S(2)}, u32[]{:S(2)}) %collective-permute-start.5) | collective-permute-done | bytes 663584 | tf_op jit(solution)/shard_map/ppermute | solution.py:370
  60.0 3.1 %collective-permute-done.4.b1 = bf16[192,1728]{1,0:T(8,128)(2,1)S(1)} collective-permute-done((bf16[192,1728]{1,0:T(8,128)(2,1)S(1)}, bf16[192,1728]{1,0:T(8,128)(2,1)S(1)}, u32[]{:S(2)}, u32[]{:S(2)}) %collective-permute-start.4) | collective-permute-done | bytes 663584 | tf_op jit(solution)/shard_map/ppermute | solution.py:370
  63.1 0.9 copy-done.1
  64.1 1.9 %collective-permute-start.8 = (bf16[192,1728]{1,0:T(8,128)(2,1)S(1)}, bf16[192,1728]{1,0:T(8,128)(2,1)S(1)}, u32[]{:S(2)}, u32[]{:S(2)}) collective-permute-start(bf16[192,1728]{1,0:T(8,128)(2,1)S(1)} %collective-permute-done.4.b1), channel_id=1, source_target_pairs={{0,2},{2,4},{4,6},{6,0},{3,1},{5,3},{7,5},{1,7},{8,10},{10,12},{12... | collective-permute-start | bytes 1990664 | tf_op jit(solution)/shard_map/ppermute | solution.py:370
  66.0 0.0 copy-start.14
  66.0 0.0 copy-start.17
  66.0 0.0 copy-start.16
  66.1 0.1 reshape.31
  66.2 2.9 %collective-permute-start.9 = (bf16[192,1728]{1,0:T(8,128)(2,1)S(1)}, bf16[192,1728]{1,0:T(8,128)(2,1)S(1)}, u32[]{:S(2)}, u32[]{:S(2)}) collective-permute-start(bf16[192,1728]{1,0:T(8,128)(2,1)S(1)} %pad_maximum_fusion.1.b0), channel_id=1, source_target_pairs={{0,1},{1,0},{2,3},{3,2},{4,5},{5,4},{6,7},{7,6},{8,9},{9,8},{10,11... | collective-permute-start | bytes 1990664 | tf_op jit(solution)/shard_map/ppermute | solution.py:367
  69.1 1.9 %collective-permute-start.10 = (bf16[192,1728]{1,0:T(8,128)(2,1)S(1)}, bf16[192,1728]{1,0:T(8,128)(2,1)S(1)}, u32[]{:S(2)}, u32[]{:S(2)}) collective-permute-start(bf16[192,1728]{1,0:T(8,128)(2,1)S(1)} %collective-permute-done.4.b1), channel_id=1, source_target_pairs={{0,1},{1,0},{2,3},{3,2},{4,5},{5,4},{6,7},{7,6},{8,9},{9,8},{10,11... | collective-permute-start | bytes 1990664 | tf_op jit(solution)/shard_map/ppermute | solution.py:367
  71.0 2.4 %collective-permute-start.11 = (bf16[192,1728]{1,0:T(8,128)(2,1)S(1)}, bf16[192,1728]{1,0:T(8,128)(2,1)S(1)}, u32[]{:S(2)}, u32[]{:S(2)}) collective-permute-start(bf16[192,1728]{1,0:T(8,128)(2,1)S(1)} %collective-permute-done.5.b2), channel_id=1, source_target_pairs={{0,1},{1,0},{2,3},{3,2},{4,5},{5,4},{6,7},{7,6},{8,9},{9,8},{10,11... | collective-permute-start | bytes 1990664 | tf_op jit(solution)/shard_map/ppermute | solution.py:367
  73.4 1.2 copy-done.2
  74.6 2.1 %shard_map.223.hw_ref = bf16[384,1152]{1,0:T(8,128)(2,1)S(1)} custom-call(bf16[384,1152]{1,0:T(8,128)(2,1)S(1)} %copy-done.2, f32[1,1152]{1,0:T(1,128)S(1)} %reshape.34.gain_ref, s32[1,1152]{1,0:T(1,128)S(1)} %reshape.35.target_ref), custom_call_target="tpu_custom_call" | custom-call | flops 3000000000 | bytes 5000000 | tf_op jit(solution)/shard_map/pallas_call | solution.py:405
  76.7 0.2 collective-permute-done.8.b3
  76.9 2.1 %collective-permute-start.12 = (bf16[192,1728]{1,0:T(8,128)(2,1)S(1)}, bf16[192,1728]{1,0:T(8,128)(2,1)S(1)}, u32[]{:S(2)}, u32[]{:S(2)}) collective-permute-start(bf16[192,1728]{1,0:T(8,128)(2,1)S(1)} %collective-permute-done.8.b3), channel_id=1, source_target_pairs={{0,1},{1,0},{2,3},{3,2},{4,5},{5,4},{6,7},{7,6},{8,9},{9,8},{10,11... | collective-permute-start | bytes 1990664 | tf_op jit(solution)/shard_map/ppermute | solution.py:367
  79.2 0.1 pad_add_fusion.1.blocks_ref
  79.4 1.6 %collective-permute-done.12.b7 = bf16[192,1728]{1,0:T(8,128)(2,1)S(1)} collective-permute-done((bf16[192,1728]{1,0:T(8,128)(2,1)S(1)}, bf16[192,1728]{1,0:T(8,128)(2,1)S(1)}, u32[]{:S(2)}, u32[]{:S(2)}) %collective-permute-start.12) | collective-permute-done | bytes 663584 | tf_op jit(solution)/shard_map/ppermute | solution.py:367
  81.0 7.4 %shard_map.224 = (bf16[1152,1728]{1,0:T(8,128)(2,1)S(1)}, bf16[640,1152]{1,0:T(8,128)(2,1)S(1)}) custom-call(s32[3,384]{1,0:T(4,128)S(1)} %pad_add_fusion.place_ref, bf16[384,1152]{1,0:T(8,128)(2,1)S(1)} %shard_map.223.hw_ref, bf16[384,1152]{1,0:T(8,128)(2,1)S(1)} %copy-done.7, bf16[384,1152]{1,0:T(8,128)(2,1)S(1)} %copy-done.9, ...), custom_call_target="tpu_custom_call" | custom-call | flops 6000000000 | bytes 8000000 | tf_op jit(solution)/shard_map/pallas_call | solution.py:418
  88.4 5.5 %shard_map.225 = (bf16[1024,1152]{1,0:T(8,128)(2,1)S(1)}, bf16[128,1152]{1,0:T(8,128)(2,1)}, f32[128,1152]{1,0:T(8,128)S(1)}, bf16[144,640]{1,0:T(8,128)(2,1)S(1)}, f32[128,128]{1,0:T(8,128)S(1)}) custom-call(s32[31]{0:T(128)S(1)} %pad_add_fusion.1.blocks_ref, bf16[1152,1728]{1,0:T(8,128)(2,1)S(1)} %get-tuple-element.30.win_ref, ...), custom_call_target="tpu_custom_call" | custom-call | flops 6000000000 | bytes 8000000 | tf_op jit(solution)/shard_map/pallas_call | solution.py:425
  93.9 1.9 %collective-permute-start.14 = (bf16[144,640]{1,0:T(8,128)(2,1)S(1)}, bf16[144,640]{1,0:T(8,128)(2,1)S(1)}, u32[]{:S(2)}, u32[]{:S(2)}) collective-permute-start(bf16[144,640]{1,0:T(8,128)(2,1)S(1)} %get-tuple-element.33.own_ref.up_ref), channel_id=1, source_target_pairs={{32,0},{64,32},{96,64},{128,96},{160,128},{192,160},{224,192},{256... | collective-permute-start | bytes 552968 | tf_op jit(solution)/shard_map/ppermute | solution.py:373
  95.8 11.9 %collective-permute-start.13 = (bf16[144,640]{1,0:T(8,128)(2,1)S(1)}, bf16[144,640]{1,0:T(8,128)(2,1)S(1)}, u32[]{:S(2)}, u32[]{:S(2)}) collective-permute-start(bf16[144,640]{1,0:T(8,128)(2,1)S(1)} %get-tuple-element.33.own_ref.up_ref), channel_id=1, source_target_pairs={{0,32},{32,64},{64,96},{96,128},{128,160},{160,192},{192,224},{224... | collective-permute-start | bytes 552968 | tf_op jit(solution)/shard_map/ppermute | solution.py:373
  107.7 2.3 %collective-permute-start.18 = (bf16[144,640]{1,0:T(8,128)(2,1)S(1)}, bf16[144,640]{1,0:T(8,128)(2,1)S(1)}, u32[]{:S(2)}, u32[]{:S(2)}) collective-permute-start(bf16[144,640]{1,0:T(8,128)(2,1)S(1)} %get-tuple-element.33.own_ref.up_ref), channel_id=1, source_target_pairs={{0,1},{1,0},{2,3},{3,2},{4,5},{5,4},{6,7},{7,6},{8,9},{9,8},{10,11... | collective-permute-start | bytes 552968 | tf_op jit(solution)/shard_map/ppermute | solution.py:367
  110.1 5.9 %collective-permute-start.17 = (bf16[144,640]{1,0:T(8,128)(2,1)S(1)}, bf16[144,640]{1,0:T(8,128)(2,1)S(1)}, u32[]{:S(2)}, u32[]{:S(2)}) collective-permute-start(bf16[144,640]{1,0:T(8,128)(2,1)S(1)} %get-tuple-element.33.own_ref.up_ref), channel_id=1, source_target_pairs={{1,2},{3,4},{5,6},{7,8},{9,10},{11,12},{13,14},{15,16},{17,18},{19... | collective-permute-start | bytes 552968 | tf_op jit(solution)/shard_map/ppermute | solution.py:376
  116.0 9.6 %collective-permute-start.16 = (bf16[288,640]{1,0:T(8,128)(2,1)S(1)}, bf16[288,640]{1,0:T(8,128)(2,1)S(1)}, u32[]{:S(2)}, u32[]{:S(2)}) collective-permute-start(bf16[288,640]{1,0:T(8,128)(2,1)S(1)} %pad_maximum_fusion.2), channel_id=1, source_target_pairs={{0,1},{1,0},{2,3},{3,2},{4,5},{5,4},{6,7},{7,6},{8,9},{9,8},{10,11... | collective-permute-start | bytes 1105928 | tf_op jit(solution)/shard_map/ppermute | solution.py:367
  125.6 2.2 %collective-permute-start.15 = (bf16[288,640]{1,0:T(8,128)(2,1)S(1)}, bf16[288,640]{1,0:T(8,128)(2,1)S(1)}, u32[]{:S(2)}, u32[]{:S(2)}) collective-permute-start(bf16[288,640]{1,0:T(8,128)(2,1)S(1)} %pad_maximum_fusion.2), channel_id=1, source_target_pairs={{1,2},{3,4},{5,6},{7,8},{9,10},{11,12},{13,14},{15,16},{17,18},{19... | collective-permute-start | bytes 1105928 | tf_op jit(solution)/shard_map/ppermute | solution.py:376
  127.8 1.8 %shard_map.227.gq_ref = bf16[128,576]{1,0:T(8,128)(2,1)S(1)} custom-call(bf16[1152,1728]{1,0:T(8,128)(2,1)S(1)} %get-tuple-element.30.win_ref, bf16[1024,1152]{1,0:T(8,128)(2,1)S(1)} %get-tuple-element.38.e_ref, bf16[144,640]{1,0:T(8,128)(2,1)S(1)} %get-tuple-element.33.own_ref.up_ref, f32[128,128]{1,0:T(8,128)S(1)} %get-tuple-element.39.stat_ref), custom_call_target="tpu_custom_call" | custom-call | flops 4000000000 | bytes 6000000 | tf_op jit(solution)/shard_map/pallas_call | solution.py:439
  129.6 0.5 shard_map.228.order_ref
  130.1 2.0 %shard_map.226 = (f32[128,640]{1,0:T(8,128)S(1)}, f32[128,640]{1,0:T(8,128)S(1)}) custom-call(s32[1]{0:T(128)} %bitcast.core_ref, bf16[1152,1728]{1,0:T(8,128)(2,1)S(1)} %get-tuple-element.30.win_ref, bf16[144,640]{1,0:T(8,128)(2,1)S(1)} %get-tuple-element.33.own_ref.up_ref, bf16[144,640]{1,0:T(8,128)(2,1)S(1)} %collective-permute-done.13.before_ref, ...), custom_call_target="tpu_custom_call" | custom-call | flops 4000000000 | bytes 6000000 | tf_op jit(solution)/shard_map/pallas_call | solution.py:444
  132.1 4.4 %collective-permute-done.15.packo_ref = bf16[288,640]{1,0:T(8,128)(2,1)S(1)} collective-permute-done((bf16[288,640]{1,0:T(8,128)(2,1)S(1)}, bf16[288,640]{1,0:T(8,128)(2,1)S(1)}, u32[]{:S(2)}, u32[]{:S(2)}) %collective-permute-start.15) | collective-permute-done | bytes 368672 | tf_op jit(solution)/shard_map/ppermute | solution.py:376
  136.5 4.9 %shard_map.229 = f32[128,1152]{1,0:T(8,128)} custom-call(s32[1]{0:T(128)} %bitcast.core_ref, bf16[1152,1728]{1,0:T(8,128)(2,1)S(1)} %get-tuple-element.30.win_ref, bf16[288,640]{1,0:T(8,128)(2,1)S(1)} %collective-permute-done.15.packo_ref, bf16[288,640]{1,0:T(8,128)(2,1)S(1)} %collective-permute-done.16.packi_ref, f32[128,640]{1,0:T(8,128)S(1)} %get-tuple-element.36.gk0_ref, ...), custom_call_target="tpu_custom_call" | custom-call | tf_op jit(solution)/shard_map/pallas_call | solution.py:449
  (57 shorter events, 0.3 us)
Async XLA Ops:
  0.6 21.2 %collective-permute-start.3 = (bf16[128,1152]{1,0:T(8,128)(2,1)}, bf16[128,1152]{1,0:T(8,128)(2,1)S(1)}, u32[]{:S(2)}, u32[]{:S(2)}) collective-permute-start(bf16[128,1152]{1,0:T(8,128)(2,1)} %bitcast.7), channel_id=1, source_target_pairs={{32,0},{64,32},{96,64},{128,96},{160,128},{192,160},{224,192},{256... | collective-permute-start | bytes 884744 | tf_op jit(solution)/shard_map/ppermute | solution.py:373
  4.6 22.5 %collective-permute-start.2 = (bf16[128,1152]{1,0:T(8,128)(2,1)}, bf16[128,1152]{1,0:T(8,128)(2,1)S(1)}, u32[]{:S(2)}, u32[]{:S(2)}) collective-permute-start(bf16[128,1152]{1,0:T(8,128)(2,1)} %bitcast.8), channel_id=1, source_target_pairs={{0,32},{32,64},{64,96},{96,128},{128,160},{160,192},{192,224},{224... | collective-permute-start | bytes 884744 | tf_op jit(solution)/shard_map/ppermute | solution.py:373
  14.9 26.8 %collective-permute-start.1 = (bf16[96,1728]{1,0:T(8,128)(2,1)S(1)}, bf16[96,1728]{1,0:T(8,128)(2,1)S(1)}, u32[]{:S(2)}, u32[]{:S(2)}) collective-permute-start(bf16[96,1728]{1,0:T(8,128)(2,1)S(1)} %fusion.2), channel_id=1, source_target_pairs={{440,0},{377,1},{474,2},{347,3},{508,4},{317,5},{286,6},{7,7},{432... | collective-permute-start | bytes 995336 | tf_op jit(solution)/shard_map/ppermute | solution.py:390
  15.6 26.2 %collective-permute-start = (bf16[96,1728]{1,0:T(8,128)(2,1)S(1)}, bf16[96,1728]{1,0:T(8,128)(2,1)S(1)}, u32[]{:S(2)}, u32[]{:S(2)}) collective-permute-start(bf16[96,1728]{1,0:T(8,128)(2,1)S(1)} %fusion.2), channel_id=1, source_target_pairs={{224,0},{33,1},{194,2},{67,3},{164,4},{101,5},{134,6},{415,7},{232... | collective-permute-start | bytes 995336 | tf_op jit(solution)/shard_map/ppermute | solution.py:390
  28.2 35.0 %collective-permute-start.7 = (bf16[384,1152]{1,0:T(8,128)(2,1)S(1)}, bf16[384,1152]{1,0:T(8,128)(2,1)S(1)}, u32[]{:S(2)}, u32[]{:S(2)}) collective-permute-start(bf16[384,1152]{1,0:T(8,128)(2,1)S(1)} %pad_maximum_fusion.x_ref), channel_id=1, source_target_pairs={{1,2},{3,4},{5,6},{7,8},{9,10},{11,12},{13,14},{15,16},{17,18},{19... | collective-permute-start | bytes 2654216 | tf_op jit(solution)/shard_map/ppermute | solution.py:376
  36.8 10.4 %collective-permute-start.6 = (bf16[384,1152]{1,0:T(8,128)(2,1)S(1)}, bf16[384,1152]{1,0:T(8,128)(2,1)S(1)}, u32[]{:S(2)}, u32[]{:S(2)}) collective-permute-start(bf16[384,1152]{1,0:T(8,128)(2,1)S(1)} %pad_maximum_fusion.x_ref), channel_id=1, source_target_pairs={{0,1},{1,0},{2,3},{3,2},{4,5},{5,4},{6,7},{7,6},{8,9},{9,8},{10,11... | collective-permute-start | bytes 2654216 | tf_op jit(solution)/shard_map/ppermute | solution.py:367
  40.8 0.9 copy-start.6
  41.9 24.1 %copy-start.11 = (s32[1,2,3,5]{3,1,2,0:T(2,128)S(1)}, s32[1,2,3,5]{3,1,2,0:T(2,128)}, u32[]{:S(2)}) copy-start(s32[1,2,3,5]{3,1,2,0:T(2,128)} %param.31) | copy-start | bytes 364
  41.9 18.1 %collective-permute-start.5 = (bf16[192,1728]{1,0:T(8,128)(2,1)S(1)}, bf16[192,1728]{1,0:T(8,128)(2,1)S(1)}, u32[]{:S(2)}, u32[]{:S(2)}) collective-permute-start(bf16[192,1728]{1,0:T(8,128)(2,1)S(1)} %pad_maximum_fusion.1.b0), channel_id=1, source_target_pairs={{2,0},{4,2},{6,4},{0,6},{1,3},{3,5},{5,7},{7,1},{10,8},{12,10},{14... | collective-permute-start | bytes 1990664 | tf_op jit(solution)/shard_map/ppermute | solution.py:370
  43.9 19.3 %collective-permute-start.4 = (bf16[192,1728]{1,0:T(8,128)(2,1)S(1)}, bf16[192,1728]{1,0:T(8,128)(2,1)S(1)}, u32[]{:S(2)}, u32[]{:S(2)}) collective-permute-start(bf16[192,1728]{1,0:T(8,128)(2,1)S(1)} %pad_maximum_fusion.1.b0), channel_id=1, source_target_pairs={{0,2},{2,4},{4,6},{6,0},{3,1},{5,3},{7,5},{1,7},{8,10},{10,12},{12... | collective-permute-start | bytes 1990664 | tf_op jit(solution)/shard_map/ppermute | solution.py:370
  49.3 0.9 copy-start.8
  63.1 0.9 copy-start.1
  64.1 12.9 %collective-permute-start.8 = (bf16[192,1728]{1,0:T(8,128)(2,1)S(1)}, bf16[192,1728]{1,0:T(8,128)(2,1)S(1)}, u32[]{:S(2)}, u32[]{:S(2)}) collective-permute-start(bf16[192,1728]{1,0:T(8,128)(2,1)S(1)} %collective-permute-done.4.b1), channel_id=1, source_target_pairs={{0,2},{2,4},{4,6},{6,0},{3,1},{5,3},{7,5},{1,7},{8,10},{10,12},{12... | collective-permute-start | bytes 1990664 | tf_op jit(solution)/shard_map/ppermute | solution.py:370
  66.0 13.1 %copy-start.13 = (s32[384]{0:T(512)S(1)}, s32[384]{0:T(512)}, u32[]{:S(2)}) copy-start(s32[384]{0:T(512)} %constant.86.clone) | copy-start | bytes 4612
  66.0 13.1 %copy-start.14 = (s32[384]{0:T(512)S(1)}, s32[384]{0:T(512)}, u32[]{:S(2)}) copy-start(s32[384]{0:T(512)} %constant.85.clone) | copy-start | bytes 4612
  66.0 13.0 %copy-start.17 = (pred[384]{0:T(512)(128)(4,1)S(1)}, pred[384]{0:T(512)(128)(4,1)}, u32[]{:S(2)}) copy-start(pred[384]{0:T(512)(128)(4,1)} %constant.88.clone) | copy-start | bytes 1156
  66.0 13.1 %copy-start.16 = (pred[384]{0:T(512)(128)(4,1)S(1)}, pred[384]{0:T(512)(128)(4,1)}, u32[]{:S(2)}) copy-start(pred[384]{0:T(512)(128)(4,1)} %constant.90.clone) | copy-start | bytes 1156
  66.1 13.0 %copy-start.10 = (s32[384]{0:T(512)S(1)}, s32[384]{0:T(512)}, u32[]{:S(2)}) copy-start(s32[384]{0:T(512)} %constant.89.clone) | copy-start | bytes 4612
  66.1 13.0 %copy-start.12 = (s32[384]{0:T(512)S(1)}, s32[384]{0:T(512)}, u32[]{:S(2)}) copy-start(s32[384]{0:T(512)} %constant.87.clone) | copy-start | bytes 4612
  66.1 13.1 %copy-start.15 = (pred[384]{0:T(512)(128)(4,1)S(1)}, pred[384]{0:T(512)(128)(4,1)}, u32[]{:S(2)}) copy-start(pred[384]{0:T(512)(128)(4,1)} %constant.91.clone) | copy-start | bytes 1156
  66.2 13.2 %collective-permute-start.9 = (bf16[192,1728]{1,0:T(8,128)(2,1)S(1)}, bf16[192,1728]{1,0:T(8,128)(2,1)S(1)}, u32[]{:S(2)}, u32[]{:S(2)}) collective-permute-start(bf16[192,1728]{1,0:T(8,128)(2,1)S(1)} %pad_maximum_fusion.1.b0), channel_id=1, source_target_pairs={{0,1},{1,0},{2,3},{3,2},{4,5},{5,4},{6,7},{7,6},{8,9},{9,8},{10,11... | collective-permute-start | bytes 1990664 | tf_op jit(solution)/shard_map/ppermute | solution.py:367
  69.1 10.3 %collective-permute-start.10 = (bf16[192,1728]{1,0:T(8,128)(2,1)S(1)}, bf16[192,1728]{1,0:T(8,128)(2,1)S(1)}, u32[]{:S(2)}, u32[]{:S(2)}) collective-permute-start(bf16[192,1728]{1,0:T(8,128)(2,1)S(1)} %collective-permute-done.4.b1), channel_id=1, source_target_pairs={{0,1},{1,0},{2,3},{3,2},{4,5},{5,4},{6,7},{7,6},{8,9},{9,8},{10,11... | collective-permute-start | bytes 1990664 | tf_op jit(solution)/shard_map/ppermute | solution.py:367
  71.0 8.3 %collective-permute-start.11 = (bf16[192,1728]{1,0:T(8,128)(2,1)S(1)}, bf16[192,1728]{1,0:T(8,128)(2,1)S(1)}, u32[]{:S(2)}, u32[]{:S(2)}) collective-permute-start(bf16[192,1728]{1,0:T(8,128)(2,1)S(1)} %collective-permute-done.5.b2), channel_id=1, source_target_pairs={{0,1},{1,0},{2,3},{3,2},{4,5},{5,4},{6,7},{7,6},{8,9},{9,8},{10,11... | collective-permute-start | bytes 1990664 | tf_op jit(solution)/shard_map/ppermute | solution.py:367
  73.4 1.2 copy-start.2
  74.6 6.4 %copy-start.7 = (bf16[384,1152]{1,0:T(8,128)(2,1)S(1)}, bf16[384,1152]{1,0:T(8,128)(2,1)}, u32[]{:S(2)}) copy-start(bf16[384,1152]{1,0:T(8,128)(2,1)} %copy-done.6) | copy-start | bytes 2654212
  74.6 6.4 %copy-start.9 = (bf16[384,1152]{1,0:T(8,128)(2,1)S(1)}, bf16[384,1152]{1,0:T(8,128)(2,1)}, u32[]{:S(2)}) copy-start(bf16[384,1152]{1,0:T(8,128)(2,1)} %copy-done.8) | copy-start | bytes 2654212
  76.9 4.0 %collective-permute-start.12 = (bf16[192,1728]{1,0:T(8,128)(2,1)S(1)}, bf16[192,1728]{1,0:T(8,128)(2,1)S(1)}, u32[]{:S(2)}, u32[]{:S(2)}) collective-permute-start(bf16[192,1728]{1,0:T(8,128)(2,1)S(1)} %collective-permute-done.8.b3), channel_id=1, source_target_pairs={{0,1},{1,0},{2,3},{3,2},{4,5},{5,4},{6,7},{7,6},{8,9},{9,8},{10,11... | collective-permute-start | bytes 1990664 | tf_op jit(solution)/shard_map/ppermute | solution.py:367
  79.3 9.1 %copy-start = (bf16[8,16,1152]{2,1,0:T(8,128)(2,1)S(1)}, bf16[8,16,1152]{2,1,0:T(8,128)(2,1)}, u32[]{:S(2)}) copy-start(bf16[8,16,1152]{2,1,0:T(8,128)(2,1)} %param.22) | copy-start | bytes 884740
  79.3 9.1 %copy-start.3 = (bf16[1152,192]{0,1:T(8,128)(2,1)S(1)}, bf16[1152,192]{0,1:T(8,128)(2,1)}, u32[]{:S(2)}) copy-start(bf16[1152,192]{0,1:T(8,128)(2,1)} %param.28) | copy-start | bytes 1327108
  79.3 9.1 %copy-start.4 = (f32[8,16,64]{2,1,0:T(8,128)S(1)}, f32[8,16,64]{2,1,0:T(8,128)}, u32[]{:S(2)}) copy-start(f32[8,16,64]{2,1,0:T(8,128)} %param.29) | copy-start | bytes 98308
  79.3 9.1 %copy-start.5 = (s32[8,16,64]{2,1,0:T(8,128)S(1)}, s32[8,16,64]{2,1,0:T(8,128)}, u32[]{:S(2)}) copy-start(s32[8,16,64]{2,1,0:T(8,128)} %param.30) | copy-start | bytes 98308
  93.9 22.0 %collective-permute-start.14 = (bf16[144,640]{1,0:T(8,128)(2,1)S(1)}, bf16[144,640]{1,0:T(8,128)(2,1)S(1)}, u32[]{:S(2)}, u32[]{:S(2)}) collective-permute-start(bf16[144,640]{1,0:T(8,128)(2,1)S(1)} %get-tuple-element.33.own_ref.up_ref), channel_id=1, source_target_pairs={{32,0},{64,32},{96,64},{128,96},{160,128},{192,160},{224,192},{256... | collective-permute-start | bytes 552968 | tf_op jit(solution)/shard_map/ppermute | solution.py:373
  95.8 20.1 %collective-permute-start.13 = (bf16[144,640]{1,0:T(8,128)(2,1)S(1)}, bf16[144,640]{1,0:T(8,128)(2,1)S(1)}, u32[]{:S(2)}, u32[]{:S(2)}) collective-permute-start(bf16[144,640]{1,0:T(8,128)(2,1)S(1)} %get-tuple-element.33.own_ref.up_ref), channel_id=1, source_target_pairs={{0,32},{32,64},{64,96},{96,128},{128,160},{160,192},{192,224},{224... | collective-permute-start | bytes 552968 | tf_op jit(solution)/shard_map/ppermute | solution.py:373
  107.7 22.3 %collective-permute-start.18 = (bf16[144,640]{1,0:T(8,128)(2,1)S(1)}, bf16[144,640]{1,0:T(8,128)(2,1)S(1)}, u32[]{:S(2)}, u32[]{:S(2)}) collective-permute-start(bf16[144,640]{1,0:T(8,128)(2,1)S(1)} %get-tuple-element.33.own_ref.up_ref), channel_id=1, source_target_pairs={{0,1},{1,0},{2,3},{3,2},{4,5},{5,4},{6,7},{7,6},{8,9},{9,8},{10,11... | collective-permute-start | bytes 552968 | tf_op jit(solution)/shard_map/ppermute | solution.py:367
  110.1 20.0 %collective-permute-start.17 = (bf16[144,640]{1,0:T(8,128)(2,1)S(1)}, bf16[144,640]{1,0:T(8,128)(2,1)S(1)}, u32[]{:S(2)}, u32[]{:S(2)}) collective-permute-start(bf16[144,640]{1,0:T(8,128)(2,1)S(1)} %get-tuple-element.33.own_ref.up_ref), channel_id=1, source_target_pairs={{1,2},{3,4},{5,6},{7,8},{9,10},{11,12},{13,14},{15,16},{17,18},{19... | collective-permute-start | bytes 552968 | tf_op jit(solution)/shard_map/ppermute | solution.py:376
  116.0 16.1 %collective-permute-start.16 = (bf16[288,640]{1,0:T(8,128)(2,1)S(1)}, bf16[288,640]{1,0:T(8,128)(2,1)S(1)}, u32[]{:S(2)}, u32[]{:S(2)}) collective-permute-start(bf16[288,640]{1,0:T(8,128)(2,1)S(1)} %pad_maximum_fusion.2), channel_id=1, source_target_pairs={{0,1},{1,0},{2,3},{3,2},{4,5},{5,4},{6,7},{7,6},{8,9},{9,8},{10,11... | collective-permute-start | bytes 1105928 | tf_op jit(solution)/shard_map/ppermute | solution.py:367
  125.6 10.9 %collective-permute-start.15 = (bf16[288,640]{1,0:T(8,128)(2,1)S(1)}, bf16[288,640]{1,0:T(8,128)(2,1)S(1)}, u32[]{:S(2)}, u32[]{:S(2)}) collective-permute-start(bf16[288,640]{1,0:T(8,128)(2,1)S(1)} %pad_maximum_fusion.2), channel_id=1, source_target_pairs={{1,2},{3,4},{5,6},{7,8},{9,10},{11,12},{13,14},{15,16},{17,18},{19... | collective-permute-start | bytes 1105928 | tf_op jit(solution)/shard_map/ppermute | solution.py:376

commit v10 on v9

--- a/solution.py
+++ b/solution.py
@@ -408,11 +408,10 @@
             cost_estimate=pl.CostEstimate(flops=3_000_000_000, bytes_accessed=5_000_000, transcendentals=0),
         )(v, gain, target)
 
-    fetched, hc = lax.optimization_barrier((fetched, hidden(column)))
     right, left = along(fetched, ring), along(fetched, back)
     right, left, he, outer = lax.optimization_barrier((right, left, hidden(inner), outer))
     fetched_too = swap(fetched)
-    across, hw = lax.optimization_barrier((along(right, ring), hidden(outer)))
+    across, hw, hc = lax.optimization_barrier((along(right, ring), hidden(outer), hidden(column)))
     blocks = (fetched, right, left, across, fetched_too, swap(right), swap(left), swap(across))
 
     win, wn = pl.pallas_call(

time: 142 us -> 147 us (1.035)
  the two profiles are of different devices: /device:TPU:47 before, /device:TPU:48 now
where the time goes in v10:
time: 147 us; the launch traced here: 146 us
  starting transfers between devices  67.2 us (46%)
  waiting for transfers between devices  40.7 us (28%)
  Pallas kernels  32.9 us (22%)
  other arithmetic  2.5 us (2%)
    ppermute x2, starting transfers between devices, rows_beside(): lax.ppermute(own, lat + ('core',), north)  21.3 us
    ppermute x7, starting transfers between devices, swap(): return lax.ppermute(v, 'core', [(0, 1), (1, 0)])  17.7 us
    ppermute x3, waiting for transfers between devices, along(): return lax.ppermute(v, ('x', 'core'), perm)  16.7 us
    ppermute x2, waiting for transfers between devices, rows_beside(): lax.ppermute(own, lat + ('core',), south)  11.5 us
    ppermute x3, starting transfers between devices, along(): return lax.ppermute(v, ('x', 'core'), perm)  9.52 us
    ppermute x3, starting transfers between devices, sides(): return (lax.ppermute(column, lon, border), swap(column))  9.47 us
    pallas_call x3, Pallas kernels, hidden(): pl.pallas_call(hidden_kernel, out_shape=shaped((3 * T, D)), in_specs=[VME...  8.66 us
    pallas_call x1, Pallas kernels, on_device(): pl.pallas_call(project_kernel, out_shape=(shaped((9 * T, QKV)), shaped((6...  8.44 us
  transfers between devices with their start and end apart: 19, of which 6 were waited for; matrix products, arithmetic and copies ran while one was open for 2% of the time, Pallas kernels for 9%

profile of v10, /device:TPU:48, one launch (start us, length us, event | category | flops | bytes accessed | tf_op | source)
XLA Modules:
  0.0 145.8 jit_solution(10299856172626134893)
XLA Ops:
  0.6 12.3 %collective-permute-start.5 = (bf16[128,1152]{1,0:T(8,128)(2,1)}, bf16[128,1152]{1,0:T(8,128)(2,1)S(1)}, u32[]{:S(2)}, u32[]{:S(2)}) collective-permute-start(bf16[128,1152]{1,0:T(8,128)(2,1)} %bitcast.7), channel_id=1, source_target_pairs={{32,0},{64,32},{96,64},{128,96},{160,128},{192,160},{224,192},{256... | collective-permute-start | bytes 884744 | tf_op jit(solution)/shard_map/ppermute | solution.py:373
  12.9 1.9 %collective-permute-start.4 = (bf16[128,1152]{1,0:T(8,128)(2,1)}, bf16[128,1152]{1,0:T(8,128)(2,1)S(1)}, u32[]{:S(2)}, u32[]{:S(2)}) collective-permute-start(bf16[128,1152]{1,0:T(8,128)(2,1)} %bitcast.8), channel_id=1, source_target_pairs={{0,32},{32,64},{64,96},{96,128},{128,160},{160,192},{192,224},{224... | collective-permute-start | bytes 884744 | tf_op jit(solution)/shard_map/ppermute | solution.py:373
  14.9 1.2 fusion.2
  16.1 1.9 %collective-permute-start.1 = (bf16[96,1728]{1,0:T(8,128)(2,1)S(1)}, bf16[96,1728]{1,0:T(8,128)(2,1)S(1)}, u32[]{:S(2)}, u32[]{:S(2)}) collective-permute-start(bf16[96,1728]{1,0:T(8,128)(2,1)S(1)} %fusion.2), channel_id=1, source_target_pairs={{440,0},{377,1},{474,2},{347,3},{508,4},{317,5},{286,6},{7,7},{432... | collective-permute-start | bytes 995336 | tf_op jit(solution)/shard_map/ppermute | solution.py:390
  18.0 3.4 %collective-permute-start = (bf16[96,1728]{1,0:T(8,128)(2,1)S(1)}, bf16[96,1728]{1,0:T(8,128)(2,1)S(1)}, u32[]{:S(2)}, u32[]{:S(2)}) collective-permute-start(bf16[96,1728]{1,0:T(8,128)(2,1)S(1)} %fusion.2), channel_id=1, source_target_pairs={{224,0},{33,1},{194,2},{67,3},{164,4},{101,5},{134,6},{415,7},{232... | collective-permute-start | bytes 995336 | tf_op jit(solution)/shard_map/ppermute | solution.py:390
  21.5 7.1 %collective-permute-done.5 = bf16[128,1152]{1,0:T(8,128)(2,1)S(1)} collective-permute-done((bf16[128,1152]{1,0:T(8,128)(2,1)}, bf16[128,1152]{1,0:T(8,128)(2,1)S(1)}, u32[]{:S(2)}, u32[]{:S(2)}) %collective-permute-start.5) | collective-permute-done | bytes 294944 | tf_op jit(solution)/shard_map/ppermute | solution.py:373
  28.6 4.4 %collective-permute-done.4 = bf16[128,1152]{1,0:T(8,128)(2,1)S(1)} collective-permute-done((bf16[128,1152]{1,0:T(8,128)(2,1)}, bf16[128,1152]{1,0:T(8,128)(2,1)S(1)}, u32[]{:S(2)}, u32[]{:S(2)}) %collective-permute-start.4) | collective-permute-done | bytes 294944 | tf_op jit(solution)/shard_map/ppermute | solution.py:373
  33.0 1.0 pad_maximum_fusion.x_ref
  34.0 0.0 copy-start.7
  34.0 0.0 copy-start.9
  34.0 0.0 copy-start.10
  34.0 0.0 copy-start.13
  34.1 2.1 %collective-permute-start.6 = (bf16[384,1152]{1,0:T(8,128)(2,1)S(1)}, bf16[384,1152]{1,0:T(8,128)(2,1)}, u32[]{:S(2)}, u32[]{:S(2)}) collective-permute-start(bf16[384,1152]{1,0:T(8,128)(2,1)S(1)} %pad_maximum_fusion.x_ref), channel_id=1, source_target_pairs={{0,1},{1,0},{2,3},{3,2},{4,5},{5,4},{6,7},{7,6},{8,9},{9,8},{10,11... | collective-permute-start | bytes 2654216 | tf_op jit(solution)/shard_map/ppermute | solution.py:367
  36.1 4.5 %collective-permute-start.7 = (bf16[384,1152]{1,0:T(8,128)(2,1)S(1)}, bf16[384,1152]{1,0:T(8,128)(2,1)}, u32[]{:S(2)}, u32[]{:S(2)}) collective-permute-start(bf16[384,1152]{1,0:T(8,128)(2,1)S(1)} %pad_maximum_fusion.x_ref), channel_id=1, source_target_pairs={{1,2},{3,4},{5,6},{7,8},{9,10},{11,12},{13,14},{15,16},{17,18},{19... | collective-permute-start | bytes 2654216 | tf_op jit(solution)/shard_map/ppermute | solution.py:376
  40.7 0.1 pad_maximum_fusion.1.b0
  40.8 5.0 %collective-permute-start.3 = (bf16[192,1728]{1,0:T(8,128)(2,1)S(1)}, bf16[192,1728]{1,0:T(8,128)(2,1)S(1)}, u32[]{:S(2)}, u32[]{:S(2)}) collective-permute-start(bf16[192,1728]{1,0:T(8,128)(2,1)S(1)} %pad_maximum_fusion.1.b0), channel_id=1, source_target_pairs={{2,0},{4,2},{6,4},{0,6},{1,3},{3,5},{5,7},{7,1},{10,8},{12,10},{14... | collective-permute-start | bytes 1990664 | tf_op jit(solution)/shard_map/ppermute | solution.py:370
  45.8 1.9 %collective-permute-start.2 = (bf16[192,1728]{1,0:T(8,128)(2,1)S(1)}, bf16[192,1728]{1,0:T(8,128)(2,1)S(1)}, u32[]{:S(2)}, u32[]{:S(2)}) collective-permute-start(bf16[192,1728]{1,0:T(8,128)(2,1)S(1)} %pad_maximum_fusion.1.b0), channel_id=1, source_target_pairs={{0,2},{2,4},{4,6},{6,0},{3,1},{5,3},{7,5},{1,7},{8,10},{10,12},{12... | collective-permute-start | bytes 1990664 | tf_op jit(solution)/shard_map/ppermute | solution.py:370
  47.8 3.3 %shard_map.221.he_ref = bf16[384,1152]{1,0:T(8,128)(2,1)S(1)} custom-call(bf16[384,1152]{1,0:T(8,128)(2,1)} %collective-permute-done.6.x_ref, f32[1,1152]{1,0:T(1,128)S(1)} %reshape.34.gain_ref, s32[1,1152]{1,0:T(1,128)S(1)} %reshape.35.target_ref), custom_call_target="tpu_custom_call" | custom-call | flops 3000000000 | bytes 5000000 | tf_op jit(solution)/shard_map/pallas_call | solution.py:405
  51.1 0.9 copy-done.4
  52.0 16.7 %collective-permute-done.3.b2 = bf16[192,1728]{1,0:T(8,128)(2,1)S(1)} collective-permute-done((bf16[192,1728]{1,0:T(8,128)(2,1)S(1)}, bf16[192,1728]{1,0:T(8,128)(2,1)S(1)}, u32[]{:S(2)}, u32[]{:S(2)}) %collective-permute-start.3) | collective-permute-done | bytes 663584 | tf_op jit(solution)/shard_map/ppermute | solution.py:370
  68.8 2.6 %collective-permute-start.8 = (bf16[192,1728]{1,0:T(8,128)(2,1)S(1)}, bf16[192,1728]{1,0:T(8,128)(2,1)}, u32[]{:S(2)}, u32[]{:S(2)}) collective-permute-start(bf16[192,1728]{1,0:T(8,128)(2,1)S(1)} %collective-permute-done.2.b1), channel_id=1, source_target_pairs={{0,2},{2,4},{4,6},{6,0},{3,1},{5,3},{7,5},{1,7},{8,10},{10,12},{12... | collective-permute-start | bytes 1990664 | tf_op jit(solution)/shard_map/ppermute | solution.py:370
  71.4 0.1 reshape.31
  71.5 2.1 %shard_map.223.hc_ref = bf16[384,1152]{1,0:T(8,128)(2,1)S(1)} custom-call(bf16[384,1152]{1,0:T(8,128)(2,1)S(1)} %pad_maximum_fusion.x_ref, f32[1,1152]{1,0:T(1,128)S(1)} %reshape.34.gain_ref, s32[1,1152]{1,0:T(1,128)S(1)} %reshape.35.target_ref), custom_call_target="tpu_custom_call" | custom-call | flops 3000000000 | bytes 5000000 | tf_op jit(solution)/shard_map/pallas_call | solution.py:405
  73.6 0.0 copy-start.11
  73.6 0.0 copy-start.15
  73.6 0.0 copy-start.16
  73.6 0.0 copy-start.19
  73.7 4.9 %collective-permute-start.9 = (bf16[192,1728]{1,0:T(8,128)(2,1)S(1)}, bf16[192,1728]{1,0:T(8,128)(2,1)S(1)}, u32[]{:S(2)}, u32[]{:S(2)}) collective-permute-start(bf16[192,1728]{1,0:T(8,128)(2,1)S(1)} %pad_maximum_fusion.1.b0), channel_id=1, source_target_pairs={{0,1},{1,0},{2,3},{3,2},{4,5},{5,4},{6,7},{7,6},{8,9},{9,8},{10,11... | collective-permute-start | bytes 1990664 | tf_op jit(solution)/shard_map/ppermute | solution.py:367
  78.6 1.9 %collective-permute-start.10 = (bf16[192,1728]{1,0:T(8,128)(2,1)S(1)}, bf16[192,1728]{1,0:T(8,128)(2,1)S(1)}, u32[]{:S(2)}, u32[]{:S(2)}) collective-permute-start(bf16[192,1728]{1,0:T(8,128)(2,1)S(1)} %collective-permute-done.2.b1), channel_id=1, source_target_pairs={{0,1},{1,0},{2,3},{3,2},{4,5},{5,4},{6,7},{7,6},{8,9},{9,8},{10,11... | collective-permute-start | bytes 1990664 | tf_op jit(solution)/shard_map/ppermute | solution.py:367
  80.5 2.4 %collective-permute-start.11 = (bf16[192,1728]{1,0:T(8,128)(2,1)S(1)}, bf16[192,1728]{1,0:T(8,128)(2,1)S(1)}, u32[]{:S(2)}, u32[]{:S(2)}) collective-permute-start(bf16[192,1728]{1,0:T(8,128)(2,1)S(1)} %collective-permute-done.3.b2), channel_id=1, source_target_pairs={{0,1},{1,0},{2,3},{3,2},{4,5},{5,4},{6,7},{7,6},{8,9},{9,8},{10,11... | collective-permute-start | bytes 1990664 | tf_op jit(solution)/shard_map/ppermute | solution.py:367
  82.9 3.3 %shard_map.222.hw_ref = bf16[384,1152]{1,0:T(8,128)(2,1)S(1)} custom-call(bf16[384,1152]{1,0:T(8,128)(2,1)} %collective-permute-done.7.x_ref, f32[1,1152]{1,0:T(1,128)S(1)} %reshape.34.gain_ref, s32[1,1152]{1,0:T(1,128)S(1)} %reshape.35.target_ref), custom_call_target="tpu_custom_call" | custom-call | flops 3000000000 | bytes 5000000 | tf_op jit(solution)/shard_map/pallas_call | solution.py:405
  86.2 2.1 %collective-permute-start.12 = (bf16[192,1728]{1,0:T(8,128)(2,1)}, bf16[192,1728]{1,0:T(8,128)(2,1)S(1)}, u32[]{:S(2)}, u32[]{:S(2)}) collective-permute-start(bf16[192,1728]{1,0:T(8,128)(2,1)} %collective-permute-done.8.b3), channel_id=1, source_target_pairs={{0,1},{1,0},{2,3},{3,2},{4,5},{5,4},{6,7},{7,6},{8,9},{9,8},{10,11... | collective-permute-start | bytes 1990664 | tf_op jit(solution)/shard_map/ppermute | solution.py:367
  88.5 0.1 pad_add_fusion.1.blocks_ref
  88.6 1.8 %collective-permute-done.12.b7 = bf16[192,1728]{1,0:T(8,128)(2,1)S(1)} collective-permute-done((bf16[192,1728]{1,0:T(8,128)(2,1)}, bf16[192,1728]{1,0:T(8,128)(2,1)S(1)}, u32[]{:S(2)}, u32[]{:S(2)}) %collective-permute-start.12) | collective-permute-done | bytes 663584 | tf_op jit(solution)/shard_map/ppermute | solution.py:367
  90.5 8.4 %shard_map.224 = (bf16[1152,1728]{1,0:T(8,128)(2,1)S(1)}, bf16[640,1152]{1,0:T(8,128)(2,1)S(1)}) custom-call(s32[3,384]{1,0:T(4,128)S(1)} %pad_add_fusion.place_ref, bf16[384,1152]{1,0:T(8,128)(2,1)S(1)} %shard_map.222.hw_ref, bf16[384,1152]{1,0:T(8,128)(2,1)S(1)} %shard_map.223.hc_ref, bf16[384,1152]{1,0:T(8,128)(2,1)S(1)} %copy-done.5, ...), custom_call_target="tpu_custom_call" | custom-call | flops 6000000000 | bytes 8000000 | tf_op jit(solution)/shard_map/pallas_call | solution.py:417
  98.9 5.5 %shard_map.225 = (bf16[1024,1152]{1,0:T(8,128)(2,1)S(1)}, bf16[128,1152]{1,0:T(8,128)(2,1)}, f32[128,1152]{1,0:T(8,128)S(1)}, bf16[144,640]{1,0:T(8,128)(2,1)S(1)}, f32[128,128]{1,0:T(8,128)S(1)}) custom-call(s32[31]{0:T(128)S(1)} %pad_add_fusion.1.blocks_ref, bf16[1152,1728]{1,0:T(8,128)(2,1)S(1)} %get-tuple-element.28.win_ref, ...), custom_call_target="tpu_custom_call" | custom-call | flops 6000000000 | bytes 8000000 | tf_op jit(solution)/shard_map/pallas_call | solution.py:424
  104.5 9.0 %collective-permute-start.14 = (bf16[144,640]{1,0:T(8,128)(2,1)S(1)}, bf16[144,640]{1,0:T(8,128)(2,1)S(1)}, u32[]{:S(2)}, u32[]{:S(2)}) collective-permute-start(bf16[144,640]{1,0:T(8,128)(2,1)S(1)} %get-tuple-element.31.own_ref.up_ref), channel_id=1, source_target_pairs={{32,0},{64,32},{96,64},{128,96},{160,128},{192,160},{224,192},{256... | collective-permute-start | bytes 552968 | tf_op jit(solution)/shard_map/ppermute | solution.py:373
  113.4 1.9 %collective-permute-start.13 = (bf16[144,640]{1,0:T(8,128)(2,1)S(1)}, bf16[144,640]{1,0:T(8,128)(2,1)S(1)}, u32[]{:S(2)}, u32[]{:S(2)}) collective-permute-start(bf16[144,640]{1,0:T(8,128)(2,1)S(1)} %get-tuple-element.31.own_ref.up_ref), channel_id=1, source_target_pairs={{0,32},{32,64},{64,96},{96,128},{128,160},{160,192},{192,224},{224... | collective-permute-start | bytes 552968 | tf_op jit(solution)/shard_map/ppermute | solution.py:373
  115.4 2.4 %collective-permute-start.18 = (bf16[144,640]{1,0:T(8,128)(2,1)S(1)}, bf16[144,640]{1,0:T(8,128)(2,1)S(1)}, u32[]{:S(2)}, u32[]{:S(2)}) collective-permute-start(bf16[144,640]{1,0:T(8,128)(2,1)S(1)} %get-tuple-element.31.own_ref.up_ref), channel_id=1, source_target_pairs={{0,1},{1,0},{2,3},{3,2},{4,5},{5,4},{6,7},{7,6},{8,9},{9,8},{10,11... | collective-permute-start | bytes 552968 | tf_op jit(solution)/shard_map/ppermute | solution.py:367
  117.8 1.9 %collective-permute-start.17 = (bf16[144,640]{1,0:T(8,128)(2,1)S(1)}, bf16[144,640]{1,0:T(8,128)(2,1)S(1)}, u32[]{:S(2)}, u32[]{:S(2)}) collective-permute-start(bf16[144,640]{1,0:T(8,128)(2,1)S(1)} %get-tuple-element.31.own_ref.up_ref), channel_id=1, source_target_pairs={{1,2},{3,4},{5,6},{7,8},{9,10},{11,12},{13,14},{15,16},{17,18},{19... | collective-permute-start | bytes 552968 | tf_op jit(solution)/shard_map/ppermute | solution.py:376
  119.8 7.1 %collective-permute-done.13.before_ref = bf16[144,640]{1,0:T(8,128)(2,1)S(1)} collective-permute-done((bf16[144,640]{1,0:T(8,128)(2,1)S(1)}, bf16[144,640]{1,0:T(8,128)(2,1)S(1)}, u32[]{:S(2)}, u32[]{:S(2)}) %collective-permute-start.13) | collective-permute-done | bytes 184352 | tf_op jit(solution)/shard_map/ppermute | solution.py:373
  126.9 1.9 %collective-permute-start.16 = (bf16[288,640]{1,0:T(8,128)(2,1)S(1)}, bf16[288,640]{1,0:T(8,128)(2,1)S(1)}, u32[]{:S(2)}, u32[]{:S(2)}) collective-permute-start(bf16[288,640]{1,0:T(8,128)(2,1)S(1)} %pad_maximum_fusion.2), channel_id=1, source_target_pairs={{0,1},{1,0},{2,3},{3,2},{4,5},{5,4},{6,7},{7,6},{8,9},{9,8},{10,11... | collective-permute-start | bytes 1105928 | tf_op jit(solution)/shard_map/ppermute | solution.py:367
  128.8 3.1 %collective-permute-start.15 = (bf16[288,640]{1,0:T(8,128)(2,1)S(1)}, bf16[288,640]{1,0:T(8,128)(2,1)S(1)}, u32[]{:S(2)}, u32[]{:S(2)}) collective-permute-start(bf16[288,640]{1,0:T(8,128)(2,1)S(1)} %pad_maximum_fusion.2), channel_id=1, source_target_pairs={{1,2},{3,4},{5,6},{7,8},{9,10},{11,12},{13,14},{15,16},{17,18},{19... | collective-permute-start | bytes 1105928 | tf_op jit(solution)/shard_map/ppermute | solution.py:376
  132.0 1.8 %shard_map.227.gq_ref = bf16[128,576]{1,0:T(8,128)(2,1)S(1)} custom-call(bf16[1152,1728]{1,0:T(8,128)(2,1)S(1)} %get-tuple-element.28.win_ref, bf16[1024,1152]{1,0:T(8,128)(2,1)S(1)} %get-tuple-element.36.e_ref, bf16[144,640]{1,0:T(8,128)(2,1)S(1)} %get-tuple-element.31.own_ref.up_ref, f32[128,128]{1,0:T(8,128)S(1)} %get-tuple-element.37.stat_ref), custom_call_target="tpu_custom_call" | custom-call | flops 4000000000 | bytes 6000000 | tf_op jit(solution)/shard_map/pallas_call | solution.py:438
  133.7 0.5 shard_map.228.order_ref
  134.2 2.0 %shard_map.226 = (f32[128,640]{1,0:T(8,128)S(1)}, f32[128,640]{1,0:T(8,128)S(1)}) custom-call(s32[1]{0:T(128)} %bitcast.core_ref, bf16[1152,1728]{1,0:T(8,128)(2,1)S(1)} %get-tuple-element.28.win_ref, bf16[144,640]{1,0:T(8,128)(2,1)S(1)} %get-tuple-element.31.own_ref.up_ref, bf16[144,640]{1,0:T(8,128)(2,1)S(1)} %collective-permute-done.13.before_ref, ...), custom_call_target="tpu_custom_call" | custom-call | flops 4000000000 | bytes 6000000 | tf_op jit(solution)/shard_map/pallas_call | solution.py:443
  136.3 3.5 %collective-permute-done.15.packo_ref = bf16[288,640]{1,0:T(8,128)(2,1)S(1)} collective-permute-done((bf16[288,640]{1,0:T(8,128)(2,1)S(1)}, bf16[288,640]{1,0:T(8,128)(2,1)S(1)}, u32[]{:S(2)}, u32[]{:S(2)}) %collective-permute-start.15) | collective-permute-done | bytes 368672 | tf_op jit(solution)/shard_map/ppermute | solution.py:376
  139.8 6.0 %shard_map.229 = f32[128,1152]{1,0:T(8,128)} custom-call(s32[1]{0:T(128)} %bitcast.core_ref, bf16[1152,1728]{1,0:T(8,128)(2,1)S(1)} %get-tuple-element.28.win_ref, bf16[288,640]{1,0:T(8,128)(2,1)S(1)} %collective-permute-done.15.packo_ref, bf16[288,640]{1,0:T(8,128)(2,1)S(1)} %collective-permute-done.16.packi_ref, f32[128,640]{1,0:T(8,128)S(1)} %get-tuple-element.34.gk0_ref, ...), custom_call_target="tpu_custom_call" | custom-call | tf_op jit(solution)/shard_map/pallas_call | solution.py:448
  (61 shorter events, 0.3 us)
Async XLA Ops:
  0.6 28.0 %collective-permute-start.5 = (bf16[128,1152]{1,0:T(8,128)(2,1)}, bf16[128,1152]{1,0:T(8,128)(2,1)S(1)}, u32[]{:S(2)}, u32[]{:S(2)}) collective-permute-start(bf16[128,1152]{1,0:T(8,128)(2,1)} %bitcast.7), channel_id=1, source_target_pairs={{32,0},{64,32},{96,64},{128,96},{160,128},{192,160},{224,192},{256... | collective-permute-start | bytes 884744 | tf_op jit(solution)/shard_map/ppermute | solution.py:373
  12.9 20.0 %collective-permute-start.4 = (bf16[128,1152]{1,0:T(8,128)(2,1)}, bf16[128,1152]{1,0:T(8,128)(2,1)S(1)}, u32[]{:S(2)}, u32[]{:S(2)}) collective-permute-start(bf16[128,1152]{1,0:T(8,128)(2,1)} %bitcast.8), channel_id=1, source_target_pairs={{0,32},{32,64},{64,96},{96,128},{128,160},{160,192},{192,224},{224... | collective-permute-start | bytes 884744 | tf_op jit(solution)/shard_map/ppermute | solution.py:373
  16.1 24.5 %collective-permute-start.1 = (bf16[96,1728]{1,0:T(8,128)(2,1)S(1)}, bf16[96,1728]{1,0:T(8,128)(2,1)S(1)}, u32[]{:S(2)}, u32[]{:S(2)}) collective-permute-start(bf16[96,1728]{1,0:T(8,128)(2,1)S(1)} %fusion.2), channel_id=1, source_target_pairs={{440,0},{377,1},{474,2},{347,3},{508,4},{317,5},{286,6},{7,7},{432... | collective-permute-start | bytes 995336 | tf_op jit(solution)/shard_map/ppermute | solution.py:390
  18.0 22.6 %collective-permute-start = (bf16[96,1728]{1,0:T(8,128)(2,1)S(1)}, bf16[96,1728]{1,0:T(8,128)(2,1)S(1)}, u32[]{:S(2)}, u32[]{:S(2)}) collective-permute-start(bf16[96,1728]{1,0:T(8,128)(2,1)S(1)} %fusion.2), channel_id=1, source_target_pairs={{224,0},{33,1},{194,2},{67,3},{164,4},{101,5},{134,6},{415,7},{232... | collective-permute-start | bytes 995336 | tf_op jit(solution)/shard_map/ppermute | solution.py:390
  34.0 13.7 %copy-start.6 = (f32[1152]{0:T(1024)S(1)}, f32[1152]{0:T(1024)}, u32[]{:S(2)}) copy-start(f32[1152]{0:T(1024)} %param.23) | copy-start | bytes 13828
  34.0 13.7 %copy-start.7 = (s32[1152]{0:T(1024)S(1)}, s32[1152]{0:T(1024)}, u32[]{:S(2)}) copy-start(s32[1152]{0:T(1024)} %constant.84.clone) | copy-start | bytes 13828
  34.0 13.7 %copy-start.8 = (s32[1152]{0:T(1024)S(1)}, s32[1152]{0:T(1024)}, u32[]{:S(2)}) copy-start(s32[1152]{0:T(1024)} %constant.82.clone) | copy-start | bytes 13828
  34.0 13.7 %copy-start.9 = (s32[1152]{0:T(1024)S(1)}, s32[1152]{0:T(1024)}, u32[]{:S(2)}) copy-start(s32[1152]{0:T(1024)} %constant.81.clone) | copy-start | bytes 13828
  34.0 13.7 %copy-start.10 = (s32[1152]{0:T(1024)S(1)}, s32[1152]{0:T(1024)}, u32[]{:S(2)}) copy-start(s32[1152]{0:T(1024)} %constant.80.clone) | copy-start | bytes 13828
  34.0 13.7 %copy-start.13 = (pred[1152]{0:T(1024)(128)(4,1)S(1)}, pred[1152]{0:T(1024)(128)(4,1)}, u32[]{:S(2)}) copy-start(pred[1152]{0:T(1024)(128)(4,1)} %constant.83.clone) | copy-start | bytes 3460
  34.1 13.8 %collective-permute-start.6 = (bf16[384,1152]{1,0:T(8,128)(2,1)S(1)}, bf16[384,1152]{1,0:T(8,128)(2,1)}, u32[]{:S(2)}, u32[]{:S(2)}) collective-permute-start(bf16[384,1152]{1,0:T(8,128)(2,1)S(1)} %pad_maximum_fusion.x_ref), channel_id=1, source_target_pairs={{0,1},{1,0},{2,3},{3,2},{4,5},{5,4},{6,7},{7,6},{8,9},{9,8},{10,11... | collective-permute-start | bytes 2654216 | tf_op jit(solution)/shard_map/ppermute | solution.py:367
  36.1 32.6 %collective-permute-start.7 = (bf16[384,1152]{1,0:T(8,128)(2,1)S(1)}, bf16[384,1152]{1,0:T(8,128)(2,1)}, u32[]{:S(2)}, u32[]{:S(2)}) collective-permute-start(bf16[384,1152]{1,0:T(8,128)(2,1)S(1)} %pad_maximum_fusion.x_ref), channel_id=1, source_target_pairs={{1,2},{3,4},{5,6},{7,8},{9,10},{11,12},{13,14},{15,16},{17,18},{19... | collective-permute-start | bytes 2654216 | tf_op jit(solution)/shard_map/ppermute | solution.py:376
  40.8 28.0 %collective-permute-start.3 = (bf16[192,1728]{1,0:T(8,128)(2,1)S(1)}, bf16[192,1728]{1,0:T(8,128)(2,1)S(1)}, u32[]{:S(2)}, u32[]{:S(2)}) collective-permute-start(bf16[192,1728]{1,0:T(8,128)(2,1)S(1)} %pad_maximum_fusion.1.b0), channel_id=1, source_target_pairs={{2,0},{4,2},{6,4},{0,6},{1,3},{3,5},{5,7},{7,1},{10,8},{12,10},{14... | collective-permute-start | bytes 1990664 | tf_op jit(solution)/shard_map/ppermute | solution.py:370
  45.8 23.0 %collective-permute-start.2 = (bf16[192,1728]{1,0:T(8,128)(2,1)S(1)}, bf16[192,1728]{1,0:T(8,128)(2,1)S(1)}, u32[]{:S(2)}, u32[]{:S(2)}) collective-permute-start(bf16[192,1728]{1,0:T(8,128)(2,1)S(1)} %pad_maximum_fusion.1.b0), channel_id=1, source_target_pairs={{0,2},{2,4},{4,6},{6,0},{3,1},{5,3},{7,5},{1,7},{8,10},{10,12},{12... | collective-permute-start | bytes 1990664 | tf_op jit(solution)/shard_map/ppermute | solution.py:370
  47.8 23.6 %copy-start.12 = (s32[1,2,3,5]{3,1,2,0:T(2,128)S(1)}, s32[1,2,3,5]{3,1,2,0:T(2,128)}, u32[]{:S(2)}) copy-start(s32[1,2,3,5]{3,1,2,0:T(2,128)} %param.31) | copy-start | bytes 364
  51.1 0.9 copy-start.4
  68.8 17.4 %collective-permute-start.8 = (bf16[192,1728]{1,0:T(8,128)(2,1)S(1)}, bf16[192,1728]{1,0:T(8,128)(2,1)}, u32[]{:S(2)}, u32[]{:S(2)}) collective-permute-start(bf16[192,1728]{1,0:T(8,128)(2,1)S(1)} %collective-permute-done.2.b1), channel_id=1, source_target_pairs={{0,2},{2,4},{4,6},{6,0},{3,1},{5,3},{7,5},{1,7},{8,10},{10,12},{12... | collective-permute-start | bytes 1990664 | tf_op jit(solution)/shard_map/ppermute | solution.py:370
  73.6 14.7 %copy-start.11 = (s32[384]{0:T(512)S(1)}, s32[384]{0:T(512)}, u32[]{:S(2)}) copy-start(s32[384]{0:T(512)} %constant.89.clone) | copy-start | bytes 4612
  73.6 14.7 %copy-start.14 = (s32[384]{0:T(512)S(1)}, s32[384]{0:T(512)}, u32[]{:S(2)}) copy-start(s32[384]{0:T(512)} %constant.87.clone) | copy-start | bytes 4612
  73.6 14.7 %copy-start.15 = (s32[384]{0:T(512)S(1)}, s32[384]{0:T(512)}, u32[]{:S(2)}) copy-start(s32[384]{0:T(512)} %constant.86.clone) | copy-start | bytes 4612
  73.6 14.7 %copy-start.16 = (s32[384]{0:T(512)S(1)}, s32[384]{0:T(512)}, u32[]{:S(2)}) copy-start(s32[384]{0:T(512)} %constant.85.clone) | copy-start | bytes 4612
  73.6 14.7 %copy-start.19 = (pred[384]{0:T(512)(128)(4,1)S(1)}, pred[384]{0:T(512)(128)(4,1)}, u32[]{:S(2)}) copy-start(pred[384]{0:T(512)(128)(4,1)} %constant.88.clone) | copy-start | bytes 1156
  73.7 14.7 %copy-start.17 = (pred[384]{0:T(512)(128)(4,1)S(1)}, pred[384]{0:T(512)(128)(4,1)}, u32[]{:S(2)}) copy-start(pred[384]{0:T(512)(128)(4,1)} %constant.91.clone) | copy-start | bytes 1156
  73.7 14.7 %copy-start.18 = (pred[384]{0:T(512)(128)(4,1)S(1)}, pred[384]{0:T(512)(128)(4,1)}, u32[]{:S(2)}) copy-start(pred[384]{0:T(512)(128)(4,1)} %constant.90.clone) | copy-start | bytes 1156
  73.7 16.8 %copy-start.5 = (bf16[384,1152]{1,0:T(8,128)(2,1)S(1)}, bf16[384,1152]{1,0:T(8,128)(2,1)}, u32[]{:S(2)}) copy-start(bf16[384,1152]{1,0:T(8,128)(2,1)} %copy-done.4) | copy-start | bytes 2654212
  73.7 14.9 %collective-permute-start.9 = (bf16[192,1728]{1,0:T(8,128)(2,1)S(1)}, bf16[192,1728]{1,0:T(8,128)(2,1)S(1)}, u32[]{:S(2)}, u32[]{:S(2)}) collective-permute-start(bf16[192,1728]{1,0:T(8,128)(2,1)S(1)} %pad_maximum_fusion.1.b0), channel_id=1, source_target_pairs={{0,1},{1,0},{2,3},{3,2},{4,5},{5,4},{6,7},{7,6},{8,9},{9,8},{10,11... | collective-permute-start | bytes 1990664 | tf_op jit(solution)/shard_map/ppermute | solution.py:367
  78.6 10.1 %collective-permute-start.10 = (bf16[192,1728]{1,0:T(8,128)(2,1)S(1)}, bf16[192,1728]{1,0:T(8,128)(2,1)S(1)}, u32[]{:S(2)}, u32[]{:S(2)}) collective-permute-start(bf16[192,1728]{1,0:T(8,128)(2,1)S(1)} %collective-permute-done.2.b1), channel_id=1, source_target_pairs={{0,1},{1,0},{2,3},{3,2},{4,5},{5,4},{6,7},{7,6},{8,9},{9,8},{10,11... | collective-permute-start | bytes 1990664 | tf_op jit(solution)/shard_map/ppermute | solution.py:367
  80.5 8.1 %collective-permute-start.11 = (bf16[192,1728]{1,0:T(8,128)(2,1)S(1)}, bf16[192,1728]{1,0:T(8,128)(2,1)S(1)}, u32[]{:S(2)}, u32[]{:S(2)}) collective-permute-start(bf16[192,1728]{1,0:T(8,128)(2,1)S(1)} %collective-permute-done.3.b2), channel_id=1, source_target_pairs={{0,1},{1,0},{2,3},{3,2},{4,5},{5,4},{6,7},{7,6},{8,9},{9,8},{10,11... | collective-permute-start | bytes 1990664 | tf_op jit(solution)/shard_map/ppermute | solution.py:367
  86.2 4.2 %collective-permute-start.12 = (bf16[192,1728]{1,0:T(8,128)(2,1)}, bf16[192,1728]{1,0:T(8,128)(2,1)S(1)}, u32[]{:S(2)}, u32[]{:S(2)}) collective-permute-start(bf16[192,1728]{1,0:T(8,128)(2,1)} %collective-permute-done.8.b3), channel_id=1, source_target_pairs={{0,1},{1,0},{2,3},{3,2},{4,5},{5,4},{6,7},{7,6},{8,9},{9,8},{10,11... | collective-permute-start | bytes 1990664 | tf_op jit(solution)/shard_map/ppermute | solution.py:367
  88.5 10.4 %copy-start = (bf16[8,16,1152]{2,1,0:T(8,128)(2,1)S(1)}, bf16[8,16,1152]{2,1,0:T(8,128)(2,1)}, u32[]{:S(2)}) copy-start(bf16[8,16,1152]{2,1,0:T(8,128)(2,1)} %param.22) | copy-start | bytes 884740
  88.6 10.4 %copy-start.1 = (bf16[1152,192]{0,1:T(8,128)(2,1)S(1)}, bf16[1152,192]{0,1:T(8,128)(2,1)}, u32[]{:S(2)}) copy-start(bf16[1152,192]{0,1:T(8,128)(2,1)} %param.28) | copy-start | bytes 1327108
  88.6 10.4 %copy-start.2 = (f32[8,16,64]{2,1,0:T(8,128)S(1)}, f32[8,16,64]{2,1,0:T(8,128)}, u32[]{:S(2)}) copy-start(f32[8,16,64]{2,1,0:T(8,128)} %param.29) | copy-start | bytes 98308
  88.6 10.4 %copy-start.3 = (s32[8,16,64]{2,1,0:T(8,128)S(1)}, s32[8,16,64]{2,1,0:T(8,128)}, u32[]{:S(2)}) copy-start(s32[8,16,64]{2,1,0:T(8,128)} %param.30) | copy-start | bytes 98308
  104.5 15.3 %collective-permute-start.14 = (bf16[144,640]{1,0:T(8,128)(2,1)S(1)}, bf16[144,640]{1,0:T(8,128)(2,1)S(1)}, u32[]{:S(2)}, u32[]{:S(2)}) collective-permute-start(bf16[144,640]{1,0:T(8,128)(2,1)S(1)} %get-tuple-element.31.own_ref.up_ref), channel_id=1, source_target_pairs={{32,0},{64,32},{96,64},{128,96},{160,128},{192,160},{224,192},{256... | collective-permute-start | bytes 552968 | tf_op jit(solution)/shard_map/ppermute | solution.py:373
  113.4 13.4 %collective-permute-start.13 = (bf16[144,640]{1,0:T(8,128)(2,1)S(1)}, bf16[144,640]{1,0:T(8,128)(2,1)S(1)}, u32[]{:S(2)}, u32[]{:S(2)}) collective-permute-start(bf16[144,640]{1,0:T(8,128)(2,1)S(1)} %get-tuple-element.31.own_ref.up_ref), channel_id=1, source_target_pairs={{0,32},{32,64},{64,96},{96,128},{128,160},{160,192},{192,224},{224... | collective-permute-start | bytes 552968 | tf_op jit(solution)/shard_map/ppermute | solution.py:373
  115.4 18.8 %collective-permute-start.18 = (bf16[144,640]{1,0:T(8,128)(2,1)S(1)}, bf16[144,640]{1,0:T(8,128)(2,1)S(1)}, u32[]{:S(2)}, u32[]{:S(2)}) collective-permute-start(bf16[144,640]{1,0:T(8,128)(2,1)S(1)} %get-tuple-element.31.own_ref.up_ref), channel_id=1, source_target_pairs={{0,1},{1,0},{2,3},{3,2},{4,5},{5,4},{6,7},{7,6},{8,9},{9,8},{10,11... | collective-permute-start | bytes 552968 | tf_op jit(solution)/shard_map/ppermute | solution.py:367
  117.8 16.4 %collective-permute-start.17 = (bf16[144,640]{1,0:T(8,128)(2,1)S(1)}, bf16[144,640]{1,0:T(8,128)(2,1)S(1)}, u32[]{:S(2)}, u32[]{:S(2)}) collective-permute-start(bf16[144,640]{1,0:T(8,128)(2,1)S(1)} %get-tuple-element.31.own_ref.up_ref), channel_id=1, source_target_pairs={{1,2},{3,4},{5,6},{7,8},{9,10},{11,12},{13,14},{15,16},{17,18},{19... | collective-permute-start | bytes 552968 | tf_op jit(solution)/shard_map/ppermute | solution.py:376
  126.9 9.4 %collective-permute-start.16 = (bf16[288,640]{1,0:T(8,128)(2,1)S(1)}, bf16[288,640]{1,0:T(8,128)(2,1)S(1)}, u32[]{:S(2)}, u32[]{:S(2)}) collective-permute-start(bf16[288,640]{1,0:T(8,128)(2,1)S(1)} %pad_maximum_fusion.2), channel_id=1, source_target_pairs={{0,1},{1,0},{2,3},{3,2},{4,5},{5,4},{6,7},{7,6},{8,9},{9,8},{10,11... | collective-permute-start | bytes 1105928 | tf_op jit(solution)/shard_map/ppermute | solution.py:367
  128.8 10.9 %collective-permute-start.15 = (bf16[288,640]{1,0:T(8,128)(2,1)S(1)}, bf16[288,640]{1,0:T(8,128)(2,1)S(1)}, u32[]{:S(2)}, u32[]{:S(2)}) collective-permute-start(bf16[288,640]{1,0:T(8,128)(2,1)S(1)} %pad_maximum_fusion.2), channel_id=1, source_target_pairs={{1,2},{3,4},{5,6},{7,8},{9,10},{11,12},{13,14},{15,16},{17,18},{19... | collective-permute-start | bytes 1105928 | tf_op jit(solution)/shard_map/ppermute | solution.py:376

commit v11 on v9

--- a/solution.py
+++ b/solution.py
@@ -99,9 +99,9 @@
     whole, lower, upper = (
         jnp.where(lane_of == place_ref[i : i + 1, :], 1.0, 0.0).astype(BF) for i in range(3)
     )
-    halves = wo_ref[:, D:QKV]
+    halves = nn(jnp.concatenate([lower, upper], axis=0), wo_ref[:, D:QKV])
     wn_ref[...] = (
-        nn(whole, wo_ref[:, 0:D]) + jnp.concatenate([nn(lower, halves), nn(upper, halves)], axis=1)
+        nn(whole, wo_ref[:, 0:D]) + jnp.concatenate([halves[0:640, :], halves[640:1280, :]], axis=1)
     ).astype(BF)
 
 
@@ -117,25 +117,26 @@
 
     core = blocks_ref[30]
 
-    def allowed(c, r, w):
-        there = jnp.logical_and(w - c >= 0, w - c < 5)
-        value = blocks_ref[(c * 3 + r) * 5 + jnp.clip(w - c, 0, 4)]
-        return jnp.where(there, value, 0).astype(F32)
+    table = {
+        (c, r, w): blocks_ref[(c * 3 + r) * 5 + w - c].astype(F32) if 0 <= w - c < 5 else jnp.float32(0.0)
+        for c in range(2)
+        for r in range(3)
+        for w in range(6)
+    }
 
     lane_c = (lax.broadcasted_iota(jnp.int32, (1, T), 1) & 8) > 0
     rows = []
     for r in range(3):
         for w in range(6):
-            rows.append(jnp.where(lane_c, allowed(1, r, jnp.int32(w)), allowed(0, r, jnp.int32(w))))
+            rows.append(jnp.where(lane_c, table[1, r, w], table[0, r, w]))
     for slot_t in range(3):
         for slot_r in range(3):
             (r0, t0), (r1, t1) = position(slot_t, slot_r)
-            r, t = jnp.where(core == 0, r0, r1), jnp.where(core == 0, t0, t1)
-            seen = jnp.where(
-                qc,
-                jnp.where(kc, allowed(1, r, 2 * t + 1), allowed(1, r, 2 * t)),
-                jnp.where(kc, allowed(0, r, 2 * t + 1), allowed(0, r, 2 * t)),
-            )
+            (m00, m01), (m10, m11) = [
+                [jnp.where(core == 0, table[c, r0, 2 * t0 + w], table[c, r1, 2 * t1 + w]) for w in range(2)]
+                for c in range(2)
+            ]
+            seen = jnp.where(qc, jnp.where(kc, m11, m10), jnp.where(kc, m01, m00))
             j = 3 * slot_t + slot_r
             bias_ref[:, j * T : (j + 1) * T] = (1.0 - seen) * OFF
     own = slice(4 * T, 5 * T)

time: 142 us -> 142 us (level)
  no operation moved by 1% of the time
where the time goes in v11:
time: 142 us; the launch traced here: 141 us
  starting transfers between devices  79.2 us (56%)
  Pallas kernels  28.5 us (20%)
  waiting for transfers between devices  24.4 us (17%)
  local copies, waits for them, and re-layouts  4.86 us (3%)
  other arithmetic  3.25 us (2%)
    ppermute x7, starting transfers between devices, swap(): return lax.ppermute(v, 'core', [(0, 1), (1, 0)])  23.1 us
    ppermute x2, starting transfers between devices, rows_beside(): lax.ppermute(own, lat + ('core',), south)  20.9 us
    ppermute x3, starting transfers between devices, sides(): return (lax.ppermute(column, lon, border), swap(column))  16.7 us
    ppermute x3, waiting for transfers between devices, along(): return lax.ppermute(v, ('x', 'core'), perm)  13.1 us
    pallas_call x1, Pallas kernels, on_device(): pl.pallas_call(project_kernel, out_shape=(shaped((9 * T, QKV)), shaped((6...  7.37 us
    ppermute x3, starting transfers between devices, along(): return lax.ppermute(v, ('x', 'core'), perm)  7.19 us
    pallas_call x3, Pallas kernels, hidden(): pl.pallas_call(hidden_kernel, out_shape=shaped((3 * T, D)), in_specs=[VME...  6.33 us
    ppermute x2, starting transfers between devices, rows_beside(): lax.ppermute(own, lat + ('core',), north)  5.91 us
  transfers between devices with their start and end apart: 19, of which 6 were waited for; matrix products, arithmetic and copies ran while one was open for 3% of the time, Pallas kernels for 7%

profile of v11, /device:TPU:47, one launch (start us, length us, event | category | flops | bytes accessed | tf_op | source)
XLA Modules:
  0.0 141.5 jit_solution(12694524730267310575)
XLA Ops:
  0.6 4.0 %collective-permute-start.3 = (bf16[128,1152]{1,0:T(8,128)(2,1)}, bf16[128,1152]{1,0:T(8,128)(2,1)S(1)}, u32[]{:S(2)}, u32[]{:S(2)}) collective-permute-start(bf16[128,1152]{1,0:T(8,128)(2,1)} %bitcast.7), channel_id=1, source_target_pairs={{32,0},{64,32},{96,64},{128,96},{160,128},{192,160},{224,192},{256... | collective-permute-start | bytes 884744 | tf_op jit(solution)/shard_map/ppermute | solution.py:374
  4.6 9.0 %collective-permute-start.2 = (bf16[128,1152]{1,0:T(8,128)(2,1)}, bf16[128,1152]{1,0:T(8,128)(2,1)S(1)}, u32[]{:S(2)}, u32[]{:S(2)}) collective-permute-start(bf16[128,1152]{1,0:T(8,128)(2,1)} %bitcast.8), channel_id=1, source_target_pairs={{0,32},{32,64},{64,96},{96,128},{128,160},{160,192},{192,224},{224... | collective-permute-start | bytes 884744 | tf_op jit(solution)/shard_map/ppermute | solution.py:374
  13.7 1.2 fusion.2
  14.9 0.7 collective-permute-start.1
  15.6 4.7 %collective-permute-start = (bf16[96,1728]{1,0:T(8,128)(2,1)S(1)}, bf16[96,1728]{1,0:T(8,128)(2,1)S(1)}, u32[]{:S(2)}, u32[]{:S(2)}) collective-permute-start(bf16[96,1728]{1,0:T(8,128)(2,1)S(1)} %fusion.2), channel_id=1, source_target_pairs={{224,0},{33,1},{194,2},{67,3},{164,4},{101,5},{134,6},{415,7},{232... | collective-permute-start | bytes 995336 | tf_op jit(solution)/shard_map/ppermute | solution.py:391
  20.3 0.7 reshape.34.gain_ref
  21.0 0.8 fusion.15
  21.8 5.3 %collective-permute-done.2 = bf16[128,1152]{1,0:T(8,128)(2,1)S(1)} collective-permute-done((bf16[128,1152]{1,0:T(8,128)(2,1)}, bf16[128,1152]{1,0:T(8,128)(2,1)S(1)}, u32[]{:S(2)}, u32[]{:S(2)}) %collective-permute-start.2) | collective-permute-done | bytes 294944 | tf_op jit(solution)/shard_map/ppermute | solution.py:374
  27.1 1.0 pad_maximum_fusion.x_ref
  28.2 8.6 %collective-permute-start.7 = (bf16[384,1152]{1,0:T(8,128)(2,1)S(1)}, bf16[384,1152]{1,0:T(8,128)(2,1)S(1)}, u32[]{:S(2)}, u32[]{:S(2)}) collective-permute-start(bf16[384,1152]{1,0:T(8,128)(2,1)S(1)} %pad_maximum_fusion.x_ref), channel_id=1, source_target_pairs={{1,2},{3,4},{5,6},{7,8},{9,10},{11,12},{13,14},{15,16},{17,18},{19... | collective-permute-start | bytes 2654216 | tf_op jit(solution)/shard_map/ppermute | solution.py:377
  36.8 1.9 %collective-permute-start.6 = (bf16[384,1152]{1,0:T(8,128)(2,1)S(1)}, bf16[384,1152]{1,0:T(8,128)(2,1)S(1)}, u32[]{:S(2)}, u32[]{:S(2)}) collective-permute-start(bf16[384,1152]{1,0:T(8,128)(2,1)S(1)} %pad_maximum_fusion.x_ref), channel_id=1, source_target_pairs={{0,1},{1,0},{2,3},{3,2},{4,5},{5,4},{6,7},{7,6},{8,9},{9,8},{10,11... | collective-permute-start | bytes 2654216 | tf_op jit(solution)/shard_map/ppermute | solution.py:368
  38.7 2.1 %shard_map.221.hc_ref = bf16[384,1152]{1,0:T(8,128)(2,1)S(1)} custom-call(bf16[384,1152]{1,0:T(8,128)(2,1)S(1)} %pad_maximum_fusion.x_ref, f32[1,1152]{1,0:T(1,128)S(1)} %reshape.34.gain_ref, s32[1,1152]{1,0:T(1,128)S(1)} %reshape.35.target_ref), custom_call_target="tpu_custom_call" | custom-call | flops 3000000000 | bytes 5000000 | tf_op jit(solution)/shard_map/pallas_call | solution.py:406
  40.8 0.9 copy-done.6
  41.8 0.1 pad_maximum_fusion.1.b0
  41.9 1.9 %collective-permute-start.5 = (bf16[192,1728]{1,0:T(8,128)(2,1)S(1)}, bf16[192,1728]{1,0:T(8,128)(2,1)S(1)}, u32[]{:S(2)}, u32[]{:S(2)}) collective-permute-start(bf16[192,1728]{1,0:T(8,128)(2,1)S(1)} %pad_maximum_fusion.1.b0), channel_id=1, source_target_pairs={{2,0},{4,2},{6,4},{0,6},{1,3},{3,5},{5,7},{7,1},{10,8},{12,10},{14... | collective-permute-start | bytes 1990664 | tf_op jit(solution)/shard_map/ppermute | solution.py:371
  43.9 3.4 %collective-permute-start.4 = (bf16[192,1728]{1,0:T(8,128)(2,1)S(1)}, bf16[192,1728]{1,0:T(8,128)(2,1)S(1)}, u32[]{:S(2)}, u32[]{:S(2)}) collective-permute-start(bf16[192,1728]{1,0:T(8,128)(2,1)S(1)} %pad_maximum_fusion.1.b0), channel_id=1, source_target_pairs={{0,2},{2,4},{4,6},{6,0},{3,1},{5,3},{7,5},{1,7},{8,10},{10,12},{12... | collective-permute-start | bytes 1990664 | tf_op jit(solution)/shard_map/ppermute | solution.py:371
  47.2 2.1 %shard_map.222.he_ref = bf16[384,1152]{1,0:T(8,128)(2,1)S(1)} custom-call(bf16[384,1152]{1,0:T(8,128)(2,1)S(1)} %collective-permute-done.6.x_ref, f32[1,1152]{1,0:T(1,128)S(1)} %reshape.34.gain_ref, s32[1,1152]{1,0:T(1,128)S(1)} %reshape.35.target_ref), custom_call_target="tpu_custom_call" | custom-call | flops 3000000000 | bytes 5000000 | tf_op jit(solution)/shard_map/pallas_call | solution.py:406
  49.4 0.9 copy-done.8
  50.3 9.7 %collective-permute-done.5.b2 = bf16[192,1728]{1,0:T(8,128)(2,1)S(1)} collective-permute-done((bf16[192,1728]{1,0:T(8,128)(2,1)S(1)}, bf16[192,1728]{1,0:T(8,128)(2,1)S(1)}, u32[]{:S(2)}, u32[]{:S(2)}) %collective-permute-start.5) | collective-permute-done | bytes 663584 | tf_op jit(solution)/shard_map/ppermute | solution.py:371
  60.0 3.1 %collective-permute-done.4.b1 = bf16[192,1728]{1,0:T(8,128)(2,1)S(1)} collective-permute-done((bf16[192,1728]{1,0:T(8,128)(2,1)S(1)}, bf16[192,1728]{1,0:T(8,128)(2,1)S(1)}, u32[]{:S(2)}, u32[]{:S(2)}) %collective-permute-start.4) | collective-permute-done | bytes 663584 | tf_op jit(solution)/shard_map/ppermute | solution.py:371
  63.1 0.9 copy-done.1
  64.1 1.9 %collective-permute-start.8 = (bf16[192,1728]{1,0:T(8,128)(2,1)S(1)}, bf16[192,1728]{1,0:T(8,128)(2,1)S(1)}, u32[]{:S(2)}, u32[]{:S(2)}) collective-permute-start(bf16[192,1728]{1,0:T(8,128)(2,1)S(1)} %collective-permute-done.4.b1), channel_id=1, source_target_pairs={{0,2},{2,4},{4,6},{6,0},{3,1},{5,3},{7,5},{1,7},{8,10},{10,12},{12... | collective-permute-start | bytes 1990664 | tf_op jit(solution)/shard_map/ppermute | solution.py:371
  66.0 0.0 copy-start.14
  66.0 0.0 copy-start.17
  66.0 0.0 copy-start.16
  66.1 0.1 reshape.31
  66.2 2.9 %collective-permute-start.9 = (bf16[192,1728]{1,0:T(8,128)(2,1)S(1)}, bf16[192,1728]{1,0:T(8,128)(2,1)S(1)}, u32[]{:S(2)}, u32[]{:S(2)}) collective-permute-start(bf16[192,1728]{1,0:T(8,128)(2,1)S(1)} %pad_maximum_fusion.1.b0), channel_id=1, source_target_pairs={{0,1},{1,0},{2,3},{3,2},{4,5},{5,4},{6,7},{7,6},{8,9},{9,8},{10,11... | collective-permute-start | bytes 1990664 | tf_op jit(solution)/shard_map/ppermute | solution.py:368
  69.1 1.9 %collective-permute-start.10 = (bf16[192,1728]{1,0:T(8,128)(2,1)S(1)}, bf16[192,1728]{1,0:T(8,128)(2,1)S(1)}, u32[]{:S(2)}, u32[]{:S(2)}) collective-permute-start(bf16[192,1728]{1,0:T(8,128)(2,1)S(1)} %collective-permute-done.4.b1), channel_id=1, source_target_pairs={{0,1},{1,0},{2,3},{3,2},{4,5},{5,4},{6,7},{7,6},{8,9},{9,8},{10,11... | collective-permute-start | bytes 1990664 | tf_op jit(solution)/shard_map/ppermute | solution.py:368
  71.0 2.4 %collective-permute-start.11 = (bf16[192,1728]{1,0:T(8,128)(2,1)S(1)}, bf16[192,1728]{1,0:T(8,128)(2,1)S(1)}, u32[]{:S(2)}, u32[]{:S(2)}) collective-permute-start(bf16[192,1728]{1,0:T(8,128)(2,1)S(1)} %collective-permute-done.5.b2), channel_id=1, source_target_pairs={{0,1},{1,0},{2,3},{3,2},{4,5},{5,4},{6,7},{7,6},{8,9},{9,8},{10,11... | collective-permute-start | bytes 1990664 | tf_op jit(solution)/shard_map/ppermute | solution.py:368
  73.4 1.2 copy-done.2
  74.6 2.1 %shard_map.223.hw_ref = bf16[384,1152]{1,0:T(8,128)(2,1)S(1)} custom-call(bf16[384,1152]{1,0:T(8,128)(2,1)S(1)} %copy-done.2, f32[1,1152]{1,0:T(1,128)S(1)} %reshape.34.gain_ref, s32[1,1152]{1,0:T(1,128)S(1)} %reshape.35.target_ref), custom_call_target="tpu_custom_call" | custom-call | flops 3000000000 | bytes 5000000 | tf_op jit(solution)/shard_map/pallas_call | solution.py:406
  76.7 0.2 collective-permute-done.8.b3
  76.9 2.1 %collective-permute-start.12 = (bf16[192,1728]{1,0:T(8,128)(2,1)S(1)}, bf16[192,1728]{1,0:T(8,128)(2,1)S(1)}, u32[]{:S(2)}, u32[]{:S(2)}) collective-permute-start(bf16[192,1728]{1,0:T(8,128)(2,1)S(1)} %collective-permute-done.8.b3), channel_id=1, source_target_pairs={{0,1},{1,0},{2,3},{3,2},{4,5},{5,4},{6,7},{7,6},{8,9},{9,8},{10,11... | collective-permute-start | bytes 1990664 | tf_op jit(solution)/shard_map/ppermute | solution.py:368
  79.2 0.1 pad_add_fusion.1.blocks_ref
  79.4 1.6 %collective-permute-done.12.b7 = bf16[192,1728]{1,0:T(8,128)(2,1)S(1)} collective-permute-done((bf16[192,1728]{1,0:T(8,128)(2,1)S(1)}, bf16[192,1728]{1,0:T(8,128)(2,1)S(1)}, u32[]{:S(2)}, u32[]{:S(2)}) %collective-permute-start.12) | collective-permute-done | bytes 663584 | tf_op jit(solution)/shard_map/ppermute | solution.py:368
  81.0 7.4 %shard_map.224 = (bf16[1152,1728]{1,0:T(8,128)(2,1)S(1)}, bf16[640,1152]{1,0:T(8,128)(2,1)S(1)}) custom-call(s32[3,384]{1,0:T(4,128)S(1)} %pad_add_fusion.place_ref, bf16[384,1152]{1,0:T(8,128)(2,1)S(1)} %shard_map.223.hw_ref, bf16[384,1152]{1,0:T(8,128)(2,1)S(1)} %copy-done.7, bf16[384,1152]{1,0:T(8,128)(2,1)S(1)} %copy-done.9, ...), custom_call_target="tpu_custom_call" | custom-call | flops 6000000000 | bytes 8000000 | tf_op jit(solution)/shard_map/pallas_call | solution.py:419
  88.4 5.6 %shard_map.225 = (bf16[1024,1152]{1,0:T(8,128)(2,1)S(1)}, bf16[128,1152]{1,0:T(8,128)(2,1)}, f32[128,1152]{1,0:T(8,128)S(1)}, bf16[144,640]{1,0:T(8,128)(2,1)S(1)}, f32[128,128]{1,0:T(8,128)S(1)}) custom-call(s32[31]{0:T(128)S(1)} %pad_add_fusion.1.blocks_ref, bf16[1152,1728]{1,0:T(8,128)(2,1)S(1)} %get-tuple-element.30.win_ref, ...), custom_call_target="tpu_custom_call" | custom-call | flops 6000000000 | bytes 8000000 | tf_op jit(solution)/shard_map/pallas_call | solution.py:426
  94.0 1.9 %collective-permute-start.14 = (bf16[144,640]{1,0:T(8,128)(2,1)S(1)}, bf16[144,640]{1,0:T(8,128)(2,1)S(1)}, u32[]{:S(2)}, u32[]{:S(2)}) collective-permute-start(bf16[144,640]{1,0:T(8,128)(2,1)S(1)} %get-tuple-element.33.own_ref.up_ref), channel_id=1, source_target_pairs={{32,0},{64,32},{96,64},{128,96},{160,128},{192,160},{224,192},{256... | collective-permute-start | bytes 552968 | tf_op jit(solution)/shard_map/ppermute | solution.py:374
  95.9 11.9 %collective-permute-start.13 = (bf16[144,640]{1,0:T(8,128)(2,1)S(1)}, bf16[144,640]{1,0:T(8,128)(2,1)S(1)}, u32[]{:S(2)}, u32[]{:S(2)}) collective-permute-start(bf16[144,640]{1,0:T(8,128)(2,1)S(1)} %get-tuple-element.33.own_ref.up_ref), channel_id=1, source_target_pairs={{0,32},{32,64},{64,96},{96,128},{128,160},{160,192},{192,224},{224... | collective-permute-start | bytes 552968 | tf_op jit(solution)/shard_map/ppermute | solution.py:374
  107.8 2.3 %collective-permute-start.18 = (bf16[144,640]{1,0:T(8,128)(2,1)S(1)}, bf16[144,640]{1,0:T(8,128)(2,1)S(1)}, u32[]{:S(2)}, u32[]{:S(2)}) collective-permute-start(bf16[144,640]{1,0:T(8,128)(2,1)S(1)} %get-tuple-element.33.own_ref.up_ref), channel_id=1, source_target_pairs={{0,1},{1,0},{2,3},{3,2},{4,5},{5,4},{6,7},{7,6},{8,9},{9,8},{10,11... | collective-permute-start | bytes 552968 | tf_op jit(solution)/shard_map/ppermute | solution.py:368
  110.1 5.9 %collective-permute-start.17 = (bf16[144,640]{1,0:T(8,128)(2,1)S(1)}, bf16[144,640]{1,0:T(8,128)(2,1)S(1)}, u32[]{:S(2)}, u32[]{:S(2)}) collective-permute-start(bf16[144,640]{1,0:T(8,128)(2,1)S(1)} %get-tuple-element.33.own_ref.up_ref), channel_id=1, source_target_pairs={{1,2},{3,4},{5,6},{7,8},{9,10},{11,12},{13,14},{15,16},{17,18},{19... | collective-permute-start | bytes 552968 | tf_op jit(solution)/shard_map/ppermute | solution.py:377
  116.1 9.6 %collective-permute-start.16 = (bf16[288,640]{1,0:T(8,128)(2,1)S(1)}, bf16[288,640]{1,0:T(8,128)(2,1)S(1)}, u32[]{:S(2)}, u32[]{:S(2)}) collective-permute-start(bf16[288,640]{1,0:T(8,128)(2,1)S(1)} %pad_maximum_fusion.2), channel_id=1, source_target_pairs={{0,1},{1,0},{2,3},{3,2},{4,5},{5,4},{6,7},{7,6},{8,9},{9,8},{10,11... | collective-permute-start | bytes 1105928 | tf_op jit(solution)/shard_map/ppermute | solution.py:368
  125.6 2.2 %collective-permute-start.15 = (bf16[288,640]{1,0:T(8,128)(2,1)S(1)}, bf16[288,640]{1,0:T(8,128)(2,1)S(1)}, u32[]{:S(2)}, u32[]{:S(2)}) collective-permute-start(bf16[288,640]{1,0:T(8,128)(2,1)S(1)} %pad_maximum_fusion.2), channel_id=1, source_target_pairs={{1,2},{3,4},{5,6},{7,8},{9,10},{11,12},{13,14},{15,16},{17,18},{19... | collective-permute-start | bytes 1105928 | tf_op jit(solution)/shard_map/ppermute | solution.py:377
  127.9 1.8 %shard_map.227.gq_ref = bf16[128,576]{1,0:T(8,128)(2,1)S(1)} custom-call(bf16[1152,1728]{1,0:T(8,128)(2,1)S(1)} %get-tuple-element.30.win_ref, bf16[1024,1152]{1,0:T(8,128)(2,1)S(1)} %get-tuple-element.38.e_ref, bf16[144,640]{1,0:T(8,128)(2,1)S(1)} %get-tuple-element.33.own_ref.up_ref, f32[128,128]{1,0:T(8,128)S(1)} %get-tuple-element.39.stat_ref), custom_call_target="tpu_custom_call" | custom-call | flops 4000000000 | bytes 6000000 | tf_op jit(solution)/shard_map/pallas_call | solution.py:440
  129.7 0.5 shard_map.228.order_ref
  130.2 2.0 %shard_map.226 = (f32[128,640]{1,0:T(8,128)S(1)}, f32[128,640]{1,0:T(8,128)S(1)}) custom-call(s32[1]{0:T(128)} %bitcast.core_ref, bf16[1152,1728]{1,0:T(8,128)(2,1)S(1)} %get-tuple-element.30.win_ref, bf16[144,640]{1,0:T(8,128)(2,1)S(1)} %get-tuple-element.33.own_ref.up_ref, bf16[144,640]{1,0:T(8,128)(2,1)S(1)} %collective-permute-done.13.before_ref, ...), custom_call_target="tpu_custom_call" | custom-call | flops 4000000000 | bytes 6000000 | tf_op jit(solution)/shard_map/pallas_call | solution.py:445
  132.2 4.4 %collective-permute-done.15.packo_ref = bf16[288,640]{1,0:T(8,128)(2,1)S(1)} collective-permute-done((bf16[288,640]{1,0:T(8,128)(2,1)S(1)}, bf16[288,640]{1,0:T(8,128)(2,1)S(1)}, u32[]{:S(2)}, u32[]{:S(2)}) %collective-permute-start.15) | collective-permute-done | bytes 368672 | tf_op jit(solution)/shard_map/ppermute | solution.py:377
  136.6 4.9 %shard_map.229 = f32[128,1152]{1,0:T(8,128)} custom-call(s32[1]{0:T(128)} %bitcast.core_ref, bf16[1152,1728]{1,0:T(8,128)(2,1)S(1)} %get-tuple-element.30.win_ref, bf16[288,640]{1,0:T(8,128)(2,1)S(1)} %collective-permute-done.15.packo_ref, bf16[288,640]{1,0:T(8,128)(2,1)S(1)} %collective-permute-done.16.packi_ref, f32[128,640]{1,0:T(8,128)S(1)} %get-tuple-element.36.gk0_ref, ...), custom_call_target="tpu_custom_call" | custom-call | tf_op jit(solution)/shard_map/pallas_call | solution.py:450
  (57 shorter events, 0.3 us)
Async XLA Ops:
  0.6 21.2 %collective-permute-start.3 = (bf16[128,1152]{1,0:T(8,128)(2,1)}, bf16[128,1152]{1,0:T(8,128)(2,1)S(1)}, u32[]{:S(2)}, u32[]{:S(2)}) collective-permute-start(bf16[128,1152]{1,0:T(8,128)(2,1)} %bitcast.7), channel_id=1, source_target_pairs={{32,0},{64,32},{96,64},{128,96},{160,128},{192,160},{224,192},{256... | collective-permute-start | bytes 884744 | tf_op jit(solution)/shard_map/ppermute | solution.py:374
  4.6 22.5 %collective-permute-start.2 = (bf16[128,1152]{1,0:T(8,128)(2,1)}, bf16[128,1152]{1,0:T(8,128)(2,1)S(1)}, u32[]{:S(2)}, u32[]{:S(2)}) collective-permute-start(bf16[128,1152]{1,0:T(8,128)(2,1)} %bitcast.8), channel_id=1, source_target_pairs={{0,32},{32,64},{64,96},{96,128},{128,160},{160,192},{192,224},{224... | collective-permute-start | bytes 884744 | tf_op jit(solution)/shard_map/ppermute | solution.py:374
  14.9 26.8 %collective-permute-start.1 = (bf16[96,1728]{1,0:T(8,128)(2,1)S(1)}, bf16[96,1728]{1,0:T(8,128)(2,1)S(1)}, u32[]{:S(2)}, u32[]{:S(2)}) collective-permute-start(bf16[96,1728]{1,0:T(8,128)(2,1)S(1)} %fusion.2), channel_id=1, source_target_pairs={{440,0},{377,1},{474,2},{347,3},{508,4},{317,5},{286,6},{7,7},{432... | collective-permute-start | bytes 995336 | tf_op jit(solution)/shard_map/ppermute | solution.py:391
  15.6 26.2 %collective-permute-start = (bf16[96,1728]{1,0:T(8,128)(2,1)S(1)}, bf16[96,1728]{1,0:T(8,128)(2,1)S(1)}, u32[]{:S(2)}, u32[]{:S(2)}) collective-permute-start(bf16[96,1728]{1,0:T(8,128)(2,1)S(1)} %fusion.2), channel_id=1, source_target_pairs={{224,0},{33,1},{194,2},{67,3},{164,4},{101,5},{134,6},{415,7},{232... | collective-permute-start | bytes 995336 | tf_op jit(solution)/shard_map/ppermute | solution.py:391
  28.2 35.0 %collective-permute-start.7 = (bf16[384,1152]{1,0:T(8,128)(2,1)S(1)}, bf16[384,1152]{1,0:T(8,128)(2,1)S(1)}, u32[]{:S(2)}, u32[]{:S(2)}) collective-permute-start(bf16[384,1152]{1,0:T(8,128)(2,1)S(1)} %pad_maximum_fusion.x_ref), channel_id=1, source_target_pairs={{1,2},{3,4},{5,6},{7,8},{9,10},{11,12},{13,14},{15,16},{17,18},{19... | collective-permute-start | bytes 2654216 | tf_op jit(solution)/shard_map/ppermute | solution.py:377
  36.8 10.4 %collective-permute-start.6 = (bf16[384,1152]{1,0:T(8,128)(2,1)S(1)}, bf16[384,1152]{1,0:T(8,128)(2,1)S(1)}, u32[]{:S(2)}, u32[]{:S(2)}) collective-permute-start(bf16[384,1152]{1,0:T(8,128)(2,1)S(1)} %pad_maximum_fusion.x_ref), channel_id=1, source_target_pairs={{0,1},{1,0},{2,3},{3,2},{4,5},{5,4},{6,7},{7,6},{8,9},{9,8},{10,11... | collective-permute-start | bytes 2654216 | tf_op jit(solution)/shard_map/ppermute | solution.py:368
  40.8 0.9 copy-start.6
  41.9 24.1 %copy-start.11 = (s32[1,2,3,5]{3,1,2,0:T(2,128)S(1)}, s32[1,2,3,5]{3,1,2,0:T(2,128)}, u32[]{:S(2)}) copy-start(s32[1,2,3,5]{3,1,2,0:T(2,128)} %param.31) | copy-start | bytes 364
  41.9 18.1 %collective-permute-start.5 = (bf16[192,1728]{1,0:T(8,128)(2,1)S(1)}, bf16[192,1728]{1,0:T(8,128)(2,1)S(1)}, u32[]{:S(2)}, u32[]{:S(2)}) collective-permute-start(bf16[192,1728]{1,0:T(8,128)(2,1)S(1)} %pad_maximum_fusion.1.b0), channel_id=1, source_target_pairs={{2,0},{4,2},{6,4},{0,6},{1,3},{3,5},{5,7},{7,1},{10,8},{12,10},{14... | collective-permute-start | bytes 1990664 | tf_op jit(solution)/shard_map/ppermute | solution.py:371
  43.9 19.3 %collective-permute-start.4 = (bf16[192,1728]{1,0:T(8,128)(2,1)S(1)}, bf16[192,1728]{1,0:T(8,128)(2,1)S(1)}, u32[]{:S(2)}, u32[]{:S(2)}) collective-permute-start(bf16[192,1728]{1,0:T(8,128)(2,1)S(1)} %pad_maximum_fusion.1.b0), channel_id=1, source_target_pairs={{0,2},{2,4},{4,6},{6,0},{3,1},{5,3},{7,5},{1,7},{8,10},{10,12},{12... | collective-permute-start | bytes 1990664 | tf_op jit(solution)/shard_map/ppermute | solution.py:371
  49.3 0.9 copy-start.8
  63.1 0.9 copy-start.1
  64.1 12.9 %collective-permute-start.8 = (bf16[192,1728]{1,0:T(8,128)(2,1)S(1)}, bf16[192,1728]{1,0:T(8,128)(2,1)S(1)}, u32[]{:S(2)}, u32[]{:S(2)}) collective-permute-start(bf16[192,1728]{1,0:T(8,128)(2,1)S(1)} %collective-permute-done.4.b1), channel_id=1, source_target_pairs={{0,2},{2,4},{4,6},{6,0},{3,1},{5,3},{7,5},{1,7},{8,10},{10,12},{12... | collective-permute-start | bytes 1990664 | tf_op jit(solution)/shard_map/ppermute | solution.py:371
  66.0 13.1 %copy-start.13 = (s32[384]{0:T(512)S(1)}, s32[384]{0:T(512)}, u32[]{:S(2)}) copy-start(s32[384]{0:T(512)} %constant.86.clone) | copy-start | bytes 4612
  66.0 13.1 %copy-start.14 = (s32[384]{0:T(512)S(1)}, s32[384]{0:T(512)}, u32[]{:S(2)}) copy-start(s32[384]{0:T(512)} %constant.85.clone) | copy-start | bytes 4612
  66.0 13.0 %copy-start.17 = (pred[384]{0:T(512)(128)(4,1)S(1)}, pred[384]{0:T(512)(128)(4,1)}, u32[]{:S(2)}) copy-start(pred[384]{0:T(512)(128)(4,1)} %constant.88.clone) | copy-start | bytes 1156
  66.0 13.1 %copy-start.16 = (pred[384]{0:T(512)(128)(4,1)S(1)}, pred[384]{0:T(512)(128)(4,1)}, u32[]{:S(2)}) copy-start(pred[384]{0:T(512)(128)(4,1)} %constant.90.clone) | copy-start | bytes 1156
  66.1 13.0 %copy-start.10 = (s32[384]{0:T(512)S(1)}, s32[384]{0:T(512)}, u32[]{:S(2)}) copy-start(s32[384]{0:T(512)} %constant.89.clone) | copy-start | bytes 4612
  66.1 13.0 %copy-start.12 = (s32[384]{0:T(512)S(1)}, s32[384]{0:T(512)}, u32[]{:S(2)}) copy-start(s32[384]{0:T(512)} %constant.87.clone) | copy-start | bytes 4612
  66.1 13.1 %copy-start.15 = (pred[384]{0:T(512)(128)(4,1)S(1)}, pred[384]{0:T(512)(128)(4,1)}, u32[]{:S(2)}) copy-start(pred[384]{0:T(512)(128)(4,1)} %constant.91.clone) | copy-start | bytes 1156
  66.2 13.2 %collective-permute-start.9 = (bf16[192,1728]{1,0:T(8,128)(2,1)S(1)}, bf16[192,1728]{1,0:T(8,128)(2,1)S(1)}, u32[]{:S(2)}, u32[]{:S(2)}) collective-permute-start(bf16[192,1728]{1,0:T(8,128)(2,1)S(1)} %pad_maximum_fusion.1.b0), channel_id=1, source_target_pairs={{0,1},{1,0},{2,3},{3,2},{4,5},{5,4},{6,7},{7,6},{8,9},{9,8},{10,11... | collective-permute-start | bytes 1990664 | tf_op jit(solution)/shard_map/ppermute | solution.py:368
  69.1 10.3 %collective-permute-start.10 = (bf16[192,1728]{1,0:T(8,128)(2,1)S(1)}, bf16[192,1728]{1,0:T(8,128)(2,1)S(1)}, u32[]{:S(2)}, u32[]{:S(2)}) collective-permute-start(bf16[192,1728]{1,0:T(8,128)(2,1)S(1)} %collective-permute-done.4.b1), channel_id=1, source_target_pairs={{0,1},{1,0},{2,3},{3,2},{4,5},{5,4},{6,7},{7,6},{8,9},{9,8},{10,11... | collective-permute-start | bytes 1990664 | tf_op jit(solution)/shard_map/ppermute | solution.py:368
  71.0 8.3 %collective-permute-start.11 = (bf16[192,1728]{1,0:T(8,128)(2,1)S(1)}, bf16[192,1728]{1,0:T(8,128)(2,1)S(1)}, u32[]{:S(2)}, u32[]{:S(2)}) collective-permute-start(bf16[192,1728]{1,0:T(8,128)(2,1)S(1)} %collective-permute-done.5.b2), channel_id=1, source_target_pairs={{0,1},{1,0},{2,3},{3,2},{4,5},{5,4},{6,7},{7,6},{8,9},{9,8},{10,11... | collective-permute-start | bytes 1990664 | tf_op jit(solution)/shard_map/ppermute | solution.py:368
  73.4 1.2 copy-start.2
  74.6 6.4 %copy-start.7 = (bf16[384,1152]{1,0:T(8,128)(2,1)S(1)}, bf16[384,1152]{1,0:T(8,128)(2,1)}, u32[]{:S(2)}) copy-start(bf16[384,1152]{1,0:T(8,128)(2,1)} %copy-done.6) | copy-start | bytes 2654212
  74.6 6.4 %copy-start.9 = (bf16[384,1152]{1,0:T(8,128)(2,1)S(1)}, bf16[384,1152]{1,0:T(8,128)(2,1)}, u32[]{:S(2)}) copy-start(bf16[384,1152]{1,0:T(8,128)(2,1)} %copy-done.8) | copy-start | bytes 2654212
  76.9 4.0 %collective-permute-start.12 = (bf16[192,1728]{1,0:T(8,128)(2,1)S(1)}, bf16[192,1728]{1,0:T(8,128)(2,1)S(1)}, u32[]{:S(2)}, u32[]{:S(2)}) collective-permute-start(bf16[192,1728]{1,0:T(8,128)(2,1)S(1)} %collective-permute-done.8.b3), channel_id=1, source_target_pairs={{0,1},{1,0},{2,3},{3,2},{4,5},{5,4},{6,7},{7,6},{8,9},{9,8},{10,11... | collective-permute-start | bytes 1990664 | tf_op jit(solution)/shard_map/ppermute | solution.py:368
  79.3 9.1 %copy-start = (bf16[8,16,1152]{2,1,0:T(8,128)(2,1)S(1)}, bf16[8,16,1152]{2,1,0:T(8,128)(2,1)}, u32[]{:S(2)}) copy-start(bf16[8,16,1152]{2,1,0:T(8,128)(2,1)} %param.22) | copy-start | bytes 884740
  79.3 9.1 %copy-start.3 = (bf16[1152,192]{0,1:T(8,128)(2,1)S(1)}, bf16[1152,192]{0,1:T(8,128)(2,1)}, u32[]{:S(2)}) copy-start(bf16[1152,192]{0,1:T(8,128)(2,1)} %param.28) | copy-start | bytes 1327108
  79.3 9.1 %copy-start.4 = (f32[8,16,64]{2,1,0:T(8,128)S(1)}, f32[8,16,64]{2,1,0:T(8,128)}, u32[]{:S(2)}) copy-start(f32[8,16,64]{2,1,0:T(8,128)} %param.29) | copy-start | bytes 98308
  79.3 9.1 %copy-start.5 = (s32[8,16,64]{2,1,0:T(8,128)S(1)}, s32[8,16,64]{2,1,0:T(8,128)}, u32[]{:S(2)}) copy-start(s32[8,16,64]{2,1,0:T(8,128)} %param.30) | copy-start | bytes 98308
  94.0 22.0 %collective-permute-start.14 = (bf16[144,640]{1,0:T(8,128)(2,1)S(1)}, bf16[144,640]{1,0:T(8,128)(2,1)S(1)}, u32[]{:S(2)}, u32[]{:S(2)}) collective-permute-start(bf16[144,640]{1,0:T(8,128)(2,1)S(1)} %get-tuple-element.33.own_ref.up_ref), channel_id=1, source_target_pairs={{32,0},{64,32},{96,64},{128,96},{160,128},{192,160},{224,192},{256... | collective-permute-start | bytes 552968 | tf_op jit(solution)/shard_map/ppermute | solution.py:374
  95.9 20.1 %collective-permute-start.13 = (bf16[144,640]{1,0:T(8,128)(2,1)S(1)}, bf16[144,640]{1,0:T(8,128)(2,1)S(1)}, u32[]{:S(2)}, u32[]{:S(2)}) collective-permute-start(bf16[144,640]{1,0:T(8,128)(2,1)S(1)} %get-tuple-element.33.own_ref.up_ref), channel_id=1, source_target_pairs={{0,32},{32,64},{64,96},{96,128},{128,160},{160,192},{192,224},{224... | collective-permute-start | bytes 552968 | tf_op jit(solution)/shard_map/ppermute | solution.py:374
  107.8 22.3 %collective-permute-start.18 = (bf16[144,640]{1,0:T(8,128)(2,1)S(1)}, bf16[144,640]{1,0:T(8,128)(2,1)S(1)}, u32[]{:S(2)}, u32[]{:S(2)}) collective-permute-start(bf16[144,640]{1,0:T(8,128)(2,1)S(1)} %get-tuple-element.33.own_ref.up_ref), channel_id=1, source_target_pairs={{0,1},{1,0},{2,3},{3,2},{4,5},{5,4},{6,7},{7,6},{8,9},{9,8},{10,11... | collective-permute-start | bytes 552968 | tf_op jit(solution)/shard_map/ppermute | solution.py:368
  110.1 20.0 %collective-permute-start.17 = (bf16[144,640]{1,0:T(8,128)(2,1)S(1)}, bf16[144,640]{1,0:T(8,128)(2,1)S(1)}, u32[]{:S(2)}, u32[]{:S(2)}) collective-permute-start(bf16[144,640]{1,0:T(8,128)(2,1)S(1)} %get-tuple-element.33.own_ref.up_ref), channel_id=1, source_target_pairs={{1,2},{3,4},{5,6},{7,8},{9,10},{11,12},{13,14},{15,16},{17,18},{19... | collective-permute-start | bytes 552968 | tf_op jit(solution)/shard_map/ppermute | solution.py:377
  116.1 16.1 %collective-permute-start.16 = (bf16[288,640]{1,0:T(8,128)(2,1)S(1)}, bf16[288,640]{1,0:T(8,128)(2,1)S(1)}, u32[]{:S(2)}, u32[]{:S(2)}) collective-permute-start(bf16[288,640]{1,0:T(8,128)(2,1)S(1)} %pad_maximum_fusion.2), channel_id=1, source_target_pairs={{0,1},{1,0},{2,3},{3,2},{4,5},{5,4},{6,7},{7,6},{8,9},{9,8},{10,11... | collective-permute-start | bytes 1105928 | tf_op jit(solution)/shard_map/ppermute | solution.py:368
  125.6 10.9 %collective-permute-start.15 = (bf16[288,640]{1,0:T(8,128)(2,1)S(1)}, bf16[288,640]{1,0:T(8,128)(2,1)S(1)}, u32[]{:S(2)}, u32[]{:S(2)}) collective-permute-start(bf16[288,640]{1,0:T(8,128)(2,1)S(1)} %pad_maximum_fusion.2), channel_id=1, source_target_pairs={{1,2},{3,4},{5,6},{7,8},{9,10},{11,12},{13,14},{15,16},{17,18},{19... | collective-permute-start | bytes 1105928 | tf_op jit(solution)/shard_map/ppermute | solution.py:377

commit v12 on v11

--- a/solution.py
+++ b/solution.py
@@ -261,25 +261,22 @@
         gv_ref[:, c - VB : d - VB] += unstacked(nn(jnp.concatenate(ps, axis=0), up), V0 + HD * e, c)
 
 
-def key_near_kernel(core_ref, win_ref, own_ref, before_ref, after_ref, outer_ref, inner_ref, gk_ref, gv_ref):
+def key_near_kernel(core_ref, win_ref, own_ref, inner_ref, gk_ref, gv_ref):
     gk_ref[...] = jnp.zeros_like(gk_ref)
     gv_ref[...] = jnp.zeros_like(gv_ref)
-    tiles = (
-        (1, 0, before_ref, 0), (1, 1, own_ref, 0), (1, 2, after_ref, 0), (0, 1, outer_ref, 0), (2, 1, inner_ref, 0)
-    )
+    tiles = [(t, r, ref, 144 * r) for t, ref in ((1, own_ref), (2, inner_ref)) for r in range(3)]
     key_side(core_ref, win_ref, tiles, gk_ref, gv_ref)
 
 
 def finish_kernel(
-    core_ref, win_ref, packo_ref, packi_ref, gk0_ref, gv0_ref, gq_ref, order_ref, x_ref, gain_ref, og_ref,
+    core_ref, win_ref, outer_ref, gk0_ref, gv0_ref, gq_ref, order_ref, x_ref, gain_ref, og_ref,
     b0, b1, b2, b3, b4, b5, b6, b7,
     out_ref, gk_ref, gv_ref, w_ref,
 ):
     collect((b0, b1, b2, b3, b4, b5, b6, b7), 0, 144, w_ref)
     gk_ref[...] = gk0_ref[...]
     gv_ref[...] = gv0_ref[...]
-    tiles = ((0, 0, packo_ref, 0), (0, 2, packo_ref, 144), (2, 0, packi_ref, 0), (2, 2, packi_ref, 144))
-    key_side(core_ref, win_ref, tiles, gk_ref, gv_ref)
+    key_side(core_ref, win_ref, [(0, r, outer_ref, 144 * r) for r in range(3)], gk_ref, gv_ref)
     gk = (gk_ref[:, 0:HW] * FACTOR).astype(BF)
     gv = gv_ref[:, 64:640].astype(BF)
     grads = jnp.concatenate([gk, gv, gq_ref[...]], axis=1)
@@ -434,24 +431,25 @@
         cost_estimate=pl.CostEstimate(flops=6_000_000_000, bytes_accessed=8_000_000, transcendentals=1_000_000),
     )(jnp.concatenate([block_mask.reshape(30), which]), win, wn, w_pixel.T, x, measured.reshape(T, 64), filter_color.reshape(T, 64))
     before, after = rows_beside(pack)
-    near_outer, near_inner = sides(pack)
-    corners, target, stat_late = lax.optimization_barrier((jnp.concatenate([before, after], axis=0), target, stat))
-    packs_outer, packs_inner = sides(corners)
+    packs, stat, target = lax.optimization_barrier((jnp.concatenate([before, pack, after], axis=0), stat, target))
+    packs_outer = lax.ppermute(packs, lon, border)
     gq = pl.pallas_call(
         query_kernel, out_shape=shaped((T, HW)), in_specs=[VMEM] * 4, out_specs=VMEM,
         scratch_shapes=[pltpu.VMEM((T, 640), F32)], compiler_params=params(16),
         cost_estimate=pl.CostEstimate(flops=4_000_000_000, bytes_accessed=6_000_000, transcendentals=0),
-    )(win, e, pack, stat_late)
+    )(win, e, pack, stat)
+    gq, packs_late = lax.optimization_barrier((gq, packs))
+    packs_inner = swap(packs_late)
     gk, gv = pl.pallas_call(
-        key_near_kernel, out_shape=(shaped((T, 640), F32),) * 2, in_specs=[SMEM] + [VMEM] * 6, out_specs=(VMEM,) * 2,
+        key_near_kernel, out_shape=(shaped((T, 640), F32),) * 2, in_specs=[SMEM] + [VMEM] * 3, out_specs=(VMEM,) * 2,
         compiler_params=params(16),
         cost_estimate=pl.CostEstimate(flops=4_000_000_000, bytes_accessed=6_000_000, transcendentals=0),
-    )(which, win, pack, before, after, near_outer, near_inner)
+    )(which, win, packs, packs_inner)
     guidance = pl.pallas_call(
-        finish_kernel, out_shape=shaped((T, D), F32), in_specs=[SMEM] + [VMEM] * 18, out_specs=VMEM,
+        finish_kernel, out_shape=shaped((T, D), F32), in_specs=[SMEM] + [VMEM] * 17, out_specs=VMEM,
         scratch_shapes=[pltpu.VMEM((T, 640), F32)] * 2 + [pltpu.VMEM((D, QKV), BF)],
         compiler_params=params(20),
-    )(which, win, packs_outer, packs_inner, gk, gv, gq, ordering(target), x, gain, og, *blocks)
+    )(which, win, packs_outer, gk, gv, gq, ordering(target), x, gain, og, *blocks)
     return den.reshape(tokens.shape), guidance.reshape(tokens.shape)
 
 

time: 142 us -> 145 us (1.021)
  the two profiles are of different devices: /device:TPU:47 before, /device:TPU:48 now
where the time goes in v12:
time: 145 us
  starting transfers between devices  66.2 us (46%)
  waiting for transfers between devices  40.5 us (28%)
  Pallas kernels  28.5 us (20%)
  local copies, waits for them, and re-layouts  4.86 us (3%)
  other arithmetic  3.27 us (2%)
    ppermute x2, starting transfers between devices, rows_beside(): lax.ppermute(own, lat + ('core',), north)  23.6 us
    ppermute x6, starting transfers between devices, swap(): return lax.ppermute(v, 'core', [(0, 1), (1, 0)])  17.8 us
    ppermute x2, waiting for transfers between devices, rows_beside(): lax.ppermute(own, lat + ('core',), south)  14 us
    ppermute x3, waiting for transfers between devices, along(): return lax.ppermute(v, ('x', 'core'), perm)  10.8 us
    ppermute x3, starting transfers between devices, along(): return lax.ppermute(v, ('x', 'core'), perm)  9.95 us
    ppermute x2, waiting for transfers between devices, rows_beside(): lax.ppermute(own, lat + ('core',), north)  7.56 us
    pallas_call x1, Pallas kernels, on_device(): pl.pallas_call(project_kernel, out_shape=(shaped((9 * T, QKV)), shaped((6...  7.38 us
    ppermute x1, waiting for transfers between devices, on_device(): packs_outer = lax.ppermute(packs, lon, border)  6.46 us
  transfers between devices with their start and end apart: 17, of which 8 were waited for; matrix products, arithmetic and copies ran while one was open for 3% of the time, Pallas kernels for 6%

profile of v12, /device:TPU:48, one launch (start us, length us, event | category | flops | bytes accessed | tf_op | source)
XLA Modules:
  0.0 144.6 jit_solution(10528535521627733562)
XLA Ops:
  0.6 12.3 %collective-permute-start.3 = (bf16[128,1152]{1,0:T(8,128)(2,1)}, bf16[128,1152]{1,0:T(8,128)(2,1)S(1)}, u32[]{:S(2)}, u32[]{:S(2)}) collective-permute-start(bf16[128,1152]{1,0:T(8,128)(2,1)} %bitcast.7), channel_id=1, source_target_pairs={{32,0},{64,32},{96,64},{128,96},{160,128},{192,160},{224,192},{256... | collective-permute-start | bytes 884744 | tf_op jit(solution)/shard_map/ppermute | solution.py:371
  12.9 1.9 %collective-permute-start.2 = (bf16[128,1152]{1,0:T(8,128)(2,1)}, bf16[128,1152]{1,0:T(8,128)(2,1)S(1)}, u32[]{:S(2)}, u32[]{:S(2)}) collective-permute-start(bf16[128,1152]{1,0:T(8,128)(2,1)} %bitcast.8), channel_id=1, source_target_pairs={{0,32},{32,64},{64,96},{96,128},{128,160},{160,192},{192,224},{224... | collective-permute-start | bytes 884744 | tf_op jit(solution)/shard_map/ppermute | solution.py:371
  14.9 1.2 fusion.2
  16.1 1.9 %collective-permute-start.1 = (bf16[96,1728]{1,0:T(8,128)(2,1)S(1)}, bf16[96,1728]{1,0:T(8,128)(2,1)S(1)}, u32[]{:S(2)}, u32[]{:S(2)}) collective-permute-start(bf16[96,1728]{1,0:T(8,128)(2,1)S(1)} %fusion.2), channel_id=1, source_target_pairs={{440,0},{377,1},{474,2},{347,3},{508,4},{317,5},{286,6},{7,7},{432... | collective-permute-start | bytes 995336 | tf_op jit(solution)/shard_map/ppermute | solution.py:388
  18.0 3.4 %collective-permute-start = (bf16[96,1728]{1,0:T(8,128)(2,1)S(1)}, bf16[96,1728]{1,0:T(8,128)(2,1)S(1)}, u32[]{:S(2)}, u32[]{:S(2)}) collective-permute-start(bf16[96,1728]{1,0:T(8,128)(2,1)S(1)} %fusion.2), channel_id=1, source_target_pairs={{224,0},{33,1},{194,2},{67,3},{164,4},{101,5},{134,6},{415,7},{232... | collective-permute-start | bytes 995336 | tf_op jit(solution)/shard_map/ppermute | solution.py:388
  21.5 0.7 reshape.34.gain_ref
  22.2 0.8 fusion.15
  23.0 5.6 %collective-permute-done.3 = bf16[128,1152]{1,0:T(8,128)(2,1)S(1)} collective-permute-done((bf16[128,1152]{1,0:T(8,128)(2,1)}, bf16[128,1152]{1,0:T(8,128)(2,1)S(1)}, u32[]{:S(2)}, u32[]{:S(2)}) %collective-permute-start.3) | collective-permute-done | bytes 294944 | tf_op jit(solution)/shard_map/ppermute | solution.py:371
  28.6 4.4 %collective-permute-done.2 = bf16[128,1152]{1,0:T(8,128)(2,1)S(1)} collective-permute-done((bf16[128,1152]{1,0:T(8,128)(2,1)}, bf16[128,1152]{1,0:T(8,128)(2,1)S(1)}, u32[]{:S(2)}, u32[]{:S(2)}) %collective-permute-start.2) | collective-permute-done | bytes 294944 | tf_op jit(solution)/shard_map/ppermute | solution.py:371
  33.0 1.0 pad_maximum_fusion.x_ref
  34.0 1.9 %collective-permute-start.7 = (bf16[384,1152]{1,0:T(8,128)(2,1)S(1)}, bf16[384,1152]{1,0:T(8,128)(2,1)S(1)}, u32[]{:S(2)}, u32[]{:S(2)}) collective-permute-start(bf16[384,1152]{1,0:T(8,128)(2,1)S(1)} %pad_maximum_fusion.x_ref), channel_id=1, source_target_pairs={{1,2},{3,4},{5,6},{7,8},{9,10},{11,12},{13,14},{15,16},{17,18},{19... | collective-permute-start | bytes 2654216 | tf_op jit(solution)/shard_map/ppermute | solution.py:374
  35.9 5.6 %collective-permute-start.6 = (bf16[384,1152]{1,0:T(8,128)(2,1)S(1)}, bf16[384,1152]{1,0:T(8,128)(2,1)S(1)}, u32[]{:S(2)}, u32[]{:S(2)}) collective-permute-start(bf16[384,1152]{1,0:T(8,128)(2,1)S(1)} %pad_maximum_fusion.x_ref), channel_id=1, source_target_pairs={{0,1},{1,0},{2,3},{3,2},{4,5},{5,4},{6,7},{7,6},{8,9},{9,8},{10,11... | collective-permute-start | bytes 2654216 | tf_op jit(solution)/shard_map/ppermute | solution.py:365
  41.5 2.1 %shard_map.221.hc_ref = bf16[384,1152]{1,0:T(8,128)(2,1)S(1)} custom-call(bf16[384,1152]{1,0:T(8,128)(2,1)S(1)} %pad_maximum_fusion.x_ref, f32[1,1152]{1,0:T(1,128)S(1)} %reshape.34.gain_ref, s32[1,1152]{1,0:T(1,128)S(1)} %reshape.35.target_ref), custom_call_target="tpu_custom_call" | custom-call | flops 3000000000 | bytes 5000000 | tf_op jit(solution)/shard_map/pallas_call | solution.py:403
  43.6 0.9 copy-done.6
  44.6 0.1 pad_maximum_fusion.1.b0
  44.7 4.7 %collective-permute-start.5 = (bf16[192,1728]{1,0:T(8,128)(2,1)S(1)}, bf16[192,1728]{1,0:T(8,128)(2,1)S(1)}, u32[]{:S(2)}, u32[]{:S(2)}) collective-permute-start(bf16[192,1728]{1,0:T(8,128)(2,1)S(1)} %pad_maximum_fusion.1.b0), channel_id=1, source_target_pairs={{2,0},{4,2},{6,4},{0,6},{1,3},{3,5},{5,7},{7,1},{10,8},{12,10},{14... | collective-permute-start | bytes 1990664 | tf_op jit(solution)/shard_map/ppermute | solution.py:368
  49.4 1.9 %collective-permute-start.4 = (bf16[192,1728]{1,0:T(8,128)(2,1)S(1)}, bf16[192,1728]{1,0:T(8,128)(2,1)S(1)}, u32[]{:S(2)}, u32[]{:S(2)}) collective-permute-start(bf16[192,1728]{1,0:T(8,128)(2,1)S(1)} %pad_maximum_fusion.1.b0), channel_id=1, source_target_pairs={{0,2},{2,4},{4,6},{6,0},{3,1},{5,3},{7,5},{1,7},{8,10},{10,12},{12... | collective-permute-start | bytes 1990664 | tf_op jit(solution)/shard_map/ppermute | solution.py:368
  51.3 2.1 %shard_map.222.he_ref = bf16[384,1152]{1,0:T(8,128)(2,1)S(1)} custom-call(bf16[384,1152]{1,0:T(8,128)(2,1)S(1)} %collective-permute-done.6.x_ref, f32[1,1152]{1,0:T(1,128)S(1)} %reshape.34.gain_ref, s32[1,1152]{1,0:T(1,128)S(1)} %reshape.35.target_ref), custom_call_target="tpu_custom_call" | custom-call | flops 3000000000 | bytes 5000000 | tf_op jit(solution)/shard_map/pallas_call | solution.py:403
  53.5 0.9 copy-done.8
  54.4 9.7 %collective-permute-done.5.b2 = bf16[192,1728]{1,0:T(8,128)(2,1)S(1)} collective-permute-done((bf16[192,1728]{1,0:T(8,128)(2,1)S(1)}, bf16[192,1728]{1,0:T(8,128)(2,1)S(1)}, u32[]{:S(2)}, u32[]{:S(2)}) %collective-permute-start.5) | collective-permute-done | bytes 663584 | tf_op jit(solution)/shard_map/ppermute | solution.py:368
  64.0 1.2 collective-permute-done.4.b1
  65.2 0.9 copy-done.1
  66.1 3.3 %collective-permute-start.8 = (bf16[192,1728]{1,0:T(8,128)(2,1)S(1)}, bf16[192,1728]{1,0:T(8,128)(2,1)S(1)}, u32[]{:S(2)}, u32[]{:S(2)}) collective-permute-start(bf16[192,1728]{1,0:T(8,128)(2,1)S(1)} %collective-permute-done.4.b1), channel_id=1, source_target_pairs={{0,2},{2,4},{4,6},{6,0},{3,1},{5,3},{7,5},{1,7},{8,10},{10,12},{12... | collective-permute-start | bytes 1990664 | tf_op jit(solution)/shard_map/ppermute | solution.py:368
  69.5 0.0 copy-start.13
  69.5 0.0 copy-start.17
  69.6 0.1 reshape.31
  69.7 3.7 %collective-permute-start.9 = (bf16[192,1728]{1,0:T(8,128)(2,1)S(1)}, bf16[192,1728]{1,0:T(8,128)(2,1)S(1)}, u32[]{:S(2)}, u32[]{:S(2)}) collective-permute-start(bf16[192,1728]{1,0:T(8,128)(2,1)S(1)} %pad_maximum_fusion.1.b0), channel_id=1, source_target_pairs={{0,1},{1,0},{2,3},{3,2},{4,5},{5,4},{6,7},{7,6},{8,9},{9,8},{10,11... | collective-permute-start | bytes 1990664 | tf_op jit(solution)/shard_map/ppermute | solution.py:365
  73.4 1.9 %collective-permute-start.10 = (bf16[192,1728]{1,0:T(8,128)(2,1)S(1)}, bf16[192,1728]{1,0:T(8,128)(2,1)S(1)}, u32[]{:S(2)}, u32[]{:S(2)}) collective-permute-start(bf16[192,1728]{1,0:T(8,128)(2,1)S(1)} %collective-permute-done.4.b1), channel_id=1, source_target_pairs={{0,1},{1,0},{2,3},{3,2},{4,5},{5,4},{6,7},{7,6},{8,9},{9,8},{10,11... | collective-permute-start | bytes 1990664 | tf_op jit(solution)/shard_map/ppermute | solution.py:365
  75.3 2.4 %collective-permute-start.11 = (bf16[192,1728]{1,0:T(8,128)(2,1)S(1)}, bf16[192,1728]{1,0:T(8,128)(2,1)S(1)}, u32[]{:S(2)}, u32[]{:S(2)}) collective-permute-start(bf16[192,1728]{1,0:T(8,128)(2,1)S(1)} %collective-permute-done.5.b2), channel_id=1, source_target_pairs={{0,1},{1,0},{2,3},{3,2},{4,5},{5,4},{6,7},{7,6},{8,9},{9,8},{10,11... | collective-permute-start | bytes 1990664 | tf_op jit(solution)/shard_map/ppermute | solution.py:365
  77.7 1.2 copy-done.2
  78.9 2.1 %shard_map.223.hw_ref = bf16[384,1152]{1,0:T(8,128)(2,1)S(1)} custom-call(bf16[384,1152]{1,0:T(8,128)(2,1)S(1)} %copy-done.2, f32[1,1152]{1,0:T(1,128)S(1)} %reshape.34.gain_ref, s32[1,1152]{1,0:T(1,128)S(1)} %reshape.35.target_ref), custom_call_target="tpu_custom_call" | custom-call | flops 3000000000 | bytes 5000000 | tf_op jit(solution)/shard_map/pallas_call | solution.py:403
  81.0 2.1 %collective-permute-start.12 = (bf16[192,1728]{1,0:T(8,128)(2,1)S(1)}, bf16[192,1728]{1,0:T(8,128)(2,1)S(1)}, u32[]{:S(2)}, u32[]{:S(2)}) collective-permute-start(bf16[192,1728]{1,0:T(8,128)(2,1)S(1)} %collective-permute-done.8.b3), channel_id=1, source_target_pairs={{0,1},{1,0},{2,3},{3,2},{4,5},{5,4},{6,7},{7,6},{8,9},{9,8},{10,11... | collective-permute-start | bytes 1990664 | tf_op jit(solution)/shard_map/ppermute | solution.py:365
  83.3 0.1 pad_add_fusion.1.blocks_ref
  83.4 1.6 %collective-permute-done.12.b7 = bf16[192,1728]{1,0:T(8,128)(2,1)S(1)} collective-permute-done((bf16[192,1728]{1,0:T(8,128)(2,1)S(1)}, bf16[192,1728]{1,0:T(8,128)(2,1)S(1)}, u32[]{:S(2)}, u32[]{:S(2)}) %collective-permute-start.12) | collective-permute-done | bytes 663584 | tf_op jit(solution)/shard_map/ppermute | solution.py:365
  85.0 7.4 %shard_map.224 = (bf16[1152,1728]{1,0:T(8,128)(2,1)S(1)}, bf16[640,1152]{1,0:T(8,128)(2,1)S(1)}) custom-call(s32[3,384]{1,0:T(4,128)S(1)} %pad_add_fusion.place_ref, bf16[384,1152]{1,0:T(8,128)(2,1)S(1)} %shard_map.223.hw_ref, bf16[384,1152]{1,0:T(8,128)(2,1)S(1)} %copy-done.7, bf16[384,1152]{1,0:T(8,128)(2,1)S(1)} %copy-done.9, ...), custom_call_target="tpu_custom_call" | custom-call | flops 6000000000 | bytes 8000000 | tf_op jit(solution)/shard_map/pallas_call | solution.py:416
  92.5 5.6 %shard_map.225 = (bf16[1024,1152]{1,0:T(8,128)(2,1)S(1)}, bf16[128,1152]{1,0:T(8,128)(2,1)}, f32[128,1152]{1,0:T(8,128)S(1)}, bf16[144,640]{1,0:T(8,128)(2,1)S(1)}, f32[128,128]{1,0:T(8,128)S(1)}) custom-call(s32[31]{0:T(128)S(1)} %pad_add_fusion.1.blocks_ref, bf16[1152,1728]{1,0:T(8,128)(2,1)S(1)} %get-tuple-element.32.win_ref, ...), custom_call_target="tpu_custom_call" | custom-call | flops 6000000000 | bytes 8000000 | tf_op jit(solution)/shard_map/pallas_call | solution.py:423
  98.1 11.3 %collective-permute-start.14 = (bf16[144,640]{1,0:T(8,128)(2,1)S(1)}, bf16[144,640]{1,0:T(8,128)(2,1)S(1)}, u32[]{:S(2)}, u32[]{:S(2)}) collective-permute-start(bf16[144,640]{1,0:T(8,128)(2,1)S(1)} %get-tuple-element.35.up_ref), channel_id=1, source_target_pairs={{32,0},{64,32},{96,64},{128,96},{160,128},{192,160},{224,192},{256... | collective-permute-start | bytes 552968 | tf_op jit(solution)/shard_map/ppermute | solution.py:371
  109.4 1.9 %collective-permute-start.13 = (bf16[144,640]{1,0:T(8,128)(2,1)S(1)}, bf16[144,640]{1,0:T(8,128)(2,1)S(1)}, u32[]{:S(2)}, u32[]{:S(2)}) collective-permute-start(bf16[144,640]{1,0:T(8,128)(2,1)S(1)} %get-tuple-element.35.up_ref), channel_id=1, source_target_pairs={{0,32},{32,64},{64,96},{96,128},{128,160},{160,192},{192,224},{224... | collective-permute-start | bytes 552968 | tf_op jit(solution)/shard_map/ppermute | solution.py:371
  111.3 2.0 %collective-permute-done.14 = bf16[144,640]{1,0:T(8,128)(2,1)S(1)} collective-permute-done((bf16[144,640]{1,0:T(8,128)(2,1)S(1)}, bf16[144,640]{1,0:T(8,128)(2,1)S(1)}, u32[]{:S(2)}, u32[]{:S(2)}) %collective-permute-start.14) | collective-permute-done | bytes 184352 | tf_op jit(solution)/shard_map/ppermute | solution.py:371
  113.3 9.7 %collective-permute-done.13 = bf16[144,640]{1,0:T(8,128)(2,1)S(1)} collective-permute-done((bf16[144,640]{1,0:T(8,128)(2,1)S(1)}, bf16[144,640]{1,0:T(8,128)(2,1)S(1)}, u32[]{:S(2)}, u32[]{:S(2)}) %collective-permute-start.13) | collective-permute-done | bytes 184352 | tf_op jit(solution)/shard_map/ppermute | solution.py:371
  122.9 0.1 pad_maximum_fusion.2.own_ref
  123.0 1.8 %shard_map.226.gq_ref = bf16[128,576]{1,0:T(8,128)(2,1)S(1)} custom-call(bf16[1152,1728]{1,0:T(8,128)(2,1)S(1)} %get-tuple-element.32.win_ref, bf16[1024,1152]{1,0:T(8,128)(2,1)S(1)} %get-tuple-element.38.e_ref, bf16[144,640]{1,0:T(8,128)(2,1)S(1)} %get-tuple-element.35.up_ref, f32[128,128]{1,0:T(8,128)S(1)} %get-tuple-element.39.stat_ref), custom_call_target="tpu_custom_call" | custom-call | flops 4000000000 | bytes 6000000 | tf_op jit(solution)/shard_map/pallas_call | solution.py:436
  124.8 2.1 %collective-permute-start.16 = (bf16[432,640]{1,0:T(8,128)(2,1)S(1)}, bf16[432,640]{1,0:T(8,128)(2,1)S(1)}, u32[]{:S(2)}, u32[]{:S(2)}) collective-permute-start(bf16[432,640]{1,0:T(8,128)(2,1)S(1)} %pad_maximum_fusion.2.own_ref), channel_id=1, source_target_pairs={{0,1},{1,0},{2,3},{3,2},{4,5},{5,4},{6,7},{7,6},{8,9},{9,8},{10,11... | collective-permute-start | bytes 1658888 | tf_op jit(solution)/shard_map/ppermute | solution.py:365
  126.9 3.8 %collective-permute-start.15 = (bf16[432,640]{1,0:T(8,128)(2,1)S(1)}, bf16[432,640]{1,0:T(8,128)(2,1)S(1)}, u32[]{:S(2)}, u32[]{:S(2)}) collective-permute-start(bf16[432,640]{1,0:T(8,128)(2,1)S(1)} %pad_maximum_fusion.2.own_ref), channel_id=1, source_target_pairs={{1,2},{3,4},{5,6},{7,8},{9,10},{11,12},{13,14},{15,16},{17,18},{19... | collective-permute-start | bytes 1658888 | tf_op jit(solution)/shard_map/ppermute | solution.py:435
  130.7 0.5 shard_map.228.order_ref
  131.2 2.2 %shard_map.227 = (f32[128,640]{1,0:T(8,128)S(1)}, f32[128,640]{1,0:T(8,128)S(1)}) custom-call(s32[1]{0:T(128)} %bitcast.core_ref, bf16[1152,1728]{1,0:T(8,128)(2,1)S(1)} %get-tuple-element.32.win_ref, bf16[432,640]{1,0:T(8,128)(2,1)S(1)} %pad_maximum_fusion.2.own_ref, bf16[432,640]{1,0:T(8,128)(2,1)S(1)} %collective-permute-done.16.inner_ref), custom_call_target="tpu_custom_call" | custom-call | flops 4000000000 | bytes 6000000 | tf_op jit(solution)/shard_map/pallas_call | solution.py:443
  133.4 6.5 %collective-permute-done.15.outer_ref = bf16[432,640]{1,0:T(8,128)(2,1)S(1)} collective-permute-done((bf16[432,640]{1,0:T(8,128)(2,1)S(1)}, bf16[432,640]{1,0:T(8,128)(2,1)S(1)}, u32[]{:S(2)}, u32[]{:S(2)}) %collective-permute-start.15) | collective-permute-done | bytes 552992 | tf_op jit(solution)/shard_map/ppermute | solution.py:435
  139.8 4.7 %shard_map.229 = f32[128,1152]{1,0:T(8,128)} custom-call(s32[1]{0:T(128)} %bitcast.core_ref, bf16[1152,1728]{1,0:T(8,128)(2,1)S(1)} %get-tuple-element.32.win_ref, bf16[432,640]{1,0:T(8,128)(2,1)S(1)} %collective-permute-done.15.outer_ref, f32[128,640]{1,0:T(8,128)S(1)} %get-tuple-element.41.gk0_ref, f32[128,640]{1,0:T(8,128)S(1)} %get-tuple-element.42.gv0_ref, ...), custom_call_target="tpu_custom_call" | custom-call | tf_op jit(solution)/shard_map/pallas_call | solution.py:448
  (53 shorter events, 0.2 us)
Async XLA Ops:
  0.6 28.0 %collective-permute-start.3 = (bf16[128,1152]{1,0:T(8,128)(2,1)}, bf16[128,1152]{1,0:T(8,128)(2,1)S(1)}, u32[]{:S(2)}, u32[]{:S(2)}) collective-permute-start(bf16[128,1152]{1,0:T(8,128)(2,1)} %bitcast.7), channel_id=1, source_target_pairs={{32,0},{64,32},{96,64},{128,96},{160,128},{192,160},{224,192},{256... | collective-permute-start | bytes 884744 | tf_op jit(solution)/shard_map/ppermute | solution.py:371
  12.9 20.0 %collective-permute-start.2 = (bf16[128,1152]{1,0:T(8,128)(2,1)}, bf16[128,1152]{1,0:T(8,128)(2,1)S(1)}, u32[]{:S(2)}, u32[]{:S(2)}) collective-permute-start(bf16[128,1152]{1,0:T(8,128)(2,1)} %bitcast.8), channel_id=1, source_target_pairs={{0,32},{32,64},{64,96},{96,128},{128,160},{160,192},{192,224},{224... | collective-permute-start | bytes 884744 | tf_op jit(solution)/shard_map/ppermute | solution.py:371
  16.1 28.4 %collective-permute-start.1 = (bf16[96,1728]{1,0:T(8,128)(2,1)S(1)}, bf16[96,1728]{1,0:T(8,128)(2,1)S(1)}, u32[]{:S(2)}, u32[]{:S(2)}) collective-permute-start(bf16[96,1728]{1,0:T(8,128)(2,1)S(1)} %fusion.2), channel_id=1, source_target_pairs={{440,0},{377,1},{474,2},{347,3},{508,4},{317,5},{286,6},{7,7},{432... | collective-permute-start | bytes 995336 | tf_op jit(solution)/shard_map/ppermute | solution.py:388
  18.0 26.5 %collective-permute-start = (bf16[96,1728]{1,0:T(8,128)(2,1)S(1)}, bf16[96,1728]{1,0:T(8,128)(2,1)S(1)}, u32[]{:S(2)}, u32[]{:S(2)}) collective-permute-start(bf16[96,1728]{1,0:T(8,128)(2,1)S(1)} %fusion.2), channel_id=1, source_target_pairs={{224,0},{33,1},{194,2},{67,3},{164,4},{101,5},{134,6},{415,7},{232... | collective-permute-start | bytes 995336 | tf_op jit(solution)/shard_map/ppermute | solution.py:388
  34.0 31.2 %collective-permute-start.7 = (bf16[384,1152]{1,0:T(8,128)(2,1)S(1)}, bf16[384,1152]{1,0:T(8,128)(2,1)S(1)}, u32[]{:S(2)}, u32[]{:S(2)}) collective-permute-start(bf16[384,1152]{1,0:T(8,128)(2,1)S(1)} %pad_maximum_fusion.x_ref), channel_id=1, source_target_pairs={{1,2},{3,4},{5,6},{7,8},{9,10},{11,12},{13,14},{15,16},{17,18},{19... | collective-permute-start | bytes 2654216 | tf_op jit(solution)/shard_map/ppermute | solution.py:374
  35.9 15.4 %collective-permute-start.6 = (bf16[384,1152]{1,0:T(8,128)(2,1)S(1)}, bf16[384,1152]{1,0:T(8,128)(2,1)S(1)}, u32[]{:S(2)}, u32[]{:S(2)}) collective-permute-start(bf16[384,1152]{1,0:T(8,128)(2,1)S(1)} %pad_maximum_fusion.x_ref), channel_id=1, source_target_pairs={{0,1},{1,0},{2,3},{3,2},{4,5},{5,4},{6,7},{7,6},{8,9},{9,8},{10,11... | collective-permute-start | bytes 2654216 | tf_op jit(solution)/shard_map/ppermute | solution.py:365
  43.6 0.9 copy-start.6
  44.7 24.8 %copy-start.11 = (s32[1,2,3,5]{3,1,2,0:T(2,128)S(1)}, s32[1,2,3,5]{3,1,2,0:T(2,128)}, u32[]{:S(2)}) copy-start(s32[1,2,3,5]{3,1,2,0:T(2,128)} %param.31) | copy-start | bytes 364
  44.7 19.4 %collective-permute-start.5 = (bf16[192,1728]{1,0:T(8,128)(2,1)S(1)}, bf16[192,1728]{1,0:T(8,128)(2,1)S(1)}, u32[]{:S(2)}, u32[]{:S(2)}) collective-permute-start(bf16[192,1728]{1,0:T(8,128)(2,1)S(1)} %pad_maximum_fusion.1.b0), channel_id=1, source_target_pairs={{2,0},{4,2},{6,4},{0,6},{1,3},{3,5},{5,7},{7,1},{10,8},{12,10},{14... | collective-permute-start | bytes 1990664 | tf_op jit(solution)/shard_map/ppermute | solution.py:368
  49.4 15.8 %collective-permute-start.4 = (bf16[192,1728]{1,0:T(8,128)(2,1)S(1)}, bf16[192,1728]{1,0:T(8,128)(2,1)S(1)}, u32[]{:S(2)}, u32[]{:S(2)}) collective-permute-start(bf16[192,1728]{1,0:T(8,128)(2,1)S(1)} %pad_maximum_fusion.1.b0), channel_id=1, source_target_pairs={{0,2},{2,4},{4,6},{6,0},{3,1},{5,3},{7,5},{1,7},{8,10},{10,12},{12... | collective-permute-start | bytes 1990664 | tf_op jit(solution)/shard_map/ppermute | solution.py:368
  53.5 0.9 copy-start.8
  65.2 0.9 copy-start.1
  66.1 14.9 %collective-permute-start.8 = (bf16[192,1728]{1,0:T(8,128)(2,1)S(1)}, bf16[192,1728]{1,0:T(8,128)(2,1)S(1)}, u32[]{:S(2)}, u32[]{:S(2)}) collective-permute-start(bf16[192,1728]{1,0:T(8,128)(2,1)S(1)} %collective-permute-done.4.b1), channel_id=1, source_target_pairs={{0,2},{2,4},{4,6},{6,0},{3,1},{5,3},{7,5},{1,7},{8,10},{10,12},{12... | collective-permute-start | bytes 1990664 | tf_op jit(solution)/shard_map/ppermute | solution.py:368
  69.5 13.6 %copy-start.13 = (s32[384]{0:T(512)S(1)}, s32[384]{0:T(512)}, u32[]{:S(2)}) copy-start(s32[384]{0:T(512)} %constant.86.clone) | copy-start | bytes 4612
  69.5 13.6 %copy-start.14 = (s32[384]{0:T(512)S(1)}, s32[384]{0:T(512)}, u32[]{:S(2)}) copy-start(s32[384]{0:T(512)} %constant.85.clone) | copy-start | bytes 4612
  69.5 13.6 %copy-start.17 = (pred[384]{0:T(512)(128)(4,1)S(1)}, pred[384]{0:T(512)(128)(4,1)}, u32[]{:S(2)}) copy-start(pred[384]{0:T(512)(128)(4,1)} %constant.88.clone) | copy-start | bytes 1156
  69.5 13.7 %copy-start.16 = (pred[384]{0:T(512)(128)(4,1)S(1)}, pred[384]{0:T(512)(128)(4,1)}, u32[]{:S(2)}) copy-start(pred[384]{0:T(512)(128)(4,1)} %constant.90.clone) | copy-start | bytes 1156
  69.5 13.6 %copy-start.10 = (s32[384]{0:T(512)S(1)}, s32[384]{0:T(512)}, u32[]{:S(2)}) copy-start(s32[384]{0:T(512)} %constant.89.clone) | copy-start | bytes 4612
  69.6 13.6 %copy-start.12 = (s32[384]{0:T(512)S(1)}, s32[384]{0:T(512)}, u32[]{:S(2)}) copy-start(s32[384]{0:T(512)} %constant.87.clone) | copy-start | bytes 4612
  69.6 13.6 %copy-start.15 = (pred[384]{0:T(512)(128)(4,1)S(1)}, pred[384]{0:T(512)(128)(4,1)}, u32[]{:S(2)}) copy-start(pred[384]{0:T(512)(128)(4,1)} %constant.91.clone) | copy-start | bytes 1156
  69.7 13.7 %collective-permute-start.9 = (bf16[192,1728]{1,0:T(8,128)(2,1)S(1)}, bf16[192,1728]{1,0:T(8,128)(2,1)S(1)}, u32[]{:S(2)}, u32[]{:S(2)}) collective-permute-start(bf16[192,1728]{1,0:T(8,128)(2,1)S(1)} %pad_maximum_fusion.1.b0), channel_id=1, source_target_pairs={{0,1},{1,0},{2,3},{3,2},{4,5},{5,4},{6,7},{7,6},{8,9},{9,8},{10,11... | collective-permute-start | bytes 1990664 | tf_op jit(solution)/shard_map/ppermute | solution.py:365
  73.4 10.1 %collective-permute-start.10 = (bf16[192,1728]{1,0:T(8,128)(2,1)S(1)}, bf16[192,1728]{1,0:T(8,128)(2,1)S(1)}, u32[]{:S(2)}, u32[]{:S(2)}) collective-permute-start(bf16[192,1728]{1,0:T(8,128)(2,1)S(1)} %collective-permute-done.4.b1), channel_id=1, source_target_pairs={{0,1},{1,0},{2,3},{3,2},{4,5},{5,4},{6,7},{7,6},{8,9},{9,8},{10,11... | collective-permute-start | bytes 1990664 | tf_op jit(solution)/shard_map/ppermute | solution.py:365
  75.3 8.1 %collective-permute-start.11 = (bf16[192,1728]{1,0:T(8,128)(2,1)S(1)}, bf16[192,1728]{1,0:T(8,128)(2,1)S(1)}, u32[]{:S(2)}, u32[]{:S(2)}) collective-permute-start(bf16[192,1728]{1,0:T(8,128)(2,1)S(1)} %collective-permute-done.5.b2), channel_id=1, source_target_pairs={{0,1},{1,0},{2,3},{3,2},{4,5},{5,4},{6,7},{7,6},{8,9},{9,8},{10,11... | collective-permute-start | bytes 1990664 | tf_op jit(solution)/shard_map/ppermute | solution.py:365
  77.7 1.2 copy-start.2
  78.9 6.2 %copy-start.7 = (bf16[384,1152]{1,0:T(8,128)(2,1)S(1)}, bf16[384,1152]{1,0:T(8,128)(2,1)}, u32[]{:S(2)}) copy-start(bf16[384,1152]{1,0:T(8,128)(2,1)} %copy-done.6) | copy-start | bytes 2654212
  78.9 6.2 %copy-start.9 = (bf16[384,1152]{1,0:T(8,128)(2,1)S(1)}, bf16[384,1152]{1,0:T(8,128)(2,1)}, u32[]{:S(2)}) copy-start(bf16[384,1152]{1,0:T(8,128)(2,1)} %copy-done.8) | copy-start | bytes 2654212
  81.0 4.0 %collective-permute-start.12 = (bf16[192,1728]{1,0:T(8,128)(2,1)S(1)}, bf16[192,1728]{1,0:T(8,128)(2,1)S(1)}, u32[]{:S(2)}, u32[]{:S(2)}) collective-permute-start(bf16[192,1728]{1,0:T(8,128)(2,1)S(1)} %collective-permute-done.8.b3), channel_id=1, source_target_pairs={{0,1},{1,0},{2,3},{3,2},{4,5},{5,4},{6,7},{7,6},{8,9},{9,8},{10,11... | collective-permute-start | bytes 1990664 | tf_op jit(solution)/shard_map/ppermute | solution.py:365
  83.3 9.1 %copy-start = (bf16[8,16,1152]{2,1,0:T(8,128)(2,1)S(1)}, bf16[8,16,1152]{2,1,0:T(8,128)(2,1)}, u32[]{:S(2)}) copy-start(bf16[8,16,1152]{2,1,0:T(8,128)(2,1)} %param.22) | copy-start | bytes 884740
  83.4 9.1 %copy-start.3 = (bf16[1152,192]{0,1:T(8,128)(2,1)S(1)}, bf16[1152,192]{0,1:T(8,128)(2,1)}, u32[]{:S(2)}) copy-start(bf16[1152,192]{0,1:T(8,128)(2,1)} %param.28) | copy-start | bytes 1327108
  83.4 9.1 %copy-start.4 = (f32[8,16,64]{2,1,0:T(8,128)S(1)}, f32[8,16,64]{2,1,0:T(8,128)}, u32[]{:S(2)}) copy-start(f32[8,16,64]{2,1,0:T(8,128)} %param.29) | copy-start | bytes 98308
  83.4 9.1 %copy-start.5 = (s32[8,16,64]{2,1,0:T(8,128)S(1)}, s32[8,16,64]{2,1,0:T(8,128)}, u32[]{:S(2)}) copy-start(s32[8,16,64]{2,1,0:T(8,128)} %param.30) | copy-start | bytes 98308
  98.1 15.2 %collective-permute-start.14 = (bf16[144,640]{1,0:T(8,128)(2,1)S(1)}, bf16[144,640]{1,0:T(8,128)(2,1)S(1)}, u32[]{:S(2)}, u32[]{:S(2)}) collective-permute-start(bf16[144,640]{1,0:T(8,128)(2,1)S(1)} %get-tuple-element.35.up_ref), channel_id=1, source_target_pairs={{32,0},{64,32},{96,64},{128,96},{160,128},{192,160},{224,192},{256... | collective-permute-start | bytes 552968 | tf_op jit(solution)/shard_map/ppermute | solution.py:371
  109.4 13.5 %collective-permute-start.13 = (bf16[144,640]{1,0:T(8,128)(2,1)S(1)}, bf16[144,640]{1,0:T(8,128)(2,1)S(1)}, u32[]{:S(2)}, u32[]{:S(2)}) collective-permute-start(bf16[144,640]{1,0:T(8,128)(2,1)S(1)} %get-tuple-element.35.up_ref), channel_id=1, source_target_pairs={{0,32},{32,64},{64,96},{96,128},{128,160},{160,192},{192,224},{224... | collective-permute-start | bytes 552968 | tf_op jit(solution)/shard_map/ppermute | solution.py:371
  124.8 6.4 %collective-permute-start.16 = (bf16[432,640]{1,0:T(8,128)(2,1)S(1)}, bf16[432,640]{1,0:T(8,128)(2,1)S(1)}, u32[]{:S(2)}, u32[]{:S(2)}) collective-permute-start(bf16[432,640]{1,0:T(8,128)(2,1)S(1)} %pad_maximum_fusion.2.own_ref), channel_id=1, source_target_pairs={{0,1},{1,0},{2,3},{3,2},{4,5},{5,4},{6,7},{7,6},{8,9},{9,8},{10,11... | collective-permute-start | bytes 1658888 | tf_op jit(solution)/shard_map/ppermute | solution.py:365
  126.9 12.9 %collective-permute-start.15 = (bf16[432,640]{1,0:T(8,128)(2,1)S(1)}, bf16[432,640]{1,0:T(8,128)(2,1)S(1)}, u32[]{:S(2)}, u32[]{:S(2)}) collective-permute-start(bf16[432,640]{1,0:T(8,128)(2,1)S(1)} %pad_maximum_fusion.2.own_ref), channel_id=1, source_target_pairs={{1,2},{3,4},{5,6},{7,8},{9,10},{11,12},{13,14},{15,16},{17,18},{19... | collective-permute-start | bytes 1658888 | tf_op jit(solution)/shard_map/ppermute | solution.py:435
